TPU v7x, 256 devices: a whole 4x4x8 slice. The times are simulated.
256 devices in a mesh: frames: 128 (over z, y, x_hi, core), mp: 2 (over x_lo).
Axes of the slice: x: 4 (x_hi: 2, x_lo: 2; x = x_hi * 2 + x_lo), y: 4, z: 8, core: 2. Of those that a mesh axis runs over, the one named last changes fastest.
Arguments:
- normed: bfloat16 [128, 512, 1536], P('frames'), may hold values from -24 to 24
- out_grad: bfloat16 [128, 512, 768], P('frames', None, 'mp'), may hold values from -24 to 24
- w_qkv: bfloat16 [1536, 3, 768], P('frames', None, 'mp'), may hold values from -0.15625 to 0.15625
Outputs:
- input_grad: bfloat16 [128, 512, 1536], P('frames', None, 'mp')
- weight_grad: float32 [1536, 3, 768], P('frames', None, 'mp')
All inputs are finite; a program needn't handle non-finite values.
Results may differ from a plain program's by a relative error of at most 0.012.
Values may be sent and summed in bfloat16 or wider, within the bound.
No kernel may reach another device: no remote copies, remote signals or barrier semaphores. Data moves between devices by JAX's collectives and lax.ppermute only.
A program may use at most 128 MiB of HBM per device.

v0:
```python
import jax
import jax.numpy as jnp
from jax import lax
from jax.experimental import pallas as pl
from jax.experimental.pallas import tpu as pltpu
from jax.sharding import Mesh, PartitionSpec as P

HEAD_DIM = 64
Z, Y, XH, C, MP = 8, 4, 2, 2, 2
F = 128
ROWS = 12
bf16, f32 = jnp.bfloat16, jnp.float32
NT = (((1,), (1,)), ((), ()))
TN = (((0,), (0,)), ((), ()))


def dot(a, b, dims):
    return lax.dot_general(a, b, dims, preferred_element_type=f32)


def assemble_kernel(where_ref, mine_ref, rest_ref, w_ref):
    y, c = where_ref[1], where_ref[2]
    for z in range(Z):
        for by in range(Y):
            a = mine_ref[z, by].astype(f32)
            b = rest_ref[z, by].astype(f32)
            first = jnp.where(c == 0, a, b)
            second = jnp.where(c == 0, b, a)
            rows = [first[:ROWS], second[:ROWS], first[ROWS:], second[ROWS:]]
            w_ref[z * Y + lax.rem(by + y, Y)] = jnp.concatenate(rows, 0).astype(bf16)


def assemble(where, mine, rest):
    n = mine.shape[-1]
    vm = pl.BlockSpec(memory_space=pltpu.VMEM)
    return pl.pallas_call(
        assemble_kernel,
        out_shape=jax.ShapeDtypeStruct((Z * Y, XH * C * ROWS, n), bf16),
        in_specs=[pl.BlockSpec(memory_space=pltpu.SMEM), vm, vm],
        out_specs=vm,
        compiler_params=pltpu.CompilerParams(vmem_limit_bytes=40 * 2**20),
        cost_estimate=pl.CostEstimate(flops=0, bytes_accessed=8 * 2**20, transcendentals=0),
        name="assemble_weight",
    )(where, mine, rest)


def core_kernel(where_ref, t_ref, o_ref, w_ref, g_ref, give_ref, keep_ref, s_ref):
    part_cols = o_ref.shape[1]
    rows, half = t_ref.shape[0], t_ref.shape[1] - part_cols
    count = rows // F
    scale = HEAD_DIM ** (-0.5)
    pairs = half // 128
    m = where_ref[3]
    near = pl.ds(pl.multiple_of(m * part_cols, part_cols), part_cols)
    away = pl.ds(pl.multiple_of((1 - m) * part_cols, part_cols), part_cols)
    for j in range(3):
        cols = slice(j * half, (j + 1) * half)
        part = jnp.dot(t_ref[:, :part_cols], w_ref[near, cols], preferred_element_type=f32)
        part += jnp.dot(o_ref[...], w_ref[away, cols], preferred_element_type=f32)
        part = part.astype(bf16)
        for pair in range(pairs):
            s_ref[j * pairs + pair] = part[:, pair * 128 : (pair + 1) * 128].astype(f32)
    for pair in range(pairs):
        at = part_cols + pair * 128
        s_ref[3 * pairs + pair] = t_ref[:, at : at + 128].astype(f32)
    low = lax.broadcasted_iota(jnp.int32, (F, 128), 1) < HEAD_DIM
    zero = jnp.zeros((F, 128), f32)

    def split(v):
        return jnp.concatenate([jnp.where(low, v, zero), jnp.where(low, zero, v)], 0).astype(bf16)

    for p in range(count):
        at = pl.ds(p, F, stride=count)
        for pair in range(pairs):
            q, k, v, u = (s_ref[j * pairs + pair, at, :] for j in range(4))
            q2 = split(q * scale)
            u2 = split(u)
            k = k.astype(bf16)
            v = v.astype(bf16)
            weights = jnp.exp(dot(q2, k, NT))
            weights = weights / jnp.sum(weights, axis=-1, keepdims=True)
            dprobs = dot(u2, v, NT)
            center = jnp.sum(weights * dprobs, axis=-1, keepdims=True)
            dscores = (weights * (dprobs - center)).astype(bf16)
            dv = dot(weights.astype(bf16), u2, TN)
            dk = dot(dscores, q2, TN)
            both = jnp.dot(dscores, k, preferred_element_type=f32) * scale
            dq = jnp.where(low, both[:F], both[F:])
            for j, part in enumerate((dq, dk, dv)):
                s_ref[j * pairs + pair, at, :] = part
    g = jnp.concatenate([s_ref[i] for i in range(3 * pairs)], 1).astype(bf16)
    g_ref[...] = g
    give_ref[...] = dot(g, w_ref[away, :], NT).astype(bf16)
    keep_ref[...] = dot(g, w_ref[near, :], NT).astype(bf16)


def core(where, tokens, others, w):
    rows, part_cols = others.shape
    half = tokens.shape[1] - part_cols
    vm = pl.BlockSpec(memory_space=pltpu.VMEM)
    return pl.pallas_call(
        core_kernel,
        out_shape=(
            jax.ShapeDtypeStruct((rows, 3 * half), bf16),
            jax.ShapeDtypeStruct((rows, part_cols), bf16),
            jax.ShapeDtypeStruct((rows, part_cols), bf16),
        ),
        in_specs=[pl.BlockSpec(memory_space=pltpu.SMEM)] + [vm] * 3,
        out_specs=(vm, vm, vm),
        scratch_shapes=[pltpu.VMEM((4 * half // 128, rows, 128), f32)],
        compiler_params=pltpu.CompilerParams(vmem_limit_bytes=48 * 2**20),
        cost_estimate=pl.CostEstimate(
            flops=4 * rows * w.shape[0] * 3 * half, bytes_accessed=8 * 2**20, transcendentals=0
        ),
        name="attention_core",
    )(where, tokens, others, w)


def term_kernel(where_ref, t_ref, o_ref, g_ref, mine_ref, rest_ref):
    z, y, c, m = (where_ref[i] for i in range(4))
    part_cols = o_ref.shape[1]
    step, unit = 384, XH * C * ROWS
    g = g_ref[...]
    for ref, of in ((t_ref, m), (o_ref, 1 - m)):
        for i in range(part_cols // step):
            total = dot(ref[:, i * step : (i + 1) * step], g, TN)
            for b in range(step // unit):
                quarters = [total[b * unit + r * ROWS :][:ROWS] for r in range(4)]
                first = jnp.concatenate([quarters[0], quarters[2]], 0)
                second = jnp.concatenate([quarters[1], quarters[3]], 0)
                by = lax.rem(b % Y + Y - y, Y)
                at = (i * step // unit + b) // Y
                t = lax.rem(of * (Z // MP) + at + Z - z, Z)
                mine_ref[by, t] = jnp.where(c == 0, first, second).astype(bf16)
                rest_ref[by, t] = jnp.where(c == 0, second, first).astype(bf16)


def terms(where, tokens, others, grads):
    n = grads.shape[1]
    vm = pl.BlockSpec(memory_space=pltpu.VMEM)
    shape = jax.ShapeDtypeStruct((Y, Z, XH * ROWS, n), bf16)
    return pl.pallas_call(
        term_kernel,
        out_shape=(shape, shape),
        in_specs=[pl.BlockSpec(memory_space=pltpu.SMEM)] + [vm] * 3,
        out_specs=(vm, vm),
        compiler_params=pltpu.CompilerParams(vmem_limit_bytes=48 * 2**20),
        cost_estimate=pl.CostEstimate(
            flops=2 * 512 * 1536 * n, bytes_accessed=8 * 2**20, transcendentals=0
        ),
        name="weight_terms",
    )(where, tokens, others, grads)


FR = ("z", "y", "xh", "c")
PAIR = [(0, 1), (1, 0)]


def shift(x, axis, size, by):
    return lax.ppermute(x, axis, [(i, (i + by) % size) for i in range(size)])


def gather_weight(w):
    xh = lax.axis_index("xh")
    other = lax.ppermute(w, "xh", PAIR)
    block = jnp.where(xh == 0, jnp.concatenate([w, other], 0), jnp.concatenate([other, w], 0))
    over_y = jnp.stack([block] + [shift(block, "y", Y, Y - t) for t in range(1, Y)], 0)
    return lax.all_gather(over_y, "z", axis=0)


def reduce_weight(mine, rest, early, late):
    xh = lax.axis_index("xh")
    got = lax.ppermute(rest, "c", PAIR)
    h = Z // 2
    own, after, far, before = (mine[i].astype(f32) + got[i].astype(f32) for i in range(Y))
    up_far = shift(far[:h].astype(bf16), "y", Y, 1)
    down_far = shift(far[h:].astype(bf16), "y", Y, Y - 1)
    up_high = shift(after[h:].astype(bf16), "y", Y, 1)
    down_low = shift(before[:h].astype(bf16), "y", Y, Y - 1)
    up_low = (after[:h] + up_far.astype(f32)).astype(bf16)
    down_high = (before[h:] + down_far.astype(f32)).astype(bf16)
    up_low, down_high, early = lax.optimization_barrier((up_low, down_high, early))
    up_low = shift(up_low, "y", Y, 1)
    down_high = shift(down_high, "y", Y, Y - 1)
    low = own[:h] + up_low.astype(f32) + down_low.astype(f32)
    high = own[h:] + up_high.astype(f32) + down_high.astype(f32)
    blocks = [low[i] for i in range(h)] + [high[i] for i in range(h)]
    total = blocks[0]
    for t in range(1, Z):
        total = total + shift(blocks[t].astype(bf16), "z", Z, t).astype(f32)
    back = late(early)
    total, back = lax.optimization_barrier((total, back))
    first, second = total[:ROWS], total[ROWS:]
    moved = lax.ppermute(jnp.where(xh == 0, second, first), "xh", PAIR)
    return jnp.where(xh == 0, first, second) + moved, back


def on_device(normed, out_grad, w_qkv):
    frames_dev, patches, width = normed.shape
    half = out_grad.shape[2]
    cols = width // MP
    count = patches // F
    n = 3 * half
    where = jnp.stack([lax.axis_index(a) for a in ("z", "y", "c", "mp")]).astype(jnp.int32)
    m = lax.axis_index("mp")
    part = lax.dynamic_slice_in_dim(normed, m * cols, cols, 2)
    tokens = jnp.concatenate([part, out_grad], axis=2).reshape(F, count, cols + half)

    mine = gather_weight(w_qkv.reshape(w_qkv.shape[0], n))
    tokens = lax.all_to_all(tokens, FR, 0, 0, tiled=True)
    others = lax.ppermute(tokens[:, :, :cols], "mp", PAIR).reshape(F * count, cols)
    tokens = tokens.reshape(F * count, cols + half)
    weight = assemble(where, mine, lax.ppermute(mine, "c", PAIR)).reshape(width, n)

    grads, give, keep = core(where, tokens, others, weight)
    got = lax.ppermute(give, "mp", PAIR)
    summed = (keep.astype(f32) + got.astype(f32)).astype(bf16)

    def to_frames(x):
        return lax.all_to_all(x.reshape(F, count, cols), FR, 0, 0, tiled=True)

    mine, rest = terms(where, tokens, others, grads)
    weight_grad, back = reduce_weight(mine, rest, summed, to_frames)
    input_grad = back.reshape(frames_dev, patches, cols)
    weight_grad = weight_grad * (1.0 / F)
    return (input_grad, weight_grad.reshape(w_qkv.shape))


def solution(mesh):
    fine = Mesh(mesh.devices.reshape(Z, Y, XH, C, MP), ("z", "y", "xh", "c", "mp"))
    in_specs = (P(FR, None, None), P(FR, None, "mp"), P(FR, None, "mp"))
    out_specs = (P(FR, None, "mp"), P(FR, None, "mp"))
    return jax.shard_map(
        on_device, mesh=fine, in_specs=in_specs, out_specs=out_specs, check_vma=False
    )
```

profile of v0, /device:TPU:6, one launch (start us, length us, event | category | flops | bytes accessed | tf_op | source)
XLA Modules:
  0.0 220.9 jit_solution(8164552215190979312)
XLA Ops:
  7.2 0.9 pad.18
  8.2 1.5 collective-permute-start.1
  9.7 0.8 concatenate.32
  10.5 3.2 %collective-permute-done.1 = bf16[12,1152]{1,0:T(8,128)(2,1)S(1)} collective-permute-done((bf16[12,1152]{1,0:T(8,128)(2,1)S(1)}, bf16[12,1152]{1,0:T(8,128)(2,1)S(1)}, u32[]{:S(2)}, u32[]{:S(2)}) %collective-permute-start.1) | collective-permute-done | bytes 27680 | tf_op jit(solution)/shard_map/ppermute | solution.py:165
  13.8 3.1 %collective-permute-start.2 = (bf16[24,1152]{1,0:T(8,128)(2,1)S(1)}, bf16[24,1152]{1,0:T(8,128)(2,1)S(1)}, u32[]{:S(2)}, u32[]{:S(2)}) collective-permute-start(bf16[24,1152]{1,0:T(8,128)(2,1)S(1)} %maximum_select_fusion.1), channel_id=1, source_target_pairs={{0,24},{8,0},{16,8},{24,16},{1,25},{9,1},{17,9},{25,17},{2,26},{10... | collective-permute-start | bytes 165896 | tf_op jit(solution)/shard_map/ppermute | solution.py:160
  16.8 0.6 collective-permute-start.3
  17.5 1.0 collective-permute-start.4
  18.7 3.9 %collective-permute-done.3 = bf16[24,1152]{1,0:T(8,128)(2,1)S(1)} collective-permute-done((bf16[24,1152]{1,0:T(8,128)(2,1)S(1)}, bf16[24,1152]{1,0:T(8,128)(2,1)S(1)}, u32[]{:S(2)}, u32[]{:S(2)}) %collective-permute-start.3) | collective-permute-done | bytes 55328 | tf_op jit(solution)/shard_map/ppermute | solution.py:160
  22.5 0.6 collective-permute-done.4
  23.1 0.7 pad_maximum_fusion.1
  24.0 1.2 reshape.116
  25.2 13.6 %all-to-all-start = ((bf16[128,4,1152]{2,1,0:T(4,128)(2,1)}), bf16[128,4,1152]{2,1,0:T(4,128)(2,1)S(1)}, u32[]{:S(2)}, u32[]{:S(2)}) async-start(bf16[128,4,1152]{2,1,0:T(4,128)(2,1)} %reshape.116), calls=%async_computation | async-start | bytes 2359296 | tf_op jit(solution)/shard_map/all_to_all | solution.py:210
  38.9 45.0 %all-gather.3.cloned.1.call-done = bf16[32,24,1152]{2,1,0:T(8,128)(2,1)} async-done(((bf16[4,24,1152]{2,1,0:T(8,128)(2,1)}), bf16[32,24,1152]{2,1,0:T(8,128)(2,1)}) %all-gather.3.cloned.1.call-update) | async-done | bytes 1769488 | tf_op jit(solution)/shard_map/all_gather | solution.py:168
  83.9 1.3 slice.139
  85.1 0.8 collective-permute-start
  86.0 3.3 %reshape.117.t_ref = bf16[512,1152]{1,0:T(8,128)(2,1)} reshape(bf16[128,4,1152]{2,1,0:T(4,128)(2,1)} %copy-done.5) | data formatting | bytes 2359296 | tf_op jit(solution)/shard_map/reshape | solution.py:212
  89.3 16.1 %collective-permute-done = bf16[128,4,768]{2,1,0:T(4,128)(2,1)} collective-permute-done((bf16[128,4,768]{2,1,0:T(4,128)(2,1)}, bf16[128,4,768]{2,1,0:T(4,128)(2,1)}, u32[]{:S(2)}, u32[]{:S(2)}) %collective-permute-start) | collective-permute-done | bytes 786464 | tf_op jit(solution)/shard_map/ppermute | solution.py:211
  105.4 2.3 %reshape.118.o_ref = bf16[512,768]{1,0:T(8,128)(2,1)} reshape(bf16[128,4,768]{2,1,0:T(4,128)(2,1)} %collective-permute-done) | data formatting | bytes 1572864 | tf_op jit(solution)/shard_map/reshape | solution.py:211
  107.7 2.5 %assemble_weight.1 = bf16[32,48,1152]{2,1,0:T(8,128)(2,1)S(1)} custom-call(s32[4]{0:T(128)S(1)} %pad_add_fusion.where_ref, bf16[8,4,24,1152]{3,2,1,0:T(8,128)(2,1)S(1)} %bitcast.80, bf16[8,4,24,1152]{3,2,1,0:T(8,128)(2,1)} %collective-permute-done.5.rest_ref), custom_call_target="tpu_custom_call" | custom-call | bytes 8388608 | tf_op jit(solution)/shard_map/assemble_weight/pallas_call | solution.py:36
  110.2 1.7 copy-done.1
  111.9 11.7 %attention_core.1 = (bf16[512,1152]{1,0:T(8,128)(2,1)S(1)}, bf16[512,768]{1,0:T(8,128)(2,1)S(1)}, bf16[512,768]{1,0:T(8,128)(2,1)S(1)}) custom-call(s32[4]{0:T(128)S(1)} %pad_add_fusion.where_ref, bf16[512,1152]{1,0:T(8,128)(2,1)S(1)} %copy-done.3, bf16[512,768]{1,0:T(8,128)(2,1)S(1)} %copy-done.4, bf16[1536,1152]{1,0:T(8,128)(2,1)} %bitcast.78), custom_call_target="tpu_custom_call" | custom-call | flops 3623878656 | bytes 8388608 | tf_op jit(solution)/shard_map/attention_core/pallas_call | solution.py:101
  123.6 4.0 %weight_terms.1 = (bf16[4,8,24,1152]{3,2,1,0:T(8,128)(2,1)S(1)}, bf16[4,8,24,1152]{3,2,1,0:T(8,128)(2,1)}) custom-call(s32[4]{0:T(128)S(1)} %pad_add_fusion.where_ref, bf16[512,1152]{1,0:T(8,128)(2,1)S(1)} %copy-done.3, bf16[512,768]{1,0:T(8,128)(2,1)S(1)} %copy-done.4, bf16[512,1152]{1,0:T(8,128)(2,1)S(1)} %get-tuple-element.12.g_ref), custom_call_target="tpu_custom_call" | custom-call | flops 1811939328 | bytes 8388608 | tf_op jit(solution)/shard_map/weight_terms/pallas_call | solution.py:142
  127.6 0.8 collective-permute-start.9
  128.5 19.1 %collective-permute-done.9 = bf16[512,768]{1,0:T(8,128)(2,1)S(1)} collective-permute-done((bf16[512,768]{1,0:T(8,128)(2,1)S(1)}, bf16[512,768]{1,0:T(8,128)(2,1)S(1)}, u32[]{:S(2)}, u32[]{:S(2)}) %collective-permute-start.9) | collective-permute-done | bytes 786464 | tf_op jit(solution)/shard_map/ppermute | solution.py:216
  148.2 3.0 %collective-permute-start.8 = (bf16[4,24,1152]{2,1,0:T(8,128)(2,1)S(1)}, bf16[4,24,1152]{2,1,0:T(8,128)(2,1)S(1)}, u32[]{:S(2)}, u32[]{:S(2)}) collective-permute-start(bf16[4,24,1152]{2,1,0:T(8,128)(2,1)S(1)} %get-tuple-element.29), channel_id=1, source_target_pairs={{0,24},{8,0},{16,8},{24,16},{1,25},{9,1},{17,9},{25,17},{2,26},{10... | collective-permute-start | bytes 663560 | tf_op jit(solution)/shard_map/ppermute | solution.py:160
  151.2 0.7 fusion.9
  151.9 3.2 %collective-permute-start.11 = (bf16[4,24,1152]{2,1,0:T(8,128)(2,1)}, bf16[4,24,1152]{2,1,0:T(8,128)(2,1)}, u32[]{:S(2)}, u32[]{:S(2)}) collective-permute-start(bf16[4,24,1152]{2,1,0:T(8,128)(2,1)} %fusion.9), channel_id=1, source_target_pairs={{0,24},{8,0},{16,8},{24,16},{1,25},{9,1},{17,9},{25,17},{2,26},{10... | collective-permute-start | bytes 663560 | tf_op jit(solution)/shard_map/ppermute | solution.py:160
  155.2 0.7 fusion.10
  155.9 1.0 collective-permute-done.8
  156.9 2.6 %collective-permute-done.7 = bf16[4,24,1152]{2,1,0:T(8,128)(2,1)S(1)} collective-permute-done((bf16[4,24,1152]{2,1,0:T(8,128)(2,1)S(1)}, bf16[4,24,1152]{2,1,0:T(8,128)(2,1)S(1)}, u32[]{:S(2)}, u32[]{:S(2)}) %collective-permute-start.7) | collective-permute-done | bytes 221216 | tf_op jit(solution)/shard_map/ppermute | solution.py:160
  159.6 0.7 fusion.6
  160.3 3.2 %collective-permute-start.16 = (bf16[4,24,1152]{2,1,0:T(8,128)(2,1)S(1)}, bf16[4,24,1152]{2,1,0:T(8,128)(2,1)}, u32[]{:S(2)}, u32[]{:S(2)}) collective-permute-start(bf16[4,24,1152]{2,1,0:T(8,128)(2,1)S(1)} %fusion.4), channel_id=1, source_target_pairs={{0,24},{8,0},{16,8},{24,16},{1,25},{9,1},{17,9},{25,17},{2,26},{10... | collective-permute-start | bytes 663560 | tf_op jit(solution)/shard_map/ppermute | solution.py:160
  163.6 1.1 reshape.121
  164.6 8.8 %all-to-all-start.1 = ((bf16[128,4,768]{2,1,0:T(4,128)(2,1)}), bf16[128,4,768]{2,1,0:T(4,128)(2,1)S(1)}, u32[]{:S(2)}, u32[]{:S(2)}) async-start(bf16[128,4,768]{2,1,0:T(4,128)(2,1)} %reshape.121), calls=%async_computation.1 | async-start | bytes 1572864 | tf_op jit(solution)/shard_map/all_to_all | solution.py:220
  173.5 1.4 fusion.18
  174.9 5.8 %collective-permute-start.17 = (bf16[24,1152]{1,0:T(8,128)(2,1)S(1)}, bf16[24,1152]{1,0:T(8,128)(2,1)S(1)}, u32[]{:S(2)}, u32[]{:S(2)}) collective-permute-start(bf16[24,1152]{1,0:T(8,128)(2,1)S(1)} %get-tuple-element.34), channel_id=1, source_target_pairs={{0,128},{32,160},{64,192},{96,224},{128,0},{160,32},{192,64},{224,... | collective-permute-start | bytes 165896 | tf_op jit(solution)/shard_map/ppermute | solution.py:160
  180.9 3.3 %collective-permute-start.19 = (bf16[24,1152]{1,0:T(8,128)(2,1)S(1)}, bf16[24,1152]{1,0:T(8,128)(2,1)S(1)}, u32[]{:S(2)}, u32[]{:S(2)}) collective-permute-start(bf16[24,1152]{1,0:T(8,128)(2,1)S(1)} %get-tuple-element.36), channel_id=1, source_target_pairs={{0,192},{32,224},{64,0},{96,32},{128,64},{160,96},{192,128},{224,1... | collective-permute-start | bytes 165896 | tf_op jit(solution)/shard_map/ppermute | solution.py:160
  184.3 1.4 collective-permute-start.20
  185.6 0.7 collective-permute-start.12
  186.4 12.5 %collective-permute-done.17 = bf16[24,1152]{1,0:T(8,128)(2,1)S(1)} collective-permute-done((bf16[24,1152]{1,0:T(8,128)(2,1)S(1)}, bf16[24,1152]{1,0:T(8,128)(2,1)S(1)}, u32[]{:S(2)}, u32[]{:S(2)}) %collective-permute-start.17) | collective-permute-done | bytes 55328 | tf_op jit(solution)/shard_map/ppermute | solution.py:160
  198.9 0.8 collective-permute-start.13
  199.7 3.2 %collective-permute-start.14 = (bf16[24,1152]{1,0:T(8,128)(2,1)S(1)}, bf16[24,1152]{1,0:T(8,128)(2,1)S(1)}, u32[]{:S(2)}, u32[]{:S(2)}) collective-permute-start(bf16[24,1152]{1,0:T(8,128)(2,1)S(1)} %get-tuple-element.32), channel_id=1, source_target_pairs={{0,96},{32,128},{64,160},{96,192},{128,224},{160,0},{192,32},{224,... | collective-permute-start | bytes 165896 | tf_op jit(solution)/shard_map/ppermute | solution.py:160
  202.9 2.8 %collective-permute-done.13 = bf16[24,1152]{1,0:T(8,128)(2,1)S(1)} collective-permute-done((bf16[24,1152]{1,0:T(8,128)(2,1)S(1)}, bf16[24,1152]{1,0:T(8,128)(2,1)S(1)}, u32[]{:S(2)}, u32[]{:S(2)}) %collective-permute-start.13) | collective-permute-done | bytes 55328 | tf_op jit(solution)/shard_map/ppermute | solution.py:160
  205.7 1.6 collective-permute-done.14
  207.4 0.7 collective-permute-start.21
  208.2 1.1 reshape.122
  209.2 4.1 %collective-permute-done.21 = f32[12,1152]{1,0:T(8,128)S(1)} collective-permute-done((f32[12,1152]{1,0:T(8,128)S(1)}, f32[12,1152]{1,0:T(8,128)S(1)}, u32[]{:S(2)}, u32[]{:S(2)}) %collective-permute-start.21) | collective-permute-done | bytes 55328 | tf_op jit(solution)/shard_map/ppermute | solution.py:194
  213.4 0.7 reshape.123
  (49 shorter events, 1.6 us)
Async XLA Ops:
  7.2 16.7 %copy-start = (bf16[1,512,1536]{2,1,0:T(8,128)(2,1)S(1)}, bf16[1,512,1536]{2,1,0:T(8,128)(2,1)}, u32[]{:S(2)}) copy-start(bf16[1,512,1536]{2,1,0:T(8,128)(2,1)} %param.3) | copy-start | bytes 4718596
  7.2 16.8 %copy-start.6 = (bf16[1,512,384]{2,1,0:T(8,128)(2,1)S(1)}, bf16[1,512,384]{2,1,0:T(8,128)(2,1)}, u32[]{:S(2)}) copy-start(bf16[1,512,384]{2,1,0:T(8,128)(2,1)} %param.4) | copy-start | bytes 1179652
  7.2 76.7 %all-gather.3.cloned.1.call-start = ((), (), s32[]{:S(2)}) async-start(), calls=%async_computation.2 | async-start | bytes 1990656 | tf_op jit(solution)/shard_map/all_gather | solution.py:168
  8.2 5.5 %collective-permute-start.1 = (bf16[12,1152]{1,0:T(8,128)(2,1)S(1)}, bf16[12,1152]{1,0:T(8,128)(2,1)S(1)}, u32[]{:S(2)}, u32[]{:S(2)}) collective-permute-start(bf16[12,1152]{1,0:T(8,128)(2,1)S(1)} %bitcast.83), channel_id=1, source_target_pairs={{0,4},{4,0},{1,5},{5,1},{2,6},{6,2},{3,7},{7,3},{8,12},{12,8},{9,1... | collective-permute-start | bytes 82952 | tf_op jit(solution)/shard_map/ppermute | solution.py:165
  13.8 4.9 %collective-permute-start.2 = (bf16[24,1152]{1,0:T(8,128)(2,1)S(1)}, bf16[24,1152]{1,0:T(8,128)(2,1)S(1)}, u32[]{:S(2)}, u32[]{:S(2)}) collective-permute-start(bf16[24,1152]{1,0:T(8,128)(2,1)S(1)} %maximum_select_fusion.1), channel_id=1, source_target_pairs={{0,24},{8,0},{16,8},{24,16},{1,25},{9,1},{17,9},{25,17},{2,26},{10... | collective-permute-start | bytes 165896 | tf_op jit(solution)/shard_map/ppermute | solution.py:160
  16.8 5.7 %collective-permute-start.3 = (bf16[24,1152]{1,0:T(8,128)(2,1)S(1)}, bf16[24,1152]{1,0:T(8,128)(2,1)S(1)}, u32[]{:S(2)}, u32[]{:S(2)}) collective-permute-start(bf16[24,1152]{1,0:T(8,128)(2,1)S(1)} %maximum_select_fusion.1), channel_id=1, source_target_pairs={{0,16},{8,24},{16,0},{24,8},{1,17},{9,25},{17,1},{25,9},{2,18},{10... | collective-permute-start | bytes 165896 | tf_op jit(solution)/shard_map/ppermute | solution.py:160
  17.5 5.6 %collective-permute-start.4 = (bf16[24,1152]{1,0:T(8,128)(2,1)S(1)}, bf16[24,1152]{1,0:T(8,128)(2,1)S(1)}, u32[]{:S(2)}, u32[]{:S(2)}) collective-permute-start(bf16[24,1152]{1,0:T(8,128)(2,1)S(1)} %maximum_select_fusion.1), channel_id=1, source_target_pairs={{0,8},{8,16},{16,24},{24,0},{1,9},{9,17},{17,25},{25,1},{2,10},{10... | collective-permute-start | bytes 165896 | tf_op jit(solution)/shard_map/ppermute | solution.py:160
  25.2 58.6 %all-to-all-start = ((bf16[128,4,1152]{2,1,0:T(4,128)(2,1)}), bf16[128,4,1152]{2,1,0:T(4,128)(2,1)S(1)}, u32[]{:S(2)}, u32[]{:S(2)}) async-start(bf16[128,4,1152]{2,1,0:T(4,128)(2,1)} %reshape.116), calls=%async_computation | async-start | bytes 2359296 | tf_op jit(solution)/shard_map/all_to_all | solution.py:210
  83.8 23.8 %collective-permute-start.5 = (bf16[8,4,24,1152]{3,2,1,0:T(8,128)(2,1)}, bf16[8,4,24,1152]{3,2,1,0:T(8,128)(2,1)}, u32[]{:S(2)}, u32[]{:S(2)}) collective-permute-start(bf16[8,4,24,1152]{3,2,1,0:T(8,128)(2,1)} %bitcast.79), channel_id=1, source_target_pairs={{0,2},{2,0},{1,3},{3,1},{4,6},{6,4},{5,7},{7,5},{8,10},{10,8},{9,1... | collective-permute-start | bytes 5308424 | tf_op jit(solution)/shard_map/ppermute | solution.py:213
  83.9 2.1 copy-start.5
  85.1 20.3 %collective-permute-start = (bf16[128,4,768]{2,1,0:T(4,128)(2,1)}, bf16[128,4,768]{2,1,0:T(4,128)(2,1)}, u32[]{:S(2)}, u32[]{:S(2)}) collective-permute-start(bf16[128,4,768]{2,1,0:T(4,128)(2,1)} %slice.139), channel_id=1, source_target_pairs={{0,1},{1,0},{2,3},{3,2},{4,5},{5,4},{6,7},{7,6},{8,9},{9,8},{10,11... | collective-permute-start | bytes 2359304 | tf_op jit(solution)/shard_map/ppermute | solution.py:211
  86.0 21.6 %copy-start.2 = (bf16[32,24,1152]{2,1,0:T(8,128)(2,1)S(1)}, bf16[32,24,1152]{2,1,0:T(8,128)(2,1)}, u32[]{:S(2)}) copy-start(bf16[32,24,1152]{2,1,0:T(8,128)(2,1)} %all-gather.3.cloned.1.call-done) | copy-start | bytes 5308420
  107.6 4.3 %copy-start.3 = (bf16[512,1152]{1,0:T(8,128)(2,1)S(1)}, bf16[512,1152]{1,0:T(8,128)(2,1)}, u32[]{:S(2)}) copy-start(bf16[512,1152]{1,0:T(8,128)(2,1)} %reshape.117.t_ref) | copy-start | bytes 3538948
  107.6 4.3 %copy-start.4 = (bf16[512,768]{1,0:T(8,128)(2,1)S(1)}, bf16[512,768]{1,0:T(8,128)(2,1)}, u32[]{:S(2)}) copy-start(bf16[512,768]{1,0:T(8,128)(2,1)} %reshape.118.o_ref) | copy-start | bytes 2359300
  110.2 1.7 copy-start.1
  127.6 20.1 %collective-permute-start.6 = (bf16[4,8,24,1152]{3,2,1,0:T(8,128)(2,1)}, bf16[4,8,24,1152]{3,2,1,0:T(8,128)(2,1)S(1)}, u32[]{:S(2)}, u32[]{:S(2)}) collective-permute-start(bf16[4,8,24,1152]{3,2,1,0:T(8,128)(2,1)} %get-tuple-element.14), channel_id=1, source_target_pairs={{0,2},{2,0},{1,3},{3,1},{4,6},{6,4},{5,7},{7,5},{8,10},{10,8},{9,1... | collective-permute-start | bytes 5308424 | tf_op jit(solution)/shard_map/ppermute | solution.py:173
  127.6 20.0 %collective-permute-start.9 = (bf16[512,768]{1,0:T(8,128)(2,1)S(1)}, bf16[512,768]{1,0:T(8,128)(2,1)S(1)}, u32[]{:S(2)}, u32[]{:S(2)}) collective-permute-start(bf16[512,768]{1,0:T(8,128)(2,1)S(1)} %get-tuple-element.16), channel_id=1, source_target_pairs={{0,1},{1,0},{2,3},{3,2},{4,5},{5,4},{6,7},{7,6},{8,9},{9,8},{10,11... | collective-permute-start | bytes 2359304 | tf_op jit(solution)/shard_map/ppermute | solution.py:216
  148.2 8.7 %collective-permute-start.8 = (bf16[4,24,1152]{2,1,0:T(8,128)(2,1)S(1)}, bf16[4,24,1152]{2,1,0:T(8,128)(2,1)S(1)}, u32[]{:S(2)}, u32[]{:S(2)}) collective-permute-start(bf16[4,24,1152]{2,1,0:T(8,128)(2,1)S(1)} %get-tuple-element.29), channel_id=1, source_target_pairs={{0,24},{8,0},{16,8},{24,16},{1,25},{9,1},{17,9},{25,17},{2,26},{10... | collective-permute-start | bytes 663560 | tf_op jit(solution)/shard_map/ppermute | solution.py:160
  151.2 8.4 %collective-permute-start.7 = (bf16[4,24,1152]{2,1,0:T(8,128)(2,1)S(1)}, bf16[4,24,1152]{2,1,0:T(8,128)(2,1)S(1)}, u32[]{:S(2)}, u32[]{:S(2)}) collective-permute-start(bf16[4,24,1152]{2,1,0:T(8,128)(2,1)S(1)} %get-tuple-element.30), channel_id=1, source_target_pairs={{0,8},{8,16},{16,24},{24,0},{1,9},{9,17},{17,25},{25,1},{2,10},{10... | collective-permute-start | bytes 663560 | tf_op jit(solution)/shard_map/ppermute | solution.py:160
  151.9 21.5 %collective-permute-start.11 = (bf16[4,24,1152]{2,1,0:T(8,128)(2,1)}, bf16[4,24,1152]{2,1,0:T(8,128)(2,1)}, u32[]{:S(2)}, u32[]{:S(2)}) collective-permute-start(bf16[4,24,1152]{2,1,0:T(8,128)(2,1)} %fusion.9), channel_id=1, source_target_pairs={{0,24},{8,0},{16,8},{24,16},{1,25},{9,1},{17,9},{25,17},{2,26},{10... | collective-permute-start | bytes 663560 | tf_op jit(solution)/shard_map/ppermute | solution.py:160
  155.9 17.6 %collective-permute-start.15 = (bf16[4,24,1152]{2,1,0:T(8,128)(2,1)}, bf16[4,24,1152]{2,1,0:T(8,128)(2,1)}, u32[]{:S(2)}, u32[]{:S(2)}) collective-permute-start(bf16[4,24,1152]{2,1,0:T(8,128)(2,1)} %fusion.10), channel_id=1, source_target_pairs={{0,8},{8,16},{16,24},{24,0},{1,9},{9,17},{17,25},{25,1},{2,10},{10... | collective-permute-start | bytes 663560 | tf_op jit(solution)/shard_map/ppermute | solution.py:160
  160.3 13.1 %collective-permute-start.10 = (bf16[4,24,1152]{2,1,0:T(8,128)(2,1)}, bf16[4,24,1152]{2,1,0:T(8,128)(2,1)}, u32[]{:S(2)}, u32[]{:S(2)}) collective-permute-start(bf16[4,24,1152]{2,1,0:T(8,128)(2,1)} %fusion.6), channel_id=1, source_target_pairs={{0,8},{8,16},{16,24},{24,0},{1,9},{9,17},{17,25},{25,1},{2,10},{10... | collective-permute-start | bytes 663560 | tf_op jit(solution)/shard_map/ppermute | solution.py:160
  160.3 13.1 %collective-permute-start.16 = (bf16[4,24,1152]{2,1,0:T(8,128)(2,1)S(1)}, bf16[4,24,1152]{2,1,0:T(8,128)(2,1)}, u32[]{:S(2)}, u32[]{:S(2)}) collective-permute-start(bf16[4,24,1152]{2,1,0:T(8,128)(2,1)S(1)} %fusion.4), channel_id=1, source_target_pairs={{0,24},{8,0},{16,8},{24,16},{1,25},{9,1},{17,9},{25,17},{2,26},{10... | collective-permute-start | bytes 663560 | tf_op jit(solution)/shard_map/ppermute | solution.py:160
  164.6 42.7 %all-to-all-start.1 = ((bf16[128,4,768]{2,1,0:T(4,128)(2,1)}), bf16[128,4,768]{2,1,0:T(4,128)(2,1)S(1)}, u32[]{:S(2)}, u32[]{:S(2)}) async-start(bf16[128,4,768]{2,1,0:T(4,128)(2,1)} %reshape.121), calls=%async_computation.1 | async-start | bytes 1572864 | tf_op jit(solution)/shard_map/all_to_all | solution.py:220
  174.9 24.0 %collective-permute-start.17 = (bf16[24,1152]{1,0:T(8,128)(2,1)S(1)}, bf16[24,1152]{1,0:T(8,128)(2,1)S(1)}, u32[]{:S(2)}, u32[]{:S(2)}) collective-permute-start(bf16[24,1152]{1,0:T(8,128)(2,1)S(1)} %get-tuple-element.34), channel_id=1, source_target_pairs={{0,128},{32,160},{64,192},{96,224},{128,0},{160,32},{192,64},{224,... | collective-permute-start | bytes 165896 | tf_op jit(solution)/shard_map/ppermute | solution.py:160
  180.7 19.0 %collective-permute-start.18 = (bf16[24,1152]{1,0:T(8,128)(2,1)S(1)}, bf16[24,1152]{1,0:T(8,128)(2,1)S(1)}, u32[]{:S(2)}, u32[]{:S(2)}) collective-permute-start(bf16[24,1152]{1,0:T(8,128)(2,1)S(1)} %get-tuple-element.37), channel_id=1, source_target_pairs={{0,160},{32,192},{64,224},{96,0},{128,32},{160,64},{192,96},{224,1... | collective-permute-start | bytes 165896 | tf_op jit(solution)/shard_map/ppermute | solution.py:160
  180.9 22.0 %collective-permute-start.19 = (bf16[24,1152]{1,0:T(8,128)(2,1)S(1)}, bf16[24,1152]{1,0:T(8,128)(2,1)S(1)}, u32[]{:S(2)}, u32[]{:S(2)}) collective-permute-start(bf16[24,1152]{1,0:T(8,128)(2,1)S(1)} %get-tuple-element.36), channel_id=1, source_target_pairs={{0,192},{32,224},{64,0},{96,32},{128,64},{160,96},{192,128},{224,1... | collective-permute-start | bytes 165896 | tf_op jit(solution)/shard_map/ppermute | solution.py:160
  184.3 18.6 %collective-permute-start.20 = (bf16[24,1152]{1,0:T(8,128)(2,1)S(1)}, bf16[24,1152]{1,0:T(8,128)(2,1)S(1)}, u32[]{:S(2)}, u32[]{:S(2)}) collective-permute-start(bf16[24,1152]{1,0:T(8,128)(2,1)S(1)} %get-tuple-element.35), channel_id=1, source_target_pairs={{0,224},{32,0},{64,32},{96,64},{128,96},{160,128},{192,160},{224,1... | collective-permute-start | bytes 165896 | tf_op jit(solution)/shard_map/ppermute | solution.py:160
  185.6 17.3 %collective-permute-start.12 = (bf16[24,1152]{1,0:T(8,128)(2,1)S(1)}, bf16[24,1152]{1,0:T(8,128)(2,1)S(1)}, u32[]{:S(2)}, u32[]{:S(2)}) collective-permute-start(bf16[24,1152]{1,0:T(8,128)(2,1)S(1)} %get-tuple-element.31), channel_id=1, source_target_pairs={{0,32},{32,64},{64,96},{96,128},{128,160},{160,192},{192,224},{224... | collective-permute-start | bytes 165896 | tf_op jit(solution)/shard_map/ppermute | solution.py:160
  198.9 6.8 %collective-permute-start.13 = (bf16[24,1152]{1,0:T(8,128)(2,1)S(1)}, bf16[24,1152]{1,0:T(8,128)(2,1)S(1)}, u32[]{:S(2)}, u32[]{:S(2)}) collective-permute-start(bf16[24,1152]{1,0:T(8,128)(2,1)S(1)} %get-tuple-element.33), channel_id=1, source_target_pairs={{0,64},{32,96},{64,128},{96,160},{128,192},{160,224},{192,0},{224,... | collective-permute-start | bytes 165896 | tf_op jit(solution)/shard_map/ppermute | solution.py:160
  199.7 7.6 %collective-permute-start.14 = (bf16[24,1152]{1,0:T(8,128)(2,1)S(1)}, bf16[24,1152]{1,0:T(8,128)(2,1)S(1)}, u32[]{:S(2)}, u32[]{:S(2)}) collective-permute-start(bf16[24,1152]{1,0:T(8,128)(2,1)S(1)} %get-tuple-element.32), channel_id=1, source_target_pairs={{0,96},{32,128},{64,160},{96,192},{128,224},{160,0},{192,32},{224,... | collective-permute-start | bytes 165896 | tf_op jit(solution)/shard_map/ppermute | solution.py:160
  207.4 5.9 %collective-permute-start.21 = (f32[12,1152]{1,0:T(8,128)S(1)}, f32[12,1152]{1,0:T(8,128)S(1)}, u32[]{:S(2)}, u32[]{:S(2)}) collective-permute-start(f32[12,1152]{1,0:T(8,128)S(1)} %slice_select_fusion), channel_id=1, source_target_pairs={{0,4},{4,0},{1,5},{5,1},{2,6},{6,2},{3,7},{7,3},{8,12},{12,8},{9,1... | collective-permute-start | bytes 165896 | tf_op jit(solution)/shard_map/ppermute | solution.py:194
Sparse Core Ops, SparseCore 0:
  24.0 59.8 all-gather.2
where the time goes:
time: 223 us; the launch traced here: 221 us
  waiting for transfers between devices  113 us (51%)
  starting transfers between devices  56 us (25%)
  Pallas kernels  18.2 us (8%)
  local copies, waits for them, and re-layouts  15.7 us (7%)
  between operations  14.3 us (6%)
  other arithmetic  3.79 us (2%)
    all_gather x1, waiting for transfers between devices, gather_weight(): return lax.all_gather(over_y, 'z', axis=0)  45 us
    ppermute x16, starting transfers between devices, shift(): return lax.ppermute(x, axis, [(i, (i + by) % size) for i in range(size)])  29.7 us
    ppermute x16, waiting for transfers between devices, shift(): return lax.ppermute(x, axis, [(i, (i + by) % size) for i in range(size)])  25.2 us
    ppermute x1, waiting for transfers between devices, on_device(): got = lax.ppermute(give, 'mp', PAIR)  19.1 us
    ppermute x1, waiting for transfers between devices, on_device(): lax.ppermute(tokens[:, :, :cols], 'mp', PAIR).reshape(F * count, cols)  16.1 us
    all_to_all x1, starting transfers between devices, on_device(): tokens = lax.all_to_all(tokens, FR, 0, 0, tiled=True)  13.6 us
    pallas_call x1, Pallas kernels, core(): pl.pallas_call(core_kernel, out_shape=(jax.ShapeDtypeStruct((rows, 3 * ha...  11.7 us
    all_to_all x1, starting transfers between devices, to_frames(): return lax.all_to_all(x.reshape(F, count, cols), FR, 0, 0, tiled=True)  8.79 us
  transfers between devices with their start and end apart: 25, of which 13 were waited for; matrix products, arithmetic and copies ran while one was open for 7% of the time, Pallas kernels for 0%

commit v1 on v0

--- a/solution.py
+++ b/solution.py
@@ -18,30 +18,37 @@
     return lax.dot_general(a, b, dims, preferred_element_type=f32)
 
 
-def assemble_kernel(where_ref, mine_ref, rest_ref, w_ref):
-    y, c = where_ref[1], where_ref[2]
-    for z in range(Z):
-        for by in range(Y):
-            a = mine_ref[z, by].astype(f32)
-            b = rest_ref[z, by].astype(f32)
+def assemble_kernel(where_ref, *refs):
+    w_ref = refs[-1]
+    z, y, c = where_ref[0], where_ref[1], where_ref[2]
+    half = Z // 2
+    for by in range(Y):
+        for t in range(Z):
+            if by == 2:
+                which, at = (3, t) if t < half else (4, t - half)
+            else:
+                which, at = (0, 1, None, 2)[by], t
+            a = refs[which][at].astype(f32)
+            b = refs[which + 5][at].astype(f32)
             first = jnp.where(c == 0, a, b)
             second = jnp.where(c == 0, b, a)
             rows = [first[:ROWS], second[:ROWS], first[ROWS:], second[ROWS:]]
-            w_ref[z * Y + lax.rem(by + y, Y)] = jnp.concatenate(rows, 0).astype(bf16)
+            to = lax.bitwise_xor(z, t) * Y + lax.rem(by + y, Y)
+            w_ref[to] = jnp.concatenate(rows, 0).astype(bf16)
 
 
 def assemble(where, mine, rest):
-    n = mine.shape[-1]
+    n = mine[0].shape[-1]
     vm = pl.BlockSpec(memory_space=pltpu.VMEM)
     return pl.pallas_call(
         assemble_kernel,
         out_shape=jax.ShapeDtypeStruct((Z * Y, XH * C * ROWS, n), bf16),
-        in_specs=[pl.BlockSpec(memory_space=pltpu.SMEM), vm, vm],
+        in_specs=[pl.BlockSpec(memory_space=pltpu.SMEM)] + [vm] * 10,
         out_specs=vm,
         compiler_params=pltpu.CompilerParams(vmem_limit_bytes=40 * 2**20),
         cost_estimate=pl.CostEstimate(flops=0, bytes_accessed=8 * 2**20, transcendentals=0),
         name="assemble_weight",
-    )(where, mine, rest)
+    )(where, *mine, *rest)
 
 
 def core_kernel(where_ref, t_ref, o_ref, w_ref, g_ref, give_ref, keep_ref, s_ref):
@@ -130,7 +137,7 @@
                 second = jnp.concatenate([quarters[1], quarters[3]], 0)
                 by = lax.rem(b % Y + Y - y, Y)
                 at = (i * step // unit + b) // Y
-                t = lax.rem(of * (Z // MP) + at + Z - z, Z)
+                t = lax.bitwise_xor(of * (Z // MP) + at, z)
                 mine_ref[by, t] = jnp.where(c == 0, first, second).astype(bf16)
                 rest_ref[by, t] = jnp.where(c == 0, second, first).astype(bf16)
 
@@ -160,35 +167,51 @@
     return lax.ppermute(x, axis, [(i, (i + by) % size) for i in range(size)])
 
 
-def gather_weight(w):
+def across(x, axis, size, by):
+    return lax.ppermute(x, axis, [(i, i ^ by) for i in range(size)])
+
+
+def over_xh_and_pair(w):
     xh = lax.axis_index("xh")
     other = lax.ppermute(w, "xh", PAIR)
     block = jnp.where(xh == 0, jnp.concatenate([w, other], 0), jnp.concatenate([other, w], 0))
-    over_y = jnp.stack([block] + [shift(block, "y", Y, Y - t) for t in range(1, Y)], 0)
-    return lax.all_gather(over_y, "z", axis=0)
-
-
-def reduce_weight(mine, rest, early, late):
+    return jnp.stack([block, across(block, "z", Z, 1)], 0)
+
+
+def over_y(own):
+    before = shift(own, "y", Y, 1)
+    after = shift(own, "y", Y, Y - 1)
+    low = shift(before[: Z // 2], "y", Y, 1)
+    high = shift(after[Z // 2 :], "y", Y, Y - 1)
+    return [own, after, before, low, high]
+
+
+def reduce_weight(mine, rest, got, finish, late):
     xh = lax.axis_index("xh")
-    got = lax.ppermute(rest, "c", PAIR)
+    other = lax.ppermute(rest, "c", PAIR)
     h = Z // 2
-    own, after, far, before = (mine[i].astype(f32) + got[i].astype(f32) for i in range(Y))
+    own, after, far, before = (mine[i].astype(f32) + other[i].astype(f32) for i in range(Y))
     up_far = shift(far[:h].astype(bf16), "y", Y, 1)
     down_far = shift(far[h:].astype(bf16), "y", Y, Y - 1)
     up_high = shift(after[h:].astype(bf16), "y", Y, 1)
     down_low = shift(before[:h].astype(bf16), "y", Y, Y - 1)
+    up_far, down_far, got = lax.optimization_barrier((up_far, down_far, got))
+    summed = finish(got)
     up_low = (after[:h] + up_far.astype(f32)).astype(bf16)
     down_high = (before[h:] + down_far.astype(f32)).astype(bf16)
-    up_low, down_high, early = lax.optimization_barrier((up_low, down_high, early))
+    up_low, down_high, summed = lax.optimization_barrier((up_low, down_high, summed))
     up_low = shift(up_low, "y", Y, 1)
     down_high = shift(down_high, "y", Y, Y - 1)
     low = own[:h] + up_low.astype(f32) + down_low.astype(f32)
     high = own[h:] + up_high.astype(f32) + down_high.astype(f32)
     blocks = [low[i] for i in range(h)] + [high[i] for i in range(h)]
+    sent = jnp.stack(blocks[1::2], 0).astype(bf16)
+    pair = across(sent, "z", Z, 1).astype(f32)
+    blocks = [blocks[2 * i] + pair[i] for i in range(h)]
     total = blocks[0]
-    for t in range(1, Z):
-        total = total + shift(blocks[t].astype(bf16), "z", Z, t).astype(f32)
-    back = late(early)
+    for i in range(1, h):
+        total = total + across(blocks[i].astype(bf16), "z", Z, 2 * i).astype(f32)
+    back = late(summed)
     total, back = lax.optimization_barrier((total, back))
     first, second = total[:ROWS], total[ROWS:]
     moved = lax.ppermute(jnp.where(xh == 0, second, first), "xh", PAIR)
@@ -206,21 +229,31 @@
     part = lax.dynamic_slice_in_dim(normed, m * cols, cols, 2)
     tokens = jnp.concatenate([part, out_grad], axis=2).reshape(F, count, cols + half)
 
-    mine = gather_weight(w_qkv.reshape(w_qkv.shape[0], n))
+    pair = over_xh_and_pair(w_qkv.reshape(w_qkv.shape[0], n))
+    tokens, pair = lax.optimization_barrier((tokens, pair))
     tokens = lax.all_to_all(tokens, FR, 0, 0, tiled=True)
-    others = lax.ppermute(tokens[:, :, :cols], "mp", PAIR).reshape(F * count, cols)
+    own = jnp.concatenate([pair] + [across(pair, "z", Z, 2 * i) for i in range(1, Z // 2)], 0)
+    part = tokens[:, :, :cols]
+    own, part = lax.optimization_barrier((own, part))
+    others = lax.ppermute(part, "mp", PAIR)
+    mine = over_y(own)
+    mine, others = lax.optimization_barrier((mine, others))
+    others = others.reshape(F * count, cols)
     tokens = tokens.reshape(F * count, cols + half)
-    weight = assemble(where, mine, lax.ppermute(mine, "c", PAIR)).reshape(width, n)
+    rest = [lax.ppermute(p, "c", PAIR) for p in mine]
+    weight = assemble(where, mine, rest).reshape(width, n)
 
     grads, give, keep = core(where, tokens, others, weight)
     got = lax.ppermute(give, "mp", PAIR)
-    summed = (keep.astype(f32) + got.astype(f32)).astype(bf16)
+
+    def finish(got):
+        return (keep.astype(f32) + got.astype(f32)).astype(bf16)
 
     def to_frames(x):
         return lax.all_to_all(x.reshape(F, count, cols), FR, 0, 0, tiled=True)
 
     mine, rest = terms(where, tokens, others, grads)
-    weight_grad, back = reduce_weight(mine, rest, summed, to_frames)
+    weight_grad, back = reduce_weight(mine, rest, got, finish, to_frames)
     input_grad = back.reshape(frames_dev, patches, cols)
     weight_grad = weight_grad * (1.0 / F)
     return (input_grad, weight_grad.reshape(w_qkv.shape))

time: 223 us -> 193 us (0.87)
  waiting for transfers between devices: 113 us -> 85.7 us
  between operations: 14.3 us -> 0.94 us
  starting transfers between devices: 56 us -> 68.1 us
    all_gather x1 -> x0, waiting for transfers between devices: 45 us -> none  [gather_weight(): return lax.all_gather(over_y, 'z', axis=0)]
    ppermute x4 -> x16, waiting for transfers between devices: 19.4 us -> 62.5 us  [the longest x8 58.2 us: across(): return lax.ppermute(x, axis, [(i, i ^ by) for i in range(size)])]
    ppermute x4 -> x16, starting transfers between devices: 2.32 us -> 20.8 us  [the longest x8 16.8 us: across(): return lax.ppermute(x, axis, [(i, i ^ by) for i in range(size)])]
    ppermute x16 -> x10, waiting for transfers between devices: 25.2 us -> 12.3 us  [shift(): return lax.ppermute(x, axis, [(i, (i + by) % size) for i in range(size)])]
    ppermute x1, waiting for transfers between devices: 19.1 us -> 6.72 us  [on_device(): got = lax.ppermute(give, 'mp', PAIR)]
    ppermute x16 -> x10, starting transfers between devices: 29.7 us -> 17.8 us  [shift(): return lax.ppermute(x, axis, [(i, (i + by) % size) for i in range(size)])]
    all_to_all x1, starting transfers between devices: 8.79 us -> 12.3 us  [to_frames(): return lax.all_to_all(x.reshape(F, count, cols), FR, 0, 0, tiled=True)]
  transfers between devices with their start and end apart: 25 -> 30, of which waited for: 13 -> 12; matrix products, arithmetic and copies ran while one was open for 7% -> 8% of each run, Pallas kernels for 0% -> 0%
where the time goes in v1:
time: 193 us; the launch traced here: 192 us
  waiting for transfers between devices  85.7 us (44%)
  starting transfers between devices  68.1 us (35%)
  Pallas kernels  18.4 us (10%)
  local copies, waits for them, and re-layouts  16.1 us (8%)
  other arithmetic  3.19 us (2%)
    ppermute x8, waiting for transfers between devices, across(): return lax.ppermute(x, axis, [(i, i ^ by) for i in range(size)])  58.2 us
    ppermute x10, starting transfers between devices, shift(): return lax.ppermute(x, axis, [(i, (i + by) % size) for i in range(size)])  17.8 us
    ppermute x8, starting transfers between devices, across(): return lax.ppermute(x, axis, [(i, i ^ by) for i in range(size)])  16.8 us
    all_to_all x1, starting transfers between devices, on_device(): tokens = lax.all_to_all(tokens, FR, 0, 0, tiled=True)  15.4 us
    all_to_all x1, starting transfers between devices, to_frames(): return lax.all_to_all(x.reshape(F, count, cols), FR, 0, 0, tiled=True)  12.3 us
    ppermute x10, waiting for transfers between devices, shift(): return lax.ppermute(x, axis, [(i, (i + by) % size) for i in range(size)])  12.3 us
    pallas_call x1, Pallas kernels, core(): pl.pallas_call(core_kernel, out_shape=(jax.ShapeDtypeStruct((rows, 3 * ha...  11.7 us
    ppermute x1, waiting for transfers between devices, on_device(): got = lax.ppermute(give, 'mp', PAIR)  6.72 us
  transfers between devices with their start and end apart: 30, of which 12 were waited for; matrix products, arithmetic and copies ran while one was open for 8% of the time, Pallas kernels for 0%

profile of v1, /device:TPU:6, one launch (start us, length us, event | category | flops | bytes accessed | tf_op | source)
XLA Modules:
  0.0 192.5 jit_solution(14945856450344746421)
XLA Ops:
  0.7 0.9 pad.24
  1.6 1.5 collective-permute-start
  3.3 0.7 copy-done.6
  4.0 1.2 reshape.116
  5.2 2.0 %collective-permute-done = bf16[12,1152]{1,0:T(8,128)(2,1)S(1)} collective-permute-done((bf16[12,1152]{1,0:T(8,128)(2,1)S(1)}, bf16[12,1152]{1,0:T(8,128)(2,1)S(1)}, u32[]{:S(2)}, u32[]{:S(2)}) %collective-permute-start) | collective-permute-done | bytes 27680 | tf_op jit(solution)/shard_map/ppermute | solution.py:176
  7.2 2.0 %collective-permute-start.1 = (bf16[24,1152]{1,0:T(8,128)(2,1)S(1)}, bf16[24,1152]{1,0:T(8,128)(2,1)S(1)}, u32[]{:S(2)}, u32[]{:S(2)}) collective-permute-start(bf16[24,1152]{1,0:T(8,128)(2,1)S(1)} %maximum_select_fusion.1), channel_id=1, source_target_pairs={{0,32},{32,0},{64,96},{96,64},{128,160},{160,128},{192,224},{224,1... | collective-permute-start | bytes 165896 | tf_op jit(solution)/shard_map/ppermute | solution.py:171
  9.2 2.2 %collective-permute-done.1 = bf16[24,1152]{1,0:T(8,128)(2,1)S(1)} collective-permute-done((bf16[24,1152]{1,0:T(8,128)(2,1)S(1)}, bf16[24,1152]{1,0:T(8,128)(2,1)S(1)}, u32[]{:S(2)}, u32[]{:S(2)}) %collective-permute-start.1) | collective-permute-done | bytes 55328 | tf_op jit(solution)/shard_map/ppermute | solution.py:171
  11.4 15.4 %all-to-all-start = ((bf16[128,4,1152]{2,1,0:T(4,128)(2,1)}), bf16[128,4,1152]{2,1,0:T(4,128)(2,1)S(1)}, u32[]{:S(2)}, u32[]{:S(2)}) async-start(bf16[128,4,1152]{2,1,0:T(4,128)(2,1)} %reshape.116), calls=%async_computation | async-start | bytes 2359296 | tf_op jit(solution)/shard_map/all_to_all | solution.py:234
  26.9 4.2 %collective-permute-start.4 = (bf16[2,24,1152]{2,1,0:T(8,128)(2,1)S(1)}, bf16[2,24,1152]{2,1,0:T(8,128)(2,1)S(1)}, u32[]{:S(2)}, u32[]{:S(2)}) collective-permute-start(bf16[2,24,1152]{2,1,0:T(8,128)(2,1)S(1)} %pad_maximum_fusion.3), channel_id=1, source_target_pairs={{0,192},{32,224},{64,128},{96,160},{128,64},{160,96},{192,0},{224,... | collective-permute-start | bytes 331784 | tf_op jit(solution)/shard_map/ppermute | solution.py:171
  31.1 1.9 collective-permute-start.3
  33.5 30.4 %collective-permute-done.4 = bf16[2,24,1152]{2,1,0:T(8,128)(2,1)S(1)} collective-permute-done((bf16[2,24,1152]{2,1,0:T(8,128)(2,1)S(1)}, bf16[2,24,1152]{2,1,0:T(8,128)(2,1)S(1)}, u32[]{:S(2)}, u32[]{:S(2)}) %collective-permute-start.4) | collective-permute-done | bytes 110624 | tf_op jit(solution)/shard_map/ppermute | solution.py:171
  64.3 0.9 collective-permute-start.9
  65.2 1.3 collective-permute-start.6
  66.5 1.9 collective-permute-start.5
  68.5 8.8 %collective-permute-done.6.refs_2_ = bf16[8,24,1152]{2,1,0:T(8,128)(2,1)} collective-permute-done((bf16[8,24,1152]{2,1,0:T(8,128)(2,1)S(1)}, bf16[8,24,1152]{2,1,0:T(8,128)(2,1)}, u32[]{:S(2)}, u32[]{:S(2)}) %collective-permute-start.6) | collective-permute-done | bytes 442400 | tf_op jit(solution)/shard_map/ppermute | solution.py:167
  77.3 1.0 slice.161
  78.5 1.0 slice.162
  79.4 3.1 %collective-permute-start.8 = (bf16[4,24,1152]{2,1,0:T(8,128)(2,1)S(1)}, bf16[4,24,1152]{2,1,0:T(8,128)(2,1)}, u32[]{:S(2)}, u32[]{:S(2)}) collective-permute-start(bf16[4,24,1152]{2,1,0:T(8,128)(2,1)S(1)} %slice.162), channel_id=1, source_target_pairs={{0,24},{8,0},{16,8},{24,16},{1,25},{9,1},{17,9},{25,17},{2,26},{10... | collective-permute-start | bytes 663560 | tf_op jit(solution)/shard_map/ppermute | solution.py:167
  82.6 2.9 %collective-permute-done.7.refs_3_ = bf16[4,24,1152]{2,1,0:T(8,128)(2,1)S(1)} collective-permute-done((bf16[4,24,1152]{2,1,0:T(8,128)(2,1)S(1)}, bf16[4,24,1152]{2,1,0:T(8,128)(2,1)S(1)}, u32[]{:S(2)}, u32[]{:S(2)}) %collective-permute-start.7) | collective-permute-done | bytes 221216 | tf_op jit(solution)/shard_map/ppermute | solution.py:167
  87.5 2.4 %reshape.118.t_ref = bf16[512,1152]{1,0:T(8,128)(2,1)S(1)} reshape(bf16[128,4,1152]{2,1,0:T(4,128)(2,1)} %copy-done.3) | data formatting | bytes 2359296 | tf_op jit(solution)/shard_map/reshape | solution.py:242
  89.9 2.3 %reshape.119.o_ref = bf16[512,768]{1,0:T(8,128)(2,1)} reshape(bf16[128,4,768]{2,1,0:T(4,128)(2,1)} %copy-done.4) | data formatting | bytes 1572864 | tf_op jit(solution)/shard_map/reshape | solution.py:241
  92.2 2.7 %assemble_weight.1 = bf16[32,48,1152]{2,1,0:T(8,128)(2,1)S(1)} custom-call(s32[4]{0:T(128)S(1)} %pad_add_fusion.where_ref, bf16[8,24,1152]{2,1,0:T(8,128)(2,1)S(1)} %pad_maximum_fusion.1.refs_0_, bf16[8,24,1152]{2,1,0:T(8,128)(2,1)} %collective-permute-done.5.refs_1_, bf16[8,24,1152]{2,1,0:T(8,128)(2,1)} %collective-permute-done.6.refs_2_, ...), custom_call_target="tpu_custom_call" | custom-call | bytes 8388608 | tf_op jit(solution)/shard_map/assemble_weight/pallas_call | solution.py:43
  94.9 1.7 copy-done.1
  96.7 11.7 %attention_core.1 = (bf16[512,1152]{1,0:T(8,128)(2,1)S(1)}, bf16[512,768]{1,0:T(8,128)(2,1)S(1)}, bf16[512,768]{1,0:T(8,128)(2,1)S(1)}) custom-call(s32[4]{0:T(128)S(1)} %pad_add_fusion.where_ref, bf16[512,1152]{1,0:T(8,128)(2,1)S(1)} %reshape.118.t_ref, bf16[512,768]{1,0:T(8,128)(2,1)S(1)} %copy-done.2, bf16[1536,1152]{1,0:T(8,128)(2,1)} %bitcast.58), custom_call_target="tpu_custom_call" | custom-call | flops 3623878656 | bytes 8388608 | tf_op jit(solution)/shard_map/attention_core/pallas_call | solution.py:108
  108.3 4.1 %weight_terms.1 = (bf16[4,8,24,1152]{3,2,1,0:T(8,128)(2,1)S(1)}, bf16[4,8,24,1152]{3,2,1,0:T(8,128)(2,1)}) custom-call(s32[4]{0:T(128)S(1)} %pad_add_fusion.where_ref, bf16[512,1152]{1,0:T(8,128)(2,1)S(1)} %reshape.118.t_ref, bf16[512,768]{1,0:T(8,128)(2,1)S(1)} %copy-done.2, bf16[512,1152]{1,0:T(8,128)(2,1)S(1)} %get-tuple-element.35.g_ref), custom_call_target="tpu_custom_call" | custom-call | flops 1811939328 | bytes 8388608 | tf_op jit(solution)/shard_map/weight_terms/pallas_call | solution.py:149
  112.9 1.2 collective-permute-start.18
  114.1 2.3 %collective-permute-done.15 = bf16[4,8,24,1152]{3,2,1,0:T(8,128)(2,1)S(1)} collective-permute-done((bf16[4,8,24,1152]{3,2,1,0:T(8,128)(2,1)}, bf16[4,8,24,1152]{3,2,1,0:T(8,128)(2,1)S(1)}, u32[]{:S(2)}, u32[]{:S(2)}) %collective-permute-start.15) | collective-permute-done | bytes 1769504 | tf_op jit(solution)/shard_map/ppermute | solution.py:191
  116.8 4.1 %collective-permute-start.17 = (bf16[4,24,1152]{2,1,0:T(8,128)(2,1)S(1)}, bf16[4,24,1152]{2,1,0:T(8,128)(2,1)S(1)}, u32[]{:S(2)}, u32[]{:S(2)}) collective-permute-start(bf16[4,24,1152]{2,1,0:T(8,128)(2,1)S(1)} %get-tuple-element.61), channel_id=1, source_target_pairs={{0,24},{8,0},{16,8},{24,16},{1,25},{9,1},{17,9},{25,17},{2,26},{10... | collective-permute-start | bytes 663560 | tf_op jit(solution)/shard_map/ppermute | solution.py:167
  121.0 0.7 fusion.8
  121.7 0.7 fusion.9
  122.4 3.2 %collective-permute-start.20 = (bf16[4,24,1152]{2,1,0:T(8,128)(2,1)}, bf16[4,24,1152]{2,1,0:T(8,128)(2,1)}, u32[]{:S(2)}, u32[]{:S(2)}) collective-permute-start(bf16[4,24,1152]{2,1,0:T(8,128)(2,1)} %fusion.8), channel_id=1, source_target_pairs={{0,24},{8,0},{16,8},{24,16},{1,25},{9,1},{17,9},{25,17},{2,26},{10... | collective-permute-start | bytes 663560 | tf_op jit(solution)/shard_map/ppermute | solution.py:167
  125.6 6.7 %collective-permute-done.18 = bf16[512,768]{1,0:T(8,128)(2,1)S(1)} collective-permute-done((bf16[512,768]{1,0:T(8,128)(2,1)S(1)}, bf16[512,768]{1,0:T(8,128)(2,1)S(1)}, u32[]{:S(2)}, u32[]{:S(2)}) %collective-permute-start.18) | collective-permute-done | bytes 786464 | tf_op jit(solution)/shard_map/ppermute | solution.py:247
  132.6 0.9 fusion.3
  133.4 1.1 collective-permute-start.19
  134.5 2.7 %collective-permute-start.22 = (bf16[4,24,1152]{2,1,0:T(8,128)(2,1)}, bf16[4,24,1152]{2,1,0:T(8,128)(2,1)}, u32[]{:S(2)}, u32[]{:S(2)}) collective-permute-start(bf16[4,24,1152]{2,1,0:T(8,128)(2,1)} %get-tuple-element.44), channel_id=1, source_target_pairs={{0,24},{8,0},{16,8},{24,16},{1,25},{9,1},{17,9},{25,17},{2,26},{10... | collective-permute-start | bytes 663560 | tf_op jit(solution)/shard_map/ppermute | solution.py:167
  137.2 1.1 reshape.121
  138.3 12.3 %all-to-all-start.1 = ((bf16[128,4,768]{2,1,0:T(4,128)(2,1)}), bf16[128,4,768]{2,1,0:T(4,128)(2,1)S(1)}, u32[]{:S(2)}, u32[]{:S(2)}) async-start(bf16[128,4,768]{2,1,0:T(4,128)(2,1)} %reshape.121), calls=%async_computation.1 | async-start | bytes 1572864 | tf_op jit(solution)/shard_map/all_to_all | solution.py:253
  150.6 1.3 fusion.20
  152.0 1.6 collective-permute-start.23
  153.5 20.4 %collective-permute-done.23 = bf16[4,24,1152]{2,1,0:T(8,128)(2,1)S(1)} collective-permute-done((bf16[4,24,1152]{2,1,0:T(8,128)(2,1)S(1)}, bf16[4,24,1152]{2,1,0:T(8,128)(2,1)S(1)}, u32[]{:S(2)}, u32[]{:S(2)}) %collective-permute-start.23) | collective-permute-done | bytes 221216 | tf_op jit(solution)/shard_map/ppermute | solution.py:171
  174.1 5.0 %collective-permute-start.25 = (bf16[24,1152]{1,0:T(8,128)(2,1)S(1)}, bf16[24,1152]{1,0:T(8,128)(2,1)S(1)}, u32[]{:S(2)}, u32[]{:S(2)}) collective-permute-start(bf16[24,1152]{1,0:T(8,128)(2,1)S(1)} %get-tuple-element.56), channel_id=1, source_target_pairs={{0,128},{32,160},{64,192},{96,224},{128,0},{160,32},{192,64},{224,... | collective-permute-start | bytes 165896 | tf_op jit(solution)/shard_map/ppermute | solution.py:171
  179.0 1.2 collective-permute-start.26
  180.6 1.6 collective-permute-done.25
  182.2 3.5 %collective-permute-done.26 = bf16[24,1152]{1,0:T(8,128)(2,1)S(1)} collective-permute-done((bf16[24,1152]{1,0:T(8,128)(2,1)S(1)}, bf16[24,1152]{1,0:T(8,128)(2,1)S(1)}, u32[]{:S(2)}, u32[]{:S(2)}) %collective-permute-start.26) | collective-permute-done | bytes 55328 | tf_op jit(solution)/shard_map/ppermute | solution.py:171
  185.9 0.7 collective-permute-start.27
  186.5 1.1 reshape.122
  187.6 4.2 %collective-permute-done.27 = f32[12,1152]{1,0:T(8,128)S(1)} collective-permute-done((f32[12,1152]{1,0:T(8,128)S(1)}, f32[12,1152]{1,0:T(8,128)S(1)}, u32[]{:S(2)}, u32[]{:S(2)}) %collective-permute-start.27) | collective-permute-done | bytes 55328 | tf_op jit(solution)/shard_map/ppermute | solution.py:217
  191.8 0.7 reshape.123
  (63 shorter events, 5.2 us)
Async XLA Ops:
  0.6 2.5 %copy-start = (bf16[1,512,1536]{2,1,0:T(8,128)(2,1)S(1)}, bf16[1,512,1536]{2,1,0:T(8,128)(2,1)}, u32[]{:S(2)}) copy-start(bf16[1,512,1536]{2,1,0:T(8,128)(2,1)} %param.3) | copy-start | bytes 4718596
  0.6 2.5 %copy-start.5 = (bf16[1,512,384]{2,1,0:T(8,128)(2,1)S(1)}, bf16[1,512,384]{2,1,0:T(8,128)(2,1)}, u32[]{:S(2)}) copy-start(bf16[1,512,384]{2,1,0:T(8,128)(2,1)} %param.4) | copy-start | bytes 1179652
  1.6 5.5 %collective-permute-start = (bf16[12,1152]{1,0:T(8,128)(2,1)S(1)}, bf16[12,1152]{1,0:T(8,128)(2,1)S(1)}, u32[]{:S(2)}, u32[]{:S(2)}) collective-permute-start(bf16[12,1152]{1,0:T(8,128)(2,1)S(1)} %bitcast.61), channel_id=1, source_target_pairs={{0,4},{4,0},{1,5},{5,1},{2,6},{6,2},{3,7},{7,3},{8,12},{12,8},{9,1... | collective-permute-start | bytes 82952 | tf_op jit(solution)/shard_map/ppermute | solution.py:176
  3.2 0.8 copy-start.6
  7.2 4.2 %collective-permute-start.1 = (bf16[24,1152]{1,0:T(8,128)(2,1)S(1)}, bf16[24,1152]{1,0:T(8,128)(2,1)S(1)}, u32[]{:S(2)}, u32[]{:S(2)}) collective-permute-start(bf16[24,1152]{1,0:T(8,128)(2,1)S(1)} %maximum_select_fusion.1), channel_id=1, source_target_pairs={{0,32},{32,0},{64,96},{96,64},{128,160},{160,128},{192,224},{224,1... | collective-permute-start | bytes 165896 | tf_op jit(solution)/shard_map/ppermute | solution.py:171
  11.4 52.6 %all-to-all-start = ((bf16[128,4,1152]{2,1,0:T(4,128)(2,1)}), bf16[128,4,1152]{2,1,0:T(4,128)(2,1)S(1)}, u32[]{:S(2)}, u32[]{:S(2)}) async-start(bf16[128,4,1152]{2,1,0:T(4,128)(2,1)} %reshape.116), calls=%async_computation | async-start | bytes 2359296 | tf_op jit(solution)/shard_map/all_to_all | solution.py:234
  26.9 37.1 %collective-permute-start.4 = (bf16[2,24,1152]{2,1,0:T(8,128)(2,1)S(1)}, bf16[2,24,1152]{2,1,0:T(8,128)(2,1)S(1)}, u32[]{:S(2)}, u32[]{:S(2)}) collective-permute-start(bf16[2,24,1152]{2,1,0:T(8,128)(2,1)S(1)} %pad_maximum_fusion.3), channel_id=1, source_target_pairs={{0,192},{32,224},{64,128},{96,160},{128,64},{160,96},{192,0},{224,... | collective-permute-start | bytes 331784 | tf_op jit(solution)/shard_map/ppermute | solution.py:171
  31.1 32.9 %collective-permute-start.3 = (bf16[2,24,1152]{2,1,0:T(8,128)(2,1)S(1)}, bf16[2,24,1152]{2,1,0:T(8,128)(2,1)S(1)}, u32[]{:S(2)}, u32[]{:S(2)}) collective-permute-start(bf16[2,24,1152]{2,1,0:T(8,128)(2,1)S(1)} %pad_maximum_fusion.3), channel_id=1, source_target_pairs={{0,128},{32,160},{64,192},{96,224},{128,0},{160,32},{192,64},{224,... | collective-permute-start | bytes 331784 | tf_op jit(solution)/shard_map/ppermute | solution.py:171
  33.0 30.9 %collective-permute-start.2 = (bf16[2,24,1152]{2,1,0:T(8,128)(2,1)S(1)}, bf16[2,24,1152]{2,1,0:T(8,128)(2,1)S(1)}, u32[]{:S(2)}, u32[]{:S(2)}) collective-permute-start(bf16[2,24,1152]{2,1,0:T(8,128)(2,1)S(1)} %pad_maximum_fusion.3), channel_id=1, source_target_pairs={{0,64},{32,96},{64,0},{96,32},{128,192},{160,224},{192,128},{224,1... | collective-permute-start | bytes 331784 | tf_op jit(solution)/shard_map/ppermute | solution.py:171
  64.0 13.3 %copy-start.3 = (bf16[128,4,1152]{2,1,0:T(4,128)(2,1)}, bf16[128,4,1152]{2,1,0:T(4,128)(2,1)S(1)}, u32[]{:S(2)}) copy-start(bf16[128,4,1152]{2,1,0:T(4,128)(2,1)S(1)} %all-to-all-done) | copy-start | bytes 3538948
  64.3 21.7 %collective-permute-start.9 = (bf16[128,4,768]{2,1,0:T(4,128)(2,1)S(1)}, bf16[128,4,768]{2,1,0:T(4,128)(2,1)S(1)}, u32[]{:S(2)}, u32[]{:S(2)}) collective-permute-start(bf16[128,4,768]{2,1,0:T(4,128)(2,1)S(1)} %slice.160), channel_id=1, source_target_pairs={{0,1},{1,0},{2,3},{3,2},{4,5},{5,4},{6,7},{7,6},{8,9},{9,8},{10,11... | collective-permute-start | bytes 2359304 | tf_op jit(solution)/shard_map/ppermute | solution.py:238
  65.2 12.0 %collective-permute-start.6 = (bf16[8,24,1152]{2,1,0:T(8,128)(2,1)S(1)}, bf16[8,24,1152]{2,1,0:T(8,128)(2,1)}, u32[]{:S(2)}, u32[]{:S(2)}) collective-permute-start(bf16[8,24,1152]{2,1,0:T(8,128)(2,1)S(1)} %pad_maximum_fusion.1.refs_0_), channel_id=1, source_target_pairs={{0,8},{8,16},{16,24},{24,0},{1,9},{9,17},{17,25},{25,1},{2,10},{10... | collective-permute-start | bytes 1327112 | tf_op jit(solution)/shard_map/ppermute | solution.py:167
  66.5 11.9 %collective-permute-start.5 = (bf16[8,24,1152]{2,1,0:T(8,128)(2,1)S(1)}, bf16[8,24,1152]{2,1,0:T(8,128)(2,1)}, u32[]{:S(2)}, u32[]{:S(2)}) collective-permute-start(bf16[8,24,1152]{2,1,0:T(8,128)(2,1)S(1)} %pad_maximum_fusion.1.refs_0_), channel_id=1, source_target_pairs={{0,24},{8,0},{16,8},{24,16},{1,25},{9,1},{17,9},{25,17},{2,26},{10... | collective-permute-start | bytes 1327112 | tf_op jit(solution)/shard_map/ppermute | solution.py:167
  78.2 7.2 %collective-permute-start.7 = (bf16[4,24,1152]{2,1,0:T(8,128)(2,1)S(1)}, bf16[4,24,1152]{2,1,0:T(8,128)(2,1)S(1)}, u32[]{:S(2)}, u32[]{:S(2)}) collective-permute-start(bf16[4,24,1152]{2,1,0:T(8,128)(2,1)S(1)} %slice.161), channel_id=1, source_target_pairs={{0,8},{8,16},{16,24},{24,0},{1,9},{9,17},{17,25},{25,1},{2,10},{10... | collective-permute-start | bytes 663560 | tf_op jit(solution)/shard_map/ppermute | solution.py:167
  79.4 6.6 %collective-permute-start.8 = (bf16[4,24,1152]{2,1,0:T(8,128)(2,1)S(1)}, bf16[4,24,1152]{2,1,0:T(8,128)(2,1)}, u32[]{:S(2)}, u32[]{:S(2)}) collective-permute-start(bf16[4,24,1152]{2,1,0:T(8,128)(2,1)S(1)} %slice.162), channel_id=1, source_target_pairs={{0,24},{8,0},{16,8},{24,16},{1,25},{9,1},{17,9},{25,17},{2,26},{10... | collective-permute-start | bytes 663560 | tf_op jit(solution)/shard_map/ppermute | solution.py:167
  86.0 0.9 copy-start.4
  86.0 6.1 %collective-permute-start.10 = (bf16[8,24,1152]{2,1,0:T(8,128)(2,1)S(1)}, bf16[8,24,1152]{2,1,0:T(8,128)(2,1)}, u32[]{:S(2)}, u32[]{:S(2)}) collective-permute-start(bf16[8,24,1152]{2,1,0:T(8,128)(2,1)S(1)} %pad_maximum_fusion.1.refs_0_), channel_id=1, source_target_pairs={{0,2},{2,0},{1,3},{3,1},{4,6},{6,4},{5,7},{7,5},{8,10},{10,8},{9,1... | collective-permute-start | bytes 1327112 | tf_op jit(solution)/shard_map/ppermute | solution.py:243
  86.0 6.2 %collective-permute-start.11 = (bf16[8,24,1152]{2,1,0:T(8,128)(2,1)}, bf16[8,24,1152]{2,1,0:T(8,128)(2,1)}, u32[]{:S(2)}, u32[]{:S(2)}) collective-permute-start(bf16[8,24,1152]{2,1,0:T(8,128)(2,1)} %collective-permute-done.5.refs_1_), channel_id=1, source_target_pairs={{0,2},{2,0},{1,3},{3,1},{4,6},{6,4},{5,7},{7,5},{8,10},{10,8},{9,1... | collective-permute-start | bytes 1327112 | tf_op jit(solution)/shard_map/ppermute | solution.py:243
  86.9 5.3 %collective-permute-start.12 = (bf16[8,24,1152]{2,1,0:T(8,128)(2,1)}, bf16[8,24,1152]{2,1,0:T(8,128)(2,1)}, u32[]{:S(2)}, u32[]{:S(2)}) collective-permute-start(bf16[8,24,1152]{2,1,0:T(8,128)(2,1)} %collective-permute-done.6.refs_2_), channel_id=1, source_target_pairs={{0,2},{2,0},{1,3},{3,1},{4,6},{6,4},{5,7},{7,5},{8,10},{10,8},{9,1... | collective-permute-start | bytes 1327112 | tf_op jit(solution)/shard_map/ppermute | solution.py:243
  86.9 5.3 %collective-permute-start.13 = (bf16[4,24,1152]{2,1,0:T(8,128)(2,1)S(1)}, bf16[4,24,1152]{2,1,0:T(8,128)(2,1)}, u32[]{:S(2)}, u32[]{:S(2)}) collective-permute-start(bf16[4,24,1152]{2,1,0:T(8,128)(2,1)S(1)} %collective-permute-done.7.refs_3_), channel_id=1, source_target_pairs={{0,2},{2,0},{1,3},{3,1},{4,6},{6,4},{5,7},{7,5},{8,10},{10,8},{9,1... | collective-permute-start | bytes 663560 | tf_op jit(solution)/shard_map/ppermute | solution.py:243
  87.4 4.8 %collective-permute-start.14 = (bf16[4,24,1152]{2,1,0:T(8,128)(2,1)}, bf16[4,24,1152]{2,1,0:T(8,128)(2,1)}, u32[]{:S(2)}, u32[]{:S(2)}) collective-permute-start(bf16[4,24,1152]{2,1,0:T(8,128)(2,1)} %collective-permute-done.8.refs_4_), channel_id=1, source_target_pairs={{0,2},{2,0},{1,3},{3,1},{4,6},{6,4},{5,7},{7,5},{8,10},{10,8},{9,1... | collective-permute-start | bytes 663560 | tf_op jit(solution)/shard_map/ppermute | solution.py:243
  92.2 4.5 %copy-start.2 = (bf16[512,768]{1,0:T(8,128)(2,1)S(1)}, bf16[512,768]{1,0:T(8,128)(2,1)}, u32[]{:S(2)}) copy-start(bf16[512,768]{1,0:T(8,128)(2,1)} %reshape.119.o_ref) | copy-start | bytes 2359300
  94.9 1.7 copy-start.1
  112.4 4.0 %collective-permute-start.15 = (bf16[4,8,24,1152]{3,2,1,0:T(8,128)(2,1)}, bf16[4,8,24,1152]{3,2,1,0:T(8,128)(2,1)S(1)}, u32[]{:S(2)}, u32[]{:S(2)}) collective-permute-start(bf16[4,8,24,1152]{3,2,1,0:T(8,128)(2,1)} %get-tuple-element.37), channel_id=1, source_target_pairs={{0,2},{2,0},{1,3},{3,1},{4,6},{6,4},{5,7},{7,5},{8,10},{10,8},{9,1... | collective-permute-start | bytes 5308424 | tf_op jit(solution)/shard_map/ppermute | solution.py:191
  112.9 19.4 %collective-permute-start.18 = (bf16[512,768]{1,0:T(8,128)(2,1)S(1)}, bf16[512,768]{1,0:T(8,128)(2,1)S(1)}, u32[]{:S(2)}, u32[]{:S(2)}) collective-permute-start(bf16[512,768]{1,0:T(8,128)(2,1)S(1)} %get-tuple-element.38), channel_id=1, source_target_pairs={{0,1},{1,0},{2,3},{3,2},{4,5},{5,4},{6,7},{7,6},{8,9},{9,8},{10,11... | collective-permute-start | bytes 2359304 | tf_op jit(solution)/shard_map/ppermute | solution.py:247
  116.8 15.5 %collective-permute-start.17 = (bf16[4,24,1152]{2,1,0:T(8,128)(2,1)S(1)}, bf16[4,24,1152]{2,1,0:T(8,128)(2,1)S(1)}, u32[]{:S(2)}, u32[]{:S(2)}) collective-permute-start(bf16[4,24,1152]{2,1,0:T(8,128)(2,1)S(1)} %get-tuple-element.61), channel_id=1, source_target_pairs={{0,24},{8,0},{16,8},{24,16},{1,25},{9,1},{17,9},{25,17},{2,26},{10... | collective-permute-start | bytes 663560 | tf_op jit(solution)/shard_map/ppermute | solution.py:167
  121.0 11.4 %collective-permute-start.16 = (bf16[4,24,1152]{2,1,0:T(8,128)(2,1)S(1)}, bf16[4,24,1152]{2,1,0:T(8,128)(2,1)S(1)}, u32[]{:S(2)}, u32[]{:S(2)}) collective-permute-start(bf16[4,24,1152]{2,1,0:T(8,128)(2,1)S(1)} %get-tuple-element.62), channel_id=1, source_target_pairs={{0,8},{8,16},{16,24},{24,0},{1,9},{9,17},{17,25},{25,1},{2,10},{10... | collective-permute-start | bytes 663560 | tf_op jit(solution)/shard_map/ppermute | solution.py:167
  122.4 28.2 %collective-permute-start.21 = (bf16[4,24,1152]{2,1,0:T(8,128)(2,1)}, bf16[4,24,1152]{2,1,0:T(8,128)(2,1)S(1)}, u32[]{:S(2)}, u32[]{:S(2)}) collective-permute-start(bf16[4,24,1152]{2,1,0:T(8,128)(2,1)} %fusion.9), channel_id=1, source_target_pairs={{0,8},{8,16},{16,24},{24,0},{1,9},{9,17},{17,25},{25,1},{2,10},{10... | collective-permute-start | bytes 663560 | tf_op jit(solution)/shard_map/ppermute | solution.py:167
  122.4 28.2 %collective-permute-start.20 = (bf16[4,24,1152]{2,1,0:T(8,128)(2,1)}, bf16[4,24,1152]{2,1,0:T(8,128)(2,1)}, u32[]{:S(2)}, u32[]{:S(2)}) collective-permute-start(bf16[4,24,1152]{2,1,0:T(8,128)(2,1)} %fusion.8), channel_id=1, source_target_pairs={{0,24},{8,0},{16,8},{24,16},{1,25},{9,1},{17,9},{25,17},{2,26},{10... | collective-permute-start | bytes 663560 | tf_op jit(solution)/shard_map/ppermute | solution.py:167
  133.4 17.2 %collective-permute-start.19 = (bf16[4,24,1152]{2,1,0:T(8,128)(2,1)}, bf16[4,24,1152]{2,1,0:T(8,128)(2,1)}, u32[]{:S(2)}, u32[]{:S(2)}) collective-permute-start(bf16[4,24,1152]{2,1,0:T(8,128)(2,1)} %get-tuple-element.43), channel_id=1, source_target_pairs={{0,8},{8,16},{16,24},{24,0},{1,9},{9,17},{17,25},{25,1},{2,10},{10... | collective-permute-start | bytes 663560 | tf_op jit(solution)/shard_map/ppermute | solution.py:167
  134.5 16.1 %collective-permute-start.22 = (bf16[4,24,1152]{2,1,0:T(8,128)(2,1)}, bf16[4,24,1152]{2,1,0:T(8,128)(2,1)}, u32[]{:S(2)}, u32[]{:S(2)}) collective-permute-start(bf16[4,24,1152]{2,1,0:T(8,128)(2,1)} %get-tuple-element.44), channel_id=1, source_target_pairs={{0,24},{8,0},{16,8},{24,16},{1,25},{9,1},{17,9},{25,17},{2,26},{10... | collective-permute-start | bytes 663560 | tf_op jit(solution)/shard_map/ppermute | solution.py:167
  138.3 47.6 %all-to-all-start.1 = ((bf16[128,4,768]{2,1,0:T(4,128)(2,1)}), bf16[128,4,768]{2,1,0:T(4,128)(2,1)S(1)}, u32[]{:S(2)}, u32[]{:S(2)}) async-start(bf16[128,4,768]{2,1,0:T(4,128)(2,1)} %reshape.121), calls=%async_computation.1 | async-start | bytes 1572864 | tf_op jit(solution)/shard_map/all_to_all | solution.py:253
  152.0 22.0 %collective-permute-start.23 = (bf16[4,24,1152]{2,1,0:T(8,128)(2,1)S(1)}, bf16[4,24,1152]{2,1,0:T(8,128)(2,1)S(1)}, u32[]{:S(2)}, u32[]{:S(2)}) collective-permute-start(bf16[4,24,1152]{2,1,0:T(8,128)(2,1)S(1)} %pad_maximum_fusion.2), channel_id=1, source_target_pairs={{0,32},{32,0},{64,96},{96,64},{128,160},{160,128},{192,224},{224,1... | collective-permute-start | bytes 663560 | tf_op jit(solution)/shard_map/ppermute | solution.py:171
  174.1 8.2 %collective-permute-start.25 = (bf16[24,1152]{1,0:T(8,128)(2,1)S(1)}, bf16[24,1152]{1,0:T(8,128)(2,1)S(1)}, u32[]{:S(2)}, u32[]{:S(2)}) collective-permute-start(bf16[24,1152]{1,0:T(8,128)(2,1)S(1)} %get-tuple-element.56), channel_id=1, source_target_pairs={{0,128},{32,160},{64,192},{96,224},{128,0},{160,32},{192,64},{224,... | collective-permute-start | bytes 165896 | tf_op jit(solution)/shard_map/ppermute | solution.py:171
  179.0 6.7 %collective-permute-start.26 = (bf16[24,1152]{1,0:T(8,128)(2,1)S(1)}, bf16[24,1152]{1,0:T(8,128)(2,1)S(1)}, u32[]{:S(2)}, u32[]{:S(2)}) collective-permute-start(bf16[24,1152]{1,0:T(8,128)(2,1)S(1)} %get-tuple-element.57), channel_id=1, source_target_pairs={{0,192},{32,224},{64,128},{96,160},{128,64},{160,96},{192,0},{224,... | collective-permute-start | bytes 165896 | tf_op jit(solution)/shard_map/ppermute | solution.py:171
  180.3 5.5 %collective-permute-start.24 = (bf16[24,1152]{1,0:T(8,128)(2,1)S(1)}, bf16[24,1152]{1,0:T(8,128)(2,1)S(1)}, u32[]{:S(2)}, u32[]{:S(2)}) collective-permute-start(bf16[24,1152]{1,0:T(8,128)(2,1)S(1)} %get-tuple-element.60), channel_id=1, source_target_pairs={{0,64},{32,96},{64,0},{96,32},{128,192},{160,224},{192,128},{224,1... | collective-permute-start | bytes 165896 | tf_op jit(solution)/shard_map/ppermute | solution.py:171
  185.9 5.9 %collective-permute-start.27 = (f32[12,1152]{1,0:T(8,128)S(1)}, f32[12,1152]{1,0:T(8,128)S(1)}, u32[]{:S(2)}, u32[]{:S(2)}) collective-permute-start(f32[12,1152]{1,0:T(8,128)S(1)} %slice_select_fusion), channel_id=1, source_target_pairs={{0,4},{4,0},{1,5},{5,1},{2,6},{6,2},{3,7},{7,3},{8,12},{12,8},{9,1... | collective-permute-start | bytes 165896 | tf_op jit(solution)/shard_map/ppermute | solution.py:217

commit v2 on v1

--- a/solution.py
+++ b/solution.py
@@ -18,46 +18,31 @@
     return lax.dot_general(a, b, dims, preferred_element_type=f32)
 
 
-def assemble_kernel(where_ref, *refs):
-    w_ref = refs[-1]
-    z, y, c = where_ref[0], where_ref[1], where_ref[2]
-    half = Z // 2
+def core_kernel(where_ref, t_ref, o_ref, *refs):
+    pieces = refs[:10]
+    g_ref, give_ref, keep_ref, w_ref, s_ref, d_ref = refs[10:]
+    z, y, c, m = (where_ref[i] for i in range(4))
+    unit = XH * C * ROWS
     for by in range(Y):
         for t in range(Z):
             if by == 2:
-                which, at = (3, t) if t < half else (4, t - half)
+                which, at = (3, t) if t < Z // 2 else (4, t - Z // 2)
             else:
                 which, at = (0, 1, None, 2)[by], t
-            a = refs[which][at].astype(f32)
-            b = refs[which + 5][at].astype(f32)
+            a = pieces[which][at].astype(f32)
+            b = pieces[which + 5][at].astype(f32)
             first = jnp.where(c == 0, a, b)
             second = jnp.where(c == 0, b, a)
             rows = [first[:ROWS], second[:ROWS], first[ROWS:], second[ROWS:]]
             to = lax.bitwise_xor(z, t) * Y + lax.rem(by + y, Y)
-            w_ref[to] = jnp.concatenate(rows, 0).astype(bf16)
-
-
-def assemble(where, mine, rest):
-    n = mine[0].shape[-1]
-    vm = pl.BlockSpec(memory_space=pltpu.VMEM)
-    return pl.pallas_call(
-        assemble_kernel,
-        out_shape=jax.ShapeDtypeStruct((Z * Y, XH * C * ROWS, n), bf16),
-        in_specs=[pl.BlockSpec(memory_space=pltpu.SMEM)] + [vm] * 10,
-        out_specs=vm,
-        compiler_params=pltpu.CompilerParams(vmem_limit_bytes=40 * 2**20),
-        cost_estimate=pl.CostEstimate(flops=0, bytes_accessed=8 * 2**20, transcendentals=0),
-        name="assemble_weight",
-    )(where, *mine, *rest)
-
-
-def core_kernel(where_ref, t_ref, o_ref, w_ref, g_ref, give_ref, keep_ref, s_ref):
+            to = pl.ds(pl.multiple_of(to * unit, unit), unit)
+            w_ref[to, :] = jnp.concatenate(rows, 0).astype(bf16)
+
     part_cols = o_ref.shape[1]
     rows, half = t_ref.shape[0], t_ref.shape[1] - part_cols
     count = rows // F
     scale = HEAD_DIM ** (-0.5)
     pairs = half // 128
-    m = where_ref[3]
     near = pl.ds(pl.multiple_of(m * part_cols, part_cols), part_cols)
     away = pl.ds(pl.multiple_of((1 - m) * part_cols, part_cols), part_cols)
     for j in range(3):
@@ -94,36 +79,42 @@
             both = jnp.dot(dscores, k, preferred_element_type=f32) * scale
             dq = jnp.where(low, both[:F], both[F:])
             for j, part in enumerate((dq, dk, dv)):
-                s_ref[j * pairs + pair, at, :] = part
-    g = jnp.concatenate([s_ref[i] for i in range(3 * pairs)], 1).astype(bf16)
+                d_ref[j * pairs + pair, at, :] = part
+    g = jnp.concatenate([d_ref[i] for i in range(3 * pairs)], 1).astype(bf16)
     g_ref[...] = g
     give_ref[...] = dot(g, w_ref[away, :], NT).astype(bf16)
     keep_ref[...] = dot(g, w_ref[near, :], NT).astype(bf16)
 
 
-def core(where, tokens, others, w):
+def core(where, tokens, others, mine, rest):
     rows, part_cols = others.shape
     half = tokens.shape[1] - part_cols
+    width, n = MP * part_cols, 3 * half
     vm = pl.BlockSpec(memory_space=pltpu.VMEM)
     return pl.pallas_call(
         core_kernel,
         out_shape=(
-            jax.ShapeDtypeStruct((rows, 3 * half), bf16),
+            jax.ShapeDtypeStruct((rows, n), bf16),
             jax.ShapeDtypeStruct((rows, part_cols), bf16),
             jax.ShapeDtypeStruct((rows, part_cols), bf16),
         ),
-        in_specs=[pl.BlockSpec(memory_space=pltpu.SMEM)] + [vm] * 3,
+        in_specs=[pl.BlockSpec(memory_space=pltpu.SMEM)] + [vm] * 12,
         out_specs=(vm, vm, vm),
-        scratch_shapes=[pltpu.VMEM((4 * half // 128, rows, 128), f32)],
+        scratch_shapes=[
+            pltpu.VMEM((width, n), bf16),
+            pltpu.VMEM((4 * half // 128, rows, 128), f32),
+            pltpu.VMEM((3 * half // 128, rows, 128), f32),
+        ],
         compiler_params=pltpu.CompilerParams(vmem_limit_bytes=48 * 2**20),
         cost_estimate=pl.CostEstimate(
-            flops=4 * rows * w.shape[0] * 3 * half, bytes_accessed=8 * 2**20, transcendentals=0
+            flops=4 * rows * width * n, bytes_accessed=8 * 2**20, transcendentals=0
         ),
         name="attention_core",
-    )(where, tokens, others, w)
-
-
-def term_kernel(where_ref, t_ref, o_ref, g_ref, mine_ref, rest_ref):
+    )(where, tokens, others, *mine, *rest)
+
+
+def term_kernel(where_ref, t_ref, o_ref, g_ref, mine_ref, *refs):
+    rest_refs, rest_ref = refs[:Y], refs[Y]
     z, y, c, m = (where_ref[i] for i in range(4))
     part_cols = o_ref.shape[1]
     step, unit = 384, XH * C * ROWS
@@ -140,17 +131,20 @@
                 t = lax.bitwise_xor(of * (Z // MP) + at, z)
                 mine_ref[by, t] = jnp.where(c == 0, first, second).astype(bf16)
                 rest_ref[by, t] = jnp.where(c == 0, second, first).astype(bf16)
+    for by in range(Y):
+        rest_refs[by][...] = rest_ref[by]
 
 
 def terms(where, tokens, others, grads):
     n = grads.shape[1]
     vm = pl.BlockSpec(memory_space=pltpu.VMEM)
-    shape = jax.ShapeDtypeStruct((Y, Z, XH * ROWS, n), bf16)
+    shape = (Y, Z, XH * ROWS, n)
     return pl.pallas_call(
         term_kernel,
-        out_shape=(shape, shape),
+        out_shape=[jax.ShapeDtypeStruct(shape, bf16)] + [jax.ShapeDtypeStruct(shape[1:], bf16)] * Y,
         in_specs=[pl.BlockSpec(memory_space=pltpu.SMEM)] + [vm] * 3,
-        out_specs=(vm, vm),
+        out_specs=[vm] * (1 + Y),
+        scratch_shapes=[pltpu.VMEM(shape, bf16)],
         compiler_params=pltpu.CompilerParams(vmem_limit_bytes=48 * 2**20),
         cost_estimate=pl.CostEstimate(
             flops=2 * 512 * 1536 * n, bytes_accessed=8 * 2**20, transcendentals=0
@@ -171,11 +165,15 @@
     return lax.ppermute(x, axis, [(i, i ^ by) for i in range(size)])
 
 
+ZX = ("z", "xh")
+
+
 def over_xh_and_pair(w):
-    xh = lax.axis_index("xh")
-    other = lax.ppermute(w, "xh", PAIR)
-    block = jnp.where(xh == 0, jnp.concatenate([w, other], 0), jnp.concatenate([other, w], 0))
-    return jnp.stack([block, across(block, "z", Z, 1)], 0)
+    even = lax.axis_index("xh") == 0
+    a, b, d = (across(w, ZX, Z * XH, by) for by in (1, 2, 3))
+    first = jnp.concatenate([jnp.where(even, w, a), jnp.where(even, a, w)], 0)
+    second = jnp.concatenate([jnp.where(even, b, d), jnp.where(even, d, b)], 0)
+    return jnp.stack([first, second], 0)
 
 
 def over_y(own):
@@ -187,8 +185,10 @@
 
 
 def reduce_weight(mine, rest, got, finish, late):
-    xh = lax.axis_index("xh")
-    other = lax.ppermute(rest, "c", PAIR)
+    even = lax.axis_index("xh") == 0
+    rest = list(rest)
+    rest[2] = lax.ppermute(rest[2], "c", PAIR)
+    other = [rest[i] if i == 2 else lax.ppermute(rest[i], "c", PAIR) for i in range(Y)]
     h = Z // 2
     own, after, far, before = (mine[i].astype(f32) + other[i].astype(f32) for i in range(Y))
     up_far = shift(far[:h].astype(bf16), "y", Y, 1)
@@ -204,18 +204,18 @@
     down_high = shift(down_high, "y", Y, Y - 1)
     low = own[:h] + up_low.astype(f32) + down_low.astype(f32)
     high = own[h:] + up_high.astype(f32) + down_high.astype(f32)
-    blocks = [low[i] for i in range(h)] + [high[i] for i in range(h)]
-    sent = jnp.stack(blocks[1::2], 0).astype(bf16)
-    pair = across(sent, "z", Z, 1).astype(f32)
-    blocks = [blocks[2 * i] + pair[i] for i in range(h)]
-    total = blocks[0]
-    for i in range(1, h):
-        total = total + across(blocks[i].astype(bf16), "z", Z, 2 * i).astype(f32)
+    blocks = jnp.concatenate([low, high], 0)
+    kept = jnp.where(even, blocks[:, :ROWS], blocks[:, ROWS:])
+    sent = jnp.where(even, blocks[:, ROWS:], blocks[:, :ROWS])
+    total = kept[0::2]
+    for by, x in ((2, kept[1::2]), (1, sent[0::2]), (3, sent[1::2])):
+        total = total + across(x.astype(bf16), ZX, Z * XH, by).astype(f32)
     back = late(summed)
     total, back = lax.optimization_barrier((total, back))
-    first, second = total[:ROWS], total[ROWS:]
-    moved = lax.ppermute(jnp.where(xh == 0, second, first), "xh", PAIR)
-    return jnp.where(xh == 0, first, second) + moved, back
+    result = total[0]
+    for i in range(1, h):
+        result = result + across(total[i].astype(bf16), "z", Z, 2 * i).astype(f32)
+    return result, back
 
 
 def on_device(normed, out_grad, w_qkv):
@@ -237,13 +237,13 @@
     own, part = lax.optimization_barrier((own, part))
     others = lax.ppermute(part, "mp", PAIR)
     mine = over_y(own)
-    mine, others = lax.optimization_barrier((mine, others))
     others = others.reshape(F * count, cols)
     tokens = tokens.reshape(F * count, cols + half)
-    rest = [lax.ppermute(p, "c", PAIR) for p in mine]
-    weight = assemble(where, mine, rest).reshape(width, n)
-
-    grads, give, keep = core(where, tokens, others, weight)
+    rest = [lax.ppermute(p, "c", PAIR) for p in mine[:3]]
+    mine, others, tokens = lax.optimization_barrier((mine, others, tokens))
+    rest = rest + [lax.ppermute(p, "c", PAIR) for p in mine[3:]]
+
+    grads, give, keep = core(where, tokens, others, mine, rest)
     got = lax.ppermute(give, "mp", PAIR)
 
     def finish(got):
@@ -252,7 +252,7 @@
     def to_frames(x):
         return lax.all_to_all(x.reshape(F, count, cols), FR, 0, 0, tiled=True)
 
-    mine, rest = terms(where, tokens, others, grads)
+    mine, *rest = terms(where, tokens, others, grads)
     weight_grad, back = reduce_weight(mine, rest, got, finish, to_frames)
     input_grad = back.reshape(frames_dev, patches, cols)
     weight_grad = weight_grad * (1.0 / F)

time: 193 us -> 200 us (1.036); the launches traced: 192 us -> 196 us
  starting transfers between devices: 68.1 us -> 80.3 us
  waiting for transfers between devices: 85.7 us -> 75.8 us
    ppermute x8 -> x9, starting transfers between devices: 3.69 us -> 11.7 us  [the longest x3 9.94 us: reduce_weight(): lax.ppermute(rest[i], 'c', PAIR)]
    ppermute x8 -> x12, starting transfers between devices: 16.8 us -> 23.4 us  [across(): return lax.ppermute(x, axis, [(i, i ^ by) for i in range(size)])]
    ppermute x8 -> x9, waiting for transfers between devices: 8.55 us -> 2.39 us  [the longest x2 1.62 us: on_device(): rest = rest + [lax.ppermute(p, 'c', PAIR) for p in mine[3:]]]
    ppermute x1, waiting for transfers between devices: 6.72 us -> 3.37 us  [on_device(): got = lax.ppermute(give, 'mp', PAIR)]
    ppermute x10, starting transfers between devices: 17.8 us -> 15.7 us  [shift(): return lax.ppermute(x, axis, [(i, (i + by) % size) for i in range(size)])]
    ppermute x8 -> x12, waiting for transfers between devices: 58.2 us -> 56.3 us  [across(): return lax.ppermute(x, axis, [(i, i ^ by) for i in range(size)])]
    pallas_call x3 -> x2, Pallas kernels: 18.4 us -> 17.5 us  [the longest x1 13.4 us: core(): pl.pallas_call(core_kernel, out_shape=(jax.ShapeDtypeStruct((rows, n), bf...]
  transfers between devices with their start and end apart: 30 -> 35, of which waited for: 12 -> 16; matrix products, arithmetic and copies ran while one was open for 8% -> 8% of each run, Pallas kernels for 0% -> 0%
where the time goes in v2:
time: 200 us; the launch traced here: 196 us
  starting transfers between devices  80.3 us (40%)
  waiting for transfers between devices  75.8 us (38%)
  Pallas kernels  17.5 us (9%)
  local copies, waits for them, and re-layouts  16.2 us (8%)
  other arithmetic  4.69 us (2%)
    ppermute x12, waiting for transfers between devices, across(): return lax.ppermute(x, axis, [(i, i ^ by) for i in range(size)])  56.3 us
    ppermute x12, starting transfers between devices, across(): return lax.ppermute(x, axis, [(i, i ^ by) for i in range(size)])  23.4 us
    ppermute x10, starting transfers between devices, shift(): return lax.ppermute(x, axis, [(i, (i + by) % size) for i in range(size)])  15.7 us
    all_to_all x1, starting transfers between devices, on_device(): tokens = lax.all_to_all(tokens, FR, 0, 0, tiled=True)  15.5 us
    ppermute x10, waiting for transfers between devices, shift(): return lax.ppermute(x, axis, [(i, (i + by) % size) for i in range(size)])  13.7 us
    pallas_call x1, Pallas kernels, core(): pl.pallas_call(core_kernel, out_shape=(jax.ShapeDtypeStruct((rows, n), bf...  13.4 us
    all_to_all x1, starting transfers between devices, to_frames(): return lax.all_to_all(x.reshape(F, count, cols), FR, 0, 0, tiled=True)  12.1 us
    ppermute x3, starting transfers between devices, reduce_weight(): lax.ppermute(rest[i], 'c', PAIR)  9.94 us
  transfers between devices with their start and end apart: 35, of which 16 were waited for; matrix products, arithmetic and copies ran while one was open for 8% of the time, Pallas kernels for 0%

profile of v2, /device:TPU:6, one launch (start us, length us, event | category | flops | bytes accessed | tf_op | source)
XLA Modules:
  0.0 195.7 jit_solution(2254703995677836263)
XLA Ops:
  0.7 0.9 pad.20
  1.6 2.0 %collective-permute-start.1 = (bf16[12,1152]{1,0:T(8,128)(2,1)S(1)}, bf16[12,1152]{1,0:T(8,128)(2,1)S(1)}, u32[]{:S(2)}, u32[]{:S(2)}) collective-permute-start(bf16[12,1152]{1,0:T(8,128)(2,1)S(1)} %bitcast.38), channel_id=1, source_target_pairs={{0,32},{4,36},{32,0},{36,4},{64,96},{68,100},{96,64},{100,68},{128... | collective-permute-start | bytes 82952 | tf_op jit(solution)/shard_map/ppermute | solution.py:165
  3.6 1.0 collective-permute-start.2
  4.6 2.1 %collective-permute-start = (bf16[12,1152]{1,0:T(8,128)(2,1)S(1)}, bf16[12,1152]{1,0:T(8,128)(2,1)S(1)}, u32[]{:S(2)}, u32[]{:S(2)}) collective-permute-start(bf16[12,1152]{1,0:T(8,128)(2,1)S(1)} %bitcast.40), channel_id=1, source_target_pairs={{0,4},{4,0},{32,36},{36,32},{64,68},{68,64},{96,100},{100,96},{128... | collective-permute-start | bytes 82952 | tf_op jit(solution)/shard_map/ppermute | solution.py:165
  6.9 1.2 reshape.36
  8.1 2.3 %collective-permute-done = bf16[12,1152]{1,0:T(8,128)(2,1)S(1)} collective-permute-done((bf16[12,1152]{1,0:T(8,128)(2,1)S(1)}, bf16[12,1152]{1,0:T(8,128)(2,1)S(1)}, u32[]{:S(2)}, u32[]{:S(2)}) %collective-permute-start) | collective-permute-done | bytes 27680 | tf_op jit(solution)/shard_map/ppermute | solution.py:165
  10.5 15.5 %all-to-all-start = ((bf16[128,4,1152]{2,1,0:T(4,128)(2,1)}), bf16[128,4,1152]{2,1,0:T(4,128)(2,1)}, u32[]{:S(2)}, u32[]{:S(2)}) async-start(bf16[128,4,1152]{2,1,0:T(4,128)(2,1)} %reshape.36), calls=%async_computation | async-start | bytes 2359296 | tf_op jit(solution)/shard_map/all_to_all | solution.py:234
  26.0 4.2 %collective-permute-start.5 = (bf16[2,24,1152]{2,1,0:T(8,128)(2,1)S(1)}, bf16[2,24,1152]{2,1,0:T(8,128)(2,1)S(1)}, u32[]{:S(2)}, u32[]{:S(2)}) collective-permute-start(bf16[2,24,1152]{2,1,0:T(8,128)(2,1)S(1)} %pad_maximum_fusion.3), channel_id=1, source_target_pairs={{0,192},{32,224},{64,128},{96,160},{128,64},{160,96},{192,0},{224,... | collective-permute-start | bytes 331784 | tf_op jit(solution)/shard_map/ppermute | solution.py:165
  30.2 1.9 collective-permute-start.4
  32.6 30.0 %collective-permute-done.5 = bf16[2,24,1152]{2,1,0:T(8,128)(2,1)S(1)} collective-permute-done((bf16[2,24,1152]{2,1,0:T(8,128)(2,1)S(1)}, bf16[2,24,1152]{2,1,0:T(8,128)(2,1)S(1)}, u32[]{:S(2)}, u32[]{:S(2)}) %collective-permute-start.5) | collective-permute-done | bytes 110624 | tf_op jit(solution)/shard_map/ppermute | solution.py:165
  62.7 1.4 slice.112
  64.5 1.3 collective-permute-start.7
  65.8 1.9 collective-permute-start.6
  67.7 8.8 %collective-permute-done.7.refs_2_ = bf16[8,24,1152]{2,1,0:T(8,128)(2,1)S(1)} collective-permute-done((bf16[8,24,1152]{2,1,0:T(8,128)(2,1)S(1)}, bf16[8,24,1152]{2,1,0:T(8,128)(2,1)S(1)}, u32[]{:S(2)}, u32[]{:S(2)}) %collective-permute-start.7) | collective-permute-done | bytes 442400 | tf_op jit(solution)/shard_map/ppermute | solution.py:161
  77.4 1.7 slice.114
  79.1 3.1 %collective-permute-start.9 = (bf16[4,24,1152]{2,1,0:T(8,128)(2,1)}, bf16[4,24,1152]{2,1,0:T(8,128)(2,1)}, u32[]{:S(2)}, u32[]{:S(2)}) collective-permute-start(bf16[4,24,1152]{2,1,0:T(8,128)(2,1)} %slice.114), channel_id=1, source_target_pairs={{0,24},{8,0},{16,8},{24,16},{1,25},{9,1},{17,9},{25,17},{2,26},{10... | collective-permute-start | bytes 663560 | tf_op jit(solution)/shard_map/ppermute | solution.py:161
  83.0 3.1 %reshape.39.t_ref = bf16[512,1152]{1,0:T(8,128)(2,1)} reshape(bf16[128,4,1152]{2,1,0:T(4,128)(2,1)} %all-to-all-done) | data formatting | bytes 2359296 | tf_op jit(solution)/shard_map/reshape | solution.py:241
  86.1 1.6 reshape.38.o_ref
  88.5 1.0 collective-permute-done.14.refs_8_
  90.1 13.4 %attention_core.1 = (bf16[512,1152]{1,0:T(8,128)(2,1)}, bf16[512,768]{1,0:T(8,128)(2,1)S(1)}, bf16[512,768]{1,0:T(8,128)(2,1)S(1)}) custom-call(s32[4]{0:T(128)S(1)} %pad_add_fusion.where_ref, bf16[512,1152]{1,0:T(8,128)(2,1)} %reshape.39.t_ref, bf16[512,768]{1,0:T(8,128)(2,1)S(1)} %reshape.38.o_ref, bf16[8,24,1152]{2,1,0:T(8,128)(2,1)S(1)} %pad_maximum_fusion.2.refs_0_, ...), custom_call_target="tpu_custom_call" | custom-call | flops 3623878656 | bytes 8388608 | tf_op jit(solution)/shard_map/attention_core/pallas_call | solution.py:94
  103.5 1.3 copy-done.2
  104.7 4.1 %weight_terms.1 = (bf16[4,8,24,1152]{3,2,1,0:T(8,128)(2,1)}, bf16[8,24,1152]{2,1,0:T(8,128)(2,1)S(1)}, bf16[8,24,1152]{2,1,0:T(8,128)(2,1)S(1)}, bf16[8,24,1152]...) custom-call(s32[4]{0:T(128)S(1)} %pad_add_fusion.where_ref, bf16[512,1152]{1,0:T(8,128)(2,1)S(1)} %copy-done.1, ...), custom_call_target="tpu_custom_call" | custom-call | flops 1811939328 | bytes 8388608 | tf_op jit(solution)/shard_map/weight_terms/pallas_call | solution.py:142
  109.1 9.4 %collective-permute-start.17 = (bf16[8,24,1152]{2,1,0:T(8,128)(2,1)S(1)}, bf16[8,24,1152]{2,1,0:T(8,128)(2,1)S(1)}, u32[]{:S(2)}, u32[]{:S(2)}) collective-permute-start(bf16[8,24,1152]{2,1,0:T(8,128)(2,1)S(1)} %get-tuple-element.43), channel_id=1, source_target_pairs={{0,2},{2,0},{1,3},{3,1},{4,6},{6,4},{5,7},{7,5},{8,10},{10,8},{9,1... | collective-permute-start | bytes 1327112 | tf_op jit(solution)/shard_map/ppermute | solution.py:191
  119.1 1.6 collective-permute-start.21
  121.4 1.8 convert_add_fusion
  123.3 2.7 %collective-permute-start.20 = (bf16[4,24,1152]{2,1,0:T(8,128)(2,1)S(1)}, bf16[4,24,1152]{2,1,0:T(8,128)(2,1)S(1)}, u32[]{:S(2)}, u32[]{:S(2)}) collective-permute-start(bf16[4,24,1152]{2,1,0:T(8,128)(2,1)S(1)} %get-tuple-element.64), channel_id=1, source_target_pairs={{0,24},{8,0},{16,8},{24,16},{1,25},{9,1},{17,9},{25,17},{2,26},{10... | collective-permute-start | bytes 663560 | tf_op jit(solution)/shard_map/ppermute | solution.py:161
  127.4 0.8 collective-permute-start.25
  128.2 2.5 %collective-permute-start.24 = (bf16[4,24,1152]{2,1,0:T(8,128)(2,1)}, bf16[4,24,1152]{2,1,0:T(8,128)(2,1)}, u32[]{:S(2)}, u32[]{:S(2)}) collective-permute-start(bf16[4,24,1152]{2,1,0:T(8,128)(2,1)} %slice.166), channel_id=1, source_target_pairs={{0,24},{8,0},{16,8},{24,16},{1,25},{9,1},{17,9},{25,17},{2,26},{10... | collective-permute-start | bytes 663560 | tf_op jit(solution)/shard_map/ppermute | solution.py:161
  130.6 0.7 collective-permute-done.20
  131.4 4.1 %collective-permute-done.19 = bf16[4,24,1152]{2,1,0:T(8,128)(2,1)S(1)} collective-permute-done((bf16[4,24,1152]{2,1,0:T(8,128)(2,1)S(1)}, bf16[4,24,1152]{2,1,0:T(8,128)(2,1)S(1)}, u32[]{:S(2)}, u32[]{:S(2)}) %collective-permute-start.19) | collective-permute-done | bytes 221216 | tf_op jit(solution)/shard_map/ppermute | solution.py:161
  135.5 3.4 %collective-permute-done.21 = bf16[512,768]{1,0:T(8,128)(2,1)S(1)} collective-permute-done((bf16[512,768]{1,0:T(8,128)(2,1)S(1)}, bf16[512,768]{1,0:T(8,128)(2,1)S(1)}, u32[]{:S(2)}, u32[]{:S(2)}) %collective-permute-start.21) | collective-permute-done | bytes 786464 | tf_op jit(solution)/shard_map/ppermute | solution.py:247
  138.8 0.7 fusion.4
  139.8 1.5 collective-permute-start.23
  141.3 1.9 collective-permute-start.26
  143.1 1.1 reshape.40
  144.2 12.1 %all-to-all-start.1 = ((bf16[128,4,768]{2,1,0:T(4,128)(2,1)}), bf16[128,4,768]{2,1,0:T(4,128)(2,1)S(1)}, u32[]{:S(2)}, u32[]{:S(2)}) async-start(bf16[128,4,768]{2,1,0:T(4,128)(2,1)} %reshape.40), calls=%async_computation.1 | async-start | bytes 1572864 | tf_op jit(solution)/shard_map/all_to_all | solution.py:253
  156.3 1.4 fusion.5
  157.9 1.0 collective-permute-start.28
  158.9 3.5 %collective-permute-start.29 = (bf16[4,12,1152]{2,1,0:T(8,128)(2,1)S(1)}, bf16[4,12,1152]{2,1,0:T(8,128)(2,1)S(1)}, u32[]{:S(2)}, u32[]{:S(2)}) collective-permute-start(bf16[4,12,1152]{2,1,0:T(8,128)(2,1)S(1)} %get-tuple-element.67), channel_id=1, source_target_pairs={{0,36},{4,32},{32,4},{36,0},{64,100},{68,96},{96,68},{100,64},{128... | collective-permute-start | bytes 331784 | tf_op jit(solution)/shard_map/ppermute | solution.py:165
  163.0 4.9 %collective-permute-done.28 = bf16[4,12,1152]{2,1,0:T(8,128)(2,1)S(1)} collective-permute-done((bf16[4,12,1152]{2,1,0:T(8,128)(2,1)S(1)}, bf16[4,12,1152]{2,1,0:T(8,128)(2,1)S(1)}, u32[]{:S(2)}, u32[]{:S(2)}) %collective-permute-start.28) | collective-permute-done | bytes 110624 | tf_op jit(solution)/shard_map/ppermute | solution.py:165
  167.9 10.8 %collective-permute-done.29 = bf16[4,12,1152]{2,1,0:T(8,128)(2,1)S(1)} collective-permute-done((bf16[4,12,1152]{2,1,0:T(8,128)(2,1)S(1)}, bf16[4,12,1152]{2,1,0:T(8,128)(2,1)S(1)}, u32[]{:S(2)}, u32[]{:S(2)}) %collective-permute-start.29) | collective-permute-done | bytes 110624 | tf_op jit(solution)/shard_map/ppermute | solution.py:165
  178.7 2.7 %collective-permute-done.27 = bf16[4,12,1152]{2,1,0:T(8,128)(2,1)S(1)} collective-permute-done((bf16[4,12,1152]{2,1,0:T(8,128)(2,1)S(1)}, bf16[4,12,1152]{2,1,0:T(8,128)(2,1)S(1)}, u32[]{:S(2)}, u32[]{:S(2)}) %collective-permute-start.27) | collective-permute-done | bytes 110624 | tf_op jit(solution)/shard_map/ppermute | solution.py:165
  181.5 2.5 %collective-permute-start.30 = (bf16[12,1152]{1,0:T(8,128)(2,1)S(1)}, bf16[12,1152]{1,0:T(8,128)(2,1)S(1)}, u32[]{:S(2)}, u32[]{:S(2)}) collective-permute-start(bf16[12,1152]{1,0:T(8,128)(2,1)S(1)} %get-tuple-element.68), channel_id=1, source_target_pairs={{0,64},{32,96},{64,0},{96,32},{128,192},{160,224},{192,128},{224,1... | collective-permute-start | bytes 82952 | tf_op jit(solution)/shard_map/ppermute | solution.py:165
  184.0 2.9 %collective-permute-start.32 = (bf16[12,1152]{1,0:T(8,128)(2,1)S(1)}, bf16[12,1152]{1,0:T(8,128)(2,1)S(1)}, u32[]{:S(2)}, u32[]{:S(2)}) collective-permute-start(bf16[12,1152]{1,0:T(8,128)(2,1)S(1)} %get-tuple-element.69), channel_id=1, source_target_pairs={{0,192},{32,224},{64,128},{96,160},{128,64},{160,96},{192,0},{224,... | collective-permute-start | bytes 82952 | tf_op jit(solution)/shard_map/ppermute | solution.py:165
  186.9 1.2 collective-permute-start.31
  188.1 1.1 reshape.41
  189.2 0.9 collective-permute-done.32
  190.1 4.7 %collective-permute-done.31 = bf16[12,1152]{1,0:T(8,128)(2,1)S(1)} collective-permute-done((bf16[12,1152]{1,0:T(8,128)(2,1)S(1)}, bf16[12,1152]{1,0:T(8,128)(2,1)S(1)}, u32[]{:S(2)}, u32[]{:S(2)}) %collective-permute-start.31) | collective-permute-done | bytes 27680 | tf_op jit(solution)/shard_map/ppermute | solution.py:165
  (67 shorter events, 9.1 us)
Async XLA Ops:
  0.6 6.1 %copy-start = (bf16[1,512,1536]{2,1,0:T(8,128)(2,1)S(1)}, bf16[1,512,1536]{2,1,0:T(8,128)(2,1)}, u32[]{:S(2)}) copy-start(bf16[1,512,1536]{2,1,0:T(8,128)(2,1)} %param.3) | copy-start | bytes 4718596
  0.6 6.1 %copy-start.3 = (bf16[1,512,384]{2,1,0:T(8,128)(2,1)S(1)}, bf16[1,512,384]{2,1,0:T(8,128)(2,1)}, u32[]{:S(2)}) copy-start(bf16[1,512,384]{2,1,0:T(8,128)(2,1)} %param.4) | copy-start | bytes 1179652
  1.6 8.8 %collective-permute-start.1 = (bf16[12,1152]{1,0:T(8,128)(2,1)S(1)}, bf16[12,1152]{1,0:T(8,128)(2,1)S(1)}, u32[]{:S(2)}, u32[]{:S(2)}) collective-permute-start(bf16[12,1152]{1,0:T(8,128)(2,1)S(1)} %bitcast.38), channel_id=1, source_target_pairs={{0,32},{4,36},{32,0},{36,4},{64,96},{68,100},{96,64},{100,68},{128... | collective-permute-start | bytes 82952 | tf_op jit(solution)/shard_map/ppermute | solution.py:165
  3.6 6.8 %collective-permute-start.2 = (bf16[12,1152]{1,0:T(8,128)(2,1)S(1)}, bf16[12,1152]{1,0:T(8,128)(2,1)S(1)}, u32[]{:S(2)}, u32[]{:S(2)}) collective-permute-start(bf16[12,1152]{1,0:T(8,128)(2,1)S(1)} %bitcast.39), channel_id=1, source_target_pairs={{0,36},{4,32},{32,4},{36,0},{64,100},{68,96},{96,68},{100,64},{128... | collective-permute-start | bytes 82952 | tf_op jit(solution)/shard_map/ppermute | solution.py:165
  4.6 5.8 %collective-permute-start = (bf16[12,1152]{1,0:T(8,128)(2,1)S(1)}, bf16[12,1152]{1,0:T(8,128)(2,1)S(1)}, u32[]{:S(2)}, u32[]{:S(2)}) collective-permute-start(bf16[12,1152]{1,0:T(8,128)(2,1)S(1)} %bitcast.40), channel_id=1, source_target_pairs={{0,4},{4,0},{32,36},{36,32},{64,68},{68,64},{96,100},{100,96},{128... | collective-permute-start | bytes 82952 | tf_op jit(solution)/shard_map/ppermute | solution.py:165
  10.5 52.2 %all-to-all-start = ((bf16[128,4,1152]{2,1,0:T(4,128)(2,1)}), bf16[128,4,1152]{2,1,0:T(4,128)(2,1)}, u32[]{:S(2)}, u32[]{:S(2)}) async-start(bf16[128,4,1152]{2,1,0:T(4,128)(2,1)} %reshape.36), calls=%async_computation | async-start | bytes 2359296 | tf_op jit(solution)/shard_map/all_to_all | solution.py:234
  26.0 36.7 %collective-permute-start.5 = (bf16[2,24,1152]{2,1,0:T(8,128)(2,1)S(1)}, bf16[2,24,1152]{2,1,0:T(8,128)(2,1)S(1)}, u32[]{:S(2)}, u32[]{:S(2)}) collective-permute-start(bf16[2,24,1152]{2,1,0:T(8,128)(2,1)S(1)} %pad_maximum_fusion.3), channel_id=1, source_target_pairs={{0,192},{32,224},{64,128},{96,160},{128,64},{160,96},{192,0},{224,... | collective-permute-start | bytes 331784 | tf_op jit(solution)/shard_map/ppermute | solution.py:165
  30.2 32.5 %collective-permute-start.4 = (bf16[2,24,1152]{2,1,0:T(8,128)(2,1)S(1)}, bf16[2,24,1152]{2,1,0:T(8,128)(2,1)S(1)}, u32[]{:S(2)}, u32[]{:S(2)}) collective-permute-start(bf16[2,24,1152]{2,1,0:T(8,128)(2,1)S(1)} %pad_maximum_fusion.3), channel_id=1, source_target_pairs={{0,128},{32,160},{64,192},{96,224},{128,0},{160,32},{192,64},{224,... | collective-permute-start | bytes 331784 | tf_op jit(solution)/shard_map/ppermute | solution.py:165
  32.1 30.5 %collective-permute-start.3 = (bf16[2,24,1152]{2,1,0:T(8,128)(2,1)S(1)}, bf16[2,24,1152]{2,1,0:T(8,128)(2,1)S(1)}, u32[]{:S(2)}, u32[]{:S(2)}) collective-permute-start(bf16[2,24,1152]{2,1,0:T(8,128)(2,1)S(1)} %pad_maximum_fusion.3), channel_id=1, source_target_pairs={{0,64},{32,96},{64,0},{96,32},{128,192},{160,224},{192,128},{224,1... | collective-permute-start | bytes 331784 | tf_op jit(solution)/shard_map/ppermute | solution.py:165
  64.1 18.6 %collective-permute-start.10 = (bf16[128,4,768]{2,1,0:T(4,128)(2,1)S(1)}, bf16[128,4,768]{2,1,0:T(4,128)(2,1)}, u32[]{:S(2)}, u32[]{:S(2)}) collective-permute-start(bf16[128,4,768]{2,1,0:T(4,128)(2,1)S(1)} %slice.112), channel_id=1, source_target_pairs={{0,1},{1,0},{2,3},{3,2},{4,5},{5,4},{6,7},{7,6},{8,9},{9,8},{10,11... | collective-permute-start | bytes 2359304 | tf_op jit(solution)/shard_map/ppermute | solution.py:238
  64.5 12.0 %collective-permute-start.7 = (bf16[8,24,1152]{2,1,0:T(8,128)(2,1)S(1)}, bf16[8,24,1152]{2,1,0:T(8,128)(2,1)S(1)}, u32[]{:S(2)}, u32[]{:S(2)}) collective-permute-start(bf16[8,24,1152]{2,1,0:T(8,128)(2,1)S(1)} %pad_maximum_fusion.2.refs_0_), channel_id=1, source_target_pairs={{0,8},{8,16},{16,24},{24,0},{1,9},{9,17},{17,25},{25,1},{2,10},{10... | collective-permute-start | bytes 1327112 | tf_op jit(solution)/shard_map/ppermute | solution.py:161
  65.8 11.6 %collective-permute-start.6 = (bf16[8,24,1152]{2,1,0:T(8,128)(2,1)S(1)}, bf16[8,24,1152]{2,1,0:T(8,128)(2,1)}, u32[]{:S(2)}, u32[]{:S(2)}) collective-permute-start(bf16[8,24,1152]{2,1,0:T(8,128)(2,1)S(1)} %pad_maximum_fusion.2.refs_0_), channel_id=1, source_target_pairs={{0,24},{8,0},{16,8},{24,16},{1,25},{9,1},{17,9},{25,17},{2,26},{10... | collective-permute-start | bytes 1327112 | tf_op jit(solution)/shard_map/ppermute | solution.py:161
  77.2 10.4 %collective-permute-start.8 = (bf16[4,24,1152]{2,1,0:T(8,128)(2,1)}, bf16[4,24,1152]{2,1,0:T(8,128)(2,1)S(1)}, u32[]{:S(2)}, u32[]{:S(2)}) collective-permute-start(bf16[4,24,1152]{2,1,0:T(8,128)(2,1)} %slice.113), channel_id=1, source_target_pairs={{0,8},{8,16},{16,24},{24,0},{1,9},{9,17},{17,25},{25,1},{2,10},{10... | collective-permute-start | bytes 663560 | tf_op jit(solution)/shard_map/ppermute | solution.py:161
  79.1 8.6 %collective-permute-start.9 = (bf16[4,24,1152]{2,1,0:T(8,128)(2,1)}, bf16[4,24,1152]{2,1,0:T(8,128)(2,1)}, u32[]{:S(2)}, u32[]{:S(2)}) collective-permute-start(bf16[4,24,1152]{2,1,0:T(8,128)(2,1)} %slice.114), channel_id=1, source_target_pairs={{0,24},{8,0},{16,8},{24,16},{1,25},{9,1},{17,9},{25,17},{2,26},{10... | collective-permute-start | bytes 663560 | tf_op jit(solution)/shard_map/ppermute | solution.py:161
  82.1 6.3 %collective-permute-start.11 = (bf16[8,24,1152]{2,1,0:T(8,128)(2,1)S(1)}, bf16[8,24,1152]{2,1,0:T(8,128)(2,1)}, u32[]{:S(2)}, u32[]{:S(2)}) collective-permute-start(bf16[8,24,1152]{2,1,0:T(8,128)(2,1)S(1)} %pad_maximum_fusion.2.refs_0_), channel_id=1, source_target_pairs={{0,2},{2,0},{1,3},{3,1},{4,6},{6,4},{5,7},{7,5},{8,10},{10,8},{9,1... | collective-permute-start | bytes 1327112 | tf_op jit(solution)/shard_map/ppermute | solution.py:242
  82.1 6.3 %collective-permute-start.13 = (bf16[8,24,1152]{2,1,0:T(8,128)(2,1)S(1)}, bf16[8,24,1152]{2,1,0:T(8,128)(2,1)}, u32[]{:S(2)}, u32[]{:S(2)}) collective-permute-start(bf16[8,24,1152]{2,1,0:T(8,128)(2,1)S(1)} %collective-permute-done.7.refs_2_), channel_id=1, source_target_pairs={{0,2},{2,0},{1,3},{3,1},{4,6},{6,4},{5,7},{7,5},{8,10},{10,8},{9,1... | collective-permute-start | bytes 1327112 | tf_op jit(solution)/shard_map/ppermute | solution.py:242
  82.7 5.7 %collective-permute-start.12 = (bf16[8,24,1152]{2,1,0:T(8,128)(2,1)}, bf16[8,24,1152]{2,1,0:T(8,128)(2,1)}, u32[]{:S(2)}, u32[]{:S(2)}) collective-permute-start(bf16[8,24,1152]{2,1,0:T(8,128)(2,1)} %collective-permute-done.6.refs_1_), channel_id=1, source_target_pairs={{0,2},{2,0},{1,3},{3,1},{4,6},{6,4},{5,7},{7,5},{8,10},{10,8},{9,1... | collective-permute-start | bytes 1327112 | tf_op jit(solution)/shard_map/ppermute | solution.py:242
  87.7 1.8 collective-permute-start.14
  88.3 1.8 collective-permute-start.15
  88.4 15.0 %copy-start.1 = (bf16[512,1152]{1,0:T(8,128)(2,1)S(1)}, bf16[512,1152]{1,0:T(8,128)(2,1)}, u32[]{:S(2)}) copy-start(bf16[512,1152]{1,0:T(8,128)(2,1)} %reshape.39.t_ref) | copy-start | bytes 3538948
  103.5 1.3 copy-start.2
  108.8 11.8 %collective-permute-start.16 = (bf16[8,24,1152]{2,1,0:T(8,128)(2,1)S(1)}, bf16[8,24,1152]{2,1,0:T(8,128)(2,1)S(1)}, u32[]{:S(2)}, u32[]{:S(2)}) collective-permute-start(bf16[8,24,1152]{2,1,0:T(8,128)(2,1)S(1)} %get-tuple-element.42), channel_id=1, source_target_pairs={{0,2},{2,0},{1,3},{3,1},{4,6},{6,4},{5,7},{7,5},{8,10},{10,8},{9,1... | collective-permute-start | bytes 1327112 | tf_op jit(solution)/shard_map/ppermute | solution.py:191
  109.1 11.5 %collective-permute-start.17 = (bf16[8,24,1152]{2,1,0:T(8,128)(2,1)S(1)}, bf16[8,24,1152]{2,1,0:T(8,128)(2,1)S(1)}, u32[]{:S(2)}, u32[]{:S(2)}) collective-permute-start(bf16[8,24,1152]{2,1,0:T(8,128)(2,1)S(1)} %get-tuple-element.43), channel_id=1, source_target_pairs={{0,2},{2,0},{1,3},{3,1},{4,6},{6,4},{5,7},{7,5},{8,10},{10,8},{9,1... | collective-permute-start | bytes 1327112 | tf_op jit(solution)/shard_map/ppermute | solution.py:191
  118.6 2.2 %collective-permute-start.18 = (bf16[8,24,1152]{2,1,0:T(8,128)(2,1)S(1)}, bf16[8,24,1152]{2,1,0:T(8,128)(2,1)S(1)}, u32[]{:S(2)}, u32[]{:S(2)}) collective-permute-start(bf16[8,24,1152]{2,1,0:T(8,128)(2,1)S(1)} %get-tuple-element.44), channel_id=1, source_target_pairs={{0,2},{2,0},{1,3},{3,1},{4,6},{6,4},{5,7},{7,5},{8,10},{10,8},{9,1... | collective-permute-start | bytes 1327112 | tf_op jit(solution)/shard_map/ppermute | solution.py:190
  118.9 2.5 %collective-permute-start.22 = (bf16[8,24,1152]{2,1,0:T(8,128)(2,1)S(1)}, bf16[8,24,1152]{2,1,0:T(8,128)(2,1)S(1)}, u32[]{:S(2)}, u32[]{:S(2)}) collective-permute-start(bf16[8,24,1152]{2,1,0:T(8,128)(2,1)S(1)} %get-tuple-element.47), channel_id=1, source_target_pairs={{0,2},{2,0},{1,3},{3,1},{4,6},{6,4},{5,7},{7,5},{8,10},{10,8},{9,1... | collective-permute-start | bytes 1327112 | tf_op jit(solution)/shard_map/ppermute | solution.py:191
  119.1 19.8 %collective-permute-start.21 = (bf16[512,768]{1,0:T(8,128)(2,1)S(1)}, bf16[512,768]{1,0:T(8,128)(2,1)S(1)}, u32[]{:S(2)}, u32[]{:S(2)}) collective-permute-start(bf16[512,768]{1,0:T(8,128)(2,1)S(1)} %get-tuple-element.45), channel_id=1, source_target_pairs={{0,1},{1,0},{2,3},{3,2},{4,5},{5,4},{6,7},{7,6},{8,9},{9,8},{10,11... | collective-permute-start | bytes 2359304 | tf_op jit(solution)/shard_map/ppermute | solution.py:247
  123.3 8.1 %collective-permute-start.20 = (bf16[4,24,1152]{2,1,0:T(8,128)(2,1)S(1)}, bf16[4,24,1152]{2,1,0:T(8,128)(2,1)S(1)}, u32[]{:S(2)}, u32[]{:S(2)}) collective-permute-start(bf16[4,24,1152]{2,1,0:T(8,128)(2,1)S(1)} %get-tuple-element.64), channel_id=1, source_target_pairs={{0,24},{8,0},{16,8},{24,16},{1,25},{9,1},{17,9},{25,17},{2,26},{10... | collective-permute-start | bytes 663560 | tf_op jit(solution)/shard_map/ppermute | solution.py:161
  126.0 9.5 %collective-permute-start.19 = (bf16[4,24,1152]{2,1,0:T(8,128)(2,1)S(1)}, bf16[4,24,1152]{2,1,0:T(8,128)(2,1)S(1)}, u32[]{:S(2)}, u32[]{:S(2)}) collective-permute-start(bf16[4,24,1152]{2,1,0:T(8,128)(2,1)S(1)} %get-tuple-element.65), channel_id=1, source_target_pairs={{0,8},{8,16},{16,24},{24,0},{1,9},{9,17},{17,25},{25,1},{2,10},{10... | collective-permute-start | bytes 663560 | tf_op jit(solution)/shard_map/ppermute | solution.py:161
  127.4 28.9 %collective-permute-start.25 = (bf16[4,24,1152]{2,1,0:T(8,128)(2,1)}, bf16[4,24,1152]{2,1,0:T(8,128)(2,1)}, u32[]{:S(2)}, u32[]{:S(2)}) collective-permute-start(bf16[4,24,1152]{2,1,0:T(8,128)(2,1)} %slice.165), channel_id=1, source_target_pairs={{0,8},{8,16},{16,24},{24,0},{1,9},{9,17},{17,25},{25,1},{2,10},{10... | collective-permute-start | bytes 663560 | tf_op jit(solution)/shard_map/ppermute | solution.py:161
  128.2 28.1 %collective-permute-start.24 = (bf16[4,24,1152]{2,1,0:T(8,128)(2,1)}, bf16[4,24,1152]{2,1,0:T(8,128)(2,1)}, u32[]{:S(2)}, u32[]{:S(2)}) collective-permute-start(bf16[4,24,1152]{2,1,0:T(8,128)(2,1)} %slice.166), channel_id=1, source_target_pairs={{0,24},{8,0},{16,8},{24,16},{1,25},{9,1},{17,9},{25,17},{2,26},{10... | collective-permute-start | bytes 663560 | tf_op jit(solution)/shard_map/ppermute | solution.py:161
  139.8 16.5 %collective-permute-start.23 = (bf16[4,24,1152]{2,1,0:T(8,128)(2,1)}, bf16[4,24,1152]{2,1,0:T(8,128)(2,1)}, u32[]{:S(2)}, u32[]{:S(2)}) collective-permute-start(bf16[4,24,1152]{2,1,0:T(8,128)(2,1)} %fusion.4), channel_id=1, source_target_pairs={{0,8},{8,16},{16,24},{24,0},{1,9},{9,17},{17,25},{25,1},{2,10},{10... | collective-permute-start | bytes 663560 | tf_op jit(solution)/shard_map/ppermute | solution.py:161
  141.3 15.0 %collective-permute-start.26 = (bf16[4,24,1152]{2,1,0:T(8,128)(2,1)S(1)}, bf16[4,24,1152]{2,1,0:T(8,128)(2,1)}, u32[]{:S(2)}, u32[]{:S(2)}) collective-permute-start(bf16[4,24,1152]{2,1,0:T(8,128)(2,1)S(1)} %fusion.3), channel_id=1, source_target_pairs={{0,24},{8,0},{16,8},{24,16},{1,25},{9,1},{17,9},{25,17},{2,26},{10... | collective-permute-start | bytes 663560 | tf_op jit(solution)/shard_map/ppermute | solution.py:161
  144.2 37.3 %all-to-all-start.1 = ((bf16[128,4,768]{2,1,0:T(4,128)(2,1)}), bf16[128,4,768]{2,1,0:T(4,128)(2,1)S(1)}, u32[]{:S(2)}, u32[]{:S(2)}) async-start(bf16[128,4,768]{2,1,0:T(4,128)(2,1)} %reshape.40), calls=%async_computation.1 | async-start | bytes 1572864 | tf_op jit(solution)/shard_map/all_to_all | solution.py:253
  157.9 10.0 %collective-permute-start.28 = (bf16[4,12,1152]{2,1,0:T(8,128)(2,1)S(1)}, bf16[4,12,1152]{2,1,0:T(8,128)(2,1)S(1)}, u32[]{:S(2)}, u32[]{:S(2)}) collective-permute-start(bf16[4,12,1152]{2,1,0:T(8,128)(2,1)S(1)} %get-tuple-element.66), channel_id=1, source_target_pairs={{0,4},{4,0},{32,36},{36,32},{64,68},{68,64},{96,100},{100,96},{128... | collective-permute-start | bytes 331784 | tf_op jit(solution)/shard_map/ppermute | solution.py:165
  158.9 19.8 %collective-permute-start.29 = (bf16[4,12,1152]{2,1,0:T(8,128)(2,1)S(1)}, bf16[4,12,1152]{2,1,0:T(8,128)(2,1)S(1)}, u32[]{:S(2)}, u32[]{:S(2)}) collective-permute-start(bf16[4,12,1152]{2,1,0:T(8,128)(2,1)S(1)} %get-tuple-element.67), channel_id=1, source_target_pairs={{0,36},{4,32},{32,4},{36,0},{64,100},{68,96},{96,68},{100,64},{128... | collective-permute-start | bytes 331784 | tf_op jit(solution)/shard_map/ppermute | solution.py:165
  162.4 19.0 %collective-permute-start.27 = (bf16[4,12,1152]{2,1,0:T(8,128)(2,1)S(1)}, bf16[4,12,1152]{2,1,0:T(8,128)(2,1)S(1)}, u32[]{:S(2)}, u32[]{:S(2)}) collective-permute-start(bf16[4,12,1152]{2,1,0:T(8,128)(2,1)S(1)} %slice.105), channel_id=1, source_target_pairs={{0,32},{4,36},{32,0},{36,4},{64,96},{68,100},{96,64},{100,68},{128... | collective-permute-start | bytes 331784 | tf_op jit(solution)/shard_map/ppermute | solution.py:165
  181.5 7.6 %collective-permute-start.30 = (bf16[12,1152]{1,0:T(8,128)(2,1)S(1)}, bf16[12,1152]{1,0:T(8,128)(2,1)S(1)}, u32[]{:S(2)}, u32[]{:S(2)}) collective-permute-start(bf16[12,1152]{1,0:T(8,128)(2,1)S(1)} %get-tuple-element.68), channel_id=1, source_target_pairs={{0,64},{32,96},{64,0},{96,32},{128,192},{160,224},{192,128},{224,1... | collective-permute-start | bytes 82952 | tf_op jit(solution)/shard_map/ppermute | solution.py:165
  184.0 6.1 %collective-permute-start.32 = (bf16[12,1152]{1,0:T(8,128)(2,1)S(1)}, bf16[12,1152]{1,0:T(8,128)(2,1)S(1)}, u32[]{:S(2)}, u32[]{:S(2)}) collective-permute-start(bf16[12,1152]{1,0:T(8,128)(2,1)S(1)} %get-tuple-element.69), channel_id=1, source_target_pairs={{0,192},{32,224},{64,128},{96,160},{128,64},{160,96},{192,0},{224,... | collective-permute-start | bytes 82952 | tf_op jit(solution)/shard_map/ppermute | solution.py:165
  186.9 7.9 %collective-permute-start.31 = (bf16[12,1152]{1,0:T(8,128)(2,1)S(1)}, bf16[12,1152]{1,0:T(8,128)(2,1)S(1)}, u32[]{:S(2)}, u32[]{:S(2)}) collective-permute-start(bf16[12,1152]{1,0:T(8,128)(2,1)S(1)} %get-tuple-element.70), channel_id=1, source_target_pairs={{0,128},{32,160},{64,192},{96,224},{128,0},{160,32},{192,64},{224,... | collective-permute-start | bytes 82952 | tf_op jit(solution)/shard_map/ppermute | solution.py:165

commit v3 on v2

--- a/solution.py
+++ b/solution.py
@@ -9,6 +9,7 @@
 Z, Y, XH, C, MP = 8, 4, 2, 2, 2
 F = 128
 ROWS = 12
+VMEM_LIMIT = 32 * 2**20
 bf16, f32 = jnp.bfloat16, jnp.float32
 NT = (((1,), (1,)), ((), ()))
 TN = (((0,), (0,)), ((), ()))
@@ -19,22 +20,21 @@
 
 
 def core_kernel(where_ref, t_ref, o_ref, *refs):
-    pieces = refs[:10]
-    g_ref, give_ref, keep_ref, w_ref, s_ref, d_ref = refs[10:]
+    pieces = refs[:16]
+    give_ref, keep_ref, mine_ref, rest_ref, w_ref, s_ref, d_ref, g_ref = refs[16:]
     z, y, c, m = (where_ref[i] for i in range(4))
     unit = XH * C * ROWS
-    for by in range(Y):
-        for t in range(Z):
-            if by == 2:
-                which, at = (3, t) if t < Z // 2 else (4, t - Z // 2)
-            else:
-                which, at = (0, 1, None, 2)[by], t
-            a = pieces[which][at].astype(f32)
-            b = pieces[which + 5][at].astype(f32)
+
+    @pl.loop(0, Z // 2)
+    def _(t):
+        for i in range(8):
+            by, high = i // 2, i % 2
+            a = pieces[i][t].astype(f32)
+            b = pieces[i + 8][t].astype(f32)
             first = jnp.where(c == 0, a, b)
             second = jnp.where(c == 0, b, a)
             rows = [first[:ROWS], second[:ROWS], first[ROWS:], second[ROWS:]]
-            to = lax.bitwise_xor(z, t) * Y + lax.rem(by + y, Y)
+            to = lax.bitwise_xor(z, t + high * (Z // 2)) * Y + lax.rem(by + y, Y)
             to = pl.ds(pl.multiple_of(to * unit, unit), unit)
             w_ref[to, :] = jnp.concatenate(rows, 0).astype(bf16)
 
@@ -61,7 +61,8 @@
     def split(v):
         return jnp.concatenate([jnp.where(low, v, zero), jnp.where(low, zero, v)], 0).astype(bf16)
 
-    for p in range(count):
+    @pl.loop(0, count)
+    def _(p):
         at = pl.ds(p, F, stride=count)
         for pair in range(pairs):
             q, k, v, u = (s_ref[j * pairs + pair, at, :] for j in range(4))
@@ -84,6 +85,21 @@
     g_ref[...] = g
     give_ref[...] = dot(g, w_ref[away, :], NT).astype(bf16)
     keep_ref[...] = dot(g, w_ref[near, :], NT).astype(bf16)
+    step = 384
+    for ref, of in ((t_ref, m), (o_ref, 1 - m)):
+
+        @pl.loop(0, part_cols // step)
+        def _(i, ref=ref, of=of):
+            total = dot(ref[:, pl.ds(pl.multiple_of(i * step, step), step)], g_ref[...], TN)
+            for b in range(step // unit):
+                quarters = [total[b * unit + r * ROWS :][:ROWS] for r in range(4)]
+                first = jnp.concatenate([quarters[0], quarters[2]], 0)
+                second = jnp.concatenate([quarters[1], quarters[3]], 0)
+                by = lax.rem(b % Y + Y - y, Y)
+                at = i * (step // unit // Y) + b // Y
+                t = lax.bitwise_xor(of * (Z // MP) + at, z)
+                mine_ref[by, t] = jnp.where(c == 0, first, second).astype(bf16)
+                rest_ref[by, t] = jnp.where(c == 0, second, first).astype(bf16)
 
 
 def core(where, tokens, others, mine, rest):
@@ -94,63 +110,60 @@
     return pl.pallas_call(
         core_kernel,
         out_shape=(
-            jax.ShapeDtypeStruct((rows, n), bf16),
             jax.ShapeDtypeStruct((rows, part_cols), bf16),
             jax.ShapeDtypeStruct((rows, part_cols), bf16),
+            jax.ShapeDtypeStruct((Y, Z, XH * ROWS, n), bf16),
+            jax.ShapeDtypeStruct((Y, Z, XH * ROWS, n), bf16),
         ),
-        in_specs=[pl.BlockSpec(memory_space=pltpu.SMEM)] + [vm] * 12,
-        out_specs=(vm, vm, vm),
+        in_specs=[pl.BlockSpec(memory_space=pltpu.SMEM)] + [vm] * 18,
+        out_specs=(vm,) * 4,
         scratch_shapes=[
             pltpu.VMEM((width, n), bf16),
             pltpu.VMEM((4 * half // 128, rows, 128), f32),
             pltpu.VMEM((3 * half // 128, rows, 128), f32),
+            pltpu.VMEM((rows, n), bf16),
         ],
-        compiler_params=pltpu.CompilerParams(vmem_limit_bytes=48 * 2**20),
+        compiler_params=pltpu.CompilerParams(vmem_limit_bytes=VMEM_LIMIT),
         cost_estimate=pl.CostEstimate(
-            flops=4 * rows * width * n, bytes_accessed=8 * 2**20, transcendentals=0
+            flops=6 * rows * width * n, bytes_accessed=8 * 2**20, transcendentals=0
         ),
         name="attention_core",
     )(where, tokens, others, *mine, *rest)
 
 
-def term_kernel(where_ref, t_ref, o_ref, g_ref, mine_ref, *refs):
-    rest_refs, rest_ref = refs[:Y], refs[Y]
-    z, y, c, m = (where_ref[i] for i in range(4))
-    part_cols = o_ref.shape[1]
-    step, unit = 384, XH * C * ROWS
-    g = g_ref[...]
-    for ref, of in ((t_ref, m), (o_ref, 1 - m)):
-        for i in range(part_cols // step):
-            total = dot(ref[:, i * step : (i + 1) * step], g, TN)
-            for b in range(step // unit):
-                quarters = [total[b * unit + r * ROWS :][:ROWS] for r in range(4)]
-                first = jnp.concatenate([quarters[0], quarters[2]], 0)
-                second = jnp.concatenate([quarters[1], quarters[3]], 0)
-                by = lax.rem(b % Y + Y - y, Y)
-                at = (i * step // unit + b) // Y
-                t = lax.bitwise_xor(of * (Z // MP) + at, z)
-                mine_ref[by, t] = jnp.where(c == 0, first, second).astype(bf16)
-                rest_ref[by, t] = jnp.where(c == 0, second, first).astype(bf16)
-    for by in range(Y):
-        rest_refs[by][...] = rest_ref[by]
-
-
-def terms(where, tokens, others, grads):
-    n = grads.shape[1]
+def combine_kernel(mine_ref, other_ref, *refs):
+    own_ref, after_ref, before_ref, far_low, far_high, after_high, before_low = refs
+    h = Z // 2
+
+    def added(by, t):
+        return mine_ref[by, t].astype(f32) + other_ref[by, t].astype(f32)
+
+    @pl.loop(0, h)
+    def _(t):
+        far_low[t] = added(2, t).astype(bf16)
+        far_high[t] = added(2, t + h).astype(bf16)
+        own_ref[t] = added(0, t)
+        own_ref[t + h] = added(0, t + h)
+        after_ref[t] = added(1, t)
+        after_high[t] = added(1, t + h).astype(bf16)
+        before_low[t] = added(3, t).astype(bf16)
+        before_ref[t] = added(3, t + h)
+
+
+def combine(mine, other):
     vm = pl.BlockSpec(memory_space=pltpu.VMEM)
-    shape = (Y, Z, XH * ROWS, n)
+    block = mine.shape[2:]
+    h = Z // 2
     return pl.pallas_call(
-        term_kernel,
-        out_shape=[jax.ShapeDtypeStruct(shape, bf16)] + [jax.ShapeDtypeStruct(shape[1:], bf16)] * Y,
-        in_specs=[pl.BlockSpec(memory_space=pltpu.SMEM)] + [vm] * 3,
-        out_specs=[vm] * (1 + Y),
-        scratch_shapes=[pltpu.VMEM(shape, bf16)],
-        compiler_params=pltpu.CompilerParams(vmem_limit_bytes=48 * 2**20),
-        cost_estimate=pl.CostEstimate(
-            flops=2 * 512 * 1536 * n, bytes_accessed=8 * 2**20, transcendentals=0
-        ),
-        name="weight_terms",
-    )(where, tokens, others, grads)
+        combine_kernel,
+        out_shape=[jax.ShapeDtypeStruct((n,) + block, f32) for n in (Z, h, h)]
+        + [jax.ShapeDtypeStruct((h,) + block, bf16)] * 4,
+        in_specs=[vm, vm],
+        out_specs=[vm] * 7,
+        compiler_params=pltpu.CompilerParams(vmem_limit_bytes=VMEM_LIMIT),
+        cost_estimate=pl.CostEstimate(flops=0, bytes_accessed=2**20, transcendentals=0),
+        name="combine_cores",
+    )(mine, other)
 
 
 FR = ("z", "y", "xh", "c")
@@ -176,29 +189,29 @@
     return jnp.stack([first, second], 0)
 
 
-def over_y(own):
-    before = shift(own, "y", Y, 1)
-    after = shift(own, "y", Y, Y - 1)
-    low = shift(before[: Z // 2], "y", Y, 1)
-    high = shift(after[Z // 2 :], "y", Y, Y - 1)
-    return [own, after, before, low, high]
+def over_y(low, high):
+    before_low = shift(low, "y", Y, 1)
+    after_high = shift(high, "y", Y, Y - 1)
+    before_high = shift(high, "y", Y, 1)
+    after_low = shift(low, "y", Y, Y - 1)
+    far_low = shift(before_low, "y", Y, 1)
+    far_high = shift(after_high, "y", Y, Y - 1)
+    return [low, high, after_low, after_high, far_low, far_high, before_low, before_high]
 
 
 def reduce_weight(mine, rest, got, finish, late):
     even = lax.axis_index("xh") == 0
-    rest = list(rest)
-    rest[2] = lax.ppermute(rest[2], "c", PAIR)
-    other = [rest[i] if i == 2 else lax.ppermute(rest[i], "c", PAIR) for i in range(Y)]
+    other = lax.ppermute(rest, "c", PAIR)
     h = Z // 2
-    own, after, far, before = (mine[i].astype(f32) + other[i].astype(f32) for i in range(Y))
-    up_far = shift(far[:h].astype(bf16), "y", Y, 1)
-    down_far = shift(far[h:].astype(bf16), "y", Y, Y - 1)
-    up_high = shift(after[h:].astype(bf16), "y", Y, 1)
-    down_low = shift(before[:h].astype(bf16), "y", Y, Y - 1)
+    own, after, before, far_low, far_high, after_high, before_low = combine(mine, other)
+    up_far = shift(far_low, "y", Y, 1)
+    down_far = shift(far_high, "y", Y, Y - 1)
+    up_high = shift(after_high, "y", Y, 1)
+    down_low = shift(before_low, "y", Y, Y - 1)
     up_far, down_far, got = lax.optimization_barrier((up_far, down_far, got))
     summed = finish(got)
-    up_low = (after[:h] + up_far.astype(f32)).astype(bf16)
-    down_high = (before[h:] + down_far.astype(f32)).astype(bf16)
+    up_low = (after + up_far.astype(f32)).astype(bf16)
+    down_high = (before + down_far.astype(f32)).astype(bf16)
     up_low, down_high, summed = lax.optimization_barrier((up_low, down_high, summed))
     up_low = shift(up_low, "y", Y, 1)
     down_high = shift(down_high, "y", Y, Y - 1)
@@ -232,18 +245,20 @@
     pair = over_xh_and_pair(w_qkv.reshape(w_qkv.shape[0], n))
     tokens, pair = lax.optimization_barrier((tokens, pair))
     tokens = lax.all_to_all(tokens, FR, 0, 0, tiled=True)
-    own = jnp.concatenate([pair] + [across(pair, "z", Z, 2 * i) for i in range(1, Z // 2)], 0)
+    two, four, six = (across(pair, "z", Z, 2 * i) for i in range(1, Z // 2))
+    low, high = jnp.concatenate([pair, two], 0), jnp.concatenate([four, six], 0)
     part = tokens[:, :, :cols]
-    own, part = lax.optimization_barrier((own, part))
+    low, high, part = lax.optimization_barrier((low, high, part))
     others = lax.ppermute(part, "mp", PAIR)
-    mine = over_y(own)
+    mine = over_y(low, high)
     others = others.reshape(F * count, cols)
     tokens = tokens.reshape(F * count, cols + half)
-    rest = [lax.ppermute(p, "c", PAIR) for p in mine[:3]]
+    rest = {i: lax.ppermute(mine[i], "c", PAIR) for i in (0, 1, 2, 3, 6, 7)}
     mine, others, tokens = lax.optimization_barrier((mine, others, tokens))
-    rest = rest + [lax.ppermute(p, "c", PAIR) for p in mine[3:]]
-
-    grads, give, keep = core(where, tokens, others, mine, rest)
+    rest.update({i: lax.ppermute(mine[i], "c", PAIR) for i in (4, 5)})
+
+    rest = [rest[i] for i in range(8)]
+    give, keep, mine, rest = core(where, tokens, others, mine, rest)
     got = lax.ppermute(give, "mp", PAIR)
 
     def finish(got):
@@ -252,7 +267,6 @@
     def to_frames(x):
         return lax.all_to_all(x.reshape(F, count, cols), FR, 0, 0, tiled=True)
 
-    mine, *rest = terms(where, tokens, others, grads)
     weight_grad, back = reduce_weight(mine, rest, got, finish, to_frames)
     input_grad = back.reshape(frames_dev, patches, cols)
     weight_grad = weight_grad * (1.0 / F)

time: 200 us -> 187 us (0.935); the launches traced: 196 us -> 187 us
  starting transfers between devices: 80.3 us -> 69 us
  waiting for transfers between devices: 75.8 us -> 81.1 us
    ppermute x9, starting transfers between devices: 11.7 us -> 2.03 us  [the longest x6 1.11 us: on_device(): rest = {i: lax.ppermute(mine[i], 'c', PAIR) for i in (0, 1, 2, 3, 6, 7)}]
    ppermute x10 -> x12, waiting for transfers between devices: 13.7 us -> 5.23 us  [shift(): return lax.ppermute(x, axis, [(i, (i + by) % size) for i in range(size)])]
    ppermute x1, waiting for transfers between devices: 3.37 us -> 10.5 us  [on_device(): got = lax.ppermute(give, 'mp', PAIR)]
    slice x5 -> x0, local copies, waits for them, and re-layouts: 3.81 us -> none  [the longest x1 1.65 us: over_y(): high = shift(after[Z // 2:], 'y', Y, Y - 1)]
    ppermute x9, waiting for transfers between devices: 2.39 us -> 4.75 us  [the longest x1 3.09 us: reduce_weight(): other = lax.ppermute(rest, 'c', PAIR)]
    ppermute x1, waiting for transfers between devices: 0.07 us -> 2.4 us  [on_device(): others = lax.ppermute(part, 'mp', PAIR)]
    ppermute x10 -> x12, starting transfers between devices: 15.7 us -> 17.2 us  [shift(): return lax.ppermute(x, axis, [(i, (i + by) % size) for i in range(size)])]
  transfers between devices with their start and end apart: 35 -> 37, of which waited for: 16 -> 17; matrix products, arithmetic and copies ran while one was open for 8% -> 8% of each run, Pallas kernels for 0% -> 0%
where the time goes in v3:
time: 187 us
  waiting for transfers between devices  81.1 us (43%)
  starting transfers between devices  69 us (37%)
  Pallas kernels  16.8 us (9%)
  local copies, waits for them, and re-layouts  14.5 us (8%)
  other arithmetic  4.49 us (2%)
    ppermute x12, waiting for transfers between devices, across(): return lax.ppermute(x, axis, [(i, i ^ by) for i in range(size)])  58.1 us
    ppermute x12, starting transfers between devices, across(): return lax.ppermute(x, axis, [(i, i ^ by) for i in range(size)])  23.3 us
    ppermute x12, starting transfers between devices, shift(): return lax.ppermute(x, axis, [(i, (i + by) % size) for i in range(size)])  17.2 us
    pallas_call x1, Pallas kernels, core(): pl.pallas_call(core_kernel, out_shape=(jax.ShapeDtypeStruct((rows, part_c...  16.4 us
    all_to_all x1, starting transfers between devices, on_device(): tokens = lax.all_to_all(tokens, FR, 0, 0, tiled=True)  15.1 us
    all_to_all x1, starting transfers between devices, to_frames(): return lax.all_to_all(x.reshape(F, count, cols), FR, 0, 0, tiled=True)  10.8 us
    ppermute x1, waiting for transfers between devices, on_device(): got = lax.ppermute(give, 'mp', PAIR)  10.5 us
    ppermute x12, waiting for transfers between devices, shift(): return lax.ppermute(x, axis, [(i, (i + by) % size) for i in range(size)])  5.23 us
  transfers between devices with their start and end apart: 37, of which 17 were waited for; matrix products, arithmetic and copies ran while one was open for 8% of the time, Pallas kernels for 0%

profile of v3, /device:TPU:6, one launch (start us, length us, event | category | flops | bytes accessed | tf_op | source)
XLA Modules:
  0.0 186.8 jit_solution(8773913758390492978)
XLA Ops:
  0.7 0.9 pad.20
  1.6 2.0 %collective-permute-start.1 = (bf16[12,1152]{1,0:T(8,128)(2,1)S(1)}, bf16[12,1152]{1,0:T(8,128)(2,1)S(1)}, u32[]{:S(2)}, u32[]{:S(2)}) collective-permute-start(bf16[12,1152]{1,0:T(8,128)(2,1)S(1)} %bitcast.26), channel_id=1, source_target_pairs={{0,32},{4,36},{32,0},{36,4},{64,96},{68,100},{96,64},{100,68},{128... | collective-permute-start | bytes 82952 | tf_op jit(solution)/shard_map/ppermute | solution.py:178
  3.6 1.0 collective-permute-start.2
  4.6 2.1 %collective-permute-start = (bf16[12,1152]{1,0:T(8,128)(2,1)S(1)}, bf16[12,1152]{1,0:T(8,128)(2,1)S(1)}, u32[]{:S(2)}, u32[]{:S(2)}) collective-permute-start(bf16[12,1152]{1,0:T(8,128)(2,1)S(1)} %bitcast.28), channel_id=1, source_target_pairs={{0,4},{4,0},{32,36},{36,32},{64,68},{68,64},{96,100},{100,96},{128... | collective-permute-start | bytes 82952 | tf_op jit(solution)/shard_map/ppermute | solution.py:178
  6.9 1.2 reshape.28
  8.1 2.3 %collective-permute-done = bf16[12,1152]{1,0:T(8,128)(2,1)S(1)} collective-permute-done((bf16[12,1152]{1,0:T(8,128)(2,1)S(1)}, bf16[12,1152]{1,0:T(8,128)(2,1)S(1)}, u32[]{:S(2)}, u32[]{:S(2)}) %collective-permute-start) | collective-permute-done | bytes 27680 | tf_op jit(solution)/shard_map/ppermute | solution.py:178
  10.5 15.1 %all-to-all-start = ((bf16[128,4,1152]{2,1,0:T(4,128)(2,1)}), bf16[128,4,1152]{2,1,0:T(4,128)(2,1)S(1)}, u32[]{:S(2)}, u32[]{:S(2)}) async-start(bf16[128,4,1152]{2,1,0:T(4,128)(2,1)} %reshape.28), calls=%async_computation | async-start | bytes 2359296 | tf_op jit(solution)/shard_map/all_to_all | solution.py:247
  25.6 2.6 %collective-permute-start.3 = (bf16[2,24,1152]{2,1,0:T(8,128)(2,1)S(1)}, bf16[2,24,1152]{2,1,0:T(8,128)(2,1)S(1)}, u32[]{:S(2)}, u32[]{:S(2)}) collective-permute-start(bf16[2,24,1152]{2,1,0:T(8,128)(2,1)S(1)} %pad_maximum_fusion.4), channel_id=1, source_target_pairs={{0,64},{32,96},{64,0},{96,32},{128,192},{160,224},{192,128},{224,1... | collective-permute-start | bytes 331784 | tf_op jit(solution)/shard_map/ppermute | solution.py:178
  28.1 3.8 %collective-permute-start.5 = (bf16[2,24,1152]{2,1,0:T(8,128)(2,1)S(1)}, bf16[2,24,1152]{2,1,0:T(8,128)(2,1)S(1)}, u32[]{:S(2)}, u32[]{:S(2)}) collective-permute-start(bf16[2,24,1152]{2,1,0:T(8,128)(2,1)S(1)} %pad_maximum_fusion.4), channel_id=1, source_target_pairs={{0,192},{32,224},{64,128},{96,160},{128,64},{160,96},{192,0},{224,... | collective-permute-start | bytes 331784 | tf_op jit(solution)/shard_map/ppermute | solution.py:178
  32.1 28.3 %collective-permute-done.3 = bf16[2,24,1152]{2,1,0:T(8,128)(2,1)S(1)} collective-permute-done((bf16[2,24,1152]{2,1,0:T(8,128)(2,1)S(1)}, bf16[2,24,1152]{2,1,0:T(8,128)(2,1)S(1)}, u32[]{:S(2)}, u32[]{:S(2)}) %collective-permute-start.3) | collective-permute-done | bytes 110624 | tf_op jit(solution)/shard_map/ppermute | solution.py:178
  60.4 0.7 pad_maximum_fusion.2.refs_0_
  61.2 5.2 %collective-permute-done.4 = bf16[2,24,1152]{2,1,0:T(8,128)(2,1)S(1)} collective-permute-done((bf16[2,24,1152]{2,1,0:T(8,128)(2,1)S(1)}, bf16[2,24,1152]{2,1,0:T(8,128)(2,1)S(1)}, u32[]{:S(2)}, u32[]{:S(2)}) %collective-permute-start.4) | collective-permute-done | bytes 110624 | tf_op jit(solution)/shard_map/ppermute | solution.py:178
  66.3 0.7 pad_maximum_fusion.3.refs_1_
  67.7 1.5 collective-permute-start.8
  69.1 1.8 collective-permute-start.7
  70.9 1.4 collective-permute-start.6
  72.9 4.5 %collective-permute-done.8.refs_6_ = bf16[4,24,1152]{2,1,0:T(8,128)(2,1)} collective-permute-done((bf16[4,24,1152]{2,1,0:T(8,128)(2,1)}, bf16[4,24,1152]{2,1,0:T(8,128)(2,1)}, u32[]{:S(2)}, u32[]{:S(2)}) %collective-permute-start.8) | collective-permute-done | bytes 221216 | tf_op jit(solution)/shard_map/ppermute | solution.py:174
  77.8 2.9 %collective-permute-start.10 = (bf16[4,24,1152]{2,1,0:T(8,128)(2,1)}, bf16[4,24,1152]{2,1,0:T(8,128)(2,1)}, u32[]{:S(2)}, u32[]{:S(2)}) collective-permute-start(bf16[4,24,1152]{2,1,0:T(8,128)(2,1)} %collective-permute-done.7.refs_3_), channel_id=1, source_target_pairs={{0,24},{8,0},{16,8},{24,16},{1,25},{9,1},{17,9},{25,17},{2,26},{10... | collective-permute-start | bytes 663560 | tf_op jit(solution)/shard_map/ppermute | solution.py:174
  80.7 0.7 collective-permute-done.11.refs_7_
  81.4 2.4 %collective-permute-done.12 = bf16[128,4,768]{2,1,0:T(4,128)(2,1)S(1)} collective-permute-done((bf16[128,4,768]{2,1,0:T(4,128)(2,1)S(1)}, bf16[128,4,768]{2,1,0:T(4,128)(2,1)S(1)}, u32[]{:S(2)}, u32[]{:S(2)}) %collective-permute-start.12) | collective-permute-done | bytes 786464 | tf_op jit(solution)/shard_map/ppermute | solution.py:252
  83.8 0.9 copy-done.6
  84.7 2.4 %reshape.31.t_ref = bf16[512,1152]{1,0:T(8,128)(2,1)S(1)} reshape(bf16[128,4,1152]{2,1,0:T(4,128)(2,1)} %copy-done.5) | data formatting | bytes 2359296 | tf_op jit(solution)/shard_map/reshape | solution.py:255
  87.1 1.6 reshape.30.o_ref
  92.0 0.9 copy-done.2
  93.0 0.9 copy-done.4
  93.9 16.4 %attention_core.1 = (bf16[512,768]{1,0:T(8,128)(2,1)S(1)}, bf16[512,768]{1,0:T(8,128)(2,1)S(1)}, bf16[4,8,24,1152]{3,2,1,0:T(8,128)(2,1)S(1)}, bf16[4,8,24,1152]{3,2,1,0:T(8,128)(2,1)S(1)}) custom-call(s32[4]{0:T(128)S(1)} %pad_add_fusion.where_ref, bf16[512,1152]{1,0:T(8,128)(2,1)S(1)} %reshape.31.t_ref, bf16[512,768]{1,0:T(8,128)(2,1)S(1)} %reshape.30.o_ref, ...), custom_call_target="tpu_custom_call" | custom-call | flops 5435817984 | bytes 8388608 | tf_op jit(solution)/shard_map/attention_core/pallas_call | solution.py:110
  111.0 3.1 %collective-permute-done.21.other_ref = bf16[4,8,24,1152]{3,2,1,0:T(8,128)(2,1)S(1)} collective-permute-done((bf16[4,8,24,1152]{3,2,1,0:T(8,128)(2,1)S(1)}, bf16[4,8,24,1152]{3,2,1,0:T(8,128)(2,1)S(1)}, u32[]{:S(2)}, u32[]{:S(2)}) %collective-permute-start.21) | collective-permute-done | bytes 1769504 | tf_op jit(solution)/shard_map/ppermute | solution.py:204
  114.5 1.3 collective-permute-start.22
  115.7 2.1 %collective-permute-start.23 = (bf16[4,24,1152]{2,1,0:T(8,128)(2,1)S(1)}, bf16[4,24,1152]{2,1,0:T(8,128)(2,1)S(1)}, u32[]{:S(2)}, u32[]{:S(2)}) collective-permute-start(bf16[4,24,1152]{2,1,0:T(8,128)(2,1)S(1)} %get-tuple-element.56), channel_id=1, source_target_pairs={{0,24},{8,0},{16,8},{24,16},{1,25},{9,1},{17,9},{25,17},{2,26},{10... | collective-permute-start | bytes 663560 | tf_op jit(solution)/shard_map/ppermute | solution.py:174
  117.8 1.1 collective-permute-start.26
  118.8 1.0 collective-permute-start.27
  119.8 10.5 %collective-permute-done.24 = bf16[512,768]{1,0:T(8,128)(2,1)S(1)} collective-permute-done((bf16[512,768]{1,0:T(8,128)(2,1)S(1)}, bf16[512,768]{1,0:T(8,128)(2,1)S(1)}, u32[]{:S(2)}, u32[]{:S(2)}) %collective-permute-start.24) | collective-permute-done | bytes 786464 | tf_op jit(solution)/shard_map/ppermute | solution.py:262
  130.3 1.1 add_convert_fusion
  131.5 1.3 collective-permute-start.25
  132.8 2.1 %collective-permute-start.28 = (bf16[4,24,1152]{2,1,0:T(8,128)(2,1)S(1)}, bf16[4,24,1152]{2,1,0:T(8,128)(2,1)}, u32[]{:S(2)}, u32[]{:S(2)}) collective-permute-start(bf16[4,24,1152]{2,1,0:T(8,128)(2,1)S(1)} %add_convert_fusion.1), channel_id=1, source_target_pairs={{0,24},{8,0},{16,8},{24,16},{1,25},{9,1},{17,9},{25,17},{2,26},{10... | collective-permute-start | bytes 663560 | tf_op jit(solution)/shard_map/ppermute | solution.py:174
  134.8 2.4 %reshape.32 = bf16[128,4,768]{2,1,0:T(4,128)(2,1)} reshape(bf16[512,768]{1,0:T(8,128)(2,1)} %add_convert_fusion) | data formatting | bytes 1572864 | tf_op jit(solution)/shard_map/reshape | solution.py:268
  137.2 10.8 %all-to-all-start.1 = ((bf16[128,4,768]{2,1,0:T(4,128)(2,1)}), bf16[128,4,768]{2,1,0:T(4,128)(2,1)}, u32[]{:S(2)}, u32[]{:S(2)}) async-start(bf16[128,4,768]{2,1,0:T(4,128)(2,1)} %reshape.32), calls=%async_computation.1 | async-start | bytes 1572864 | tf_op jit(solution)/shard_map/all_to_all | solution.py:268
  148.0 1.4 convert_add_fusion.1
  149.6 1.0 collective-permute-start.30
  150.7 3.5 %collective-permute-start.31 = (bf16[4,12,1152]{2,1,0:T(8,128)(2,1)S(1)}, bf16[4,12,1152]{2,1,0:T(8,128)(2,1)S(1)}, u32[]{:S(2)}, u32[]{:S(2)}) collective-permute-start(bf16[4,12,1152]{2,1,0:T(8,128)(2,1)S(1)} %get-tuple-element.75), channel_id=1, source_target_pairs={{0,36},{4,32},{32,4},{36,0},{64,100},{68,96},{96,68},{100,64},{128... | collective-permute-start | bytes 331784 | tf_op jit(solution)/shard_map/ppermute | solution.py:178
  154.7 5.0 %collective-permute-done.30 = bf16[4,12,1152]{2,1,0:T(8,128)(2,1)S(1)} collective-permute-done((bf16[4,12,1152]{2,1,0:T(8,128)(2,1)S(1)}, bf16[4,12,1152]{2,1,0:T(8,128)(2,1)S(1)}, u32[]{:S(2)}, u32[]{:S(2)}) %collective-permute-start.30) | collective-permute-done | bytes 110624 | tf_op jit(solution)/shard_map/ppermute | solution.py:178
  159.7 10.3 %collective-permute-done.31 = bf16[4,12,1152]{2,1,0:T(8,128)(2,1)S(1)} collective-permute-done((bf16[4,12,1152]{2,1,0:T(8,128)(2,1)S(1)}, bf16[4,12,1152]{2,1,0:T(8,128)(2,1)S(1)}, u32[]{:S(2)}, u32[]{:S(2)}) %collective-permute-start.31) | collective-permute-done | bytes 110624 | tf_op jit(solution)/shard_map/ppermute | solution.py:178
  170.0 2.7 %collective-permute-done.29 = bf16[4,12,1152]{2,1,0:T(8,128)(2,1)S(1)} collective-permute-done((bf16[4,12,1152]{2,1,0:T(8,128)(2,1)S(1)}, bf16[4,12,1152]{2,1,0:T(8,128)(2,1)S(1)}, u32[]{:S(2)}, u32[]{:S(2)}) %collective-permute-start.29) | collective-permute-done | bytes 110624 | tf_op jit(solution)/shard_map/ppermute | solution.py:178
  172.8 2.5 %collective-permute-start.32 = (bf16[12,1152]{1,0:T(8,128)(2,1)S(1)}, bf16[12,1152]{1,0:T(8,128)(2,1)S(1)}, u32[]{:S(2)}, u32[]{:S(2)}) collective-permute-start(bf16[12,1152]{1,0:T(8,128)(2,1)S(1)} %get-tuple-element.76), channel_id=1, source_target_pairs={{0,64},{32,96},{64,0},{96,32},{128,192},{160,224},{192,128},{224,1... | collective-permute-start | bytes 82952 | tf_op jit(solution)/shard_map/ppermute | solution.py:178
  175.3 2.9 %collective-permute-start.34 = (bf16[12,1152]{1,0:T(8,128)(2,1)S(1)}, bf16[12,1152]{1,0:T(8,128)(2,1)S(1)}, u32[]{:S(2)}, u32[]{:S(2)}) collective-permute-start(bf16[12,1152]{1,0:T(8,128)(2,1)S(1)} %get-tuple-element.77), channel_id=1, source_target_pairs={{0,192},{32,224},{64,128},{96,160},{128,64},{160,96},{192,0},{224,... | collective-permute-start | bytes 82952 | tf_op jit(solution)/shard_map/ppermute | solution.py:178
  178.2 1.2 collective-permute-start.33
  179.4 2.3 %reshape.33 = bf16[1,512,768]{2,1,0:T(8,128)(2,1)} reshape(bf16[128,4,768]{2,1,0:T(4,128)(2,1)} %all-to-all-done.1) | data formatting | bytes 1572864 | tf_op jit(solution)/shard_map/reshape | solution.py:271
  181.7 4.4 %collective-permute-done.33 = bf16[12,1152]{1,0:T(8,128)(2,1)S(1)} collective-permute-done((bf16[12,1152]{1,0:T(8,128)(2,1)S(1)}, bf16[12,1152]{1,0:T(8,128)(2,1)S(1)}, u32[]{:S(2)}, u32[]{:S(2)}) %collective-permute-start.33) | collective-permute-done | bytes 27680 | tf_op jit(solution)/shard_map/ppermute | solution.py:178
  (74 shorter events, 8.2 us)
Async XLA Ops:
  0.6 6.1 %copy-start = (bf16[1,512,1536]{2,1,0:T(8,128)(2,1)S(1)}, bf16[1,512,1536]{2,1,0:T(8,128)(2,1)}, u32[]{:S(2)}) copy-start(bf16[1,512,1536]{2,1,0:T(8,128)(2,1)} %param.3) | copy-start | bytes 4718596
  0.6 6.1 %copy-start.7 = (bf16[1,512,384]{2,1,0:T(8,128)(2,1)S(1)}, bf16[1,512,384]{2,1,0:T(8,128)(2,1)}, u32[]{:S(2)}) copy-start(bf16[1,512,384]{2,1,0:T(8,128)(2,1)} %param.4) | copy-start | bytes 1179652
  1.6 8.8 %collective-permute-start.1 = (bf16[12,1152]{1,0:T(8,128)(2,1)S(1)}, bf16[12,1152]{1,0:T(8,128)(2,1)S(1)}, u32[]{:S(2)}, u32[]{:S(2)}) collective-permute-start(bf16[12,1152]{1,0:T(8,128)(2,1)S(1)} %bitcast.26), channel_id=1, source_target_pairs={{0,32},{4,36},{32,0},{36,4},{64,96},{68,100},{96,64},{100,68},{128... | collective-permute-start | bytes 82952 | tf_op jit(solution)/shard_map/ppermute | solution.py:178
  3.6 6.8 %collective-permute-start.2 = (bf16[12,1152]{1,0:T(8,128)(2,1)S(1)}, bf16[12,1152]{1,0:T(8,128)(2,1)S(1)}, u32[]{:S(2)}, u32[]{:S(2)}) collective-permute-start(bf16[12,1152]{1,0:T(8,128)(2,1)S(1)} %bitcast.27), channel_id=1, source_target_pairs={{0,36},{4,32},{32,4},{36,0},{64,100},{68,96},{96,68},{100,64},{128... | collective-permute-start | bytes 82952 | tf_op jit(solution)/shard_map/ppermute | solution.py:178
  4.6 5.8 %collective-permute-start = (bf16[12,1152]{1,0:T(8,128)(2,1)S(1)}, bf16[12,1152]{1,0:T(8,128)(2,1)S(1)}, u32[]{:S(2)}, u32[]{:S(2)}) collective-permute-start(bf16[12,1152]{1,0:T(8,128)(2,1)S(1)} %bitcast.28), channel_id=1, source_target_pairs={{0,4},{4,0},{32,36},{36,32},{64,68},{68,64},{96,100},{100,96},{128... | collective-permute-start | bytes 82952 | tf_op jit(solution)/shard_map/ppermute | solution.py:178
  10.5 56.5 %all-to-all-start = ((bf16[128,4,1152]{2,1,0:T(4,128)(2,1)}), bf16[128,4,1152]{2,1,0:T(4,128)(2,1)S(1)}, u32[]{:S(2)}, u32[]{:S(2)}) async-start(bf16[128,4,1152]{2,1,0:T(4,128)(2,1)} %reshape.28), calls=%async_computation | async-start | bytes 2359296 | tf_op jit(solution)/shard_map/all_to_all | solution.py:247
  25.6 34.9 %collective-permute-start.3 = (bf16[2,24,1152]{2,1,0:T(8,128)(2,1)S(1)}, bf16[2,24,1152]{2,1,0:T(8,128)(2,1)S(1)}, u32[]{:S(2)}, u32[]{:S(2)}) collective-permute-start(bf16[2,24,1152]{2,1,0:T(8,128)(2,1)S(1)} %pad_maximum_fusion.4), channel_id=1, source_target_pairs={{0,64},{32,96},{64,0},{96,32},{128,192},{160,224},{192,128},{224,1... | collective-permute-start | bytes 331784 | tf_op jit(solution)/shard_map/ppermute | solution.py:178
  28.1 33.0 %collective-permute-start.5 = (bf16[2,24,1152]{2,1,0:T(8,128)(2,1)S(1)}, bf16[2,24,1152]{2,1,0:T(8,128)(2,1)S(1)}, u32[]{:S(2)}, u32[]{:S(2)}) collective-permute-start(bf16[2,24,1152]{2,1,0:T(8,128)(2,1)S(1)} %pad_maximum_fusion.4), channel_id=1, source_target_pairs={{0,192},{32,224},{64,128},{96,160},{128,64},{160,96},{192,0},{224,... | collective-permute-start | bytes 331784 | tf_op jit(solution)/shard_map/ppermute | solution.py:178
  31.9 34.4 %collective-permute-start.4 = (bf16[2,24,1152]{2,1,0:T(8,128)(2,1)S(1)}, bf16[2,24,1152]{2,1,0:T(8,128)(2,1)S(1)}, u32[]{:S(2)}, u32[]{:S(2)}) collective-permute-start(bf16[2,24,1152]{2,1,0:T(8,128)(2,1)S(1)} %pad_maximum_fusion.4), channel_id=1, source_target_pairs={{0,128},{32,160},{64,192},{96,224},{128,0},{160,32},{192,64},{224,... | collective-permute-start | bytes 331784 | tf_op jit(solution)/shard_map/ppermute | solution.py:178
  67.0 16.8 %copy-start.5 = (bf16[128,4,1152]{2,1,0:T(4,128)(2,1)}, bf16[128,4,1152]{2,1,0:T(4,128)(2,1)S(1)}, u32[]{:S(2)}) copy-start(bf16[128,4,1152]{2,1,0:T(4,128)(2,1)S(1)} %all-to-all-done) | copy-start | bytes 3538948
  67.3 16.5 %collective-permute-start.12 = (bf16[128,4,768]{2,1,0:T(4,128)(2,1)S(1)}, bf16[128,4,768]{2,1,0:T(4,128)(2,1)S(1)}, u32[]{:S(2)}, u32[]{:S(2)}) collective-permute-start(bf16[128,4,768]{2,1,0:T(4,128)(2,1)S(1)} %slice.60), channel_id=1, source_target_pairs={{0,1},{1,0},{2,3},{3,2},{4,5},{5,4},{6,7},{7,6},{8,9},{9,8},{10,11... | collective-permute-start | bytes 2359304 | tf_op jit(solution)/shard_map/ppermute | solution.py:252
  67.7 9.8 %collective-permute-start.8 = (bf16[4,24,1152]{2,1,0:T(8,128)(2,1)}, bf16[4,24,1152]{2,1,0:T(8,128)(2,1)}, u32[]{:S(2)}, u32[]{:S(2)}) collective-permute-start(bf16[4,24,1152]{2,1,0:T(8,128)(2,1)} %pad_maximum_fusion.2.refs_0_), channel_id=1, source_target_pairs={{0,8},{8,16},{16,24},{24,0},{1,9},{9,17},{17,25},{25,1},{2,10},{10... | collective-permute-start | bytes 663560 | tf_op jit(solution)/shard_map/ppermute | solution.py:174
  69.1 8.7 %collective-permute-start.7 = (bf16[4,24,1152]{2,1,0:T(8,128)(2,1)}, bf16[4,24,1152]{2,1,0:T(8,128)(2,1)}, u32[]{:S(2)}, u32[]{:S(2)}) collective-permute-start(bf16[4,24,1152]{2,1,0:T(8,128)(2,1)} %pad_maximum_fusion.3.refs_1_), channel_id=1, source_target_pairs={{0,24},{8,0},{16,8},{24,16},{1,25},{9,1},{17,9},{25,17},{2,26},{10... | collective-permute-start | bytes 663560 | tf_op jit(solution)/shard_map/ppermute | solution.py:174
  70.9 9.8 %collective-permute-start.6 = (bf16[4,24,1152]{2,1,0:T(8,128)(2,1)}, bf16[4,24,1152]{2,1,0:T(8,128)(2,1)S(1)}, u32[]{:S(2)}, u32[]{:S(2)}) collective-permute-start(bf16[4,24,1152]{2,1,0:T(8,128)(2,1)} %pad_maximum_fusion.2.refs_0_), channel_id=1, source_target_pairs={{0,24},{8,0},{16,8},{24,16},{1,25},{9,1},{17,9},{25,17},{2,26},{10... | collective-permute-start | bytes 663560 | tf_op jit(solution)/shard_map/ppermute | solution.py:174
  72.3 9.1 %collective-permute-start.11 = (bf16[4,24,1152]{2,1,0:T(8,128)(2,1)}, bf16[4,24,1152]{2,1,0:T(8,128)(2,1)S(1)}, u32[]{:S(2)}, u32[]{:S(2)}) collective-permute-start(bf16[4,24,1152]{2,1,0:T(8,128)(2,1)} %pad_maximum_fusion.3.refs_1_), channel_id=1, source_target_pairs={{0,8},{8,16},{16,24},{24,0},{1,9},{9,17},{17,25},{25,1},{2,10},{10... | collective-permute-start | bytes 663560 | tf_op jit(solution)/shard_map/ppermute | solution.py:174
  77.5 11.2 %collective-permute-start.9 = (bf16[4,24,1152]{2,1,0:T(8,128)(2,1)}, bf16[4,24,1152]{2,1,0:T(8,128)(2,1)}, u32[]{:S(2)}, u32[]{:S(2)}) collective-permute-start(bf16[4,24,1152]{2,1,0:T(8,128)(2,1)} %collective-permute-done.8.refs_6_), channel_id=1, source_target_pairs={{0,8},{8,16},{16,24},{24,0},{1,9},{9,17},{17,25},{25,1},{2,10},{10... | collective-permute-start | bytes 663560 | tf_op jit(solution)/shard_map/ppermute | solution.py:174
  77.8 11.5 %collective-permute-start.10 = (bf16[4,24,1152]{2,1,0:T(8,128)(2,1)}, bf16[4,24,1152]{2,1,0:T(8,128)(2,1)}, u32[]{:S(2)}, u32[]{:S(2)}) collective-permute-start(bf16[4,24,1152]{2,1,0:T(8,128)(2,1)} %collective-permute-done.7.refs_3_), channel_id=1, source_target_pairs={{0,24},{8,0},{16,8},{24,16},{1,25},{9,1},{17,9},{25,17},{2,26},{10... | collective-permute-start | bytes 663560 | tf_op jit(solution)/shard_map/ppermute | solution.py:174
  80.7 3.1 %copy-start.1 = (bf16[4,24,1152]{2,1,0:T(8,128)(2,1)}, bf16[4,24,1152]{2,1,0:T(8,128)(2,1)S(1)}, u32[]{:S(2)}) copy-start(bf16[4,24,1152]{2,1,0:T(8,128)(2,1)S(1)} %collective-permute-done.6.refs_2_) | copy-start | bytes 663556
  80.7 8.7 %collective-permute-start.13 = (bf16[4,24,1152]{2,1,0:T(8,128)(2,1)}, bf16[4,24,1152]{2,1,0:T(8,128)(2,1)}, u32[]{:S(2)}, u32[]{:S(2)}) collective-permute-start(bf16[4,24,1152]{2,1,0:T(8,128)(2,1)} %pad_maximum_fusion.2.refs_0_), channel_id=1, source_target_pairs={{0,2},{2,0},{1,3},{3,1},{4,6},{6,4},{5,7},{7,5},{8,10},{10,8},{9,1... | collective-permute-start | bytes 663560 | tf_op jit(solution)/shard_map/ppermute | solution.py:256
  81.4 2.4 %copy-start.3 = (bf16[4,24,1152]{2,1,0:T(8,128)(2,1)}, bf16[4,24,1152]{2,1,0:T(8,128)(2,1)S(1)}, u32[]{:S(2)}) copy-start(bf16[4,24,1152]{2,1,0:T(8,128)(2,1)S(1)} %collective-permute-done.11.refs_7_) | copy-start | bytes 663556
  81.4 8.4 %collective-permute-start.14 = (bf16[4,24,1152]{2,1,0:T(8,128)(2,1)}, bf16[4,24,1152]{2,1,0:T(8,128)(2,1)}, u32[]{:S(2)}, u32[]{:S(2)}) collective-permute-start(bf16[4,24,1152]{2,1,0:T(8,128)(2,1)} %pad_maximum_fusion.3.refs_1_), channel_id=1, source_target_pairs={{0,2},{2,0},{1,3},{3,1},{4,6},{6,4},{5,7},{7,5},{8,10},{10,8},{9,1... | collective-permute-start | bytes 663560 | tf_op jit(solution)/shard_map/ppermute | solution.py:256
  83.8 0.9 copy-start.6
  84.7 5.2 %collective-permute-start.19 = (bf16[4,24,1152]{2,1,0:T(8,128)(2,1)}, bf16[4,24,1152]{2,1,0:T(8,128)(2,1)}, u32[]{:S(2)}, u32[]{:S(2)}) collective-permute-start(bf16[4,24,1152]{2,1,0:T(8,128)(2,1)} %collective-permute-done.8.refs_6_), channel_id=1, source_target_pairs={{0,2},{2,0},{1,3},{3,1},{4,6},{6,4},{5,7},{7,5},{8,10},{10,8},{9,1... | collective-permute-start | bytes 663560 | tf_op jit(solution)/shard_map/ppermute | solution.py:256
  88.7 2.0 %collective-permute-start.15 = (bf16[4,24,1152]{2,1,0:T(8,128)(2,1)}, bf16[4,24,1152]{2,1,0:T(8,128)(2,1)}, u32[]{:S(2)}, u32[]{:S(2)}) collective-permute-start(bf16[4,24,1152]{2,1,0:T(8,128)(2,1)} %copy-done.1), channel_id=1, source_target_pairs={{0,2},{2,0},{1,3},{3,1},{4,6},{6,4},{5,7},{7,5},{8,10},{10,8},{9,1... | collective-permute-start | bytes 663560 | tf_op jit(solution)/shard_map/ppermute | solution.py:256
  89.3 1.8 collective-permute-start.20
  89.4 2.0 %collective-permute-start.16 = (bf16[4,24,1152]{2,1,0:T(8,128)(2,1)}, bf16[4,24,1152]{2,1,0:T(8,128)(2,1)}, u32[]{:S(2)}, u32[]{:S(2)}) collective-permute-start(bf16[4,24,1152]{2,1,0:T(8,128)(2,1)} %collective-permute-done.7.refs_3_), channel_id=1, source_target_pairs={{0,2},{2,0},{1,3},{3,1},{4,6},{6,4},{5,7},{7,5},{8,10},{10,8},{9,1... | collective-permute-start | bytes 663560 | tf_op jit(solution)/shard_map/ppermute | solution.py:256
  89.8 1.9 %collective-permute-start.17 = (bf16[4,24,1152]{2,1,0:T(8,128)(2,1)}, bf16[4,24,1152]{2,1,0:T(8,128)(2,1)}, u32[]{:S(2)}, u32[]{:S(2)}) collective-permute-start(bf16[4,24,1152]{2,1,0:T(8,128)(2,1)} %collective-permute-done.9.refs_4_), channel_id=1, source_target_pairs={{0,2},{2,0},{1,3},{3,1},{4,6},{6,4},{5,7},{7,5},{8,10},{10,8},{9,1... | collective-permute-start | bytes 663560 | tf_op jit(solution)/shard_map/ppermute | solution.py:258
  89.9 2.1 %collective-permute-start.18 = (bf16[4,24,1152]{2,1,0:T(8,128)(2,1)}, bf16[4,24,1152]{2,1,0:T(8,128)(2,1)}, u32[]{:S(2)}, u32[]{:S(2)}) collective-permute-start(bf16[4,24,1152]{2,1,0:T(8,128)(2,1)} %collective-permute-done.10.refs_5_), channel_id=1, source_target_pairs={{0,2},{2,0},{1,3},{3,1},{4,6},{6,4},{5,7},{7,5},{8,10},{10,8},{9,1... | collective-permute-start | bytes 663560 | tf_op jit(solution)/shard_map/ppermute | solution.py:258
  92.0 0.9 copy-start.2
  93.0 0.9 copy-start.4
  110.3 3.8 %collective-permute-start.21 = (bf16[4,8,24,1152]{3,2,1,0:T(8,128)(2,1)S(1)}, bf16[4,8,24,1152]{3,2,1,0:T(8,128)(2,1)S(1)}, u32[]{:S(2)}, u32[]{:S(2)}) collective-permute-start(bf16[4,8,24,1152]{3,2,1,0:T(8,128)(2,1)S(1)} %get-tuple-element.52), channel_id=1, source_target_pairs={{0,2},{2,0},{1,3},{3,1},{4,6},{6,4},{5,7},{7,5},{8,10},{10,8},{9,1... | collective-permute-start | bytes 5308424 | tf_op jit(solution)/shard_map/ppermute | solution.py:204
  110.7 19.6 %collective-permute-start.24 = (bf16[512,768]{1,0:T(8,128)(2,1)S(1)}, bf16[512,768]{1,0:T(8,128)(2,1)S(1)}, u32[]{:S(2)}, u32[]{:S(2)}) collective-permute-start(bf16[512,768]{1,0:T(8,128)(2,1)S(1)} %get-tuple-element.57), channel_id=1, source_target_pairs={{0,1},{1,0},{2,3},{3,2},{4,5},{5,4},{6,7},{7,6},{8,9},{9,8},{10,11... | collective-permute-start | bytes 2359304 | tf_op jit(solution)/shard_map/ppermute | solution.py:262
  114.5 15.9 %collective-permute-start.22 = (bf16[4,24,1152]{2,1,0:T(8,128)(2,1)S(1)}, bf16[4,24,1152]{2,1,0:T(8,128)(2,1)S(1)}, u32[]{:S(2)}, u32[]{:S(2)}) collective-permute-start(bf16[4,24,1152]{2,1,0:T(8,128)(2,1)S(1)} %get-tuple-element.55), channel_id=1, source_target_pairs={{0,8},{8,16},{16,24},{24,0},{1,9},{9,17},{17,25},{25,1},{2,10},{10... | collective-permute-start | bytes 663560 | tf_op jit(solution)/shard_map/ppermute | solution.py:174
  115.7 14.6 %collective-permute-start.23 = (bf16[4,24,1152]{2,1,0:T(8,128)(2,1)S(1)}, bf16[4,24,1152]{2,1,0:T(8,128)(2,1)S(1)}, u32[]{:S(2)}, u32[]{:S(2)}) collective-permute-start(bf16[4,24,1152]{2,1,0:T(8,128)(2,1)S(1)} %get-tuple-element.56), channel_id=1, source_target_pairs={{0,24},{8,0},{16,8},{24,16},{1,25},{9,1},{17,9},{25,17},{2,26},{10... | collective-permute-start | bytes 663560 | tf_op jit(solution)/shard_map/ppermute | solution.py:174
  117.8 30.2 %collective-permute-start.26 = (bf16[4,24,1152]{2,1,0:T(8,128)(2,1)S(1)}, bf16[4,24,1152]{2,1,0:T(8,128)(2,1)}, u32[]{:S(2)}, u32[]{:S(2)}) collective-permute-start(bf16[4,24,1152]{2,1,0:T(8,128)(2,1)S(1)} %get-tuple-element.64), channel_id=1, source_target_pairs={{0,24},{8,0},{16,8},{24,16},{1,25},{9,1},{17,9},{25,17},{2,26},{10... | collective-permute-start | bytes 663560 | tf_op jit(solution)/shard_map/ppermute | solution.py:174
  118.8 29.1 %collective-permute-start.27 = (bf16[4,24,1152]{2,1,0:T(8,128)(2,1)S(1)}, bf16[4,24,1152]{2,1,0:T(8,128)(2,1)}, u32[]{:S(2)}, u32[]{:S(2)}) collective-permute-start(bf16[4,24,1152]{2,1,0:T(8,128)(2,1)S(1)} %get-tuple-element.65), channel_id=1, source_target_pairs={{0,8},{8,16},{16,24},{24,0},{1,9},{9,17},{17,25},{25,1},{2,10},{10... | collective-permute-start | bytes 663560 | tf_op jit(solution)/shard_map/ppermute | solution.py:174
  131.5 16.5 %collective-permute-start.25 = (bf16[4,24,1152]{2,1,0:T(8,128)(2,1)S(1)}, bf16[4,24,1152]{2,1,0:T(8,128)(2,1)}, u32[]{:S(2)}, u32[]{:S(2)}) collective-permute-start(bf16[4,24,1152]{2,1,0:T(8,128)(2,1)S(1)} %add_convert_fusion.2), channel_id=1, source_target_pairs={{0,8},{8,16},{16,24},{24,0},{1,9},{9,17},{17,25},{25,1},{2,10},{10... | collective-permute-start | bytes 663560 | tf_op jit(solution)/shard_map/ppermute | solution.py:174
  132.8 15.2 %collective-permute-start.28 = (bf16[4,24,1152]{2,1,0:T(8,128)(2,1)S(1)}, bf16[4,24,1152]{2,1,0:T(8,128)(2,1)}, u32[]{:S(2)}, u32[]{:S(2)}) collective-permute-start(bf16[4,24,1152]{2,1,0:T(8,128)(2,1)S(1)} %add_convert_fusion.1), channel_id=1, source_target_pairs={{0,24},{8,0},{16,8},{24,16},{1,25},{9,1},{17,9},{25,17},{2,26},{10... | collective-permute-start | bytes 663560 | tf_op jit(solution)/shard_map/ppermute | solution.py:174
  137.2 35.6 %all-to-all-start.1 = ((bf16[128,4,768]{2,1,0:T(4,128)(2,1)}), bf16[128,4,768]{2,1,0:T(4,128)(2,1)}, u32[]{:S(2)}, u32[]{:S(2)}) async-start(bf16[128,4,768]{2,1,0:T(4,128)(2,1)} %reshape.32), calls=%async_computation.1 | async-start | bytes 1572864 | tf_op jit(solution)/shard_map/all_to_all | solution.py:268
  149.6 10.1 %collective-permute-start.30 = (bf16[4,12,1152]{2,1,0:T(8,128)(2,1)S(1)}, bf16[4,12,1152]{2,1,0:T(8,128)(2,1)S(1)}, u32[]{:S(2)}, u32[]{:S(2)}) collective-permute-start(bf16[4,12,1152]{2,1,0:T(8,128)(2,1)S(1)} %get-tuple-element.74), channel_id=1, source_target_pairs={{0,4},{4,0},{32,36},{36,32},{64,68},{68,64},{96,100},{100,96},{128... | collective-permute-start | bytes 331784 | tf_op jit(solution)/shard_map/ppermute | solution.py:178
  150.7 19.3 %collective-permute-start.31 = (bf16[4,12,1152]{2,1,0:T(8,128)(2,1)S(1)}, bf16[4,12,1152]{2,1,0:T(8,128)(2,1)S(1)}, u32[]{:S(2)}, u32[]{:S(2)}) collective-permute-start(bf16[4,12,1152]{2,1,0:T(8,128)(2,1)S(1)} %get-tuple-element.75), channel_id=1, source_target_pairs={{0,36},{4,32},{32,4},{36,0},{64,100},{68,96},{96,68},{100,64},{128... | collective-permute-start | bytes 331784 | tf_op jit(solution)/shard_map/ppermute | solution.py:178
  154.1 18.6 %collective-permute-start.29 = (bf16[4,12,1152]{2,1,0:T(8,128)(2,1)S(1)}, bf16[4,12,1152]{2,1,0:T(8,128)(2,1)S(1)}, u32[]{:S(2)}, u32[]{:S(2)}) collective-permute-start(bf16[4,12,1152]{2,1,0:T(8,128)(2,1)S(1)} %slice.53), channel_id=1, source_target_pairs={{0,32},{4,36},{32,0},{36,4},{64,96},{68,100},{96,64},{100,68},{128... | collective-permute-start | bytes 331784 | tf_op jit(solution)/shard_map/ppermute | solution.py:178
  172.8 8.8 %collective-permute-start.32 = (bf16[12,1152]{1,0:T(8,128)(2,1)S(1)}, bf16[12,1152]{1,0:T(8,128)(2,1)S(1)}, u32[]{:S(2)}, u32[]{:S(2)}) collective-permute-start(bf16[12,1152]{1,0:T(8,128)(2,1)S(1)} %get-tuple-element.76), channel_id=1, source_target_pairs={{0,64},{32,96},{64,0},{96,32},{128,192},{160,224},{192,128},{224,1... | collective-permute-start | bytes 82952 | tf_op jit(solution)/shard_map/ppermute | solution.py:178
  175.3 6.4 %collective-permute-start.34 = (bf16[12,1152]{1,0:T(8,128)(2,1)S(1)}, bf16[12,1152]{1,0:T(8,128)(2,1)S(1)}, u32[]{:S(2)}, u32[]{:S(2)}) collective-permute-start(bf16[12,1152]{1,0:T(8,128)(2,1)S(1)} %get-tuple-element.77), channel_id=1, source_target_pairs={{0,192},{32,224},{64,128},{96,160},{128,64},{160,96},{192,0},{224,... | collective-permute-start | bytes 82952 | tf_op jit(solution)/shard_map/ppermute | solution.py:178
  178.2 7.9 %collective-permute-start.33 = (bf16[12,1152]{1,0:T(8,128)(2,1)S(1)}, bf16[12,1152]{1,0:T(8,128)(2,1)S(1)}, u32[]{:S(2)}, u32[]{:S(2)}) collective-permute-start(bf16[12,1152]{1,0:T(8,128)(2,1)S(1)} %get-tuple-element.78), channel_id=1, source_target_pairs={{0,128},{32,160},{64,192},{96,224},{128,0},{160,32},{192,64},{224,... | collective-permute-start | bytes 82952 | tf_op jit(solution)/shard_map/ppermute | solution.py:178

commit v4 on v3

--- a/solution.py
+++ b/solution.py
@@ -9,7 +9,8 @@
 Z, Y, XH, C, MP = 8, 4, 2, 2, 2
 F = 128
 ROWS = 12
-VMEM_LIMIT = 32 * 2**20
+VMEM_LIMIT = 20 * 2**20
+FIRST = 320
 bf16, f32 = jnp.bfloat16, jnp.float32
 NT = (((1,), (1,)), ((), ()))
 TN = (((0,), (0,)), ((), ()))
@@ -189,32 +190,24 @@
     return jnp.stack([first, second], 0)
 
 
-def over_y(low, high):
-    before_low = shift(low, "y", Y, 1)
-    after_high = shift(high, "y", Y, Y - 1)
-    before_high = shift(high, "y", Y, 1)
-    after_low = shift(low, "y", Y, Y - 1)
-    far_low = shift(before_low, "y", Y, 1)
-    far_high = shift(after_high, "y", Y, Y - 1)
-    return [low, high, after_low, after_high, far_low, far_high, before_low, before_high]
-
-
-def reduce_weight(mine, rest, got, finish, late):
+def swapped(*xs):
+    return [lax.ppermute(x, "c", PAIR) for x in xs]
+
+
+def reduce_weight(mine, rest, first, second, finish, to_frames):
     even = lax.axis_index("xh") == 0
     other = lax.ppermute(rest, "c", PAIR)
+    first = lax.ppermute(first, "mp", PAIR)
     h = Z // 2
     own, after, before, far_low, far_high, after_high, before_low = combine(mine, other)
     up_far = shift(far_low, "y", Y, 1)
     down_far = shift(far_high, "y", Y, Y - 1)
     up_high = shift(after_high, "y", Y, 1)
     down_low = shift(before_low, "y", Y, Y - 1)
-    up_far, down_far, got = lax.optimization_barrier((up_far, down_far, got))
-    summed = finish(got)
-    up_low = (after + up_far.astype(f32)).astype(bf16)
-    down_high = (before + down_far.astype(f32)).astype(bf16)
-    up_low, down_high, summed = lax.optimization_barrier((up_low, down_high, summed))
-    up_low = shift(up_low, "y", Y, 1)
-    down_high = shift(down_high, "y", Y, Y - 1)
+    up_far, down_far, first, second = lax.optimization_barrier((up_far, down_far, first, second))
+    second = lax.ppermute(second, "mp", PAIR)
+    up_low = shift((after + up_far.astype(f32)).astype(bf16), "y", Y, 1)
+    down_high = shift((before + down_far.astype(f32)).astype(bf16), "y", Y, Y - 1)
     low = own[:h] + up_low.astype(f32) + down_low.astype(f32)
     high = own[h:] + up_high.astype(f32) + down_high.astype(f32)
     blocks = jnp.concatenate([low, high], 0)
@@ -223,8 +216,9 @@
     total = kept[0::2]
     for by, x in ((2, kept[1::2]), (1, sent[0::2]), (3, sent[1::2])):
         total = total + across(x.astype(bf16), ZX, Z * XH, by).astype(f32)
-    back = late(summed)
-    total, back = lax.optimization_barrier((total, back))
+    summed = finish(first, second)
+    total, summed = lax.optimization_barrier((total, summed))
+    back = to_frames(summed)
     result = total[0]
     for i in range(1, h):
         result = result + across(total[i].astype(bf16), "z", Z, 2 * i).astype(f32)
@@ -250,24 +244,33 @@
     part = tokens[:, :, :cols]
     low, high, part = lax.optimization_barrier((low, high, part))
     others = lax.ppermute(part, "mp", PAIR)
-    mine = over_y(low, high)
+    before_low = shift(low, "y", Y, 1)
+    after_high = shift(high, "y", Y, Y - 1)
+    before_high = shift(high, "y", Y, 1)
+    after_low = shift(low, "y", Y, Y - 1)
+    tokens = tokens.reshape(F * count, cols + half)
+    own = swapped(low, high)
+    before_low, after_high, tokens, own = lax.optimization_barrier(
+        (before_low, after_high, tokens, own)
+    )
+    far_low = shift(before_low, "y", Y, 1)
+    far_high = shift(after_high, "y", Y, Y - 1)
+    near = swapped(after_low, after_high, before_low, before_high)
+    far_low, far_high, near, others = lax.optimization_barrier((far_low, far_high, near, others))
     others = others.reshape(F * count, cols)
-    tokens = tokens.reshape(F * count, cols + half)
-    rest = {i: lax.ppermute(mine[i], "c", PAIR) for i in (0, 1, 2, 3, 6, 7)}
-    mine, others, tokens = lax.optimization_barrier((mine, others, tokens))
-    rest.update({i: lax.ppermute(mine[i], "c", PAIR) for i in (4, 5)})
-
-    rest = [rest[i] for i in range(8)]
+    mine = [low, high, after_low, after_high, far_low, far_high, before_low, before_high]
+    rest = own + near[:2] + swapped(far_low, far_high) + near[2:]
     give, keep, mine, rest = core(where, tokens, others, mine, rest)
-    got = lax.ppermute(give, "mp", PAIR)
-
-    def finish(got):
+    first, second = give[:FIRST], give[FIRST:]
+
+    def finish(first, second):
+        got = jnp.concatenate([first, second], 0)
         return (keep.astype(f32) + got.astype(f32)).astype(bf16)
 
     def to_frames(x):
         return lax.all_to_all(x.reshape(F, count, cols), FR, 0, 0, tiled=True)
 
-    weight_grad, back = reduce_weight(mine, rest, got, finish, to_frames)
+    weight_grad, back = reduce_weight(mine, rest, first, second, finish, to_frames)
     input_grad = back.reshape(frames_dev, patches, cols)
     weight_grad = weight_grad * (1.0 / F)
     return (input_grad, weight_grad.reshape(w_qkv.shape))

time: 187 us -> 196 us (1.048)
  local copies, waits for them, and re-layouts: 14.5 us -> 20 us
  other arithmetic: 4.49 us -> 1.01 us
  starting transfers between devices: 69 us -> 72.3 us
  waiting for transfers between devices: 81.1 us -> 83.6 us
    ppermute x12, waiting for transfers between devices: 5.23 us -> 16.9 us  [shift(): return lax.ppermute(x, axis, [(i, (i + by) % size) for i in range(size)])]
    ppermute x9 -> x10, waiting for transfers between devices: 12.2 us -> 4 us  [the longest x1 3.97 us: reduce_weight(): first = lax.ppermute(first, 'mp', PAIR)]
    unnamed x18 -> x34, local copies, waits for them, and re-layouts: 3.7 us -> 9.61 us
    ppermute x9 -> x10, starting transfers between devices: 1.91 us -> 4.9 us  [the longest x1 1.85 us: reduce_weight(): first = lax.ppermute(first, 'mp', PAIR)]
    ppermute x12, waiting for transfers between devices: 58.1 us -> 61.1 us  [across(): return lax.ppermute(x, axis, [(i, i ^ by) for i in range(size)])]
    ppermute x1, waiting for transfers between devices: 2.4 us -> 0.01 us  [on_device(): others = lax.ppermute(part, 'mp', PAIR)]
    ppermute x12, starting transfers between devices: 17.2 us -> 19.5 us  [shift(): return lax.ppermute(x, axis, [(i, (i + by) % size) for i in range(size)])]
    all_to_all x1, starting transfers between devices: 10.8 us -> 8.58 us  [to_frames(): return lax.all_to_all(x.reshape(F, count, cols), FR, 0, 0, tiled=True)]
  transfers between devices with their start and end apart: 37 -> 38, of which waited for: 17 -> 16; matrix products, arithmetic and copies ran while one was open for 8% -> 4% of each run, Pallas kernels for 0% -> 0%
where the time goes in v4:
time: 196 us; the launch traced here: 194 us
  waiting for transfers between devices  83.6 us (43%)
  starting transfers between devices  72.3 us (37%)
  local copies, waits for them, and re-layouts  20 us (10%)
  Pallas kernels  16.4 us (8%)
    ppermute x12, waiting for transfers between devices, across(): return lax.ppermute(x, axis, [(i, i ^ by) for i in range(size)])  61.1 us
    ppermute x12, starting transfers between devices, across(): return lax.ppermute(x, axis, [(i, i ^ by) for i in range(size)])  23.3 us
    ppermute x12, starting transfers between devices, shift(): return lax.ppermute(x, axis, [(i, (i + by) % size) for i in range(size)])  19.5 us
    ppermute x12, waiting for transfers between devices, shift(): return lax.ppermute(x, axis, [(i, (i + by) % size) for i in range(size)])  16.9 us
    pallas_call x1, Pallas kernels, core(): pl.pallas_call(core_kernel, out_shape=(jax.ShapeDtypeStruct((rows, part_c...  16 us
    all_to_all x1, starting transfers between devices, on_device(): tokens = lax.all_to_all(tokens, FR, 0, 0, tiled=True)  15.5 us
    unnamed x34, local copies, waits for them, and re-layouts  9.61 us
    all_to_all x1, starting transfers between devices, to_frames(): return lax.all_to_all(x.reshape(F, count, cols), FR, 0, 0, tiled=True)  8.58 us
  transfers between devices with their start and end apart: 38, of which 16 were waited for; matrix products, arithmetic and copies ran while one was open for 4% of the time, Pallas kernels for 0%

profile of v4, /device:TPU:6, one launch (start us, length us, event | category | flops | bytes accessed | tf_op | source)
XLA Modules:
  0.0 194.4 jit_solution(8245807101598381903)
XLA Ops:
  1.6 2.0 %collective-permute-start.1 = (bf16[12,1152]{1,0:T(8,128)(2,1)S(1)}, bf16[12,1152]{1,0:T(8,128)(2,1)S(1)}, u32[]{:S(2)}, u32[]{:S(2)}) collective-permute-start(bf16[12,1152]{1,0:T(8,128)(2,1)S(1)} %bitcast.26), channel_id=1, source_target_pairs={{0,32},{4,36},{32,0},{36,4},{64,96},{68,100},{96,64},{100,68},{128... | collective-permute-start | bytes 82952 | tf_op jit(solution)/shard_map/ppermute | solution.py:179
  3.6 1.0 collective-permute-start.2
  4.6 2.1 %collective-permute-start = (bf16[12,1152]{1,0:T(8,128)(2,1)S(1)}, bf16[12,1152]{1,0:T(8,128)(2,1)S(1)}, u32[]{:S(2)}, u32[]{:S(2)}) collective-permute-start(bf16[12,1152]{1,0:T(8,128)(2,1)S(1)} %bitcast.28), channel_id=1, source_target_pairs={{0,4},{4,0},{32,36},{36,32},{64,68},{68,64},{96,100},{100,96},{128... | collective-permute-start | bytes 82952 | tf_op jit(solution)/shard_map/ppermute | solution.py:179
  6.9 1.2 reshape.28
  8.0 2.3 %collective-permute-done = bf16[12,1152]{1,0:T(8,128)(2,1)S(1)} collective-permute-done((bf16[12,1152]{1,0:T(8,128)(2,1)S(1)}, bf16[12,1152]{1,0:T(8,128)(2,1)S(1)}, u32[]{:S(2)}, u32[]{:S(2)}) %collective-permute-start) | collective-permute-done | bytes 27680 | tf_op jit(solution)/shard_map/ppermute | solution.py:179
  10.5 15.5 %all-to-all-start = ((bf16[128,4,1152]{2,1,0:T(4,128)(2,1)}), bf16[128,4,1152]{2,1,0:T(4,128)(2,1)}, u32[]{:S(2)}, u32[]{:S(2)}) async-start(bf16[128,4,1152]{2,1,0:T(4,128)(2,1)} %reshape.28), calls=%async_computation | async-start | bytes 2359296 | tf_op jit(solution)/shard_map/all_to_all | solution.py:241
  26.0 2.6 %collective-permute-start.3 = (bf16[2,24,1152]{2,1,0:T(8,128)(2,1)S(1)}, bf16[2,24,1152]{2,1,0:T(8,128)(2,1)S(1)}, u32[]{:S(2)}, u32[]{:S(2)}) collective-permute-start(bf16[2,24,1152]{2,1,0:T(8,128)(2,1)S(1)} %pad_maximum_fusion.4), channel_id=1, source_target_pairs={{0,64},{32,96},{64,0},{96,32},{128,192},{160,224},{192,128},{224,1... | collective-permute-start | bytes 331784 | tf_op jit(solution)/shard_map/ppermute | solution.py:179
  28.5 3.8 %collective-permute-start.5 = (bf16[2,24,1152]{2,1,0:T(8,128)(2,1)S(1)}, bf16[2,24,1152]{2,1,0:T(8,128)(2,1)S(1)}, u32[]{:S(2)}, u32[]{:S(2)}) collective-permute-start(bf16[2,24,1152]{2,1,0:T(8,128)(2,1)S(1)} %pad_maximum_fusion.4), channel_id=1, source_target_pairs={{0,192},{32,224},{64,128},{96,160},{128,64},{160,96},{192,0},{224,... | collective-permute-start | bytes 331784 | tf_op jit(solution)/shard_map/ppermute | solution.py:179
  32.6 27.9 %collective-permute-done.3 = bf16[2,24,1152]{2,1,0:T(8,128)(2,1)S(1)} collective-permute-done((bf16[2,24,1152]{2,1,0:T(8,128)(2,1)S(1)}, bf16[2,24,1152]{2,1,0:T(8,128)(2,1)S(1)}, u32[]{:S(2)}, u32[]{:S(2)}) %collective-permute-start.3) | collective-permute-done | bytes 110624 | tf_op jit(solution)/shard_map/ppermute | solution.py:179
  60.5 5.9 %collective-permute-done.4 = bf16[2,24,1152]{2,1,0:T(8,128)(2,1)S(1)} collective-permute-done((bf16[2,24,1152]{2,1,0:T(8,128)(2,1)S(1)}, bf16[2,24,1152]{2,1,0:T(8,128)(2,1)S(1)}, u32[]{:S(2)}, u32[]{:S(2)}) %collective-permute-start.4) | collective-permute-done | bytes 110624 | tf_op jit(solution)/shard_map/ppermute | solution.py:179
  66.4 2.4 %slice.68 = bf16[128,4,768]{2,1,0:T(4,128)(2,1)} slice(bf16[128,4,1152]{2,1,0:T(4,128)(2,1)} %all-to-all-done), slice={[0:128], [0:4], [0:768]} | slice | bytes 1572864 | tf_op jit(solution)/shard_map/slice | solution.py:244
  69.0 2.6 %collective-permute-start.12 = (bf16[4,24,1152]{2,1,0:T(8,128)(2,1)S(1)}, bf16[4,24,1152]{2,1,0:T(8,128)(2,1)S(1)}, u32[]{:S(2)}, u32[]{:S(2)}) collective-permute-start(bf16[4,24,1152]{2,1,0:T(8,128)(2,1)S(1)} %pad_maximum_fusion.2.refs_0_), channel_id=1, source_target_pairs={{0,24},{8,0},{16,8},{24,16},{1,25},{9,1},{17,9},{25,17},{2,26},{10... | collective-permute-start | bytes 663560 | tf_op jit(solution)/shard_map/ppermute | solution.py:175
  72.5 2.6 %collective-permute-done.12.refs_2_ = bf16[4,24,1152]{2,1,0:T(8,128)(2,1)S(1)} collective-permute-done((bf16[4,24,1152]{2,1,0:T(8,128)(2,1)S(1)}, bf16[4,24,1152]{2,1,0:T(8,128)(2,1)S(1)}, u32[]{:S(2)}, u32[]{:S(2)}) %collective-permute-start.12) | collective-permute-done | bytes 221216 | tf_op jit(solution)/shard_map/ppermute | solution.py:175
  75.8 3.7 %collective-permute-start.7 = (bf16[4,24,1152]{2,1,0:T(8,128)(2,1)S(1)}, bf16[4,24,1152]{2,1,0:T(8,128)(2,1)}, u32[]{:S(2)}, u32[]{:S(2)}) collective-permute-start(bf16[4,24,1152]{2,1,0:T(8,128)(2,1)S(1)} %pad_maximum_fusion.3.refs_1_), channel_id=1, source_target_pairs={{0,24},{8,0},{16,8},{24,16},{1,25},{9,1},{17,9},{25,17},{2,26},{10... | collective-permute-start | bytes 663560 | tf_op jit(solution)/shard_map/ppermute | solution.py:175
  79.5 1.5 collective-permute-done.6.refs_6_
  81.1 4.5 %collective-permute-done.16.refs_7_ = bf16[4,24,1152]{2,1,0:T(8,128)(2,1)} collective-permute-done((bf16[4,24,1152]{2,1,0:T(8,128)(2,1)S(1)}, bf16[4,24,1152]{2,1,0:T(8,128)(2,1)}, u32[]{:S(2)}, u32[]{:S(2)}) %collective-permute-start.16) | collective-permute-done | bytes 221216 | tf_op jit(solution)/shard_map/ppermute | solution.py:175
  85.5 2.4 %reshape.30.t_ref = bf16[512,1152]{1,0:T(8,128)(2,1)S(1)} reshape(bf16[128,4,1152]{2,1,0:T(4,128)(2,1)} %all-to-all-done) | data formatting | bytes 2359296 | tf_op jit(solution)/shard_map/reshape | solution.py:251
  88.7 3.1 %collective-permute-start.11 = (bf16[4,24,1152]{2,1,0:T(8,128)(2,1)}, bf16[4,24,1152]{2,1,0:T(8,128)(2,1)}, u32[]{:S(2)}, u32[]{:S(2)}) collective-permute-start(bf16[4,24,1152]{2,1,0:T(8,128)(2,1)} %collective-permute-done.7.refs_3_), channel_id=1, source_target_pairs={{0,24},{8,0},{16,8},{24,16},{1,25},{9,1},{17,9},{25,17},{2,26},{10... | collective-permute-start | bytes 663560 | tf_op jit(solution)/shard_map/ppermute | solution.py:175
  92.5 4.7 %collective-permute-done.10.refs_4_ = bf16[4,24,1152]{2,1,0:T(8,128)(2,1)} collective-permute-done((bf16[4,24,1152]{2,1,0:T(8,128)(2,1)S(1)}, bf16[4,24,1152]{2,1,0:T(8,128)(2,1)}, u32[]{:S(2)}, u32[]{:S(2)}) %collective-permute-start.10) | collective-permute-done | bytes 221216 | tf_op jit(solution)/shard_map/ppermute | solution.py:175
  98.5 1.6 reshape.31.o_ref
  101.1 0.9 copy-done.4
  102.0 0.9 copy-done.6
  103.0 0.9 copy-done.8
  103.9 0.9 copy-done.10
  104.8 0.9 copy-done.12
  105.8 0.9 copy-done.14
  106.7 16.0 %attention_core.1 = (bf16[512,768]{1,0:T(8,128)(2,1)S(1)}, bf16[512,768]{1,0:T(8,128)(2,1)S(1)}, bf16[4,8,24,1152]{3,2,1,0:T(8,128)(2,1)S(1)}, bf16[4,8,24,1152]{3,2,1,0:T(8,128)(2,1)S(1)}) custom-call(s32[4]{0:T(128)S(1)} %pad_add_fusion.where_ref, bf16[512,1152]{1,0:T(8,128)(2,1)S(1)} %reshape.30.t_ref, bf16[512,768]{1,0:T(8,128)(2,1)S(1)} %reshape.31.o_ref, ...), custom_call_target="tpu_custom_call" | custom-call | flops 5435817984 | bytes 8388608 | tf_op jit(solution)/shard_map/attention_core/pallas_call | solution.py:111
  123.0 1.9 collective-permute-start.24
  124.9 1.7 collective-permute-done.21.other_ref
  127.2 3.3 %collective-permute-start.23 = (bf16[4,24,1152]{2,1,0:T(8,128)(2,1)S(1)}, bf16[4,24,1152]{2,1,0:T(8,128)(2,1)S(1)}, u32[]{:S(2)}, u32[]{:S(2)}) collective-permute-start(bf16[4,24,1152]{2,1,0:T(8,128)(2,1)S(1)} %get-tuple-element.58), channel_id=1, source_target_pairs={{0,24},{8,0},{16,8},{24,16},{1,25},{9,1},{17,9},{25,17},{2,26},{10... | collective-permute-start | bytes 663560 | tf_op jit(solution)/shard_map/ppermute | solution.py:175
  130.5 2.0 %collective-permute-start.26 = (bf16[4,24,1152]{2,1,0:T(8,128)(2,1)S(1)}, bf16[4,24,1152]{2,1,0:T(8,128)(2,1)S(1)}, u32[]{:S(2)}, u32[]{:S(2)}) collective-permute-start(bf16[4,24,1152]{2,1,0:T(8,128)(2,1)S(1)} %get-tuple-element.61), channel_id=1, source_target_pairs={{0,24},{8,0},{16,8},{24,16},{1,25},{9,1},{17,9},{25,17},{2,26},{10... | collective-permute-start | bytes 663560 | tf_op jit(solution)/shard_map/ppermute | solution.py:175
  132.6 4.0 %collective-permute-done.24 = bf16[320,768]{1,0:T(8,128)(2,1)S(1)} collective-permute-done((bf16[320,768]{1,0:T(8,128)(2,1)S(1)}, bf16[320,768]{1,0:T(8,128)(2,1)S(1)}, u32[]{:S(2)}, u32[]{:S(2)}) %collective-permute-start.24) | collective-permute-done | bytes 491552 | tf_op jit(solution)/shard_map/ppermute | solution.py:200
  136.7 1.5 collective-permute-start.25
  138.3 2.0 %collective-permute-start.28 = (bf16[4,24,1152]{2,1,0:T(8,128)(2,1)S(1)}, bf16[4,24,1152]{2,1,0:T(8,128)(2,1)S(1)}, u32[]{:S(2)}, u32[]{:S(2)}) collective-permute-start(bf16[4,24,1152]{2,1,0:T(8,128)(2,1)S(1)} %add_convert_fusion.1), channel_id=1, source_target_pairs={{0,24},{8,0},{16,8},{24,16},{1,25},{9,1},{17,9},{25,17},{2,26},{10... | collective-permute-start | bytes 663560 | tf_op jit(solution)/shard_map/ppermute | solution.py:175
  140.3 1.7 collective-permute-start.32
  142.0 3.6 %collective-permute-done.25 = bf16[4,24,1152]{2,1,0:T(8,128)(2,1)S(1)} collective-permute-done((bf16[4,24,1152]{2,1,0:T(8,128)(2,1)S(1)}, bf16[4,24,1152]{2,1,0:T(8,128)(2,1)S(1)}, u32[]{:S(2)}, u32[]{:S(2)}) %collective-permute-start.25) | collective-permute-done | bytes 221216 | tf_op jit(solution)/shard_map/ppermute | solution.py:175
  146.0 1.3 collective-permute-start.30
  147.3 2.6 %collective-permute-start.31 = (bf16[4,12,1152]{2,1,0:T(8,128)(2,1)S(1)}, bf16[4,12,1152]{2,1,0:T(8,128)(2,1)S(1)}, u32[]{:S(2)}, u32[]{:S(2)}) collective-permute-start(bf16[4,12,1152]{2,1,0:T(8,128)(2,1)S(1)} %get-tuple-element.75), channel_id=1, source_target_pairs={{0,36},{4,32},{32,4},{36,0},{64,100},{68,96},{96,68},{100,64},{128... | collective-permute-start | bytes 331784 | tf_op jit(solution)/shard_map/ppermute | solution.py:179
  149.9 1.2 collective-permute-start.29
  151.3 4.0 %collective-permute-done.30 = bf16[4,12,1152]{2,1,0:T(8,128)(2,1)S(1)} collective-permute-done((bf16[4,12,1152]{2,1,0:T(8,128)(2,1)S(1)}, bf16[4,12,1152]{2,1,0:T(8,128)(2,1)S(1)}, u32[]{:S(2)}, u32[]{:S(2)}) %collective-permute-start.30) | collective-permute-done | bytes 110624 | tf_op jit(solution)/shard_map/ppermute | solution.py:179
  157.1 1.1 reshape.32
  158.2 8.6 %all-to-all-start.1 = ((bf16[128,4,768]{2,1,0:T(4,128)(2,1)}), bf16[128,4,768]{2,1,0:T(4,128)(2,1)S(1)}, u32[]{:S(2)}, u32[]{:S(2)}) async-start(bf16[128,4,768]{2,1,0:T(4,128)(2,1)} %reshape.32), calls=%async_computation.1 | async-start | bytes 1572864 | tf_op jit(solution)/shard_map/all_to_all | solution.py:271
  166.8 2.6 %collective-permute-start.33 = (bf16[12,1152]{1,0:T(8,128)(2,1)S(1)}, bf16[12,1152]{1,0:T(8,128)(2,1)S(1)}, u32[]{:S(2)}, u32[]{:S(2)}) collective-permute-start(bf16[12,1152]{1,0:T(8,128)(2,1)S(1)} %get-tuple-element.76), channel_id=1, source_target_pairs={{0,64},{32,96},{64,0},{96,32},{128,192},{160,224},{192,128},{224,1... | collective-permute-start | bytes 82952 | tf_op jit(solution)/shard_map/ppermute | solution.py:179
  169.4 3.8 %collective-permute-start.35 = (bf16[12,1152]{1,0:T(8,128)(2,1)S(1)}, bf16[12,1152]{1,0:T(8,128)(2,1)S(1)}, u32[]{:S(2)}, u32[]{:S(2)}) collective-permute-start(bf16[12,1152]{1,0:T(8,128)(2,1)S(1)} %get-tuple-element.77), channel_id=1, source_target_pairs={{0,192},{32,224},{64,128},{96,160},{128,64},{160,96},{192,0},{224,... | collective-permute-start | bytes 82952 | tf_op jit(solution)/shard_map/ppermute | solution.py:179
  173.4 15.2 %collective-permute-done.33 = bf16[12,1152]{1,0:T(8,128)(2,1)S(1)} collective-permute-done((bf16[12,1152]{1,0:T(8,128)(2,1)S(1)}, bf16[12,1152]{1,0:T(8,128)(2,1)S(1)}, u32[]{:S(2)}, u32[]{:S(2)}) %collective-permute-start.33) | collective-permute-done | bytes 27680 | tf_op jit(solution)/shard_map/ppermute | solution.py:179
  188.5 1.3 collective-permute-done.35
  189.8 2.9 %collective-permute-done.34 = bf16[12,1152]{1,0:T(8,128)(2,1)S(1)} collective-permute-done((bf16[12,1152]{1,0:T(8,128)(2,1)S(1)}, bf16[12,1152]{1,0:T(8,128)(2,1)S(1)}, u32[]{:S(2)}, u32[]{:S(2)}) %collective-permute-start.34) | collective-permute-done | bytes 27680 | tf_op jit(solution)/shard_map/ppermute | solution.py:179
  193.4 1.1 reshape.33
  (94 shorter events, 11.6 us)
Async XLA Ops:
  0.6 6.1 %copy-start = (bf16[1,512,1536]{2,1,0:T(8,128)(2,1)S(1)}, bf16[1,512,1536]{2,1,0:T(8,128)(2,1)}, u32[]{:S(2)}) copy-start(bf16[1,512,1536]{2,1,0:T(8,128)(2,1)} %param.3) | copy-start | bytes 4718596
  0.6 6.1 %copy-start.15 = (bf16[1,512,384]{2,1,0:T(8,128)(2,1)S(1)}, bf16[1,512,384]{2,1,0:T(8,128)(2,1)}, u32[]{:S(2)}) copy-start(bf16[1,512,384]{2,1,0:T(8,128)(2,1)} %param.4) | copy-start | bytes 1179652
  1.6 8.8 %collective-permute-start.1 = (bf16[12,1152]{1,0:T(8,128)(2,1)S(1)}, bf16[12,1152]{1,0:T(8,128)(2,1)S(1)}, u32[]{:S(2)}, u32[]{:S(2)}) collective-permute-start(bf16[12,1152]{1,0:T(8,128)(2,1)S(1)} %bitcast.26), channel_id=1, source_target_pairs={{0,32},{4,36},{32,0},{36,4},{64,96},{68,100},{96,64},{100,68},{128... | collective-permute-start | bytes 82952 | tf_op jit(solution)/shard_map/ppermute | solution.py:179
  3.6 6.8 %collective-permute-start.2 = (bf16[12,1152]{1,0:T(8,128)(2,1)S(1)}, bf16[12,1152]{1,0:T(8,128)(2,1)S(1)}, u32[]{:S(2)}, u32[]{:S(2)}) collective-permute-start(bf16[12,1152]{1,0:T(8,128)(2,1)S(1)} %bitcast.27), channel_id=1, source_target_pairs={{0,36},{4,32},{32,4},{36,0},{64,100},{68,96},{96,68},{100,64},{128... | collective-permute-start | bytes 82952 | tf_op jit(solution)/shard_map/ppermute | solution.py:179
  4.6 5.8 %collective-permute-start = (bf16[12,1152]{1,0:T(8,128)(2,1)S(1)}, bf16[12,1152]{1,0:T(8,128)(2,1)S(1)}, u32[]{:S(2)}, u32[]{:S(2)}) collective-permute-start(bf16[12,1152]{1,0:T(8,128)(2,1)S(1)} %bitcast.28), channel_id=1, source_target_pairs={{0,4},{4,0},{32,36},{36,32},{64,68},{68,64},{96,100},{100,96},{128... | collective-permute-start | bytes 82952 | tf_op jit(solution)/shard_map/ppermute | solution.py:179
  10.5 55.9 %all-to-all-start = ((bf16[128,4,1152]{2,1,0:T(4,128)(2,1)}), bf16[128,4,1152]{2,1,0:T(4,128)(2,1)}, u32[]{:S(2)}, u32[]{:S(2)}) async-start(bf16[128,4,1152]{2,1,0:T(4,128)(2,1)} %reshape.28), calls=%async_computation | async-start | bytes 2359296 | tf_op jit(solution)/shard_map/all_to_all | solution.py:241
  26.0 34.5 %collective-permute-start.3 = (bf16[2,24,1152]{2,1,0:T(8,128)(2,1)S(1)}, bf16[2,24,1152]{2,1,0:T(8,128)(2,1)S(1)}, u32[]{:S(2)}, u32[]{:S(2)}) collective-permute-start(bf16[2,24,1152]{2,1,0:T(8,128)(2,1)S(1)} %pad_maximum_fusion.4), channel_id=1, source_target_pairs={{0,64},{32,96},{64,0},{96,32},{128,192},{160,224},{192,128},{224,1... | collective-permute-start | bytes 331784 | tf_op jit(solution)/shard_map/ppermute | solution.py:179
  28.5 31.9 %collective-permute-start.5 = (bf16[2,24,1152]{2,1,0:T(8,128)(2,1)S(1)}, bf16[2,24,1152]{2,1,0:T(8,128)(2,1)S(1)}, u32[]{:S(2)}, u32[]{:S(2)}) collective-permute-start(bf16[2,24,1152]{2,1,0:T(8,128)(2,1)S(1)} %pad_maximum_fusion.4), channel_id=1, source_target_pairs={{0,192},{32,224},{64,128},{96,160},{128,64},{160,96},{192,0},{224,... | collective-permute-start | bytes 331784 | tf_op jit(solution)/shard_map/ppermute | solution.py:179
  32.3 34.0 %collective-permute-start.4 = (bf16[2,24,1152]{2,1,0:T(8,128)(2,1)S(1)}, bf16[2,24,1152]{2,1,0:T(8,128)(2,1)S(1)}, u32[]{:S(2)}, u32[]{:S(2)}) collective-permute-start(bf16[2,24,1152]{2,1,0:T(8,128)(2,1)S(1)} %pad_maximum_fusion.4), channel_id=1, source_target_pairs={{0,128},{32,160},{64,192},{96,224},{128,0},{160,32},{192,64},{224,... | collective-permute-start | bytes 331784 | tf_op jit(solution)/shard_map/ppermute | solution.py:179
  60.5 25.1 %copy-start.1 = (bf16[4,24,1152]{2,1,0:T(8,128)(2,1)}, bf16[4,24,1152]{2,1,0:T(8,128)(2,1)S(1)}, u32[]{:S(2)}) copy-start(bf16[4,24,1152]{2,1,0:T(8,128)(2,1)S(1)} %pad_maximum_fusion.2.refs_0_) | copy-start | bytes 663556
  66.4 21.5 %copy-start.3 = (bf16[4,24,1152]{2,1,0:T(8,128)(2,1)}, bf16[4,24,1152]{2,1,0:T(8,128)(2,1)S(1)}, u32[]{:S(2)}) copy-start(bf16[4,24,1152]{2,1,0:T(8,128)(2,1)S(1)} %pad_maximum_fusion.3.refs_1_) | copy-start | bytes 663556
  68.7 29.2 %collective-permute-start.18 = (bf16[128,4,768]{2,1,0:T(4,128)(2,1)}, bf16[128,4,768]{2,1,0:T(4,128)(2,1)}, u32[]{:S(2)}, u32[]{:S(2)}) collective-permute-start(bf16[128,4,768]{2,1,0:T(4,128)(2,1)} %slice.68), channel_id=1, source_target_pairs={{0,1},{1,0},{2,3},{3,2},{4,5},{5,4},{6,7},{7,6},{8,9},{9,8},{10,11... | collective-permute-start | bytes 2359304 | tf_op jit(solution)/shard_map/ppermute | solution.py:246
  69.0 6.1 %collective-permute-start.12 = (bf16[4,24,1152]{2,1,0:T(8,128)(2,1)S(1)}, bf16[4,24,1152]{2,1,0:T(8,128)(2,1)S(1)}, u32[]{:S(2)}, u32[]{:S(2)}) collective-permute-start(bf16[4,24,1152]{2,1,0:T(8,128)(2,1)S(1)} %pad_maximum_fusion.2.refs_0_), channel_id=1, source_target_pairs={{0,24},{8,0},{16,8},{24,16},{1,25},{9,1},{17,9},{25,17},{2,26},{10... | collective-permute-start | bytes 663560 | tf_op jit(solution)/shard_map/ppermute | solution.py:175
  71.6 3.5 %collective-permute-start.8 = (bf16[4,24,1152]{2,1,0:T(8,128)(2,1)S(1)}, bf16[4,24,1152]{2,1,0:T(8,128)(2,1)S(1)}, u32[]{:S(2)}, u32[]{:S(2)}) collective-permute-start(bf16[4,24,1152]{2,1,0:T(8,128)(2,1)S(1)} %pad_maximum_fusion.2.refs_0_), channel_id=1, source_target_pairs={{0,2},{2,0},{1,3},{3,1},{4,6},{6,4},{5,7},{7,5},{8,10},{10,8},{9,1... | collective-permute-start | bytes 663560 | tf_op jit(solution)/shard_map/ppermute | solution.py:194
  71.6 9.4 %collective-permute-start.6 = (bf16[4,24,1152]{2,1,0:T(8,128)(2,1)S(1)}, bf16[4,24,1152]{2,1,0:T(8,128)(2,1)S(1)}, u32[]{:S(2)}, u32[]{:S(2)}) collective-permute-start(bf16[4,24,1152]{2,1,0:T(8,128)(2,1)S(1)} %pad_maximum_fusion.2.refs_0_), channel_id=1, source_target_pairs={{0,8},{8,16},{16,24},{24,0},{1,9},{9,17},{17,25},{25,1},{2,10},{10... | collective-permute-start | bytes 663560 | tf_op jit(solution)/shard_map/ppermute | solution.py:175
  71.6 13.9 %collective-permute-start.16 = (bf16[4,24,1152]{2,1,0:T(8,128)(2,1)S(1)}, bf16[4,24,1152]{2,1,0:T(8,128)(2,1)}, u32[]{:S(2)}, u32[]{:S(2)}) collective-permute-start(bf16[4,24,1152]{2,1,0:T(8,128)(2,1)S(1)} %pad_maximum_fusion.3.refs_1_), channel_id=1, source_target_pairs={{0,8},{8,16},{16,24},{24,0},{1,9},{9,17},{17,25},{25,1},{2,10},{10... | collective-permute-start | bytes 663560 | tf_op jit(solution)/shard_map/ppermute | solution.py:175
  75.1 23.4 %copy-start.5 = (bf16[4,24,1152]{2,1,0:T(8,128)(2,1)}, bf16[4,24,1152]{2,1,0:T(8,128)(2,1)S(1)}, u32[]{:S(2)}) copy-start(bf16[4,24,1152]{2,1,0:T(8,128)(2,1)S(1)} %collective-permute-done.12.refs_2_) | copy-start | bytes 663556
  75.1 12.8 %collective-permute-start.9 = (bf16[4,24,1152]{2,1,0:T(8,128)(2,1)S(1)}, bf16[4,24,1152]{2,1,0:T(8,128)(2,1)}, u32[]{:S(2)}, u32[]{:S(2)}) collective-permute-start(bf16[4,24,1152]{2,1,0:T(8,128)(2,1)S(1)} %pad_maximum_fusion.3.refs_1_), channel_id=1, source_target_pairs={{0,2},{2,0},{1,3},{3,1},{4,6},{6,4},{5,7},{7,5},{8,10},{10,8},{9,1... | collective-permute-start | bytes 663560 | tf_op jit(solution)/shard_map/ppermute | solution.py:194
  75.8 12.1 %collective-permute-start.7 = (bf16[4,24,1152]{2,1,0:T(8,128)(2,1)S(1)}, bf16[4,24,1152]{2,1,0:T(8,128)(2,1)}, u32[]{:S(2)}, u32[]{:S(2)}) collective-permute-start(bf16[4,24,1152]{2,1,0:T(8,128)(2,1)S(1)} %pad_maximum_fusion.3.refs_1_), channel_id=1, source_target_pairs={{0,24},{8,0},{16,8},{24,16},{1,25},{9,1},{17,9},{25,17},{2,26},{10... | collective-permute-start | bytes 663560 | tf_op jit(solution)/shard_map/ppermute | solution.py:175
  81.1 17.4 %copy-start.9 = (bf16[4,24,1152]{2,1,0:T(8,128)(2,1)}, bf16[4,24,1152]{2,1,0:T(8,128)(2,1)S(1)}, u32[]{:S(2)}) copy-start(bf16[4,24,1152]{2,1,0:T(8,128)(2,1)S(1)} %collective-permute-done.6.refs_6_) | copy-start | bytes 663556
  81.1 7.5 %collective-permute-start.13 = (bf16[4,24,1152]{2,1,0:T(8,128)(2,1)S(1)}, bf16[4,24,1152]{2,1,0:T(8,128)(2,1)}, u32[]{:S(2)}, u32[]{:S(2)}) collective-permute-start(bf16[4,24,1152]{2,1,0:T(8,128)(2,1)S(1)} %collective-permute-done.12.refs_2_), channel_id=1, source_target_pairs={{0,2},{2,0},{1,3},{3,1},{4,6},{6,4},{5,7},{7,5},{8,10},{10,8},{9,1... | collective-permute-start | bytes 663560 | tf_op jit(solution)/shard_map/ppermute | solution.py:194
  85.5 3.2 %collective-permute-start.17 = (bf16[4,24,1152]{2,1,0:T(8,128)(2,1)}, bf16[4,24,1152]{2,1,0:T(8,128)(2,1)}, u32[]{:S(2)}, u32[]{:S(2)}) collective-permute-start(bf16[4,24,1152]{2,1,0:T(8,128)(2,1)} %collective-permute-done.16.refs_7_), channel_id=1, source_target_pairs={{0,2},{2,0},{1,3},{3,1},{4,6},{6,4},{5,7},{7,5},{8,10},{10,8},{9,1... | collective-permute-start | bytes 663560 | tf_op jit(solution)/shard_map/ppermute | solution.py:194
  87.9 3.9 %collective-permute-start.15 = (bf16[4,24,1152]{2,1,0:T(8,128)(2,1)S(1)}, bf16[4,24,1152]{2,1,0:T(8,128)(2,1)S(1)}, u32[]{:S(2)}, u32[]{:S(2)}) collective-permute-start(bf16[4,24,1152]{2,1,0:T(8,128)(2,1)S(1)} %collective-permute-done.6.refs_6_), channel_id=1, source_target_pairs={{0,2},{2,0},{1,3},{3,1},{4,6},{6,4},{5,7},{7,5},{8,10},{10,8},{9,1... | collective-permute-start | bytes 663560 | tf_op jit(solution)/shard_map/ppermute | solution.py:194
  88.5 8.7 %collective-permute-start.10 = (bf16[4,24,1152]{2,1,0:T(8,128)(2,1)S(1)}, bf16[4,24,1152]{2,1,0:T(8,128)(2,1)}, u32[]{:S(2)}, u32[]{:S(2)}) collective-permute-start(bf16[4,24,1152]{2,1,0:T(8,128)(2,1)S(1)} %collective-permute-done.6.refs_6_), channel_id=1, source_target_pairs={{0,8},{8,16},{16,24},{24,0},{1,9},{9,17},{17,25},{25,1},{2,10},{10... | collective-permute-start | bytes 663560 | tf_op jit(solution)/shard_map/ppermute | solution.py:175
  88.5 8.7 %collective-permute-start.14 = (bf16[4,24,1152]{2,1,0:T(8,128)(2,1)}, bf16[4,24,1152]{2,1,0:T(8,128)(2,1)S(1)}, u32[]{:S(2)}, u32[]{:S(2)}) collective-permute-start(bf16[4,24,1152]{2,1,0:T(8,128)(2,1)} %collective-permute-done.7.refs_3_), channel_id=1, source_target_pairs={{0,2},{2,0},{1,3},{3,1},{4,6},{6,4},{5,7},{7,5},{8,10},{10,8},{9,1... | collective-permute-start | bytes 663560 | tf_op jit(solution)/shard_map/ppermute | solution.py:194
  88.7 9.2 %collective-permute-start.11 = (bf16[4,24,1152]{2,1,0:T(8,128)(2,1)}, bf16[4,24,1152]{2,1,0:T(8,128)(2,1)}, u32[]{:S(2)}, u32[]{:S(2)}) collective-permute-start(bf16[4,24,1152]{2,1,0:T(8,128)(2,1)} %collective-permute-done.7.refs_3_), channel_id=1, source_target_pairs={{0,24},{8,0},{16,8},{24,16},{1,25},{9,1},{17,9},{25,17},{2,26},{10... | collective-permute-start | bytes 663560 | tf_op jit(solution)/shard_map/ppermute | solution.py:175
  98.0 2.2 %collective-permute-start.19 = (bf16[4,24,1152]{2,1,0:T(8,128)(2,1)}, bf16[4,24,1152]{2,1,0:T(8,128)(2,1)}, u32[]{:S(2)}, u32[]{:S(2)}) collective-permute-start(bf16[4,24,1152]{2,1,0:T(8,128)(2,1)} %collective-permute-done.10.refs_4_), channel_id=1, source_target_pairs={{0,2},{2,0},{1,3},{3,1},{4,6},{6,4},{5,7},{7,5},{8,10},{10,8},{9,1... | collective-permute-start | bytes 663560 | tf_op jit(solution)/shard_map/ppermute | solution.py:194
  98.0 2.2 %collective-permute-start.20 = (bf16[4,24,1152]{2,1,0:T(8,128)(2,1)}, bf16[4,24,1152]{2,1,0:T(8,128)(2,1)}, u32[]{:S(2)}, u32[]{:S(2)}) collective-permute-start(bf16[4,24,1152]{2,1,0:T(8,128)(2,1)} %collective-permute-done.11.refs_5_), channel_id=1, source_target_pairs={{0,2},{2,0},{1,3},{3,1},{4,6},{6,4},{5,7},{7,5},{8,10},{10,8},{9,1... | collective-permute-start | bytes 663560 | tf_op jit(solution)/shard_map/ppermute | solution.py:194
  100.1 0.9 copy-start.2
  101.1 0.9 copy-start.4
  104.8 0.9 copy-start.12
  105.8 0.9 copy-start.14
  122.8 3.8 %collective-permute-start.21 = (bf16[4,8,24,1152]{3,2,1,0:T(8,128)(2,1)S(1)}, bf16[4,8,24,1152]{3,2,1,0:T(8,128)(2,1)S(1)}, u32[]{:S(2)}, u32[]{:S(2)}) collective-permute-start(bf16[4,8,24,1152]{3,2,1,0:T(8,128)(2,1)S(1)} %get-tuple-element.54), channel_id=1, source_target_pairs={{0,2},{2,0},{1,3},{3,1},{4,6},{6,4},{5,7},{7,5},{8,10},{10,8},{9,1... | collective-permute-start | bytes 5308424 | tf_op jit(solution)/shard_map/ppermute | solution.py:199
  123.0 13.6 %collective-permute-start.24 = (bf16[320,768]{1,0:T(8,128)(2,1)S(1)}, bf16[320,768]{1,0:T(8,128)(2,1)S(1)}, u32[]{:S(2)}, u32[]{:S(2)}) collective-permute-start(bf16[320,768]{1,0:T(8,128)(2,1)S(1)} %slice.55), channel_id=1, source_target_pairs={{0,1},{1,0},{2,3},{3,2},{4,5},{5,4},{6,7},{7,6},{8,9},{9,8},{10,11... | collective-permute-start | bytes 1474568 | tf_op jit(solution)/shard_map/ppermute | solution.py:200
  126.9 9.7 %collective-permute-start.22 = (bf16[4,24,1152]{2,1,0:T(8,128)(2,1)S(1)}, bf16[4,24,1152]{2,1,0:T(8,128)(2,1)S(1)}, u32[]{:S(2)}, u32[]{:S(2)}) collective-permute-start(bf16[4,24,1152]{2,1,0:T(8,128)(2,1)S(1)} %get-tuple-element.57), channel_id=1, source_target_pairs={{0,8},{8,16},{16,24},{24,0},{1,9},{9,17},{17,25},{25,1},{2,10},{10... | collective-permute-start | bytes 663560 | tf_op jit(solution)/shard_map/ppermute | solution.py:175
  127.2 9.4 %collective-permute-start.23 = (bf16[4,24,1152]{2,1,0:T(8,128)(2,1)S(1)}, bf16[4,24,1152]{2,1,0:T(8,128)(2,1)S(1)}, u32[]{:S(2)}, u32[]{:S(2)}) collective-permute-start(bf16[4,24,1152]{2,1,0:T(8,128)(2,1)S(1)} %get-tuple-element.58), channel_id=1, source_target_pairs={{0,24},{8,0},{16,8},{24,16},{1,25},{9,1},{17,9},{25,17},{2,26},{10... | collective-permute-start | bytes 663560 | tf_op jit(solution)/shard_map/ppermute | solution.py:175
  130.5 11.5 %collective-permute-start.26 = (bf16[4,24,1152]{2,1,0:T(8,128)(2,1)S(1)}, bf16[4,24,1152]{2,1,0:T(8,128)(2,1)S(1)}, u32[]{:S(2)}, u32[]{:S(2)}) collective-permute-start(bf16[4,24,1152]{2,1,0:T(8,128)(2,1)S(1)} %get-tuple-element.61), channel_id=1, source_target_pairs={{0,24},{8,0},{16,8},{24,16},{1,25},{9,1},{17,9},{25,17},{2,26},{10... | collective-permute-start | bytes 663560 | tf_op jit(solution)/shard_map/ppermute | solution.py:175
  132.6 9.5 %collective-permute-start.27 = (bf16[4,24,1152]{2,1,0:T(8,128)(2,1)S(1)}, bf16[4,24,1152]{2,1,0:T(8,128)(2,1)S(1)}, u32[]{:S(2)}, u32[]{:S(2)}) collective-permute-start(bf16[4,24,1152]{2,1,0:T(8,128)(2,1)S(1)} %get-tuple-element.62), channel_id=1, source_target_pairs={{0,8},{8,16},{16,24},{24,0},{1,9},{9,17},{17,25},{25,1},{2,10},{10... | collective-permute-start | bytes 663560 | tf_op jit(solution)/shard_map/ppermute | solution.py:175
  136.7 9.0 %collective-permute-start.25 = (bf16[4,24,1152]{2,1,0:T(8,128)(2,1)S(1)}, bf16[4,24,1152]{2,1,0:T(8,128)(2,1)S(1)}, u32[]{:S(2)}, u32[]{:S(2)}) collective-permute-start(bf16[4,24,1152]{2,1,0:T(8,128)(2,1)S(1)} %add_convert_fusion.2), channel_id=1, source_target_pairs={{0,8},{8,16},{16,24},{24,0},{1,9},{9,17},{17,25},{25,1},{2,10},{10... | collective-permute-start | bytes 663560 | tf_op jit(solution)/shard_map/ppermute | solution.py:175
  138.3 7.4 %collective-permute-start.28 = (bf16[4,24,1152]{2,1,0:T(8,128)(2,1)S(1)}, bf16[4,24,1152]{2,1,0:T(8,128)(2,1)S(1)}, u32[]{:S(2)}, u32[]{:S(2)}) collective-permute-start(bf16[4,24,1152]{2,1,0:T(8,128)(2,1)S(1)} %add_convert_fusion.1), channel_id=1, source_target_pairs={{0,24},{8,0},{16,8},{24,16},{1,25},{9,1},{17,9},{25,17},{2,26},{10... | collective-permute-start | bytes 663560 | tf_op jit(solution)/shard_map/ppermute | solution.py:175
  140.3 10.8 %collective-permute-start.32 = (bf16[192,768]{1,0:T(8,128)(2,1)S(1)}, bf16[192,768]{1,0:T(8,128)(2,1)S(1)}, u32[]{:S(2)}, u32[]{:S(2)}) collective-permute-start(bf16[192,768]{1,0:T(8,128)(2,1)S(1)} %slice.56), channel_id=1, source_target_pairs={{0,1},{1,0},{2,3},{3,2},{4,5},{5,4},{6,7},{7,6},{8,9},{9,8},{10,11... | collective-permute-start | bytes 884744 | tf_op jit(solution)/shard_map/ppermute | solution.py:208
  146.0 9.3 %collective-permute-start.30 = (bf16[4,12,1152]{2,1,0:T(8,128)(2,1)S(1)}, bf16[4,12,1152]{2,1,0:T(8,128)(2,1)S(1)}, u32[]{:S(2)}, u32[]{:S(2)}) collective-permute-start(bf16[4,12,1152]{2,1,0:T(8,128)(2,1)S(1)} %get-tuple-element.74), channel_id=1, source_target_pairs={{0,4},{4,0},{32,36},{36,32},{64,68},{68,64},{96,100},{100,96},{128... | collective-permute-start | bytes 331784 | tf_op jit(solution)/shard_map/ppermute | solution.py:179
  147.3 8.8 %collective-permute-start.31 = (bf16[4,12,1152]{2,1,0:T(8,128)(2,1)S(1)}, bf16[4,12,1152]{2,1,0:T(8,128)(2,1)S(1)}, u32[]{:S(2)}, u32[]{:S(2)}) collective-permute-start(bf16[4,12,1152]{2,1,0:T(8,128)(2,1)S(1)} %get-tuple-element.75), channel_id=1, source_target_pairs={{0,36},{4,32},{32,4},{36,0},{64,100},{68,96},{96,68},{100,64},{128... | collective-permute-start | bytes 331784 | tf_op jit(solution)/shard_map/ppermute | solution.py:179
  149.9 7.1 %collective-permute-start.29 = (bf16[4,12,1152]{2,1,0:T(8,128)(2,1)S(1)}, bf16[4,12,1152]{2,1,0:T(8,128)(2,1)S(1)}, u32[]{:S(2)}, u32[]{:S(2)}) collective-permute-start(bf16[4,12,1152]{2,1,0:T(8,128)(2,1)S(1)} %slice.61), channel_id=1, source_target_pairs={{0,32},{4,36},{32,0},{36,4},{64,96},{68,100},{96,64},{100,68},{128... | collective-permute-start | bytes 331784 | tf_op jit(solution)/shard_map/ppermute | solution.py:179
  158.2 35.2 %all-to-all-start.1 = ((bf16[128,4,768]{2,1,0:T(4,128)(2,1)}), bf16[128,4,768]{2,1,0:T(4,128)(2,1)S(1)}, u32[]{:S(2)}, u32[]{:S(2)}) async-start(bf16[128,4,768]{2,1,0:T(4,128)(2,1)} %reshape.32), calls=%async_computation.1 | async-start | bytes 1572864 | tf_op jit(solution)/shard_map/all_to_all | solution.py:271
  166.8 21.8 %collective-permute-start.33 = (bf16[12,1152]{1,0:T(8,128)(2,1)S(1)}, bf16[12,1152]{1,0:T(8,128)(2,1)S(1)}, u32[]{:S(2)}, u32[]{:S(2)}) collective-permute-start(bf16[12,1152]{1,0:T(8,128)(2,1)S(1)} %get-tuple-element.76), channel_id=1, source_target_pairs={{0,64},{32,96},{64,0},{96,32},{128,192},{160,224},{192,128},{224,1... | collective-permute-start | bytes 82952 | tf_op jit(solution)/shard_map/ppermute | solution.py:179
  169.4 20.5 %collective-permute-start.35 = (bf16[12,1152]{1,0:T(8,128)(2,1)S(1)}, bf16[12,1152]{1,0:T(8,128)(2,1)S(1)}, u32[]{:S(2)}, u32[]{:S(2)}) collective-permute-start(bf16[12,1152]{1,0:T(8,128)(2,1)S(1)} %get-tuple-element.77), channel_id=1, source_target_pairs={{0,192},{32,224},{64,128},{96,160},{128,64},{160,96},{192,0},{224,... | collective-permute-start | bytes 82952 | tf_op jit(solution)/shard_map/ppermute | solution.py:179
  173.2 19.5 %collective-permute-start.34 = (bf16[12,1152]{1,0:T(8,128)(2,1)S(1)}, bf16[12,1152]{1,0:T(8,128)(2,1)S(1)}, u32[]{:S(2)}, u32[]{:S(2)}) collective-permute-start(bf16[12,1152]{1,0:T(8,128)(2,1)S(1)} %get-tuple-element.78), channel_id=1, source_target_pairs={{0,128},{32,160},{64,192},{96,224},{128,0},{160,32},{192,64},{224,... | collective-permute-start | bytes 82952 | tf_op jit(solution)/shard_map/ppermute | solution.py:179
  (6 other events, 4.9 us)

commit v5 on v4

--- a/solution.py
+++ b/solution.py
@@ -9,8 +9,8 @@
 Z, Y, XH, C, MP = 8, 4, 2, 2, 2
 F = 128
 ROWS = 12
-VMEM_LIMIT = 20 * 2**20
-FIRST = 320
+VMEM_LIMIT = 40 * 2**20
+CUTS = (192,)
 bf16, f32 = jnp.bfloat16, jnp.float32
 NT = (((1,), (1,)), ((), ()))
 TN = (((0,), (0,)), ((), ()))
@@ -21,17 +21,22 @@
 
 
 def core_kernel(where_ref, t_ref, o_ref, *refs):
-    pieces = refs[:16]
-    give_ref, keep_ref, mine_ref, rest_ref, w_ref, s_ref, d_ref, g_ref = refs[16:]
+    blocks = refs[:16]
+    give_ref, keep_ref, mine_ref, rest_ref, w_ref, s_ref, d_ref, g_ref, pieces, sems = refs[16:]
+    copies = [pltpu.make_async_copy(blocks[i], pieces.at[i], sems.at[i]) for i in range(16)]
+    for copy in copies:
+        copy.start()
     z, y, c, m = (where_ref[i] for i in range(4))
     unit = XH * C * ROWS
+    for copy in copies:
+        copy.wait()
 
     @pl.loop(0, Z // 2)
     def _(t):
         for i in range(8):
             by, high = i // 2, i % 2
-            a = pieces[i][t].astype(f32)
-            b = pieces[i + 8][t].astype(f32)
+            a = pieces[i, t].astype(f32)
+            b = pieces[i + 8, t].astype(f32)
             first = jnp.where(c == 0, a, b)
             second = jnp.where(c == 0, b, a)
             rows = [first[:ROWS], second[:ROWS], first[ROWS:], second[ROWS:]]
@@ -116,13 +121,16 @@
             jax.ShapeDtypeStruct((Y, Z, XH * ROWS, n), bf16),
             jax.ShapeDtypeStruct((Y, Z, XH * ROWS, n), bf16),
         ),
-        in_specs=[pl.BlockSpec(memory_space=pltpu.SMEM)] + [vm] * 18,
+        in_specs=[pl.BlockSpec(memory_space=pltpu.SMEM), vm, vm]
+        + [pl.BlockSpec(memory_space=pl.ANY)] * 16,
         out_specs=(vm,) * 4,
         scratch_shapes=[
             pltpu.VMEM((width, n), bf16),
             pltpu.VMEM((4 * half // 128, rows, 128), f32),
             pltpu.VMEM((3 * half // 128, rows, 128), f32),
             pltpu.VMEM((rows, n), bf16),
+            pltpu.VMEM((16,) + mine[0].shape, bf16),
+            pltpu.SemaphoreType.DMA((16,)),
         ],
         compiler_params=pltpu.CompilerParams(vmem_limit_bytes=VMEM_LIMIT),
         cost_estimate=pl.CostEstimate(
@@ -194,7 +202,8 @@
     return [lax.ppermute(x, "c", PAIR) for x in xs]
 
 
-def reduce_weight(mine, rest, first, second, finish, to_frames):
+def reduce_weight(mine, rest, parts, finish, to_frames):
+    first, second = parts
     even = lax.axis_index("xh") == 0
     other = lax.ppermute(rest, "c", PAIR)
     first = lax.ppermute(first, "mp", PAIR)
@@ -248,29 +257,29 @@
     after_high = shift(high, "y", Y, Y - 1)
     before_high = shift(high, "y", Y, 1)
     after_low = shift(low, "y", Y, Y - 1)
+    far_low = shift(before_low, "y", Y, 1)
+    far_high = shift(after_high, "y", Y, Y - 1)
     tokens = tokens.reshape(F * count, cols + half)
     own = swapped(low, high)
-    before_low, after_high, tokens, own = lax.optimization_barrier(
-        (before_low, after_high, tokens, own)
-    )
-    far_low = shift(before_low, "y", Y, 1)
-    far_high = shift(after_high, "y", Y, Y - 1)
-    near = swapped(after_low, after_high, before_low, before_high)
-    far_low, far_high, near, others = lax.optimization_barrier((far_low, far_high, near, others))
+    near = [after_low, after_high, before_low, before_high]
+    near, own, tokens = lax.optimization_barrier((near, own, tokens))
+    near_rest = swapped(*near)
+    far = [far_low, far_high]
+    far, near_rest, others = lax.optimization_barrier((far, near_rest, others))
     others = others.reshape(F * count, cols)
-    mine = [low, high, after_low, after_high, far_low, far_high, before_low, before_high]
-    rest = own + near[:2] + swapped(far_low, far_high) + near[2:]
+    mine = [low, high] + near[:2] + far + near[2:]
+    rest = own + near_rest[:2] + swapped(*far) + near_rest[2:]
     give, keep, mine, rest = core(where, tokens, others, mine, rest)
-    first, second = give[:FIRST], give[FIRST:]
-
-    def finish(first, second):
-        got = jnp.concatenate([first, second], 0)
+    parts = jnp.split(give, CUTS)
+
+    def finish(*got):
+        got = jnp.concatenate(got, 0)
         return (keep.astype(f32) + got.astype(f32)).astype(bf16)
 
     def to_frames(x):
         return lax.all_to_all(x.reshape(F, count, cols), FR, 0, 0, tiled=True)
 
-    weight_grad, back = reduce_weight(mine, rest, first, second, finish, to_frames)
+    weight_grad, back = reduce_weight(mine, rest, parts, finish, to_frames)
     input_grad = back.reshape(frames_dev, patches, cols)
     weight_grad = weight_grad * (1.0 / F)
     return (input_grad, weight_grad.reshape(w_qkv.shape))

time: 196 us -> 206 us (1.051)
  waiting for transfers between devices: 83.6 us -> 98 us
  starting transfers between devices: 72.3 us -> 64 us
  local copies, waits for them, and re-layouts: 20 us -> 22.3 us
    ppermute x12, waiting for transfers between devices: 16.9 us -> 26.9 us  [shift(): return lax.ppermute(x, axis, [(i, (i + by) % size) for i in range(size)])]
    ppermute x1, waiting for transfers between devices: 0.01 us -> 6.94 us  [reduce_weight(): second = lax.ppermute(second, 'mp', PAIR)]
    ppermute x12, starting transfers between devices: 19.5 us -> 14.4 us  [shift(): return lax.ppermute(x, axis, [(i, (i + by) % size) for i in range(size)])]
    ppermute x1, waiting for transfers between devices: 3.97 us -> 0.01 us  [reduce_weight(): first = lax.ppermute(first, 'mp', PAIR)]
    unnamed x34 -> x38, local copies, waits for them, and re-layouts: 9.61 us -> 11.9 us
  transfers between devices with their start and end apart: 38 -> 38, of which waited for: 16 -> 17; matrix products, arithmetic and copies ran while one was open for 4% -> 3% of each run, Pallas kernels for 0% -> 0%
where the time goes in v5:
time: 206 us; the launch traced here: 204 us
  waiting for transfers between devices  98 us (48%)
  starting transfers between devices  64 us (31%)
  local copies, waits for them, and re-layouts  22.3 us (11%)
  Pallas kernels  18 us (9%)
    ppermute x12, waiting for transfers between devices, across(): return lax.ppermute(x, axis, [(i, i ^ by) for i in range(size)])  61 us
    ppermute x12, waiting for transfers between devices, shift(): return lax.ppermute(x, axis, [(i, (i + by) % size) for i in range(size)])  26.9 us
    ppermute x12, starting transfers between devices, across(): return lax.ppermute(x, axis, [(i, i ^ by) for i in range(size)])  23.3 us
    pallas_call x1, Pallas kernels, core(): pl.pallas_call(core_kernel, out_shape=(jax.ShapeDtypeStruct((rows, part_c...  17.6 us
    all_to_all x1, starting transfers between devices, on_device(): tokens = lax.all_to_all(tokens, FR, 0, 0, tiled=True)  15.5 us
    ppermute x12, starting transfers between devices, shift(): return lax.ppermute(x, axis, [(i, (i + by) % size) for i in range(size)])  14.4 us
    unnamed x38, local copies, waits for them, and re-layouts  11.9 us
    all_to_all x1, starting transfers between devices, to_frames(): return lax.all_to_all(x.reshape(F, count, cols), FR, 0, 0, tiled=True)  8.57 us
  transfers between devices with their start and end apart: 38, of which 17 were waited for; matrix products, arithmetic and copies ran while one was open for 3% of the time, Pallas kernels for 0%

profile of v5, /device:TPU:6, one launch (start us, length us, event | category | flops | bytes accessed | tf_op | source)
XLA Modules:
  0.0 204.3 jit_solution(17998847453092332217)
XLA Ops:
  0.7 0.9 pad.22
  1.6 2.0 collective-permute-start.1
  3.6 1.0 collective-permute-start.2
  4.6 2.1 %collective-permute-start = (bf16[12,1152]{1,0:T(8,128)(2,1)S(1)}, bf16[12,1152]{1,0:T(8,128)(2,1)S(1)}, u32[]{:S(2)}, u32[]{:S(2)}) collective-permute-start(bf16[12,1152]{1,0:T(8,128)(2,1)S(1)} %bitcast.28), channel_id=1, source_target_pairs={{0,4},{4,0},{32,36},{36,32},{64,68},{68,64},{96,100},{100,96},{128... | collective-permute-start | bytes 82952 | tf_op jit(solution)/shard_map/ppermute | solution.py:187
  6.9 1.2 reshape.28
  8.0 2.3 %collective-permute-done = bf16[12,1152]{1,0:T(8,128)(2,1)S(1)} collective-permute-done((bf16[12,1152]{1,0:T(8,128)(2,1)S(1)}, bf16[12,1152]{1,0:T(8,128)(2,1)S(1)}, u32[]{:S(2)}, u32[]{:S(2)}) %collective-permute-start) | collective-permute-done | bytes 27680 | tf_op jit(solution)/shard_map/ppermute | solution.py:187
  10.5 15.5 %all-to-all-start = ((bf16[128,4,1152]{2,1,0:T(4,128)(2,1)}), bf16[128,4,1152]{2,1,0:T(4,128)(2,1)}, u32[]{:S(2)}, u32[]{:S(2)}) async-start(bf16[128,4,1152]{2,1,0:T(4,128)(2,1)} %reshape.28), calls=%async_computation | async-start | bytes 2359296 | tf_op jit(solution)/shard_map/all_to_all | solution.py:250
  26.0 2.6 %collective-permute-start.3 = (bf16[2,24,1152]{2,1,0:T(8,128)(2,1)S(1)}, bf16[2,24,1152]{2,1,0:T(8,128)(2,1)S(1)}, u32[]{:S(2)}, u32[]{:S(2)}) collective-permute-start(bf16[2,24,1152]{2,1,0:T(8,128)(2,1)S(1)} %pad_maximum_fusion.4), channel_id=1, source_target_pairs={{0,64},{32,96},{64,0},{96,32},{128,192},{160,224},{192,128},{224,1... | collective-permute-start | bytes 331784 | tf_op jit(solution)/shard_map/ppermute | solution.py:187
  28.5 3.8 %collective-permute-start.5 = (bf16[2,24,1152]{2,1,0:T(8,128)(2,1)S(1)}, bf16[2,24,1152]{2,1,0:T(8,128)(2,1)S(1)}, u32[]{:S(2)}, u32[]{:S(2)}) collective-permute-start(bf16[2,24,1152]{2,1,0:T(8,128)(2,1)S(1)} %pad_maximum_fusion.4), channel_id=1, source_target_pairs={{0,192},{32,224},{64,128},{96,160},{128,64},{160,96},{192,0},{224,... | collective-permute-start | bytes 331784 | tf_op jit(solution)/shard_map/ppermute | solution.py:187
  32.6 27.9 %collective-permute-done.3 = bf16[2,24,1152]{2,1,0:T(8,128)(2,1)S(1)} collective-permute-done((bf16[2,24,1152]{2,1,0:T(8,128)(2,1)S(1)}, bf16[2,24,1152]{2,1,0:T(8,128)(2,1)S(1)}, u32[]{:S(2)}, u32[]{:S(2)}) %collective-permute-start.3) | collective-permute-done | bytes 110624 | tf_op jit(solution)/shard_map/ppermute | solution.py:187
  60.5 5.9 %collective-permute-done.4 = bf16[2,24,1152]{2,1,0:T(8,128)(2,1)S(1)} collective-permute-done((bf16[2,24,1152]{2,1,0:T(8,128)(2,1)S(1)}, bf16[2,24,1152]{2,1,0:T(8,128)(2,1)S(1)}, u32[]{:S(2)}, u32[]{:S(2)}) %collective-permute-start.4) | collective-permute-done | bytes 110624 | tf_op jit(solution)/shard_map/ppermute | solution.py:187
  66.4 2.4 %slice.60 = bf16[128,4,768]{2,1,0:T(4,128)(2,1)} slice(bf16[128,4,1152]{2,1,0:T(4,128)(2,1)} %all-to-all-done), slice={[0:128], [0:4], [0:768]} | slice | bytes 1572864 | tf_op jit(solution)/shard_map/slice | solution.py:253
  68.7 1.5 collective-permute-start.8
  70.5 1.8 collective-permute-start.6
  73.2 5.0 %collective-permute-done.8.refs_6_ = bf16[4,24,1152]{2,1,0:T(8,128)(2,1)S(1)} collective-permute-done((bf16[4,24,1152]{2,1,0:T(8,128)(2,1)S(1)}, bf16[4,24,1152]{2,1,0:T(8,128)(2,1)S(1)}, u32[]{:S(2)}, u32[]{:S(2)}) %collective-permute-start.8) | collective-permute-done | bytes 221216 | tf_op jit(solution)/shard_map/ppermute | solution.py:183
  78.2 1.4 collective-permute-start.7
  79.6 2.4 %reshape.30.t_ref = bf16[512,1152]{1,0:T(8,128)(2,1)S(1)} reshape(bf16[128,4,1152]{2,1,0:T(4,128)(2,1)} %all-to-all-done) | data formatting | bytes 2359296 | tf_op jit(solution)/shard_map/reshape | solution.py:262
  82.7 2.3 %collective-permute-done.7.refs_3_ = bf16[4,24,1152]{2,1,0:T(8,128)(2,1)} collective-permute-done((bf16[4,24,1152]{2,1,0:T(8,128)(2,1)S(1)}, bf16[4,24,1152]{2,1,0:T(8,128)(2,1)}, u32[]{:S(2)}, u32[]{:S(2)}) %collective-permute-start.7) | collective-permute-done | bytes 221216 | tf_op jit(solution)/shard_map/ppermute | solution.py:183
  85.5 4.4 %collective-permute-done.12.refs_4_ = bf16[4,24,1152]{2,1,0:T(8,128)(2,1)} collective-permute-done((bf16[4,24,1152]{2,1,0:T(8,128)(2,1)S(1)}, bf16[4,24,1152]{2,1,0:T(8,128)(2,1)}, u32[]{:S(2)}, u32[]{:S(2)}) %collective-permute-start.12) | collective-permute-done | bytes 221216 | tf_op jit(solution)/shard_map/ppermute | solution.py:183
  92.7 6.1 %collective-permute-done.13.refs_5_ = bf16[4,24,1152]{2,1,0:T(8,128)(2,1)} collective-permute-done((bf16[4,24,1152]{2,1,0:T(8,128)(2,1)}, bf16[4,24,1152]{2,1,0:T(8,128)(2,1)}, u32[]{:S(2)}, u32[]{:S(2)}) %collective-permute-start.13) | collective-permute-done | bytes 221216 | tf_op jit(solution)/shard_map/ppermute | solution.py:183
  99.3 1.6 reshape.31.o_ref
  100.9 0.9 copy-done.2
  101.9 0.9 copy-done.4
  102.8 0.9 copy-done.6
  103.7 0.9 copy-done.8
  104.7 0.9 copy-done.10
  105.6 0.9 copy-done.12
  106.5 0.9 copy-done.14
  107.5 0.9 copy-done.16
  108.4 17.6 %attention_core.1 = (bf16[512,768]{1,0:T(8,128)(2,1)S(1)}, bf16[512,768]{1,0:T(8,128)(2,1)S(1)}, bf16[4,8,24,1152]{3,2,1,0:T(8,128)(2,1)S(1)}, bf16[4,8,24,1152]{3,2,1,0:T(8,128)(2,1)S(1)}) custom-call(s32[4]{0:T(128)S(1)} %pad_add_fusion.where_ref, bf16[512,1152]{1,0:T(8,128)(2,1)S(1)} %reshape.30.t_ref, bf16[512,768]{1,0:T(8,128)(2,1)S(1)} %reshape.31.o_ref, ...), custom_call_target="tpu_custom_call" | custom-call | flops 5435817984 | bytes 8388608 | tf_op jit(solution)/shard_map/attention_core/pallas_call | solution.py:116
  126.7 3.1 %collective-permute-done.21.other_ref = bf16[4,8,24,1152]{3,2,1,0:T(8,128)(2,1)S(1)} collective-permute-done((bf16[4,8,24,1152]{3,2,1,0:T(8,128)(2,1)S(1)}, bf16[4,8,24,1152]{3,2,1,0:T(8,128)(2,1)S(1)}, u32[]{:S(2)}, u32[]{:S(2)}) %collective-permute-start.21) | collective-permute-done | bytes 1769504 | tf_op jit(solution)/shard_map/ppermute | solution.py:208
  130.3 3.2 %collective-permute-start.23 = (bf16[4,24,1152]{2,1,0:T(8,128)(2,1)S(1)}, bf16[4,24,1152]{2,1,0:T(8,128)(2,1)S(1)}, u32[]{:S(2)}, u32[]{:S(2)}) collective-permute-start(bf16[4,24,1152]{2,1,0:T(8,128)(2,1)S(1)} %get-tuple-element.62), channel_id=1, source_target_pairs={{0,24},{8,0},{16,8},{24,16},{1,25},{9,1},{17,9},{25,17},{2,26},{10... | collective-permute-start | bytes 663560 | tf_op jit(solution)/shard_map/ppermute | solution.py:183
  133.9 1.7 collective-permute-start.27
  135.7 4.1 %collective-permute-done.22 = bf16[4,24,1152]{2,1,0:T(8,128)(2,1)S(1)} collective-permute-done((bf16[4,24,1152]{2,1,0:T(8,128)(2,1)S(1)}, bf16[4,24,1152]{2,1,0:T(8,128)(2,1)S(1)}, u32[]{:S(2)}, u32[]{:S(2)}) %collective-permute-start.22) | collective-permute-done | bytes 221216 | tf_op jit(solution)/shard_map/ppermute | solution.py:183
  140.0 3.3 %collective-permute-start.28 = (bf16[4,24,1152]{2,1,0:T(8,128)(2,1)S(1)}, bf16[4,24,1152]{2,1,0:T(8,128)(2,1)S(1)}, u32[]{:S(2)}, u32[]{:S(2)}) collective-permute-start(bf16[4,24,1152]{2,1,0:T(8,128)(2,1)S(1)} %add_convert_fusion.1), channel_id=1, source_target_pairs={{0,24},{8,0},{16,8},{24,16},{1,25},{9,1},{17,9},{25,17},{2,26},{10... | collective-permute-start | bytes 663560 | tf_op jit(solution)/shard_map/ppermute | solution.py:183
  144.5 3.9 %collective-permute-done.25 = bf16[4,24,1152]{2,1,0:T(8,128)(2,1)S(1)} collective-permute-done((bf16[4,24,1152]{2,1,0:T(8,128)(2,1)S(1)}, bf16[4,24,1152]{2,1,0:T(8,128)(2,1)S(1)}, u32[]{:S(2)}, u32[]{:S(2)}) %collective-permute-start.25) | collective-permute-done | bytes 221216 | tf_op jit(solution)/shard_map/ppermute | solution.py:183
  149.6 3.2 %collective-permute-start.31 = (bf16[4,12,1152]{2,1,0:T(8,128)(2,1)S(1)}, bf16[4,12,1152]{2,1,0:T(8,128)(2,1)S(1)}, u32[]{:S(2)}, u32[]{:S(2)}) collective-permute-start(bf16[4,12,1152]{2,1,0:T(8,128)(2,1)S(1)} %get-tuple-element.79), channel_id=1, source_target_pairs={{0,36},{4,32},{32,4},{36,0},{64,100},{68,96},{96,68},{100,64},{128... | collective-permute-start | bytes 331784 | tf_op jit(solution)/shard_map/ppermute | solution.py:187
  152.7 1.2 collective-permute-start.29
  154.2 5.6 %collective-permute-done.30 = bf16[4,12,1152]{2,1,0:T(8,128)(2,1)S(1)} collective-permute-done((bf16[4,12,1152]{2,1,0:T(8,128)(2,1)S(1)}, bf16[4,12,1152]{2,1,0:T(8,128)(2,1)S(1)}, u32[]{:S(2)}, u32[]{:S(2)}) %collective-permute-start.30) | collective-permute-done | bytes 110624 | tf_op jit(solution)/shard_map/ppermute | solution.py:187
  159.9 6.9 %collective-permute-done.32 = bf16[320,768]{1,0:T(8,128)(2,1)S(1)} collective-permute-done((bf16[320,768]{1,0:T(8,128)(2,1)S(1)}, bf16[320,768]{1,0:T(8,128)(2,1)S(1)}, u32[]{:S(2)}, u32[]{:S(2)}) %collective-permute-start.32) | collective-permute-done | bytes 491552 | tf_op jit(solution)/shard_map/ppermute | solution.py:217
  167.0 1.1 reshape.32
  168.1 8.6 %all-to-all-start.1 = ((bf16[128,4,768]{2,1,0:T(4,128)(2,1)}), bf16[128,4,768]{2,1,0:T(4,128)(2,1)S(1)}, u32[]{:S(2)}, u32[]{:S(2)}) async-start(bf16[128,4,768]{2,1,0:T(4,128)(2,1)} %reshape.32), calls=%async_computation.1 | async-start | bytes 1572864 | tf_op jit(solution)/shard_map/all_to_all | solution.py:280
  176.7 2.6 %collective-permute-start.33 = (bf16[12,1152]{1,0:T(8,128)(2,1)S(1)}, bf16[12,1152]{1,0:T(8,128)(2,1)S(1)}, u32[]{:S(2)}, u32[]{:S(2)}) collective-permute-start(bf16[12,1152]{1,0:T(8,128)(2,1)S(1)} %get-tuple-element.80), channel_id=1, source_target_pairs={{0,64},{32,96},{64,0},{96,32},{128,192},{160,224},{192,128},{224,1... | collective-permute-start | bytes 82952 | tf_op jit(solution)/shard_map/ppermute | solution.py:187
  179.3 3.8 %collective-permute-start.35 = (bf16[12,1152]{1,0:T(8,128)(2,1)S(1)}, bf16[12,1152]{1,0:T(8,128)(2,1)S(1)}, u32[]{:S(2)}, u32[]{:S(2)}) collective-permute-start(bf16[12,1152]{1,0:T(8,128)(2,1)S(1)} %get-tuple-element.81), channel_id=1, source_target_pairs={{0,192},{32,224},{64,128},{96,160},{128,64},{160,96},{192,0},{224,... | collective-permute-start | bytes 82952 | tf_op jit(solution)/shard_map/ppermute | solution.py:187
  183.3 15.2 %collective-permute-done.33 = bf16[12,1152]{1,0:T(8,128)(2,1)S(1)} collective-permute-done((bf16[12,1152]{1,0:T(8,128)(2,1)S(1)}, bf16[12,1152]{1,0:T(8,128)(2,1)S(1)}, u32[]{:S(2)}, u32[]{:S(2)}) %collective-permute-start.33) | collective-permute-done | bytes 27680 | tf_op jit(solution)/shard_map/ppermute | solution.py:187
  198.4 1.3 collective-permute-done.35
  199.7 2.9 %collective-permute-done.34 = bf16[12,1152]{1,0:T(8,128)(2,1)S(1)} collective-permute-done((bf16[12,1152]{1,0:T(8,128)(2,1)S(1)}, bf16[12,1152]{1,0:T(8,128)(2,1)S(1)}, u32[]{:S(2)}, u32[]{:S(2)}) %collective-permute-start.34) | collective-permute-done | bytes 27680 | tf_op jit(solution)/shard_map/ppermute | solution.py:187
  203.3 1.1 reshape.33
  (98 shorter events, 11.8 us)
Async XLA Ops:
  0.6 6.1 %copy-start = (bf16[1,512,1536]{2,1,0:T(8,128)(2,1)S(1)}, bf16[1,512,1536]{2,1,0:T(8,128)(2,1)}, u32[]{:S(2)}) copy-start(bf16[1,512,1536]{2,1,0:T(8,128)(2,1)} %param.3) | copy-start | bytes 4718596
  0.6 6.1 %copy-start.17 = (bf16[1,512,384]{2,1,0:T(8,128)(2,1)S(1)}, bf16[1,512,384]{2,1,0:T(8,128)(2,1)}, u32[]{:S(2)}) copy-start(bf16[1,512,384]{2,1,0:T(8,128)(2,1)} %param.4) | copy-start | bytes 1179652
  1.6 8.8 %collective-permute-start.1 = (bf16[12,1152]{1,0:T(8,128)(2,1)S(1)}, bf16[12,1152]{1,0:T(8,128)(2,1)S(1)}, u32[]{:S(2)}, u32[]{:S(2)}) collective-permute-start(bf16[12,1152]{1,0:T(8,128)(2,1)S(1)} %bitcast.26), channel_id=1, source_target_pairs={{0,32},{4,36},{32,0},{36,4},{64,96},{68,100},{96,64},{100,68},{128... | collective-permute-start | bytes 82952 | tf_op jit(solution)/shard_map/ppermute | solution.py:187
  3.6 6.8 %collective-permute-start.2 = (bf16[12,1152]{1,0:T(8,128)(2,1)S(1)}, bf16[12,1152]{1,0:T(8,128)(2,1)S(1)}, u32[]{:S(2)}, u32[]{:S(2)}) collective-permute-start(bf16[12,1152]{1,0:T(8,128)(2,1)S(1)} %bitcast.27), channel_id=1, source_target_pairs={{0,36},{4,32},{32,4},{36,0},{64,100},{68,96},{96,68},{100,64},{128... | collective-permute-start | bytes 82952 | tf_op jit(solution)/shard_map/ppermute | solution.py:187
  4.6 5.8 %collective-permute-start = (bf16[12,1152]{1,0:T(8,128)(2,1)S(1)}, bf16[12,1152]{1,0:T(8,128)(2,1)S(1)}, u32[]{:S(2)}, u32[]{:S(2)}) collective-permute-start(bf16[12,1152]{1,0:T(8,128)(2,1)S(1)} %bitcast.28), channel_id=1, source_target_pairs={{0,4},{4,0},{32,36},{36,32},{64,68},{68,64},{96,100},{100,96},{128... | collective-permute-start | bytes 82952 | tf_op jit(solution)/shard_map/ppermute | solution.py:187
  10.5 55.9 %all-to-all-start = ((bf16[128,4,1152]{2,1,0:T(4,128)(2,1)}), bf16[128,4,1152]{2,1,0:T(4,128)(2,1)}, u32[]{:S(2)}, u32[]{:S(2)}) async-start(bf16[128,4,1152]{2,1,0:T(4,128)(2,1)} %reshape.28), calls=%async_computation | async-start | bytes 2359296 | tf_op jit(solution)/shard_map/all_to_all | solution.py:250
  26.0 34.5 %collective-permute-start.3 = (bf16[2,24,1152]{2,1,0:T(8,128)(2,1)S(1)}, bf16[2,24,1152]{2,1,0:T(8,128)(2,1)S(1)}, u32[]{:S(2)}, u32[]{:S(2)}) collective-permute-start(bf16[2,24,1152]{2,1,0:T(8,128)(2,1)S(1)} %pad_maximum_fusion.4), channel_id=1, source_target_pairs={{0,64},{32,96},{64,0},{96,32},{128,192},{160,224},{192,128},{224,1... | collective-permute-start | bytes 331784 | tf_op jit(solution)/shard_map/ppermute | solution.py:187
  28.5 31.9 %collective-permute-start.5 = (bf16[2,24,1152]{2,1,0:T(8,128)(2,1)S(1)}, bf16[2,24,1152]{2,1,0:T(8,128)(2,1)S(1)}, u32[]{:S(2)}, u32[]{:S(2)}) collective-permute-start(bf16[2,24,1152]{2,1,0:T(8,128)(2,1)S(1)} %pad_maximum_fusion.4), channel_id=1, source_target_pairs={{0,192},{32,224},{64,128},{96,160},{128,64},{160,96},{192,0},{224,... | collective-permute-start | bytes 331784 | tf_op jit(solution)/shard_map/ppermute | solution.py:187
  32.3 34.0 %collective-permute-start.4 = (bf16[2,24,1152]{2,1,0:T(8,128)(2,1)S(1)}, bf16[2,24,1152]{2,1,0:T(8,128)(2,1)S(1)}, u32[]{:S(2)}, u32[]{:S(2)}) collective-permute-start(bf16[2,24,1152]{2,1,0:T(8,128)(2,1)S(1)} %pad_maximum_fusion.4), channel_id=1, source_target_pairs={{0,128},{32,160},{64,192},{96,224},{128,0},{160,32},{192,64},{224,... | collective-permute-start | bytes 331784 | tf_op jit(solution)/shard_map/ppermute | solution.py:187
  60.5 21.5 %copy-start.1 = (bf16[4,24,1152]{2,1,0:T(8,128)(2,1)}, bf16[4,24,1152]{2,1,0:T(8,128)(2,1)S(1)}, u32[]{:S(2)}) copy-start(bf16[4,24,1152]{2,1,0:T(8,128)(2,1)S(1)} %pad_maximum_fusion.2.refs_0_) | copy-start | bytes 663556
  66.4 15.6 %copy-start.3 = (bf16[4,24,1152]{2,1,0:T(8,128)(2,1)}, bf16[4,24,1152]{2,1,0:T(8,128)(2,1)S(1)}, u32[]{:S(2)}) copy-start(bf16[4,24,1152]{2,1,0:T(8,128)(2,1)S(1)} %pad_maximum_fusion.3.refs_1_) | copy-start | bytes 663556
  68.7 3.5 %collective-permute-start.10 = (bf16[4,24,1152]{2,1,0:T(8,128)(2,1)S(1)}, bf16[4,24,1152]{2,1,0:T(8,128)(2,1)S(1)}, u32[]{:S(2)}, u32[]{:S(2)}) collective-permute-start(bf16[4,24,1152]{2,1,0:T(8,128)(2,1)S(1)} %pad_maximum_fusion.2.refs_0_), channel_id=1, source_target_pairs={{0,2},{2,0},{1,3},{3,1},{4,6},{6,4},{5,7},{7,5},{8,10},{10,8},{9,1... | collective-permute-start | bytes 663560 | tf_op jit(solution)/shard_map/ppermute | solution.py:202
  68.7 9.4 %collective-permute-start.8 = (bf16[4,24,1152]{2,1,0:T(8,128)(2,1)S(1)}, bf16[4,24,1152]{2,1,0:T(8,128)(2,1)S(1)}, u32[]{:S(2)}, u32[]{:S(2)}) collective-permute-start(bf16[4,24,1152]{2,1,0:T(8,128)(2,1)S(1)} %pad_maximum_fusion.2.refs_0_), channel_id=1, source_target_pairs={{0,8},{8,16},{16,24},{24,0},{1,9},{9,17},{17,25},{25,1},{2,10},{10... | collective-permute-start | bytes 663560 | tf_op jit(solution)/shard_map/ppermute | solution.py:183
  70.2 28.5 %collective-permute-start.18 = (bf16[128,4,768]{2,1,0:T(4,128)(2,1)}, bf16[128,4,768]{2,1,0:T(4,128)(2,1)}, u32[]{:S(2)}, u32[]{:S(2)}) collective-permute-start(bf16[128,4,768]{2,1,0:T(4,128)(2,1)} %slice.60), channel_id=1, source_target_pairs={{0,1},{1,0},{2,3},{3,2},{4,5},{5,4},{6,7},{7,6},{8,9},{9,8},{10,11... | collective-permute-start | bytes 2359304 | tf_op jit(solution)/shard_map/ppermute | solution.py:255
  70.5 11.5 %collective-permute-start.6 = (bf16[4,24,1152]{2,1,0:T(8,128)(2,1)S(1)}, bf16[4,24,1152]{2,1,0:T(8,128)(2,1)}, u32[]{:S(2)}, u32[]{:S(2)}) collective-permute-start(bf16[4,24,1152]{2,1,0:T(8,128)(2,1)S(1)} %pad_maximum_fusion.2.refs_0_), channel_id=1, source_target_pairs={{0,24},{8,0},{16,8},{24,16},{1,25},{9,1},{17,9},{25,17},{2,26},{10... | collective-permute-start | bytes 663560 | tf_op jit(solution)/shard_map/ppermute | solution.py:183
  72.3 10.4 %collective-permute-start.11 = (bf16[4,24,1152]{2,1,0:T(8,128)(2,1)S(1)}, bf16[4,24,1152]{2,1,0:T(8,128)(2,1)}, u32[]{:S(2)}, u32[]{:S(2)}) collective-permute-start(bf16[4,24,1152]{2,1,0:T(8,128)(2,1)S(1)} %pad_maximum_fusion.3.refs_1_), channel_id=1, source_target_pairs={{0,2},{2,0},{1,3},{3,1},{4,6},{6,4},{5,7},{7,5},{8,10},{10,8},{9,1... | collective-permute-start | bytes 663560 | tf_op jit(solution)/shard_map/ppermute | solution.py:202
  73.0 9.7 %collective-permute-start.9 = (bf16[4,24,1152]{2,1,0:T(8,128)(2,1)S(1)}, bf16[4,24,1152]{2,1,0:T(8,128)(2,1)}, u32[]{:S(2)}, u32[]{:S(2)}) collective-permute-start(bf16[4,24,1152]{2,1,0:T(8,128)(2,1)S(1)} %pad_maximum_fusion.3.refs_1_), channel_id=1, source_target_pairs={{0,8},{8,16},{16,24},{24,0},{1,9},{9,17},{17,25},{25,1},{2,10},{10... | collective-permute-start | bytes 663560 | tf_op jit(solution)/shard_map/ppermute | solution.py:183
  78.2 21.1 %copy-start.7 = (bf16[4,24,1152]{2,1,0:T(8,128)(2,1)}, bf16[4,24,1152]{2,1,0:T(8,128)(2,1)S(1)}, u32[]{:S(2)}) copy-start(bf16[4,24,1152]{2,1,0:T(8,128)(2,1)S(1)} %collective-permute-done.8.refs_6_) | copy-start | bytes 663556
  78.2 6.8 %collective-permute-start.7 = (bf16[4,24,1152]{2,1,0:T(8,128)(2,1)S(1)}, bf16[4,24,1152]{2,1,0:T(8,128)(2,1)}, u32[]{:S(2)}, u32[]{:S(2)}) collective-permute-start(bf16[4,24,1152]{2,1,0:T(8,128)(2,1)S(1)} %pad_maximum_fusion.3.refs_1_), channel_id=1, source_target_pairs={{0,24},{8,0},{16,8},{24,16},{1,25},{9,1},{17,9},{25,17},{2,26},{10... | collective-permute-start | bytes 663560 | tf_op jit(solution)/shard_map/ppermute | solution.py:183
  82.0 7.9 %collective-permute-start.12 = (bf16[4,24,1152]{2,1,0:T(8,128)(2,1)S(1)}, bf16[4,24,1152]{2,1,0:T(8,128)(2,1)}, u32[]{:S(2)}, u32[]{:S(2)}) collective-permute-start(bf16[4,24,1152]{2,1,0:T(8,128)(2,1)S(1)} %collective-permute-done.8.refs_6_), channel_id=1, source_target_pairs={{0,8},{8,16},{16,24},{24,0},{1,9},{9,17},{17,25},{25,1},{2,10},{10... | collective-permute-start | bytes 663560 | tf_op jit(solution)/shard_map/ppermute | solution.py:183
  85.0 4.9 %collective-permute-start.14 = (bf16[4,24,1152]{2,1,0:T(8,128)(2,1)}, bf16[4,24,1152]{2,1,0:T(8,128)(2,1)S(1)}, u32[]{:S(2)}, u32[]{:S(2)}) collective-permute-start(bf16[4,24,1152]{2,1,0:T(8,128)(2,1)} %collective-permute-done.6.refs_2_), channel_id=1, source_target_pairs={{0,2},{2,0},{1,3},{3,1},{4,6},{6,4},{5,7},{7,5},{8,10},{10,8},{9,1... | collective-permute-start | bytes 663560 | tf_op jit(solution)/shard_map/ppermute | solution.py:202
  85.0 5.6 %collective-permute-start.15 = (bf16[4,24,1152]{2,1,0:T(8,128)(2,1)}, bf16[4,24,1152]{2,1,0:T(8,128)(2,1)S(1)}, u32[]{:S(2)}, u32[]{:S(2)}) collective-permute-start(bf16[4,24,1152]{2,1,0:T(8,128)(2,1)} %collective-permute-done.7.refs_3_), channel_id=1, source_target_pairs={{0,2},{2,0},{1,3},{3,1},{4,6},{6,4},{5,7},{7,5},{8,10},{10,8},{9,1... | collective-permute-start | bytes 663560 | tf_op jit(solution)/shard_map/ppermute | solution.py:202
  85.5 5.8 %collective-permute-start.16 = (bf16[4,24,1152]{2,1,0:T(8,128)(2,1)S(1)}, bf16[4,24,1152]{2,1,0:T(8,128)(2,1)S(1)}, u32[]{:S(2)}, u32[]{:S(2)}) collective-permute-start(bf16[4,24,1152]{2,1,0:T(8,128)(2,1)S(1)} %collective-permute-done.8.refs_6_), channel_id=1, source_target_pairs={{0,2},{2,0},{1,3},{3,1},{4,6},{6,4},{5,7},{7,5},{8,10},{10,8},{9,1... | collective-permute-start | bytes 663560 | tf_op jit(solution)/shard_map/ppermute | solution.py:202
  89.9 2.1 %collective-permute-start.17 = (bf16[4,24,1152]{2,1,0:T(8,128)(2,1)}, bf16[4,24,1152]{2,1,0:T(8,128)(2,1)S(1)}, u32[]{:S(2)}, u32[]{:S(2)}) collective-permute-start(bf16[4,24,1152]{2,1,0:T(8,128)(2,1)} %collective-permute-done.9.refs_7_), channel_id=1, source_target_pairs={{0,2},{2,0},{1,3},{3,1},{4,6},{6,4},{5,7},{7,5},{8,10},{10,8},{9,1... | collective-permute-start | bytes 663560 | tf_op jit(solution)/shard_map/ppermute | solution.py:202
  90.6 8.2 %collective-permute-start.13 = (bf16[4,24,1152]{2,1,0:T(8,128)(2,1)}, bf16[4,24,1152]{2,1,0:T(8,128)(2,1)}, u32[]{:S(2)}, u32[]{:S(2)}) collective-permute-start(bf16[4,24,1152]{2,1,0:T(8,128)(2,1)} %collective-permute-done.7.refs_3_), channel_id=1, source_target_pairs={{0,24},{8,0},{16,8},{24,16},{1,25},{9,1},{17,9},{25,17},{2,26},{10... | collective-permute-start | bytes 663560 | tf_op jit(solution)/shard_map/ppermute | solution.py:183
  98.7 2.2 %collective-permute-start.19 = (bf16[4,24,1152]{2,1,0:T(8,128)(2,1)}, bf16[4,24,1152]{2,1,0:T(8,128)(2,1)}, u32[]{:S(2)}, u32[]{:S(2)}) collective-permute-start(bf16[4,24,1152]{2,1,0:T(8,128)(2,1)} %collective-permute-done.12.refs_4_), channel_id=1, source_target_pairs={{0,2},{2,0},{1,3},{3,1},{4,6},{6,4},{5,7},{7,5},{8,10},{10,8},{9,1... | collective-permute-start | bytes 663560 | tf_op jit(solution)/shard_map/ppermute | solution.py:202
  98.7 2.2 %collective-permute-start.20 = (bf16[4,24,1152]{2,1,0:T(8,128)(2,1)}, bf16[4,24,1152]{2,1,0:T(8,128)(2,1)}, u32[]{:S(2)}, u32[]{:S(2)}) collective-permute-start(bf16[4,24,1152]{2,1,0:T(8,128)(2,1)} %collective-permute-done.13.refs_5_), channel_id=1, source_target_pairs={{0,2},{2,0},{1,3},{3,1},{4,6},{6,4},{5,7},{7,5},{8,10},{10,8},{9,1... | collective-permute-start | bytes 663560 | tf_op jit(solution)/shard_map/ppermute | solution.py:202
  100.9 0.9 copy-start.2
  101.9 0.9 copy-start.4
  102.8 0.9 copy-start.6
  106.5 0.9 copy-start.14
  107.5 0.9 copy-start.16
  126.0 3.8 %collective-permute-start.21 = (bf16[4,8,24,1152]{3,2,1,0:T(8,128)(2,1)S(1)}, bf16[4,8,24,1152]{3,2,1,0:T(8,128)(2,1)S(1)}, u32[]{:S(2)}, u32[]{:S(2)}) collective-permute-start(bf16[4,8,24,1152]{3,2,1,0:T(8,128)(2,1)S(1)} %get-tuple-element.58), channel_id=1, source_target_pairs={{0,2},{2,0},{1,3},{3,1},{4,6},{6,4},{5,7},{7,5},{8,10},{10,8},{9,1... | collective-permute-start | bytes 5308424 | tf_op jit(solution)/shard_map/ppermute | solution.py:208
  126.3 9.4 %collective-permute-start.24 = (bf16[192,768]{1,0:T(8,128)(2,1)S(1)}, bf16[192,768]{1,0:T(8,128)(2,1)S(1)}, u32[]{:S(2)}, u32[]{:S(2)}) collective-permute-start(bf16[192,768]{1,0:T(8,128)(2,1)S(1)} %split.6), channel_id=1, source_target_pairs={{0,1},{1,0},{2,3},{3,2},{4,5},{5,4},{6,7},{7,6},{8,9},{9,8},{10,11... | collective-permute-start | bytes 884744 | tf_op jit(solution)/shard_map/ppermute | solution.py:209
  130.2 9.6 %collective-permute-start.22 = (bf16[4,24,1152]{2,1,0:T(8,128)(2,1)S(1)}, bf16[4,24,1152]{2,1,0:T(8,128)(2,1)S(1)}, u32[]{:S(2)}, u32[]{:S(2)}) collective-permute-start(bf16[4,24,1152]{2,1,0:T(8,128)(2,1)S(1)} %get-tuple-element.61), channel_id=1, source_target_pairs={{0,8},{8,16},{16,24},{24,0},{1,9},{9,17},{17,25},{25,1},{2,10},{10... | collective-permute-start | bytes 663560 | tf_op jit(solution)/shard_map/ppermute | solution.py:183
  130.3 9.5 %collective-permute-start.23 = (bf16[4,24,1152]{2,1,0:T(8,128)(2,1)S(1)}, bf16[4,24,1152]{2,1,0:T(8,128)(2,1)S(1)}, u32[]{:S(2)}, u32[]{:S(2)}) collective-permute-start(bf16[4,24,1152]{2,1,0:T(8,128)(2,1)S(1)} %get-tuple-element.62), channel_id=1, source_target_pairs={{0,24},{8,0},{16,8},{24,16},{1,25},{9,1},{17,9},{25,17},{2,26},{10... | collective-permute-start | bytes 663560 | tf_op jit(solution)/shard_map/ppermute | solution.py:183
  133.6 10.5 %collective-permute-start.26 = (bf16[4,24,1152]{2,1,0:T(8,128)(2,1)S(1)}, bf16[4,24,1152]{2,1,0:T(8,128)(2,1)S(1)}, u32[]{:S(2)}, u32[]{:S(2)}) collective-permute-start(bf16[4,24,1152]{2,1,0:T(8,128)(2,1)S(1)} %get-tuple-element.65), channel_id=1, source_target_pairs={{0,24},{8,0},{16,8},{24,16},{1,25},{9,1},{17,9},{25,17},{2,26},{10... | collective-permute-start | bytes 663560 | tf_op jit(solution)/shard_map/ppermute | solution.py:183
  133.9 10.6 %collective-permute-start.27 = (bf16[4,24,1152]{2,1,0:T(8,128)(2,1)S(1)}, bf16[4,24,1152]{2,1,0:T(8,128)(2,1)S(1)}, u32[]{:S(2)}, u32[]{:S(2)}) collective-permute-start(bf16[4,24,1152]{2,1,0:T(8,128)(2,1)S(1)} %get-tuple-element.66), channel_id=1, source_target_pairs={{0,8},{8,16},{16,24},{24,0},{1,9},{9,17},{17,25},{25,1},{2,10},{10... | collective-permute-start | bytes 663560 | tf_op jit(solution)/shard_map/ppermute | solution.py:183
  139.8 8.6 %collective-permute-start.25 = (bf16[4,24,1152]{2,1,0:T(8,128)(2,1)S(1)}, bf16[4,24,1152]{2,1,0:T(8,128)(2,1)S(1)}, u32[]{:S(2)}, u32[]{:S(2)}) collective-permute-start(bf16[4,24,1152]{2,1,0:T(8,128)(2,1)S(1)} %add_convert_fusion.2), channel_id=1, source_target_pairs={{0,8},{8,16},{16,24},{24,0},{1,9},{9,17},{17,25},{25,1},{2,10},{10... | collective-permute-start | bytes 663560 | tf_op jit(solution)/shard_map/ppermute | solution.py:183
  140.0 8.5 %collective-permute-start.28 = (bf16[4,24,1152]{2,1,0:T(8,128)(2,1)S(1)}, bf16[4,24,1152]{2,1,0:T(8,128)(2,1)S(1)}, u32[]{:S(2)}, u32[]{:S(2)}) collective-permute-start(bf16[4,24,1152]{2,1,0:T(8,128)(2,1)S(1)} %add_convert_fusion.1), channel_id=1, source_target_pairs={{0,24},{8,0},{16,8},{24,16},{1,25},{9,1},{17,9},{25,17},{2,26},{10... | collective-permute-start | bytes 663560 | tf_op jit(solution)/shard_map/ppermute | solution.py:183
  148.8 11.0 %collective-permute-start.30 = (bf16[4,12,1152]{2,1,0:T(8,128)(2,1)S(1)}, bf16[4,12,1152]{2,1,0:T(8,128)(2,1)S(1)}, u32[]{:S(2)}, u32[]{:S(2)}) collective-permute-start(bf16[4,12,1152]{2,1,0:T(8,128)(2,1)S(1)} %get-tuple-element.78), channel_id=1, source_target_pairs={{0,4},{4,0},{32,36},{36,32},{64,68},{68,64},{96,100},{100,96},{128... | collective-permute-start | bytes 331784 | tf_op jit(solution)/shard_map/ppermute | solution.py:187
  149.6 10.2 %collective-permute-start.31 = (bf16[4,12,1152]{2,1,0:T(8,128)(2,1)S(1)}, bf16[4,12,1152]{2,1,0:T(8,128)(2,1)S(1)}, u32[]{:S(2)}, u32[]{:S(2)}) collective-permute-start(bf16[4,12,1152]{2,1,0:T(8,128)(2,1)S(1)} %get-tuple-element.79), channel_id=1, source_target_pairs={{0,36},{4,32},{32,4},{36,0},{64,100},{68,96},{96,68},{100,64},{128... | collective-permute-start | bytes 331784 | tf_op jit(solution)/shard_map/ppermute | solution.py:187
  152.7 7.1 %collective-permute-start.29 = (bf16[4,12,1152]{2,1,0:T(8,128)(2,1)S(1)}, bf16[4,12,1152]{2,1,0:T(8,128)(2,1)S(1)}, u32[]{:S(2)}, u32[]{:S(2)}) collective-permute-start(bf16[4,12,1152]{2,1,0:T(8,128)(2,1)S(1)} %slice.53), channel_id=1, source_target_pairs={{0,32},{4,36},{32,0},{36,4},{64,96},{68,100},{96,64},{100,68},{128... | collective-permute-start | bytes 331784 | tf_op jit(solution)/shard_map/ppermute | solution.py:187
  153.9 12.9 %collective-permute-start.32 = (bf16[320,768]{1,0:T(8,128)(2,1)S(1)}, bf16[320,768]{1,0:T(8,128)(2,1)S(1)}, u32[]{:S(2)}, u32[]{:S(2)}) collective-permute-start(bf16[320,768]{1,0:T(8,128)(2,1)S(1)} %split.7), channel_id=1, source_target_pairs={{0,1},{1,0},{2,3},{3,2},{4,5},{5,4},{6,7},{7,6},{8,9},{9,8},{10,11... | collective-permute-start | bytes 1474568 | tf_op jit(solution)/shard_map/ppermute | solution.py:217
  168.1 35.2 %all-to-all-start.1 = ((bf16[128,4,768]{2,1,0:T(4,128)(2,1)}), bf16[128,4,768]{2,1,0:T(4,128)(2,1)S(1)}, u32[]{:S(2)}, u32[]{:S(2)}) async-start(bf16[128,4,768]{2,1,0:T(4,128)(2,1)} %reshape.32), calls=%async_computation.1 | async-start | bytes 1572864 | tf_op jit(solution)/shard_map/all_to_all | solution.py:280
  176.7 21.8 %collective-permute-start.33 = (bf16[12,1152]{1,0:T(8,128)(2,1)S(1)}, bf16[12,1152]{1,0:T(8,128)(2,1)S(1)}, u32[]{:S(2)}, u32[]{:S(2)}) collective-permute-start(bf16[12,1152]{1,0:T(8,128)(2,1)S(1)} %get-tuple-element.80), channel_id=1, source_target_pairs={{0,64},{32,96},{64,0},{96,32},{128,192},{160,224},{192,128},{224,1... | collective-permute-start | bytes 82952 | tf_op jit(solution)/shard_map/ppermute | solution.py:187
  179.3 20.5 %collective-permute-start.35 = (bf16[12,1152]{1,0:T(8,128)(2,1)S(1)}, bf16[12,1152]{1,0:T(8,128)(2,1)S(1)}, u32[]{:S(2)}, u32[]{:S(2)}) collective-permute-start(bf16[12,1152]{1,0:T(8,128)(2,1)S(1)} %get-tuple-element.81), channel_id=1, source_target_pairs={{0,192},{32,224},{64,128},{96,160},{128,64},{160,96},{192,0},{224,... | collective-permute-start | bytes 82952 | tf_op jit(solution)/shard_map/ppermute | solution.py:187
  183.1 19.5 %collective-permute-start.34 = (bf16[12,1152]{1,0:T(8,128)(2,1)S(1)}, bf16[12,1152]{1,0:T(8,128)(2,1)S(1)}, u32[]{:S(2)}, u32[]{:S(2)}) collective-permute-start(bf16[12,1152]{1,0:T(8,128)(2,1)S(1)} %get-tuple-element.82), channel_id=1, source_target_pairs={{0,128},{32,160},{64,192},{96,224},{128,0},{160,32},{192,64},{224,... | collective-permute-start | bytes 82952 | tf_op jit(solution)/shard_map/ppermute | solution.py:187
  (8 other events, 6.3 us)

commit v6 on v3

--- a/solution.py
+++ b/solution.py
@@ -218,16 +218,17 @@
     low = own[:h] + up_low.astype(f32) + down_low.astype(f32)
     high = own[h:] + up_high.astype(f32) + down_high.astype(f32)
     blocks = jnp.concatenate([low, high], 0)
-    kept = jnp.where(even, blocks[:, :ROWS], blocks[:, ROWS:])
-    sent = jnp.where(even, blocks[:, ROWS:], blocks[:, :ROWS])
-    total = kept[0::2]
-    for by, x in ((2, kept[1::2]), (1, sent[0::2]), (3, sent[1::2])):
-        total = total + across(x.astype(bf16), ZX, Z * XH, by).astype(f32)
+    pair = blocks[:2]
+    for i in range(1, h):
+        sent = blocks[2 * i : 2 * i + 2].astype(bf16)
+        pair = pair + across(sent, "z", Z, 2 * i).astype(f32)
     back = late(summed)
-    total, back = lax.optimization_barrier((total, back))
-    result = total[0]
-    for i in range(1, h):
-        result = result + across(total[i].astype(bf16), "z", Z, 2 * i).astype(f32)
+    pair, back = lax.optimization_barrier((pair, back))
+    kept = jnp.where(even, pair[:, :ROWS], pair[:, ROWS:])
+    sent = jnp.where(even, pair[:, ROWS:], pair[:, :ROWS])
+    result = kept[0]
+    for by, x in ((1, sent[0]), (3, sent[1]), (2, kept[1])):
+        result = result + across(x.astype(bf16), ZX, Z * XH, by).astype(f32)
     return result, back
 
 
@@ -243,7 +244,6 @@
     tokens = jnp.concatenate([part, out_grad], axis=2).reshape(F, count, cols + half)
 
     pair = over_xh_and_pair(w_qkv.reshape(w_qkv.shape[0], n))
-    tokens, pair = lax.optimization_barrier((tokens, pair))
     tokens = lax.all_to_all(tokens, FR, 0, 0, tiled=True)
     two, four, six = (across(pair, "z", Z, 2 * i) for i in range(1, Z // 2))
     low, high = jnp.concatenate([pair, two], 0), jnp.concatenate([four, six], 0)
@@ -253,6 +253,7 @@
     mine = over_y(low, high)
     others = others.reshape(F * count, cols)
     tokens = tokens.reshape(F * count, cols + half)
+    mine[2], mine[7], tokens = lax.optimization_barrier((mine[2], mine[7], tokens))
     rest = {i: lax.ppermute(mine[i], "c", PAIR) for i in (0, 1, 2, 3, 6, 7)}
     mine, others, tokens = lax.optimization_barrier((mine, others, tokens))
     rest.update({i: lax.ppermute(mine[i], "c", PAIR) for i in (4, 5)})

time: 187 us -> 192 us (1.027); the launches traced: 187 us -> 189 us
  starting transfers between devices: 69 us -> 75.3 us
  waiting for transfers between devices: 81.1 us -> 75.9 us
    ppermute x12, waiting for transfers between devices: 58.1 us -> 55 us  [across(): return lax.ppermute(x, axis, [(i, i ^ by) for i in range(size)])]
    all_to_all x1, starting transfers between devices: 10.8 us -> 13.6 us  [to_frames(): return lax.all_to_all(x.reshape(F, count, cols), FR, 0, 0, tiled=True)]
    unnamed x18 -> x20, local copies, waits for them, and re-layouts: 3.7 us -> 4.19 us
  transfers between devices with their start and end apart: 37 -> 37, of which waited for: 17 -> 16; matrix products, arithmetic and copies ran while one was open for 8% -> 7% of each run, Pallas kernels for 0% -> 0%
where the time goes in v6:
time: 192 us; the launch traced here: 189 us
  waiting for transfers between devices  75.9 us (40%)
  starting transfers between devices  75.3 us (39%)
  Pallas kernels  16.8 us (9%)
  local copies, waits for them, and re-layouts  15 us (8%)
  other arithmetic  5.56 us (3%)
    ppermute x12, waiting for transfers between devices, across(): return lax.ppermute(x, axis, [(i, i ^ by) for i in range(size)])  55 us
    ppermute x12, starting transfers between devices, across(): return lax.ppermute(x, axis, [(i, i ^ by) for i in range(size)])  23.4 us
    ppermute x12, starting transfers between devices, shift(): return lax.ppermute(x, axis, [(i, (i + by) % size) for i in range(size)])  18.5 us
    pallas_call x1, Pallas kernels, core(): pl.pallas_call(core_kernel, out_shape=(jax.ShapeDtypeStruct((rows, part_c...  16.4 us
    all_to_all x1, starting transfers between devices, on_device(): tokens = lax.all_to_all(tokens, FR, 0, 0, tiled=True)  15.5 us
    all_to_all x1, starting transfers between devices, to_frames(): return lax.all_to_all(x.reshape(F, count, cols), FR, 0, 0, tiled=True)  13.6 us
    ppermute x1, waiting for transfers between devices, on_device(): got = lax.ppermute(give, 'mp', PAIR)  10.3 us
    ppermute x12, waiting for transfers between devices, shift(): return lax.ppermute(x, axis, [(i, (i + by) % size) for i in range(size)])  5.31 us
  transfers between devices with their start and end apart: 37, of which 16 were waited for; matrix products, arithmetic and copies ran while one was open for 7% of the time, Pallas kernels for 0%

profile of v6, /device:TPU:6, one launch (start us, length us, event | category | flops | bytes accessed | tf_op | source)
XLA Modules:
  0.0 189.5 jit_solution(4019331612748898631)
XLA Ops:
  0.7 1.4 copy-done
  2.2 1.2 reshape.29
  3.4 15.5 %all-to-all-start = ((bf16[128,4,1152]{2,1,0:T(4,128)(2,1)}), bf16[128,4,1152]{2,1,0:T(4,128)(2,1)S(1)}, u32[]{:S(2)}, u32[]{:S(2)}) async-start(bf16[128,4,1152]{2,1,0:T(4,128)(2,1)} %reshape.29), calls=%async_computation | async-start | bytes 2359296 | tf_op jit(solution)/shard_map/all_to_all | solution.py:247
  19.0 1.0 collective-permute-start
  20.0 1.1 collective-permute-start.1
  21.2 3.0 %collective-permute-start.2 = (bf16[12,1152]{1,0:T(8,128)(2,1)S(1)}, bf16[12,1152]{1,0:T(8,128)(2,1)S(1)}, u32[]{:S(2)}, u32[]{:S(2)}) collective-permute-start(bf16[12,1152]{1,0:T(8,128)(2,1)S(1)} %bitcast.30), channel_id=1, source_target_pairs={{0,36},{4,32},{32,4},{36,0},{64,100},{68,96},{96,68},{100,64},{128... | collective-permute-start | bytes 82952 | tf_op jit(solution)/shard_map/ppermute | solution.py:178
  24.8 22.5 %collective-permute-done.1 = bf16[12,1152]{1,0:T(8,128)(2,1)S(1)} collective-permute-done((bf16[12,1152]{1,0:T(8,128)(2,1)S(1)}, bf16[12,1152]{1,0:T(8,128)(2,1)S(1)}, u32[]{:S(2)}, u32[]{:S(2)}) %collective-permute-start.1) | collective-permute-done | bytes 27680 | tf_op jit(solution)/shard_map/ppermute | solution.py:178
  47.9 1.6 collective-permute-start.3
  49.5 3.8 %collective-permute-start.5 = (bf16[2,24,1152]{2,1,0:T(8,128)(2,1)S(1)}, bf16[2,24,1152]{2,1,0:T(8,128)(2,1)S(1)}, u32[]{:S(2)}, u32[]{:S(2)}) collective-permute-start(bf16[2,24,1152]{2,1,0:T(8,128)(2,1)S(1)} %pad_maximum_fusion.3), channel_id=1, source_target_pairs={{0,192},{32,224},{64,128},{96,160},{128,64},{160,96},{192,0},{224,... | collective-permute-start | bytes 331784 | tf_op jit(solution)/shard_map/ppermute | solution.py:178
  53.3 1.2 collective-permute-start.4
  54.4 1.2 collective-permute-done.3
  56.4 6.3 %collective-permute-done.5 = bf16[2,24,1152]{2,1,0:T(8,128)(2,1)S(1)} collective-permute-done((bf16[2,24,1152]{2,1,0:T(8,128)(2,1)S(1)}, bf16[2,24,1152]{2,1,0:T(8,128)(2,1)S(1)}, u32[]{:S(2)}, u32[]{:S(2)}) %collective-permute-start.5) | collective-permute-done | bytes 110624 | tf_op jit(solution)/shard_map/ppermute | solution.py:178
  63.6 0.9 collective-permute-start.12
  64.5 2.0 %collective-permute-start.9 = (bf16[4,24,1152]{2,1,0:T(8,128)(2,1)}, bf16[4,24,1152]{2,1,0:T(8,128)(2,1)}, u32[]{:S(2)}, u32[]{:S(2)}) collective-permute-start(bf16[4,24,1152]{2,1,0:T(8,128)(2,1)} %pad_maximum_fusion.1.refs_0_), channel_id=1, source_target_pairs={{0,8},{8,16},{16,24},{24,0},{1,9},{9,17},{17,25},{25,1},{2,10},{10... | collective-permute-start | bytes 663560 | tf_op jit(solution)/shard_map/ppermute | solution.py:174
  66.5 1.3 collective-permute-start.8
  67.8 1.9 collective-permute-start.6
  69.8 3.1 %collective-permute-done.9.refs_6_ = bf16[4,24,1152]{2,1,0:T(8,128)(2,1)} collective-permute-done((bf16[4,24,1152]{2,1,0:T(8,128)(2,1)}, bf16[4,24,1152]{2,1,0:T(8,128)(2,1)}, u32[]{:S(2)}, u32[]{:S(2)}) %collective-permute-start.9) | collective-permute-done | bytes 221216 | tf_op jit(solution)/shard_map/ppermute | solution.py:174
  72.9 2.2 %collective-permute-start.10 = (bf16[4,24,1152]{2,1,0:T(8,128)(2,1)}, bf16[4,24,1152]{2,1,0:T(8,128)(2,1)}, u32[]{:S(2)}, u32[]{:S(2)}) collective-permute-start(bf16[4,24,1152]{2,1,0:T(8,128)(2,1)} %collective-permute-done.9.refs_6_), channel_id=1, source_target_pairs={{0,8},{8,16},{16,24},{24,0},{1,9},{9,17},{17,25},{25,1},{2,10},{10... | collective-permute-start | bytes 663560 | tf_op jit(solution)/shard_map/ppermute | solution.py:174
  75.2 2.2 %collective-permute-start.11 = (bf16[4,24,1152]{2,1,0:T(8,128)(2,1)}, bf16[4,24,1152]{2,1,0:T(8,128)(2,1)}, u32[]{:S(2)}, u32[]{:S(2)}) collective-permute-start(bf16[4,24,1152]{2,1,0:T(8,128)(2,1)} %collective-permute-done.8.refs_3_), channel_id=1, source_target_pairs={{0,24},{8,0},{16,8},{24,16},{1,25},{9,1},{17,9},{25,17},{2,26},{10... | collective-permute-start | bytes 663560 | tf_op jit(solution)/shard_map/ppermute | solution.py:174
  77.4 2.1 %collective-permute-done.6.refs_2_ = bf16[4,24,1152]{2,1,0:T(8,128)(2,1)S(1)} collective-permute-done((bf16[4,24,1152]{2,1,0:T(8,128)(2,1)}, bf16[4,24,1152]{2,1,0:T(8,128)(2,1)S(1)}, u32[]{:S(2)}, u32[]{:S(2)}) %collective-permute-start.6) | collective-permute-done | bytes 221216 | tf_op jit(solution)/shard_map/ppermute | solution.py:174
  80.0 1.1 collective-permute-done.12
  81.2 0.9 copy-done.6
  82.0 2.4 %reshape.30.t_ref = bf16[512,1152]{1,0:T(8,128)(2,1)S(1)} reshape(bf16[128,4,1152]{2,1,0:T(4,128)(2,1)} %copy-done.5) | data formatting | bytes 2359296 | tf_op jit(solution)/shard_map/reshape | solution.py:255
  84.4 1.6 reshape.31.o_ref
  87.7 1.0 collective-permute-done.16.refs_11_
  89.4 0.9 copy-done.2
  90.3 0.9 copy-done.4
  91.2 16.4 %attention_core.1 = (bf16[512,768]{1,0:T(8,128)(2,1)S(1)}, bf16[512,768]{1,0:T(8,128)(2,1)S(1)}, bf16[4,8,24,1152]{3,2,1,0:T(8,128)(2,1)S(1)}, bf16[4,8,24,1152]{3,2,1,0:T(8,128)(2,1)S(1)}) custom-call(s32[4]{0:T(128)S(1)} %pad_add_fusion.where_ref, bf16[512,1152]{1,0:T(8,128)(2,1)S(1)} %reshape.30.t_ref, bf16[512,768]{1,0:T(8,128)(2,1)S(1)} %reshape.31.o_ref, ...), custom_call_target="tpu_custom_call" | custom-call | flops 5435817984 | bytes 8388608 | tf_op jit(solution)/shard_map/attention_core/pallas_call | solution.py:110
  108.0 0.8 collective-permute-start.24
  108.9 2.5 %collective-permute-done.21.other_ref = bf16[4,8,24,1152]{3,2,1,0:T(8,128)(2,1)S(1)} collective-permute-done((bf16[4,8,24,1152]{3,2,1,0:T(8,128)(2,1)S(1)}, bf16[4,8,24,1152]{3,2,1,0:T(8,128)(2,1)S(1)}, u32[]{:S(2)}, u32[]{:S(2)}) %collective-permute-start.21) | collective-permute-done | bytes 1769504 | tf_op jit(solution)/shard_map/ppermute | solution.py:204
  111.8 2.5 %collective-permute-start.22 = (bf16[4,24,1152]{2,1,0:T(8,128)(2,1)S(1)}, bf16[4,24,1152]{2,1,0:T(8,128)(2,1)S(1)}, u32[]{:S(2)}, u32[]{:S(2)}) collective-permute-start(bf16[4,24,1152]{2,1,0:T(8,128)(2,1)S(1)} %get-tuple-element.57), channel_id=1, source_target_pairs={{0,8},{8,16},{16,24},{24,0},{1,9},{9,17},{17,25},{25,1},{2,10},{10... | collective-permute-start | bytes 663560 | tf_op jit(solution)/shard_map/ppermute | solution.py:174
  114.3 1.1 collective-permute-start.23
  115.4 2.0 %collective-permute-start.26 = (bf16[4,24,1152]{2,1,0:T(8,128)(2,1)S(1)}, bf16[4,24,1152]{2,1,0:T(8,128)(2,1)S(1)}, u32[]{:S(2)}, u32[]{:S(2)}) collective-permute-start(bf16[4,24,1152]{2,1,0:T(8,128)(2,1)S(1)} %get-tuple-element.66), channel_id=1, source_target_pairs={{0,24},{8,0},{16,8},{24,16},{1,25},{9,1},{17,9},{25,17},{2,26},{10... | collective-permute-start | bytes 663560 | tf_op jit(solution)/shard_map/ppermute | solution.py:174
  117.4 10.3 %collective-permute-done.24 = bf16[512,768]{1,0:T(8,128)(2,1)S(1)} collective-permute-done((bf16[512,768]{1,0:T(8,128)(2,1)S(1)}, bf16[512,768]{1,0:T(8,128)(2,1)S(1)}, u32[]{:S(2)}, u32[]{:S(2)}) %collective-permute-start.24) | collective-permute-done | bytes 786464 | tf_op jit(solution)/shard_map/ppermute | solution.py:263
  127.7 1.1 add_convert_fusion
  128.8 0.7 add_convert_fusion.3
  129.5 0.7 add_convert_fusion.2
  130.2 2.4 %collective-permute-start.25 = (bf16[4,24,1152]{2,1,0:T(8,128)(2,1)}, bf16[4,24,1152]{2,1,0:T(8,128)(2,1)}, u32[]{:S(2)}, u32[]{:S(2)}) collective-permute-start(bf16[4,24,1152]{2,1,0:T(8,128)(2,1)} %add_convert_fusion.3), channel_id=1, source_target_pairs={{0,8},{8,16},{16,24},{24,0},{1,9},{9,17},{17,25},{25,1},{2,10},{10... | collective-permute-start | bytes 663560 | tf_op jit(solution)/shard_map/ppermute | solution.py:174
  132.7 0.8 collective-permute-start.29
  133.5 2.4 %reshape.32 = bf16[128,4,768]{2,1,0:T(4,128)(2,1)} reshape(bf16[512,768]{1,0:T(8,128)(2,1)} %add_convert_fusion) | data formatting | bytes 1572864 | tf_op jit(solution)/shard_map/reshape | solution.py:269
  135.8 13.6 %all-to-all-start.1 = ((bf16[128,4,768]{2,1,0:T(4,128)(2,1)}), bf16[128,4,768]{2,1,0:T(4,128)(2,1)}, u32[]{:S(2)}, u32[]{:S(2)}) async-start(bf16[128,4,768]{2,1,0:T(4,128)(2,1)} %reshape.32), calls=%async_computation.1 | async-start | bytes 1572864 | tf_op jit(solution)/shard_map/all_to_all | solution.py:269
  149.5 1.2 add_convert_fusion.1
  150.7 2.6 %collective-permute-start.27 = (bf16[2,24,1152]{2,1,0:T(8,128)(2,1)S(1)}, bf16[2,24,1152]{2,1,0:T(8,128)(2,1)S(1)}, u32[]{:S(2)}, u32[]{:S(2)}) collective-permute-start(bf16[2,24,1152]{2,1,0:T(8,128)(2,1)S(1)} %slice.95), channel_id=1, source_target_pairs={{0,64},{32,96},{64,0},{96,32},{128,192},{160,224},{192,128},{224,1... | collective-permute-start | bytes 331784 | tf_op jit(solution)/shard_map/ppermute | solution.py:178
  153.3 4.1 %collective-permute-start.30 = (bf16[2,24,1152]{2,1,0:T(8,128)(2,1)S(1)}, bf16[2,24,1152]{2,1,0:T(8,128)(2,1)S(1)}, u32[]{:S(2)}, u32[]{:S(2)}) collective-permute-start(bf16[2,24,1152]{2,1,0:T(8,128)(2,1)S(1)} %get-tuple-element.74), channel_id=1, source_target_pairs={{0,128},{32,160},{64,192},{96,224},{128,0},{160,32},{192,64},{224,... | collective-permute-start | bytes 331784 | tf_op jit(solution)/shard_map/ppermute | solution.py:178
  157.4 18.2 %collective-permute-done.27 = bf16[2,24,1152]{2,1,0:T(8,128)(2,1)S(1)} collective-permute-done((bf16[2,24,1152]{2,1,0:T(8,128)(2,1)S(1)}, bf16[2,24,1152]{2,1,0:T(8,128)(2,1)S(1)}, u32[]{:S(2)}, u32[]{:S(2)}) %collective-permute-start.27) | collective-permute-done | bytes 110624 | tf_op jit(solution)/shard_map/ppermute | solution.py:178
  175.6 5.6 %collective-permute-done.30 = bf16[2,24,1152]{2,1,0:T(8,128)(2,1)S(1)} collective-permute-done((bf16[2,24,1152]{2,1,0:T(8,128)(2,1)S(1)}, bf16[2,24,1152]{2,1,0:T(8,128)(2,1)S(1)}, u32[]{:S(2)}, u32[]{:S(2)}) %collective-permute-start.30) | collective-permute-done | bytes 110624 | tf_op jit(solution)/shard_map/ppermute | solution.py:178
  182.2 4.4 %collective-permute-start.33 = (bf16[12,1152]{1,0:T(8,128)(2,1)S(1)}, bf16[12,1152]{1,0:T(8,128)(2,1)S(1)}, u32[]{:S(2)}, u32[]{:S(2)}) collective-permute-start(bf16[12,1152]{1,0:T(8,128)(2,1)S(1)} %get-tuple-element.77), channel_id=1, source_target_pairs={{0,36},{4,32},{32,4},{36,0},{64,100},{68,96},{96,68},{100,64},{128... | collective-permute-start | bytes 82952 | tf_op jit(solution)/shard_map/ppermute | solution.py:178
  186.5 2.3 %reshape.33 = bf16[1,512,768]{2,1,0:T(8,128)(2,1)} reshape(bf16[128,4,768]{2,1,0:T(4,128)(2,1)} %all-to-all-done.1) | data formatting | bytes 1572864 | tf_op jit(solution)/shard_map/reshape | solution.py:272
  (76 shorter events, 8.6 us)
Async XLA Ops:
  0.6 1.4 copy-start
  0.6 1.5 copy-start.7
  3.4 15.5 %copy-start.8 = (bf16[12,3,384]{2,1,0:T(4,128)(2,1)S(1)}, bf16[12,3,384]{2,1,0:T(4,128)(2,1)}, u32[]{:S(2)}) copy-start(bf16[12,3,384]{2,1,0:T(4,128)(2,1)} %param.5) | copy-start | bytes 82948
  3.4 59.9 %all-to-all-start = ((bf16[128,4,1152]{2,1,0:T(4,128)(2,1)}), bf16[128,4,1152]{2,1,0:T(4,128)(2,1)S(1)}, u32[]{:S(2)}, u32[]{:S(2)}) async-start(bf16[128,4,1152]{2,1,0:T(4,128)(2,1)} %reshape.29), calls=%async_computation | async-start | bytes 2359296 | tf_op jit(solution)/shard_map/all_to_all | solution.py:247
  19.0 5.7 %collective-permute-start = (bf16[12,1152]{1,0:T(8,128)(2,1)S(1)}, bf16[12,1152]{1,0:T(8,128)(2,1)S(1)}, u32[]{:S(2)}, u32[]{:S(2)}) collective-permute-start(bf16[12,1152]{1,0:T(8,128)(2,1)S(1)} %bitcast.28), channel_id=1, source_target_pairs={{0,4},{4,0},{32,36},{36,32},{64,68},{68,64},{96,100},{100,96},{128... | collective-permute-start | bytes 82952 | tf_op jit(solution)/shard_map/ppermute | solution.py:178
  20.0 27.2 %collective-permute-start.1 = (bf16[12,1152]{1,0:T(8,128)(2,1)S(1)}, bf16[12,1152]{1,0:T(8,128)(2,1)S(1)}, u32[]{:S(2)}, u32[]{:S(2)}) collective-permute-start(bf16[12,1152]{1,0:T(8,128)(2,1)S(1)} %bitcast.29), channel_id=1, source_target_pairs={{0,32},{4,36},{32,0},{36,4},{64,96},{68,100},{96,64},{100,68},{128... | collective-permute-start | bytes 82952 | tf_op jit(solution)/shard_map/ppermute | solution.py:178
  21.2 26.6 %collective-permute-start.2 = (bf16[12,1152]{1,0:T(8,128)(2,1)S(1)}, bf16[12,1152]{1,0:T(8,128)(2,1)S(1)}, u32[]{:S(2)}, u32[]{:S(2)}) collective-permute-start(bf16[12,1152]{1,0:T(8,128)(2,1)S(1)} %bitcast.30), channel_id=1, source_target_pairs={{0,36},{4,32},{32,4},{36,0},{64,100},{68,96},{96,68},{100,64},{128... | collective-permute-start | bytes 82952 | tf_op jit(solution)/shard_map/ppermute | solution.py:178
  47.9 7.8 %collective-permute-start.3 = (bf16[2,24,1152]{2,1,0:T(8,128)(2,1)S(1)}, bf16[2,24,1152]{2,1,0:T(8,128)(2,1)S(1)}, u32[]{:S(2)}, u32[]{:S(2)}) collective-permute-start(bf16[2,24,1152]{2,1,0:T(8,128)(2,1)S(1)} %pad_maximum_fusion.3), channel_id=1, source_target_pairs={{0,64},{32,96},{64,0},{96,32},{128,192},{160,224},{192,128},{224,1... | collective-permute-start | bytes 331784 | tf_op jit(solution)/shard_map/ppermute | solution.py:178
  49.5 13.1 %collective-permute-start.5 = (bf16[2,24,1152]{2,1,0:T(8,128)(2,1)S(1)}, bf16[2,24,1152]{2,1,0:T(8,128)(2,1)S(1)}, u32[]{:S(2)}, u32[]{:S(2)}) collective-permute-start(bf16[2,24,1152]{2,1,0:T(8,128)(2,1)S(1)} %pad_maximum_fusion.3), channel_id=1, source_target_pairs={{0,192},{32,224},{64,128},{96,160},{128,64},{160,96},{192,0},{224,... | collective-permute-start | bytes 331784 | tf_op jit(solution)/shard_map/ppermute | solution.py:178
  53.3 9.4 %collective-permute-start.4 = (bf16[2,24,1152]{2,1,0:T(8,128)(2,1)S(1)}, bf16[2,24,1152]{2,1,0:T(8,128)(2,1)S(1)}, u32[]{:S(2)}, u32[]{:S(2)}) collective-permute-start(bf16[2,24,1152]{2,1,0:T(8,128)(2,1)S(1)} %pad_maximum_fusion.3), channel_id=1, source_target_pairs={{0,128},{32,160},{64,192},{96,224},{128,0},{160,32},{192,64},{224,... | collective-permute-start | bytes 331784 | tf_op jit(solution)/shard_map/ppermute | solution.py:178
  63.3 17.8 %copy-start.5 = (bf16[128,4,1152]{2,1,0:T(4,128)(2,1)}, bf16[128,4,1152]{2,1,0:T(4,128)(2,1)S(1)}, u32[]{:S(2)}) copy-start(bf16[128,4,1152]{2,1,0:T(4,128)(2,1)S(1)} %all-to-all-done) | copy-start | bytes 3538948
  63.6 17.5 %collective-permute-start.12 = (bf16[128,4,768]{2,1,0:T(4,128)(2,1)S(1)}, bf16[128,4,768]{2,1,0:T(4,128)(2,1)S(1)}, u32[]{:S(2)}, u32[]{:S(2)}) collective-permute-start(bf16[128,4,768]{2,1,0:T(4,128)(2,1)S(1)} %slice.60), channel_id=1, source_target_pairs={{0,1},{1,0},{2,3},{3,2},{4,5},{5,4},{6,7},{7,6},{8,9},{9,8},{10,11... | collective-permute-start | bytes 2359304 | tf_op jit(solution)/shard_map/ppermute | solution.py:252
  64.5 8.4 %collective-permute-start.9 = (bf16[4,24,1152]{2,1,0:T(8,128)(2,1)}, bf16[4,24,1152]{2,1,0:T(8,128)(2,1)}, u32[]{:S(2)}, u32[]{:S(2)}) collective-permute-start(bf16[4,24,1152]{2,1,0:T(8,128)(2,1)} %pad_maximum_fusion.1.refs_0_), channel_id=1, source_target_pairs={{0,8},{8,16},{16,24},{24,0},{1,9},{9,17},{17,25},{25,1},{2,10},{10... | collective-permute-start | bytes 663560 | tf_op jit(solution)/shard_map/ppermute | solution.py:174
  66.5 8.7 %collective-permute-start.8 = (bf16[4,24,1152]{2,1,0:T(8,128)(2,1)}, bf16[4,24,1152]{2,1,0:T(8,128)(2,1)}, u32[]{:S(2)}, u32[]{:S(2)}) collective-permute-start(bf16[4,24,1152]{2,1,0:T(8,128)(2,1)} %pad_maximum_fusion.2.refs_1_), channel_id=1, source_target_pairs={{0,24},{8,0},{16,8},{24,16},{1,25},{9,1},{17,9},{25,17},{2,26},{10... | collective-permute-start | bytes 663560 | tf_op jit(solution)/shard_map/ppermute | solution.py:174
  67.8 11.7 %collective-permute-start.6 = (bf16[4,24,1152]{2,1,0:T(8,128)(2,1)}, bf16[4,24,1152]{2,1,0:T(8,128)(2,1)S(1)}, u32[]{:S(2)}, u32[]{:S(2)}) collective-permute-start(bf16[4,24,1152]{2,1,0:T(8,128)(2,1)} %pad_maximum_fusion.1.refs_0_), channel_id=1, source_target_pairs={{0,24},{8,0},{16,8},{24,16},{1,25},{9,1},{17,9},{25,17},{2,26},{10... | collective-permute-start | bytes 663560 | tf_op jit(solution)/shard_map/ppermute | solution.py:174
  69.6 9.9 %collective-permute-start.7 = (bf16[4,24,1152]{2,1,0:T(8,128)(2,1)}, bf16[4,24,1152]{2,1,0:T(8,128)(2,1)S(1)}, u32[]{:S(2)}, u32[]{:S(2)}) collective-permute-start(bf16[4,24,1152]{2,1,0:T(8,128)(2,1)} %pad_maximum_fusion.2.refs_1_), channel_id=1, source_target_pairs={{0,8},{8,16},{16,24},{24,0},{1,9},{9,17},{17,25},{25,1},{2,10},{10... | collective-permute-start | bytes 663560 | tf_op jit(solution)/shard_map/ppermute | solution.py:174
  72.9 13.1 %collective-permute-start.10 = (bf16[4,24,1152]{2,1,0:T(8,128)(2,1)}, bf16[4,24,1152]{2,1,0:T(8,128)(2,1)}, u32[]{:S(2)}, u32[]{:S(2)}) collective-permute-start(bf16[4,24,1152]{2,1,0:T(8,128)(2,1)} %collective-permute-done.9.refs_6_), channel_id=1, source_target_pairs={{0,8},{8,16},{16,24},{24,0},{1,9},{9,17},{17,25},{25,1},{2,10},{10... | collective-permute-start | bytes 663560 | tf_op jit(solution)/shard_map/ppermute | solution.py:174
  75.2 11.4 %collective-permute-start.11 = (bf16[4,24,1152]{2,1,0:T(8,128)(2,1)}, bf16[4,24,1152]{2,1,0:T(8,128)(2,1)}, u32[]{:S(2)}, u32[]{:S(2)}) collective-permute-start(bf16[4,24,1152]{2,1,0:T(8,128)(2,1)} %collective-permute-done.8.refs_3_), channel_id=1, source_target_pairs={{0,24},{8,0},{16,8},{24,16},{1,25},{9,1},{17,9},{25,17},{2,26},{10... | collective-permute-start | bytes 663560 | tf_op jit(solution)/shard_map/ppermute | solution.py:174
  79.5 1.7 copy-start.1
  79.5 7.2 %collective-permute-start.13 = (bf16[4,24,1152]{2,1,0:T(8,128)(2,1)}, bf16[4,24,1152]{2,1,0:T(8,128)(2,1)}, u32[]{:S(2)}, u32[]{:S(2)}) collective-permute-start(bf16[4,24,1152]{2,1,0:T(8,128)(2,1)} %pad_maximum_fusion.1.refs_0_), channel_id=1, source_target_pairs={{0,2},{2,0},{1,3},{3,1},{4,6},{6,4},{5,7},{7,5},{8,10},{10,8},{9,1... | collective-permute-start | bytes 663560 | tf_op jit(solution)/shard_map/ppermute | solution.py:257
  79.5 1.7 copy-start.3
  79.5 7.6 %collective-permute-start.14 = (bf16[4,24,1152]{2,1,0:T(8,128)(2,1)}, bf16[4,24,1152]{2,1,0:T(8,128)(2,1)}, u32[]{:S(2)}, u32[]{:S(2)}) collective-permute-start(bf16[4,24,1152]{2,1,0:T(8,128)(2,1)} %pad_maximum_fusion.2.refs_1_), channel_id=1, source_target_pairs={{0,2},{2,0},{1,3},{3,1},{4,6},{6,4},{5,7},{7,5},{8,10},{10,8},{9,1... | collective-permute-start | bytes 663560 | tf_op jit(solution)/shard_map/ppermute | solution.py:257
  81.2 0.9 copy-start.6
  82.0 5.2 %collective-permute-start.19 = (bf16[4,24,1152]{2,1,0:T(8,128)(2,1)}, bf16[4,24,1152]{2,1,0:T(8,128)(2,1)}, u32[]{:S(2)}, u32[]{:S(2)}) collective-permute-start(bf16[4,24,1152]{2,1,0:T(8,128)(2,1)} %collective-permute-done.9.refs_6_), channel_id=1, source_target_pairs={{0,2},{2,0},{1,3},{3,1},{4,6},{6,4},{5,7},{7,5},{8,10},{10,8},{9,1... | collective-permute-start | bytes 663560 | tf_op jit(solution)/shard_map/ppermute | solution.py:257
  86.0 2.7 %collective-permute-start.15 = (bf16[4,24,1152]{2,1,0:T(8,128)(2,1)}, bf16[4,24,1152]{2,1,0:T(8,128)(2,1)}, u32[]{:S(2)}, u32[]{:S(2)}) collective-permute-start(bf16[4,24,1152]{2,1,0:T(8,128)(2,1)} %copy-done.1), channel_id=1, source_target_pairs={{0,2},{2,0},{1,3},{3,1},{4,6},{6,4},{5,7},{7,5},{8,10},{10,8},{9,1... | collective-permute-start | bytes 663560 | tf_op jit(solution)/shard_map/ppermute | solution.py:257
  86.6 2.1 %collective-permute-start.20 = (bf16[4,24,1152]{2,1,0:T(8,128)(2,1)}, bf16[4,24,1152]{2,1,0:T(8,128)(2,1)}, u32[]{:S(2)}, u32[]{:S(2)}) collective-permute-start(bf16[4,24,1152]{2,1,0:T(8,128)(2,1)} %copy-done.3), channel_id=1, source_target_pairs={{0,2},{2,0},{1,3},{3,1},{4,6},{6,4},{5,7},{7,5},{8,10},{10,8},{9,1... | collective-permute-start | bytes 663560 | tf_op jit(solution)/shard_map/ppermute | solution.py:257
  86.7 2.0 %collective-permute-start.16 = (bf16[4,24,1152]{2,1,0:T(8,128)(2,1)}, bf16[4,24,1152]{2,1,0:T(8,128)(2,1)}, u32[]{:S(2)}, u32[]{:S(2)}) collective-permute-start(bf16[4,24,1152]{2,1,0:T(8,128)(2,1)} %collective-permute-done.8.refs_3_), channel_id=1, source_target_pairs={{0,2},{2,0},{1,3},{3,1},{4,6},{6,4},{5,7},{7,5},{8,10},{10,8},{9,1... | collective-permute-start | bytes 663560 | tf_op jit(solution)/shard_map/ppermute | solution.py:257
  87.1 1.9 %collective-permute-start.17 = (bf16[4,24,1152]{2,1,0:T(8,128)(2,1)}, bf16[4,24,1152]{2,1,0:T(8,128)(2,1)}, u32[]{:S(2)}, u32[]{:S(2)}) collective-permute-start(bf16[4,24,1152]{2,1,0:T(8,128)(2,1)} %collective-permute-done.10.refs_4_), channel_id=1, source_target_pairs={{0,2},{2,0},{1,3},{3,1},{4,6},{6,4},{5,7},{7,5},{8,10},{10,8},{9,1... | collective-permute-start | bytes 663560 | tf_op jit(solution)/shard_map/ppermute | solution.py:259
  87.2 2.1 %collective-permute-start.18 = (bf16[4,24,1152]{2,1,0:T(8,128)(2,1)}, bf16[4,24,1152]{2,1,0:T(8,128)(2,1)}, u32[]{:S(2)}, u32[]{:S(2)}) collective-permute-start(bf16[4,24,1152]{2,1,0:T(8,128)(2,1)} %collective-permute-done.11.refs_5_), channel_id=1, source_target_pairs={{0,2},{2,0},{1,3},{3,1},{4,6},{6,4},{5,7},{7,5},{8,10},{10,8},{9,1... | collective-permute-start | bytes 663560 | tf_op jit(solution)/shard_map/ppermute | solution.py:259
  89.4 0.9 copy-start.2
  90.3 0.9 copy-start.4
  107.6 3.8 %collective-permute-start.21 = (bf16[4,8,24,1152]{3,2,1,0:T(8,128)(2,1)S(1)}, bf16[4,8,24,1152]{3,2,1,0:T(8,128)(2,1)S(1)}, u32[]{:S(2)}, u32[]{:S(2)}) collective-permute-start(bf16[4,8,24,1152]{3,2,1,0:T(8,128)(2,1)S(1)} %get-tuple-element.54), channel_id=1, source_target_pairs={{0,2},{2,0},{1,3},{3,1},{4,6},{6,4},{5,7},{7,5},{8,10},{10,8},{9,1... | collective-permute-start | bytes 5308424 | tf_op jit(solution)/shard_map/ppermute | solution.py:204
  108.0 19.6 %collective-permute-start.24 = (bf16[512,768]{1,0:T(8,128)(2,1)S(1)}, bf16[512,768]{1,0:T(8,128)(2,1)S(1)}, u32[]{:S(2)}, u32[]{:S(2)}) collective-permute-start(bf16[512,768]{1,0:T(8,128)(2,1)S(1)} %get-tuple-element.59), channel_id=1, source_target_pairs={{0,1},{1,0},{2,3},{3,2},{4,5},{5,4},{6,7},{7,6},{8,9},{9,8},{10,11... | collective-permute-start | bytes 2359304 | tf_op jit(solution)/shard_map/ppermute | solution.py:263
  111.8 15.9 %collective-permute-start.22 = (bf16[4,24,1152]{2,1,0:T(8,128)(2,1)S(1)}, bf16[4,24,1152]{2,1,0:T(8,128)(2,1)S(1)}, u32[]{:S(2)}, u32[]{:S(2)}) collective-permute-start(bf16[4,24,1152]{2,1,0:T(8,128)(2,1)S(1)} %get-tuple-element.57), channel_id=1, source_target_pairs={{0,8},{8,16},{16,24},{24,0},{1,9},{9,17},{17,25},{25,1},{2,10},{10... | collective-permute-start | bytes 663560 | tf_op jit(solution)/shard_map/ppermute | solution.py:174
  114.3 13.4 %collective-permute-start.23 = (bf16[4,24,1152]{2,1,0:T(8,128)(2,1)S(1)}, bf16[4,24,1152]{2,1,0:T(8,128)(2,1)S(1)}, u32[]{:S(2)}, u32[]{:S(2)}) collective-permute-start(bf16[4,24,1152]{2,1,0:T(8,128)(2,1)S(1)} %get-tuple-element.58), channel_id=1, source_target_pairs={{0,24},{8,0},{16,8},{24,16},{1,25},{9,1},{17,9},{25,17},{2,26},{10... | collective-permute-start | bytes 663560 | tf_op jit(solution)/shard_map/ppermute | solution.py:174
  115.4 34.1 %collective-permute-start.26 = (bf16[4,24,1152]{2,1,0:T(8,128)(2,1)S(1)}, bf16[4,24,1152]{2,1,0:T(8,128)(2,1)S(1)}, u32[]{:S(2)}, u32[]{:S(2)}) collective-permute-start(bf16[4,24,1152]{2,1,0:T(8,128)(2,1)S(1)} %get-tuple-element.66), channel_id=1, source_target_pairs={{0,24},{8,0},{16,8},{24,16},{1,25},{9,1},{17,9},{25,17},{2,26},{10... | collective-permute-start | bytes 663560 | tf_op jit(solution)/shard_map/ppermute | solution.py:174
  117.4 32.0 %collective-permute-start.28 = (bf16[4,24,1152]{2,1,0:T(8,128)(2,1)S(1)}, bf16[4,24,1152]{2,1,0:T(8,128)(2,1)S(1)}, u32[]{:S(2)}, u32[]{:S(2)}) collective-permute-start(bf16[4,24,1152]{2,1,0:T(8,128)(2,1)S(1)} %get-tuple-element.67), channel_id=1, source_target_pairs={{0,8},{8,16},{16,24},{24,0},{1,9},{9,17},{17,25},{25,1},{2,10},{10... | collective-permute-start | bytes 663560 | tf_op jit(solution)/shard_map/ppermute | solution.py:174
  130.2 19.2 %collective-permute-start.25 = (bf16[4,24,1152]{2,1,0:T(8,128)(2,1)}, bf16[4,24,1152]{2,1,0:T(8,128)(2,1)}, u32[]{:S(2)}, u32[]{:S(2)}) collective-permute-start(bf16[4,24,1152]{2,1,0:T(8,128)(2,1)} %add_convert_fusion.3), channel_id=1, source_target_pairs={{0,8},{8,16},{16,24},{24,0},{1,9},{9,17},{17,25},{25,1},{2,10},{10... | collective-permute-start | bytes 663560 | tf_op jit(solution)/shard_map/ppermute | solution.py:174
  132.7 16.8 %collective-permute-start.29 = (bf16[4,24,1152]{2,1,0:T(8,128)(2,1)}, bf16[4,24,1152]{2,1,0:T(8,128)(2,1)}, u32[]{:S(2)}, u32[]{:S(2)}) collective-permute-start(bf16[4,24,1152]{2,1,0:T(8,128)(2,1)} %add_convert_fusion.2), channel_id=1, source_target_pairs={{0,24},{8,0},{16,8},{24,16},{1,25},{9,1},{17,9},{25,17},{2,26},{10... | collective-permute-start | bytes 663560 | tf_op jit(solution)/shard_map/ppermute | solution.py:174
  135.8 45.5 %all-to-all-start.1 = ((bf16[128,4,768]{2,1,0:T(4,128)(2,1)}), bf16[128,4,768]{2,1,0:T(4,128)(2,1)}, u32[]{:S(2)}, u32[]{:S(2)}) async-start(bf16[128,4,768]{2,1,0:T(4,128)(2,1)} %reshape.32), calls=%async_computation.1 | async-start | bytes 1572864 | tf_op jit(solution)/shard_map/all_to_all | solution.py:269
  150.7 24.9 %collective-permute-start.27 = (bf16[2,24,1152]{2,1,0:T(8,128)(2,1)S(1)}, bf16[2,24,1152]{2,1,0:T(8,128)(2,1)S(1)}, u32[]{:S(2)}, u32[]{:S(2)}) collective-permute-start(bf16[2,24,1152]{2,1,0:T(8,128)(2,1)S(1)} %slice.95), channel_id=1, source_target_pairs={{0,64},{32,96},{64,0},{96,32},{128,192},{160,224},{192,128},{224,1... | collective-permute-start | bytes 331784 | tf_op jit(solution)/shard_map/ppermute | solution.py:178
  153.3 28.0 %collective-permute-start.30 = (bf16[2,24,1152]{2,1,0:T(8,128)(2,1)S(1)}, bf16[2,24,1152]{2,1,0:T(8,128)(2,1)S(1)}, u32[]{:S(2)}, u32[]{:S(2)}) collective-permute-start(bf16[2,24,1152]{2,1,0:T(8,128)(2,1)S(1)} %get-tuple-element.74), channel_id=1, source_target_pairs={{0,128},{32,160},{64,192},{96,224},{128,0},{160,32},{192,64},{224,... | collective-permute-start | bytes 331784 | tf_op jit(solution)/shard_map/ppermute | solution.py:178
  157.4 23.9 %collective-permute-start.31 = (bf16[2,24,1152]{2,1,0:T(8,128)(2,1)S(1)}, bf16[2,24,1152]{2,1,0:T(8,128)(2,1)S(1)}, u32[]{:S(2)}, u32[]{:S(2)}) collective-permute-start(bf16[2,24,1152]{2,1,0:T(8,128)(2,1)S(1)} %get-tuple-element.75), channel_id=1, source_target_pairs={{0,192},{32,224},{64,128},{96,160},{128,64},{160,96},{192,0},{224,... | collective-permute-start | bytes 331784 | tf_op jit(solution)/shard_map/ppermute | solution.py:178
  181.4 7.3 %collective-permute-start.34 = (bf16[12,1152]{1,0:T(8,128)(2,1)S(1)}, bf16[12,1152]{1,0:T(8,128)(2,1)S(1)}, u32[]{:S(2)}, u32[]{:S(2)}) collective-permute-start(bf16[12,1152]{1,0:T(8,128)(2,1)S(1)} %fusion.6), channel_id=1, source_target_pairs={{0,32},{4,36},{32,0},{36,4},{64,96},{68,100},{96,64},{100,68},{128... | collective-permute-start | bytes 82952 | tf_op jit(solution)/shard_map/ppermute | solution.py:178
  181.5 7.2 %collective-permute-start.32 = (bf16[12,1152]{1,0:T(8,128)(2,1)S(1)}, bf16[12,1152]{1,0:T(8,128)(2,1)S(1)}, u32[]{:S(2)}, u32[]{:S(2)}) collective-permute-start(bf16[12,1152]{1,0:T(8,128)(2,1)S(1)} %get-tuple-element.76), channel_id=1, source_target_pairs={{0,4},{4,0},{32,36},{36,32},{64,68},{68,64},{96,100},{100,96},{128... | collective-permute-start | bytes 82952 | tf_op jit(solution)/shard_map/ppermute | solution.py:178
  182.2 6.6 %collective-permute-start.33 = (bf16[12,1152]{1,0:T(8,128)(2,1)S(1)}, bf16[12,1152]{1,0:T(8,128)(2,1)S(1)}, u32[]{:S(2)}, u32[]{:S(2)}) collective-permute-start(bf16[12,1152]{1,0:T(8,128)(2,1)S(1)} %get-tuple-element.77), channel_id=1, source_target_pairs={{0,36},{4,32},{32,4},{36,0},{64,100},{68,96},{96,68},{100,64},{128... | collective-permute-start | bytes 82952 | tf_op jit(solution)/shard_map/ppermute | solution.py:178

commit v7 on v3

--- a/solution.py
+++ b/solution.py
@@ -20,22 +20,20 @@
 
 
 def core_kernel(where_ref, t_ref, o_ref, *refs):
-    pieces = refs[:16]
-    give_ref, keep_ref, mine_ref, rest_ref, w_ref, s_ref, d_ref, g_ref = refs[16:]
+    own_ref, other_ref = refs[:2]
+    give_ref, keep_ref, mine_ref, rest_ref, w_ref, s_ref, d_ref, g_ref = refs[2:]
     z, y, c, m = (where_ref[i] for i in range(4))
     unit = XH * C * ROWS
 
-    @pl.loop(0, Z // 2)
+    @pl.loop(0, Z)
     def _(t):
-        for i in range(8):
-            by, high = i // 2, i % 2
-            a = pieces[i][t].astype(f32)
-            b = pieces[i + 8][t].astype(f32)
+        for i in range(Y):
+            a = own_ref[i, t].astype(f32)
+            b = other_ref[i, t].astype(f32)
             first = jnp.where(c == 0, a, b)
             second = jnp.where(c == 0, b, a)
             rows = [first[:ROWS], second[:ROWS], first[ROWS:], second[ROWS:]]
-            to = lax.bitwise_xor(z, t + high * (Z // 2)) * Y + lax.rem(by + y, Y)
-            to = pl.ds(pl.multiple_of(to * unit, unit), unit)
+            to = pl.ds(pl.multiple_of((lax.bitwise_xor(z, t) * Y + i) * unit, unit), unit)
             w_ref[to, :] = jnp.concatenate(rows, 0).astype(bf16)
 
     part_cols = o_ref.shape[1]
@@ -45,13 +43,11 @@
     pairs = half // 128
     near = pl.ds(pl.multiple_of(m * part_cols, part_cols), part_cols)
     away = pl.ds(pl.multiple_of((1 - m) * part_cols, part_cols), part_cols)
-    for j in range(3):
-        cols = slice(j * half, (j + 1) * half)
-        part = jnp.dot(t_ref[:, :part_cols], w_ref[near, cols], preferred_element_type=f32)
-        part += jnp.dot(o_ref[...], w_ref[away, cols], preferred_element_type=f32)
-        part = part.astype(bf16)
-        for pair in range(pairs):
-            s_ref[j * pairs + pair] = part[:, pair * 128 : (pair + 1) * 128].astype(f32)
+    part = jnp.dot(t_ref[:, :part_cols], w_ref[near, :], preferred_element_type=f32)
+    part += jnp.dot(o_ref[...], w_ref[away, :], preferred_element_type=f32)
+    part = part.astype(bf16)
+    for i in range(3 * pairs):
+        s_ref[i] = part[:, i * 128 : (i + 1) * 128].astype(f32)
     for pair in range(pairs):
         at = part_cols + pair * 128
         s_ref[3 * pairs + pair] = t_ref[:, at : at + 128].astype(f32)
@@ -87,10 +83,8 @@
     keep_ref[...] = dot(g, w_ref[near, :], NT).astype(bf16)
     step = 384
     for ref, of in ((t_ref, m), (o_ref, 1 - m)):
-
-        @pl.loop(0, part_cols // step)
-        def _(i, ref=ref, of=of):
-            total = dot(ref[:, pl.ds(pl.multiple_of(i * step, step), step)], g_ref[...], TN)
+        for i in range(part_cols // step):
+            total = dot(ref[:, i * step : (i + 1) * step], g_ref[...], TN)
             for b in range(step // unit):
                 quarters = [total[b * unit + r * ROWS :][:ROWS] for r in range(4)]
                 first = jnp.concatenate([quarters[0], quarters[2]], 0)
@@ -102,7 +96,7 @@
                 rest_ref[by, t] = jnp.where(c == 0, second, first).astype(bf16)
 
 
-def core(where, tokens, others, mine, rest):
+def core(where, tokens, others, own, other):
     rows, part_cols = others.shape
     half = tokens.shape[1] - part_cols
     width, n = MP * part_cols, 3 * half
@@ -115,7 +109,7 @@
             jax.ShapeDtypeStruct((Y, Z, XH * ROWS, n), bf16),
             jax.ShapeDtypeStruct((Y, Z, XH * ROWS, n), bf16),
         ),
-        in_specs=[pl.BlockSpec(memory_space=pltpu.SMEM)] + [vm] * 18,
+        in_specs=[pl.BlockSpec(memory_space=pltpu.SMEM)] + [vm] * 4,
         out_specs=(vm,) * 4,
         scratch_shapes=[
             pltpu.VMEM((width, n), bf16),
@@ -128,7 +122,7 @@
             flops=6 * rows * width * n, bytes_accessed=8 * 2**20, transcendentals=0
         ),
         name="attention_core",
-    )(where, tokens, others, *mine, *rest)
+    )(where, tokens, others, own, other)
 
 
 def combine_kernel(mine_ref, other_ref, *refs):
@@ -181,22 +175,13 @@
 ZX = ("z", "xh")
 
 
-def over_xh_and_pair(w):
+def over_z(w):
     even = lax.axis_index("xh") == 0
-    a, b, d = (across(w, ZX, Z * XH, by) for by in (1, 2, 3))
-    first = jnp.concatenate([jnp.where(even, w, a), jnp.where(even, a, w)], 0)
-    second = jnp.concatenate([jnp.where(even, b, d), jnp.where(even, d, b)], 0)
-    return jnp.stack([first, second], 0)
-
-
-def over_y(low, high):
-    before_low = shift(low, "y", Y, 1)
-    after_high = shift(high, "y", Y, Y - 1)
-    before_high = shift(high, "y", Y, 1)
-    after_low = shift(low, "y", Y, Y - 1)
-    far_low = shift(before_low, "y", Y, 1)
-    far_high = shift(after_high, "y", Y, Y - 1)
-    return [low, high, after_low, after_high, far_low, far_high, before_low, before_high]
+    own = jnp.stack([w] + [across(w, "z", Z, 2 * i) for i in range(1, Z // 2)], 0)
+    a, b, d = (across(own, ZX, Z * XH, by) for by in (1, 2, 3))
+    first = jnp.concatenate([jnp.where(even, own, a), jnp.where(even, a, own)], 1)
+    second = jnp.concatenate([jnp.where(even, b, d), jnp.where(even, d, b)], 1)
+    return jnp.stack([first, second], 1).reshape(Z, XH * ROWS, w.shape[1])
 
 
 def reduce_weight(mine, rest, got, finish, late):
@@ -242,23 +227,17 @@
     part = lax.dynamic_slice_in_dim(normed, m * cols, cols, 2)
     tokens = jnp.concatenate([part, out_grad], axis=2).reshape(F, count, cols + half)
 
-    pair = over_xh_and_pair(w_qkv.reshape(w_qkv.shape[0], n))
-    tokens, pair = lax.optimization_barrier((tokens, pair))
+    own = over_z(w_qkv.reshape(w_qkv.shape[0], n))
     tokens = lax.all_to_all(tokens, FR, 0, 0, tiled=True)
-    two, four, six = (across(pair, "z", Z, 2 * i) for i in range(1, Z // 2))
-    low, high = jnp.concatenate([pair, two], 0), jnp.concatenate([four, six], 0)
     part = tokens[:, :, :cols]
-    low, high, part = lax.optimization_barrier((low, high, part))
+    own, part = lax.optimization_barrier((own, part))
     others = lax.ppermute(part, "mp", PAIR)
-    mine = over_y(low, high)
+    own = lax.all_to_all(jnp.broadcast_to(own[None], (Y,) + own.shape), "y", 0, 0, tiled=True)
+    tokens = tokens.reshape(F * count, cols + half)
+    own, tokens, others = lax.optimization_barrier((own, tokens, others))
     others = others.reshape(F * count, cols)
-    tokens = tokens.reshape(F * count, cols + half)
-    rest = {i: lax.ppermute(mine[i], "c", PAIR) for i in (0, 1, 2, 3, 6, 7)}
-    mine, others, tokens = lax.optimization_barrier((mine, others, tokens))
-    rest.update({i: lax.ppermute(mine[i], "c", PAIR) for i in (4, 5)})
-
-    rest = [rest[i] for i in range(8)]
-    give, keep, mine, rest = core(where, tokens, others, mine, rest)
+    other = lax.ppermute(own, "c", PAIR)
+    give, keep, mine, rest = core(where, tokens, others, own, other)
     got = lax.ppermute(give, "mp", PAIR)
 
     def finish(got):

time: 187 us -> 187 us (level)
  starting transfers between devices: 69 us -> 62.6 us
  waiting for transfers between devices: 81.1 us -> 86.6 us
  local copies, waits for them, and re-layouts: 14.5 us -> 18.5 us
  Pallas kernels: 16.8 us -> 14.7 us
    ppermute x1, waiting for transfers between devices: 2.4 us -> 14.3 us  [on_device(): others = lax.ppermute(part, 'mp', PAIR)]
    ppermute x12 -> x6, starting transfers between devices: 17.2 us -> 8.65 us  [shift(): return lax.ppermute(x, axis, [(i, (i + by) % size) for i in range(size)])]
    ppermute x12 -> x6, waiting for transfers between devices: 5.23 us -> 0.02 us  [shift(): return lax.ppermute(x, axis, [(i, (i + by) % size) for i in range(size)])]
    all_to_all x0 -> x1, starting transfers between devices: none -> 4.63 us  [on_device(): lax.all_to_all(jnp.broadcast_to(own[None], (Y,) + own.shape), 'y', 0, 0,...]
    ppermute x12, waiting for transfers between devices: 58.1 us -> 54 us  [across(): return lax.ppermute(x, axis, [(i, i ^ by) for i in range(size)])]
    all_to_all x0 -> x1, waiting for transfers between devices: none -> 3.5 us  [on_device(): lax.all_to_all(jnp.broadcast_to(own[None], (Y,) + own.shape), 'y', 0, 0,...]
    all_to_all x1, starting transfers between devices: 10.8 us -> 7.88 us  [to_frames(): return lax.all_to_all(x.reshape(F, count, cols), FR, 0, 0, tiled=True)]
    pallas_call x1, Pallas kernels: 16.4 us -> 14.3 us  [core(): pl.pallas_call(core_kernel, out_shape=(jax.ShapeDtypeStruct((rows, part_c...]
  transfers between devices with their start and end apart: 37 -> 25, of which waited for: 17 -> 13; matrix products, arithmetic and copies ran while one was open for 8% -> 7% of each run, Pallas kernels for 0% -> 0%
where the time goes in v7:
time: 187 us
  waiting for transfers between devices  86.6 us (46%)
  starting transfers between devices  62.6 us (33%)
  local copies, waits for them, and re-layouts  18.5 us (10%)
  Pallas kernels  14.7 us (8%)
  other arithmetic  3.26 us (2%)
    ppermute x12, waiting for transfers between devices, across(): return lax.ppermute(x, axis, [(i, i ^ by) for i in range(size)])  54 us
    ppermute x12, starting transfers between devices, across(): return lax.ppermute(x, axis, [(i, i ^ by) for i in range(size)])  24 us
    all_to_all x1, starting transfers between devices, on_device(): tokens = lax.all_to_all(tokens, FR, 0, 0, tiled=True)  15.5 us
    pallas_call x1, Pallas kernels, core(): pl.pallas_call(core_kernel, out_shape=(jax.ShapeDtypeStruct((rows, part_c...  14.3 us
    ppermute x1, waiting for transfers between devices, on_device(): others = lax.ppermute(part, 'mp', PAIR)  14.3 us
    ppermute x1, waiting for transfers between devices, on_device(): got = lax.ppermute(give, 'mp', PAIR)  10.5 us
    ppermute x6, starting transfers between devices, shift(): return lax.ppermute(x, axis, [(i, (i + by) % size) for i in range(size)])  8.65 us
    all_to_all x1, starting transfers between devices, to_frames(): return lax.all_to_all(x.reshape(F, count, cols), FR, 0, 0, tiled=True)  7.88 us
  transfers between devices with their start and end apart: 25, of which 13 were waited for; matrix products, arithmetic and copies ran while one was open for 7% of the time, Pallas kernels for 0%

profile of v7, /device:TPU:6, one launch (start us, length us, event | category | flops | bytes accessed | tf_op | source)
XLA Modules:
  0.0 186.7 jit_solution(1954366317039035503)
XLA Ops:
  0.7 1.4 copy-done
  2.2 1.2 reshape.34
  3.4 15.5 %all-to-all-start = ((bf16[128,4,1152]{2,1,0:T(4,128)(2,1)}), bf16[128,4,1152]{2,1,0:T(4,128)(2,1)S(1)}, u32[]{:S(2)}, u32[]{:S(2)}) async-start(bf16[128,4,1152]{2,1,0:T(4,128)(2,1)} %reshape.34), calls=%async_computation | async-start | bytes 2359296 | tf_op jit(solution)/shard_map/all_to_all | solution.py:231
  19.0 4.2 %collective-permute-start.2 = (bf16[12,1152]{1,0:T(8,128)(2,1)S(1)}, bf16[12,1152]{1,0:T(8,128)(2,1)S(1)}, u32[]{:S(2)}, u32[]{:S(2)}) collective-permute-start(bf16[12,1152]{1,0:T(8,128)(2,1)S(1)} %bitcast.37), channel_id=1, source_target_pairs={{0,192},{32,224},{64,128},{96,160},{128,64},{160,96},{192,0},{224,... | collective-permute-start | bytes 82952 | tf_op jit(solution)/shard_map/ppermute | solution.py:172
  23.2 1.9 %collective-permute-start.1 = (bf16[12,1152]{1,0:T(8,128)(2,1)S(1)}, bf16[12,1152]{1,0:T(8,128)(2,1)S(1)}, u32[]{:S(2)}, u32[]{:S(2)}) collective-permute-start(bf16[12,1152]{1,0:T(8,128)(2,1)S(1)} %bitcast.38), channel_id=1, source_target_pairs={{0,128},{32,160},{64,192},{96,224},{128,0},{160,32},{192,64},{224,... | collective-permute-start | bytes 82952 | tf_op jit(solution)/shard_map/ppermute | solution.py:172
  25.1 0.5 collective-permute-start
  25.7 25.7 %collective-permute-done.2 = bf16[12,1152]{1,0:T(8,128)(2,1)S(1)} collective-permute-done((bf16[12,1152]{1,0:T(8,128)(2,1)S(1)}, bf16[12,1152]{1,0:T(8,128)(2,1)S(1)}, u32[]{:S(2)}, u32[]{:S(2)}) %collective-permute-start.2) | collective-permute-done | bytes 27680 | tf_op jit(solution)/shard_map/ppermute | solution.py:172
  51.5 0.6 collective-permute-start.3
  52.1 5.1 %collective-permute-start.5 = (bf16[4,12,1152]{2,1,0:T(8,128)(2,1)S(1)}, bf16[4,12,1152]{2,1,0:T(8,128)(2,1)S(1)}, u32[]{:S(2)}, u32[]{:S(2)}) collective-permute-start(bf16[4,12,1152]{2,1,0:T(8,128)(2,1)S(1)} %pad_maximum_fusion.3), channel_id=1, source_target_pairs={{0,36},{4,32},{32,4},{36,0},{64,100},{68,96},{96,68},{100,64},{128... | collective-permute-start | bytes 331784 | tf_op jit(solution)/shard_map/ppermute | solution.py:172
  57.2 3.7 %collective-permute-done.3 = bf16[4,12,1152]{2,1,0:T(8,128)(2,1)S(1)} collective-permute-done((bf16[4,12,1152]{2,1,0:T(8,128)(2,1)S(1)}, bf16[4,12,1152]{2,1,0:T(8,128)(2,1)S(1)}, u32[]{:S(2)}, u32[]{:S(2)}) %collective-permute-start.3) | collective-permute-done | bytes 110624 | tf_op jit(solution)/shard_map/ppermute | solution.py:172
  60.9 1.0 collective-permute-done.5
  61.9 1.2 collective-permute-done.4
  63.4 1.3 slice.60
  64.7 1.3 broadcast_in_dim.2
  66.0 4.6 %all-to-all-start.1 = ((bf16[4,8,24,1152]{3,2,1,0:T(8,128)(2,1)}), bf16[4,8,24,1152]{3,2,1,0:T(8,128)(2,1)S(1)}, u32[]{:S(2)}, u32[]{:S(2)}) async-start(bf16[4,8,24,1152]{3,2,1,0:T(8,128)(2,1)} %broadcast_in_dim.2), calls=%async_computation.1 | async-start | bytes 3538944 | tf_op jit(solution)/shard_map/all_to_all | solution.py:235
  70.7 0.8 collective-permute-start.6
  71.5 3.1 %reshape.35.t_ref = bf16[512,1152]{1,0:T(8,128)(2,1)} reshape(bf16[128,4,1152]{2,1,0:T(4,128)(2,1)} %copy-done.3) | data formatting | bytes 2359296 | tf_op jit(solution)/shard_map/reshape | solution.py:236
  74.6 14.3 %collective-permute-done.6 = bf16[128,4,768]{2,1,0:T(4,128)(2,1)} collective-permute-done((bf16[128,4,768]{2,1,0:T(4,128)(2,1)}, bf16[128,4,768]{2,1,0:T(4,128)(2,1)}, u32[]{:S(2)}, u32[]{:S(2)}) %collective-permute-start.6) | collective-permute-done | bytes 786464 | tf_op jit(solution)/shard_map/ppermute | solution.py:234
  88.9 3.5 %all-to-all-done.1.refs_0_ = bf16[4,8,24,1152]{3,2,1,0:T(8,128)(2,1)S(1)} async-done(((bf16[4,8,24,1152]{3,2,1,0:T(8,128)(2,1)}), bf16[4,8,24,1152]{3,2,1,0:T(8,128)(2,1)S(1)}, u32[]{:S(2)}, u32[]{:S(2)}) %all-to-all-start.1) | async-done | bytes 1769504 | tf_op jit(solution)/shard_map/all_to_all | solution.py:235
  92.5 2.3 %reshape.36.o_ref = bf16[512,768]{1,0:T(8,128)(2,1)} reshape(bf16[128,4,768]{2,1,0:T(4,128)(2,1)} %collective-permute-done.6) | data formatting | bytes 1572864 | tf_op jit(solution)/shard_map/reshape | solution.py:238
  94.8 1.5 collective-permute-done.7.refs_1_
  96.3 1.3 copy-done.1
  97.5 1.1 copy-done.2
  98.7 14.3 %attention_core.1 = (bf16[512,768]{1,0:T(8,128)(2,1)S(1)}, bf16[512,768]{1,0:T(8,128)(2,1)S(1)}, bf16[4,8,24,1152]{3,2,1,0:T(8,128)(2,1)S(1)}, bf16[4,8,24,1152]{3,2,1,0:T(8,128)(2,1)S(1)}) custom-call(s32[4]{0:T(128)S(1)} %pad_add_fusion.where_ref, bf16[512,1152]{1,0:T(8,128)(2,1)S(1)} %copy-done.1, bf16[512,768]{1,0:T(8,128)(2,1)S(1)} %copy-done.2, ...), custom_call_target="tpu_custom_call" | custom-call | flops 5435817984 | bytes 8388608 | tf_op jit(solution)/shard_map/attention_core/pallas_call | solution.py:104
  113.2 0.8 collective-permute-start.11
  114.1 2.7 %collective-permute-done.8.other_ref = bf16[4,8,24,1152]{3,2,1,0:T(8,128)(2,1)S(1)} collective-permute-done((bf16[4,8,24,1152]{3,2,1,0:T(8,128)(2,1)S(1)}, bf16[4,8,24,1152]{3,2,1,0:T(8,128)(2,1)S(1)}, u32[]{:S(2)}, u32[]{:S(2)}) %collective-permute-start.8) | collective-permute-done | bytes 1769504 | tf_op jit(solution)/shard_map/ppermute | solution.py:189
  117.2 0.6 collective-permute-start.9
  117.8 2.7 %collective-permute-start.10 = (bf16[4,24,1152]{2,1,0:T(8,128)(2,1)S(1)}, bf16[4,24,1152]{2,1,0:T(8,128)(2,1)S(1)}, u32[]{:S(2)}, u32[]{:S(2)}) collective-permute-start(bf16[4,24,1152]{2,1,0:T(8,128)(2,1)S(1)} %get-tuple-element.36), channel_id=1, source_target_pairs={{0,24},{8,0},{16,8},{24,16},{1,25},{9,1},{17,9},{25,17},{2,26},{10... | collective-permute-start | bytes 663560 | tf_op jit(solution)/shard_map/ppermute | solution.py:168
  120.5 2.0 %collective-permute-start.14 = (bf16[4,24,1152]{2,1,0:T(8,128)(2,1)S(1)}, bf16[4,24,1152]{2,1,0:T(8,128)(2,1)}, u32[]{:S(2)}, u32[]{:S(2)}) collective-permute-start(bf16[4,24,1152]{2,1,0:T(8,128)(2,1)S(1)} %get-tuple-element.45), channel_id=1, source_target_pairs={{0,8},{8,16},{16,24},{24,0},{1,9},{9,17},{17,25},{25,1},{2,10},{10... | collective-permute-start | bytes 663560 | tf_op jit(solution)/shard_map/ppermute | solution.py:168
  122.5 10.5 %collective-permute-done.11 = bf16[512,768]{1,0:T(8,128)(2,1)S(1)} collective-permute-done((bf16[512,768]{1,0:T(8,128)(2,1)S(1)}, bf16[512,768]{1,0:T(8,128)(2,1)S(1)}, u32[]{:S(2)}, u32[]{:S(2)}) %collective-permute-start.11) | collective-permute-done | bytes 786464 | tf_op jit(solution)/shard_map/ppermute | solution.py:241
  133.1 1.1 add_convert_fusion
  134.2 0.6 collective-permute-start.12
  134.9 2.7 %collective-permute-start.15 = (bf16[4,24,1152]{2,1,0:T(8,128)(2,1)S(1)}, bf16[4,24,1152]{2,1,0:T(8,128)(2,1)}, u32[]{:S(2)}, u32[]{:S(2)}) collective-permute-start(bf16[4,24,1152]{2,1,0:T(8,128)(2,1)S(1)} %add_convert_fusion.1), channel_id=1, source_target_pairs={{0,24},{8,0},{16,8},{24,16},{1,25},{9,1},{17,9},{25,17},{2,26},{10... | collective-permute-start | bytes 663560 | tf_op jit(solution)/shard_map/ppermute | solution.py:168
  137.6 2.4 %reshape.37 = bf16[128,4,768]{2,1,0:T(4,128)(2,1)} reshape(bf16[512,768]{1,0:T(8,128)(2,1)} %add_convert_fusion) | data formatting | bytes 1572864 | tf_op jit(solution)/shard_map/reshape | solution.py:247
  139.9 7.9 %all-to-all-start.2 = ((bf16[128,4,768]{2,1,0:T(4,128)(2,1)}), bf16[128,4,768]{2,1,0:T(4,128)(2,1)}, u32[]{:S(2)}, u32[]{:S(2)}) async-start(bf16[128,4,768]{2,1,0:T(4,128)(2,1)} %reshape.37), calls=%async_computation.2 | async-start | bytes 1572864 | tf_op jit(solution)/shard_map/all_to_all | solution.py:247
  147.9 1.4 convert_add_fusion.1
  149.5 1.0 collective-permute-start.17
  150.5 3.5 %collective-permute-start.18 = (bf16[4,12,1152]{2,1,0:T(8,128)(2,1)S(1)}, bf16[4,12,1152]{2,1,0:T(8,128)(2,1)S(1)}, u32[]{:S(2)}, u32[]{:S(2)}) collective-permute-start(bf16[4,12,1152]{2,1,0:T(8,128)(2,1)S(1)} %get-tuple-element.55), channel_id=1, source_target_pairs={{0,36},{4,32},{32,4},{36,0},{64,100},{68,96},{96,68},{100,64},{128... | collective-permute-start | bytes 331784 | tf_op jit(solution)/shard_map/ppermute | solution.py:172
  154.0 0.6 collective-permute-start.16
  154.6 5.0 %collective-permute-done.17 = bf16[4,12,1152]{2,1,0:T(8,128)(2,1)S(1)} collective-permute-done((bf16[4,12,1152]{2,1,0:T(8,128)(2,1)S(1)}, bf16[4,12,1152]{2,1,0:T(8,128)(2,1)S(1)}, u32[]{:S(2)}, u32[]{:S(2)}) %collective-permute-start.17) | collective-permute-done | bytes 110624 | tf_op jit(solution)/shard_map/ppermute | solution.py:172
  159.6 10.3 %collective-permute-done.18 = bf16[4,12,1152]{2,1,0:T(8,128)(2,1)S(1)} collective-permute-done((bf16[4,12,1152]{2,1,0:T(8,128)(2,1)S(1)}, bf16[4,12,1152]{2,1,0:T(8,128)(2,1)S(1)}, u32[]{:S(2)}, u32[]{:S(2)}) %collective-permute-start.18) | collective-permute-done | bytes 110624 | tf_op jit(solution)/shard_map/ppermute | solution.py:172
  169.9 2.7 %collective-permute-done.16 = bf16[4,12,1152]{2,1,0:T(8,128)(2,1)S(1)} collective-permute-done((bf16[4,12,1152]{2,1,0:T(8,128)(2,1)S(1)}, bf16[4,12,1152]{2,1,0:T(8,128)(2,1)S(1)}, u32[]{:S(2)}, u32[]{:S(2)}) %collective-permute-start.16) | collective-permute-done | bytes 110624 | tf_op jit(solution)/shard_map/ppermute | solution.py:172
  172.7 2.5 %collective-permute-start.19 = (bf16[12,1152]{1,0:T(8,128)(2,1)S(1)}, bf16[12,1152]{1,0:T(8,128)(2,1)S(1)}, u32[]{:S(2)}, u32[]{:S(2)}) collective-permute-start(bf16[12,1152]{1,0:T(8,128)(2,1)S(1)} %get-tuple-element.60), channel_id=1, source_target_pairs={{0,64},{32,96},{64,0},{96,32},{128,192},{160,224},{192,128},{224,1... | collective-permute-start | bytes 82952 | tf_op jit(solution)/shard_map/ppermute | solution.py:172
  175.2 2.9 %collective-permute-start.21 = (bf16[12,1152]{1,0:T(8,128)(2,1)S(1)}, bf16[12,1152]{1,0:T(8,128)(2,1)S(1)}, u32[]{:S(2)}, u32[]{:S(2)}) collective-permute-start(bf16[12,1152]{1,0:T(8,128)(2,1)S(1)} %get-tuple-element.61), channel_id=1, source_target_pairs={{0,192},{32,224},{64,128},{96,160},{128,64},{160,96},{192,0},{224,... | collective-permute-start | bytes 82952 | tf_op jit(solution)/shard_map/ppermute | solution.py:172
  178.1 1.2 collective-permute-start.20
  179.3 2.3 %reshape.38 = bf16[1,512,768]{2,1,0:T(8,128)(2,1)} reshape(bf16[128,4,768]{2,1,0:T(4,128)(2,1)} %all-to-all-done.2) | data formatting | bytes 1572864 | tf_op jit(solution)/shard_map/reshape | solution.py:250
  181.6 4.4 %collective-permute-done.20 = bf16[12,1152]{1,0:T(8,128)(2,1)S(1)} collective-permute-done((bf16[12,1152]{1,0:T(8,128)(2,1)S(1)}, bf16[12,1152]{1,0:T(8,128)(2,1)S(1)}, u32[]{:S(2)}, u32[]{:S(2)}) %collective-permute-start.20) | collective-permute-done | bytes 27680 | tf_op jit(solution)/shard_map/ppermute | solution.py:172
  186.0 0.7 reshape.39
  (48 shorter events, 1.7 us)
Async XLA Ops:
  0.6 1.4 copy-start
  0.6 1.5 copy-start.4
  3.4 15.5 %copy-start.5 = (bf16[12,3,384]{2,1,0:T(4,128)(2,1)S(1)}, bf16[12,3,384]{2,1,0:T(4,128)(2,1)}, u32[]{:S(2)}) copy-start(bf16[12,3,384]{2,1,0:T(4,128)(2,1)} %param.5) | copy-start | bytes 82948
  3.4 60.0 %all-to-all-start = ((bf16[128,4,1152]{2,1,0:T(4,128)(2,1)}), bf16[128,4,1152]{2,1,0:T(4,128)(2,1)S(1)}, u32[]{:S(2)}, u32[]{:S(2)}) async-start(bf16[128,4,1152]{2,1,0:T(4,128)(2,1)} %reshape.34), calls=%async_computation | async-start | bytes 2359296 | tf_op jit(solution)/shard_map/all_to_all | solution.py:231
  19.0 32.4 %collective-permute-start.2 = (bf16[12,1152]{1,0:T(8,128)(2,1)S(1)}, bf16[12,1152]{1,0:T(8,128)(2,1)S(1)}, u32[]{:S(2)}, u32[]{:S(2)}) collective-permute-start(bf16[12,1152]{1,0:T(8,128)(2,1)S(1)} %bitcast.37), channel_id=1, source_target_pairs={{0,192},{32,224},{64,128},{96,160},{128,64},{160,96},{192,0},{224,... | collective-permute-start | bytes 82952 | tf_op jit(solution)/shard_map/ppermute | solution.py:172
  23.2 28.2 %collective-permute-start.1 = (bf16[12,1152]{1,0:T(8,128)(2,1)S(1)}, bf16[12,1152]{1,0:T(8,128)(2,1)S(1)}, u32[]{:S(2)}, u32[]{:S(2)}) collective-permute-start(bf16[12,1152]{1,0:T(8,128)(2,1)S(1)} %bitcast.38), channel_id=1, source_target_pairs={{0,128},{32,160},{64,192},{96,224},{128,0},{160,32},{192,64},{224,... | collective-permute-start | bytes 82952 | tf_op jit(solution)/shard_map/ppermute | solution.py:172
  25.1 26.3 %collective-permute-start = (bf16[12,1152]{1,0:T(8,128)(2,1)S(1)}, bf16[12,1152]{1,0:T(8,128)(2,1)S(1)}, u32[]{:S(2)}, u32[]{:S(2)}) collective-permute-start(bf16[12,1152]{1,0:T(8,128)(2,1)S(1)} %bitcast.39), channel_id=1, source_target_pairs={{0,64},{32,96},{64,0},{96,32},{128,192},{160,224},{192,128},{224,1... | collective-permute-start | bytes 82952 | tf_op jit(solution)/shard_map/ppermute | solution.py:172
  51.5 9.4 %collective-permute-start.3 = (bf16[4,12,1152]{2,1,0:T(8,128)(2,1)S(1)}, bf16[4,12,1152]{2,1,0:T(8,128)(2,1)S(1)}, u32[]{:S(2)}, u32[]{:S(2)}) collective-permute-start(bf16[4,12,1152]{2,1,0:T(8,128)(2,1)S(1)} %pad_maximum_fusion.3), channel_id=1, source_target_pairs={{0,4},{4,0},{32,36},{36,32},{64,68},{68,64},{96,100},{100,96},{128... | collective-permute-start | bytes 331784 | tf_op jit(solution)/shard_map/ppermute | solution.py:172
  52.1 9.8 %collective-permute-start.5 = (bf16[4,12,1152]{2,1,0:T(8,128)(2,1)S(1)}, bf16[4,12,1152]{2,1,0:T(8,128)(2,1)S(1)}, u32[]{:S(2)}, u32[]{:S(2)}) collective-permute-start(bf16[4,12,1152]{2,1,0:T(8,128)(2,1)S(1)} %pad_maximum_fusion.3), channel_id=1, source_target_pairs={{0,36},{4,32},{32,4},{36,0},{64,100},{68,96},{96,68},{100,64},{128... | collective-permute-start | bytes 331784 | tf_op jit(solution)/shard_map/ppermute | solution.py:172
  57.2 5.9 %collective-permute-start.4 = (bf16[4,12,1152]{2,1,0:T(8,128)(2,1)S(1)}, bf16[4,12,1152]{2,1,0:T(8,128)(2,1)S(1)}, u32[]{:S(2)}, u32[]{:S(2)}) collective-permute-start(bf16[4,12,1152]{2,1,0:T(8,128)(2,1)S(1)} %pad_maximum_fusion.3), channel_id=1, source_target_pairs={{0,32},{4,36},{32,0},{36,4},{64,96},{68,100},{96,64},{100,68},{128... | collective-permute-start | bytes 331784 | tf_op jit(solution)/shard_map/ppermute | solution.py:172
  63.4 2.6 %copy-start.3 = (bf16[128,4,1152]{2,1,0:T(4,128)(2,1)}, bf16[128,4,1152]{2,1,0:T(4,128)(2,1)S(1)}, u32[]{:S(2)}) copy-start(bf16[128,4,1152]{2,1,0:T(4,128)(2,1)S(1)} %all-to-all-done) | copy-start | bytes 3538948
  66.0 26.4 %all-to-all-start.1 = ((bf16[4,8,24,1152]{3,2,1,0:T(8,128)(2,1)}), bf16[4,8,24,1152]{3,2,1,0:T(8,128)(2,1)S(1)}, u32[]{:S(2)}, u32[]{:S(2)}) async-start(bf16[4,8,24,1152]{3,2,1,0:T(8,128)(2,1)} %broadcast_in_dim.2), calls=%async_computation.1 | async-start | bytes 3538944 | tf_op jit(solution)/shard_map/all_to_all | solution.py:235
  70.7 18.3 %collective-permute-start.6 = (bf16[128,4,768]{2,1,0:T(4,128)(2,1)}, bf16[128,4,768]{2,1,0:T(4,128)(2,1)}, u32[]{:S(2)}, u32[]{:S(2)}) collective-permute-start(bf16[128,4,768]{2,1,0:T(4,128)(2,1)} %slice.60), channel_id=1, source_target_pairs={{0,1},{1,0},{2,3},{3,2},{4,5},{5,4},{6,7},{7,6},{8,9},{9,8},{10,11... | collective-permute-start | bytes 2359304 | tf_op jit(solution)/shard_map/ppermute | solution.py:234
  92.4 3.8 %collective-permute-start.7 = (bf16[4,8,24,1152]{3,2,1,0:T(8,128)(2,1)S(1)}, bf16[4,8,24,1152]{3,2,1,0:T(8,128)(2,1)}, u32[]{:S(2)}, u32[]{:S(2)}) collective-permute-start(bf16[4,8,24,1152]{3,2,1,0:T(8,128)(2,1)S(1)} %all-to-all-done.1.refs_0_), channel_id=1, source_target_pairs={{0,2},{2,0},{1,3},{3,1},{4,6},{6,4},{5,7},{7,5},{8,10},{10,8},{9,1... | collective-permute-start | bytes 5308424 | tf_op jit(solution)/shard_map/ppermute | solution.py:239
  96.3 1.3 copy-start.1
  97.5 1.1 copy-start.2
  113.0 3.8 %collective-permute-start.8 = (bf16[4,8,24,1152]{3,2,1,0:T(8,128)(2,1)S(1)}, bf16[4,8,24,1152]{3,2,1,0:T(8,128)(2,1)S(1)}, u32[]{:S(2)}, u32[]{:S(2)}) collective-permute-start(bf16[4,8,24,1152]{3,2,1,0:T(8,128)(2,1)S(1)} %get-tuple-element.32), channel_id=1, source_target_pairs={{0,2},{2,0},{1,3},{3,1},{4,6},{6,4},{5,7},{7,5},{8,10},{10,8},{9,1... | collective-permute-start | bytes 5308424 | tf_op jit(solution)/shard_map/ppermute | solution.py:189
  113.2 19.8 %collective-permute-start.11 = (bf16[512,768]{1,0:T(8,128)(2,1)S(1)}, bf16[512,768]{1,0:T(8,128)(2,1)S(1)}, u32[]{:S(2)}, u32[]{:S(2)}) collective-permute-start(bf16[512,768]{1,0:T(8,128)(2,1)S(1)} %get-tuple-element.37), channel_id=1, source_target_pairs={{0,1},{1,0},{2,3},{3,2},{4,5},{5,4},{6,7},{7,6},{8,9},{9,8},{10,11... | collective-permute-start | bytes 2359304 | tf_op jit(solution)/shard_map/ppermute | solution.py:241
  117.2 15.9 %collective-permute-start.9 = (bf16[4,24,1152]{2,1,0:T(8,128)(2,1)S(1)}, bf16[4,24,1152]{2,1,0:T(8,128)(2,1)S(1)}, u32[]{:S(2)}, u32[]{:S(2)}) collective-permute-start(bf16[4,24,1152]{2,1,0:T(8,128)(2,1)S(1)} %get-tuple-element.35), channel_id=1, source_target_pairs={{0,8},{8,16},{16,24},{24,0},{1,9},{9,17},{17,25},{25,1},{2,10},{10... | collective-permute-start | bytes 663560 | tf_op jit(solution)/shard_map/ppermute | solution.py:168
  117.8 15.2 %collective-permute-start.10 = (bf16[4,24,1152]{2,1,0:T(8,128)(2,1)S(1)}, bf16[4,24,1152]{2,1,0:T(8,128)(2,1)S(1)}, u32[]{:S(2)}, u32[]{:S(2)}) collective-permute-start(bf16[4,24,1152]{2,1,0:T(8,128)(2,1)S(1)} %get-tuple-element.36), channel_id=1, source_target_pairs={{0,24},{8,0},{16,8},{24,16},{1,25},{9,1},{17,9},{25,17},{2,26},{10... | collective-permute-start | bytes 663560 | tf_op jit(solution)/shard_map/ppermute | solution.py:168
  120.5 27.3 %collective-permute-start.13 = (bf16[4,24,1152]{2,1,0:T(8,128)(2,1)S(1)}, bf16[4,24,1152]{2,1,0:T(8,128)(2,1)}, u32[]{:S(2)}, u32[]{:S(2)}) collective-permute-start(bf16[4,24,1152]{2,1,0:T(8,128)(2,1)S(1)} %get-tuple-element.44), channel_id=1, source_target_pairs={{0,24},{8,0},{16,8},{24,16},{1,25},{9,1},{17,9},{25,17},{2,26},{10... | collective-permute-start | bytes 663560 | tf_op jit(solution)/shard_map/ppermute | solution.py:168
  120.5 27.3 %collective-permute-start.14 = (bf16[4,24,1152]{2,1,0:T(8,128)(2,1)S(1)}, bf16[4,24,1152]{2,1,0:T(8,128)(2,1)}, u32[]{:S(2)}, u32[]{:S(2)}) collective-permute-start(bf16[4,24,1152]{2,1,0:T(8,128)(2,1)S(1)} %get-tuple-element.45), channel_id=1, source_target_pairs={{0,8},{8,16},{16,24},{24,0},{1,9},{9,17},{17,25},{25,1},{2,10},{10... | collective-permute-start | bytes 663560 | tf_op jit(solution)/shard_map/ppermute | solution.py:168
  134.2 13.6 %collective-permute-start.12 = (bf16[4,24,1152]{2,1,0:T(8,128)(2,1)S(1)}, bf16[4,24,1152]{2,1,0:T(8,128)(2,1)}, u32[]{:S(2)}, u32[]{:S(2)}) collective-permute-start(bf16[4,24,1152]{2,1,0:T(8,128)(2,1)S(1)} %add_convert_fusion.2), channel_id=1, source_target_pairs={{0,8},{8,16},{16,24},{24,0},{1,9},{9,17},{17,25},{25,1},{2,10},{10... | collective-permute-start | bytes 663560 | tf_op jit(solution)/shard_map/ppermute | solution.py:168
  134.9 13.0 %collective-permute-start.15 = (bf16[4,24,1152]{2,1,0:T(8,128)(2,1)S(1)}, bf16[4,24,1152]{2,1,0:T(8,128)(2,1)}, u32[]{:S(2)}, u32[]{:S(2)}) collective-permute-start(bf16[4,24,1152]{2,1,0:T(8,128)(2,1)S(1)} %add_convert_fusion.1), channel_id=1, source_target_pairs={{0,24},{8,0},{16,8},{24,16},{1,25},{9,1},{17,9},{25,17},{2,26},{10... | collective-permute-start | bytes 663560 | tf_op jit(solution)/shard_map/ppermute | solution.py:168
  139.9 32.7 %all-to-all-start.2 = ((bf16[128,4,768]{2,1,0:T(4,128)(2,1)}), bf16[128,4,768]{2,1,0:T(4,128)(2,1)}, u32[]{:S(2)}, u32[]{:S(2)}) async-start(bf16[128,4,768]{2,1,0:T(4,128)(2,1)} %reshape.37), calls=%async_computation.2 | async-start | bytes 1572864 | tf_op jit(solution)/shard_map/all_to_all | solution.py:247
  149.5 10.1 %collective-permute-start.17 = (bf16[4,12,1152]{2,1,0:T(8,128)(2,1)S(1)}, bf16[4,12,1152]{2,1,0:T(8,128)(2,1)S(1)}, u32[]{:S(2)}, u32[]{:S(2)}) collective-permute-start(bf16[4,12,1152]{2,1,0:T(8,128)(2,1)S(1)} %get-tuple-element.54), channel_id=1, source_target_pairs={{0,4},{4,0},{32,36},{36,32},{64,68},{68,64},{96,100},{100,96},{128... | collective-permute-start | bytes 331784 | tf_op jit(solution)/shard_map/ppermute | solution.py:172
  150.5 19.3 %collective-permute-start.18 = (bf16[4,12,1152]{2,1,0:T(8,128)(2,1)S(1)}, bf16[4,12,1152]{2,1,0:T(8,128)(2,1)S(1)}, u32[]{:S(2)}, u32[]{:S(2)}) collective-permute-start(bf16[4,12,1152]{2,1,0:T(8,128)(2,1)S(1)} %get-tuple-element.55), channel_id=1, source_target_pairs={{0,36},{4,32},{32,4},{36,0},{64,100},{68,96},{96,68},{100,64},{128... | collective-permute-start | bytes 331784 | tf_op jit(solution)/shard_map/ppermute | solution.py:172
  154.0 18.6 %collective-permute-start.16 = (bf16[4,12,1152]{2,1,0:T(8,128)(2,1)S(1)}, bf16[4,12,1152]{2,1,0:T(8,128)(2,1)S(1)}, u32[]{:S(2)}, u32[]{:S(2)}) collective-permute-start(bf16[4,12,1152]{2,1,0:T(8,128)(2,1)S(1)} %slice.53), channel_id=1, source_target_pairs={{0,32},{4,36},{32,0},{36,4},{64,96},{68,100},{96,64},{100,68},{128... | collective-permute-start | bytes 331784 | tf_op jit(solution)/shard_map/ppermute | solution.py:172
  172.7 8.8 %collective-permute-start.19 = (bf16[12,1152]{1,0:T(8,128)(2,1)S(1)}, bf16[12,1152]{1,0:T(8,128)(2,1)S(1)}, u32[]{:S(2)}, u32[]{:S(2)}) collective-permute-start(bf16[12,1152]{1,0:T(8,128)(2,1)S(1)} %get-tuple-element.60), channel_id=1, source_target_pairs={{0,64},{32,96},{64,0},{96,32},{128,192},{160,224},{192,128},{224,1... | collective-permute-start | bytes 82952 | tf_op jit(solution)/shard_map/ppermute | solution.py:172
  175.2 6.4 %collective-permute-start.21 = (bf16[12,1152]{1,0:T(8,128)(2,1)S(1)}, bf16[12,1152]{1,0:T(8,128)(2,1)S(1)}, u32[]{:S(2)}, u32[]{:S(2)}) collective-permute-start(bf16[12,1152]{1,0:T(8,128)(2,1)S(1)} %get-tuple-element.61), channel_id=1, source_target_pairs={{0,192},{32,224},{64,128},{96,160},{128,64},{160,96},{192,0},{224,... | collective-permute-start | bytes 82952 | tf_op jit(solution)/shard_map/ppermute | solution.py:172
  178.1 7.9 %collective-permute-start.20 = (bf16[12,1152]{1,0:T(8,128)(2,1)S(1)}, bf16[12,1152]{1,0:T(8,128)(2,1)S(1)}, u32[]{:S(2)}, u32[]{:S(2)}) collective-permute-start(bf16[12,1152]{1,0:T(8,128)(2,1)S(1)} %get-tuple-element.62), channel_id=1, source_target_pairs={{0,128},{32,160},{64,192},{96,224},{128,0},{160,32},{192,64},{224,... | collective-permute-start | bytes 82952 | tf_op jit(solution)/shard_map/ppermute | solution.py:172

commit v8 on v7

--- a/solution.py
+++ b/solution.py
@@ -19,21 +19,25 @@
     return lax.dot_general(a, b, dims, preferred_element_type=f32)
 
 
-def core_kernel(where_ref, t_ref, o_ref, *refs):
-    own_ref, other_ref = refs[:2]
-    give_ref, keep_ref, mine_ref, rest_ref, w_ref, s_ref, d_ref, g_ref = refs[2:]
+def core_kernel(where_ref, t_ref, *refs):
+    parts, pieces = refs[:2], refs[2:18]
+    give_ref, keep_ref, mine_ref, rest_ref, w_ref, s_ref, d_ref, g_ref, o_ref = refs[18:]
+    for i, part in enumerate(parts):
+        o_ref[i * part.shape[0] : (i + 1) * part.shape[0]] = part[...]
     z, y, c, m = (where_ref[i] for i in range(4))
     unit = XH * C * ROWS
 
-    @pl.loop(0, Z)
+    @pl.loop(0, Z // 2)
     def _(t):
-        for i in range(Y):
-            a = own_ref[i, t].astype(f32)
-            b = other_ref[i, t].astype(f32)
+        for i in range(8):
+            by, high = i // 2, i % 2
+            a = pieces[i][t].astype(f32)
+            b = pieces[i + 8][t].astype(f32)
             first = jnp.where(c == 0, a, b)
             second = jnp.where(c == 0, b, a)
             rows = [first[:ROWS], second[:ROWS], first[ROWS:], second[ROWS:]]
-            to = pl.ds(pl.multiple_of((lax.bitwise_xor(z, t) * Y + i) * unit, unit), unit)
+            to = lax.bitwise_xor(z, t + high * (Z // 2)) * Y + lax.rem(by + y, Y)
+            to = pl.ds(pl.multiple_of(to * unit, unit), unit)
             w_ref[to, :] = jnp.concatenate(rows, 0).astype(bf16)
 
     part_cols = o_ref.shape[1]
@@ -83,8 +87,10 @@
     keep_ref[...] = dot(g, w_ref[near, :], NT).astype(bf16)
     step = 384
     for ref, of in ((t_ref, m), (o_ref, 1 - m)):
-        for i in range(part_cols // step):
-            total = dot(ref[:, i * step : (i + 1) * step], g_ref[...], TN)
+
+        @pl.loop(0, part_cols // step)
+        def _(i, ref=ref, of=of):
+            total = dot(ref[:, pl.ds(pl.multiple_of(i * step, step), step)], g_ref[...], TN)
             for b in range(step // unit):
                 quarters = [total[b * unit + r * ROWS :][:ROWS] for r in range(4)]
                 first = jnp.concatenate([quarters[0], quarters[2]], 0)
@@ -97,7 +103,7 @@
 
 
 def core(where, tokens, others, own, other):
-    rows, part_cols = others.shape
+    rows, part_cols = tokens.shape[0], others[0].shape[1]
     half = tokens.shape[1] - part_cols
     width, n = MP * part_cols, 3 * half
     vm = pl.BlockSpec(memory_space=pltpu.VMEM)
@@ -109,20 +115,21 @@
             jax.ShapeDtypeStruct((Y, Z, XH * ROWS, n), bf16),
             jax.ShapeDtypeStruct((Y, Z, XH * ROWS, n), bf16),
         ),
-        in_specs=[pl.BlockSpec(memory_space=pltpu.SMEM)] + [vm] * 4,
+        in_specs=[pl.BlockSpec(memory_space=pltpu.SMEM)] + [vm] * 19,
         out_specs=(vm,) * 4,
         scratch_shapes=[
             pltpu.VMEM((width, n), bf16),
             pltpu.VMEM((4 * half // 128, rows, 128), f32),
             pltpu.VMEM((3 * half // 128, rows, 128), f32),
             pltpu.VMEM((rows, n), bf16),
+            pltpu.VMEM((rows, part_cols), bf16),
         ],
         compiler_params=pltpu.CompilerParams(vmem_limit_bytes=VMEM_LIMIT),
         cost_estimate=pl.CostEstimate(
             flops=6 * rows * width * n, bytes_accessed=8 * 2**20, transcendentals=0
         ),
         name="attention_core",
-    )(where, tokens, others, own, other)
+    )(where, tokens, *others, *own, *other)
 
 
 def combine_kernel(mine_ref, other_ref, *refs):
@@ -179,9 +186,13 @@
     even = lax.axis_index("xh") == 0
     own = jnp.stack([w] + [across(w, "z", Z, 2 * i) for i in range(1, Z // 2)], 0)
     a, b, d = (across(own, ZX, Z * XH, by) for by in (1, 2, 3))
-    first = jnp.concatenate([jnp.where(even, own, a), jnp.where(even, a, own)], 1)
-    second = jnp.concatenate([jnp.where(even, b, d), jnp.where(even, d, b)], 1)
-    return jnp.stack([first, second], 1).reshape(Z, XH * ROWS, w.shape[1])
+
+    def part(at):
+        first = jnp.concatenate([jnp.where(even, own, a)[at], jnp.where(even, a, own)[at]], 1)
+        second = jnp.concatenate([jnp.where(even, b, d)[at], jnp.where(even, d, b)[at]], 1)
+        return jnp.stack([first, second], 1).reshape(Z // 2, XH * ROWS, w.shape[1])
+
+    return part(slice(0, 2)), part(slice(2, 4))
 
 
 def reduce_weight(mine, rest, got, finish, late):
@@ -227,16 +238,24 @@
     part = lax.dynamic_slice_in_dim(normed, m * cols, cols, 2)
     tokens = jnp.concatenate([part, out_grad], axis=2).reshape(F, count, cols + half)
 
-    own = over_z(w_qkv.reshape(w_qkv.shape[0], n))
+    low, high = over_z(w_qkv.reshape(w_qkv.shape[0], n))
     tokens = lax.all_to_all(tokens, FR, 0, 0, tiled=True)
-    part = tokens[:, :, :cols]
-    own, part = lax.optimization_barrier((own, part))
-    others = lax.ppermute(part, "mp", PAIR)
-    own = lax.all_to_all(jnp.broadcast_to(own[None], (Y,) + own.shape), "y", 0, 0, tiled=True)
+    first, second = tokens[: F // 2, :, :cols], tokens[F // 2 :, :, :cols]
+    first = lax.ppermute(first, "mp", PAIR)
+    low, high, first, second = lax.optimization_barrier((low, high, first, second))
+    second = lax.ppermute(second, "mp", PAIR)
+    before_low = shift(low, "y", Y, 1)
+    after_high = shift(high, "y", Y, Y - 1)
+    before_high = shift(high, "y", Y, 1)
+    after_low = shift(low, "y", Y, Y - 1)
     tokens = tokens.reshape(F * count, cols + half)
-    own, tokens, others = lax.optimization_barrier((own, tokens, others))
-    others = others.reshape(F * count, cols)
-    other = lax.ppermute(own, "c", PAIR)
+    before_low, after_high, tokens = lax.optimization_barrier((before_low, after_high, tokens))
+    far_low = shift(before_low, "y", Y, 1)
+    far_high = shift(after_high, "y", Y, Y - 1)
+    far_low, far_high, second = lax.optimization_barrier((far_low, far_high, second))
+    others = [x.reshape(F // 2 * count, cols) for x in (first, second)]
+    own = [low, high, after_low, after_high, far_low, far_high, before_low, before_high]
+    other = [lax.ppermute(x, "c", PAIR) for x in own]
     give, keep, mine, rest = core(where, tokens, others, own, other)
     got = lax.ppermute(give, "mp", PAIR)
 

time: 187 us -> 201 us (1.075)
  starting transfers between devices: 62.6 us -> 67 us
  local copies, waits for them, and re-layouts: 18.5 us -> 21.8 us
  other arithmetic: 3.26 us -> 5.95 us
    all_to_all x1, waiting for transfers between devices: 0.01 us -> 22.1 us  [on_device(): tokens = lax.all_to_all(tokens, FR, 0, 0, tiled=True)]
    ppermute x12, waiting for transfers between devices: 54 us -> 35.8 us  [across(): return lax.ppermute(x, axis, [(i, i ^ by) for i in range(size)])]
    ppermute x6 -> x12, starting transfers between devices: 8.65 us -> 18.3 us  [shift(): return lax.ppermute(x, axis, [(i, (i + by) % size) for i in range(size)])]
    ppermute x6 -> x12, waiting for transfers between devices: 0.02 us -> 7.48 us  [shift(): return lax.ppermute(x, axis, [(i, (i + by) % size) for i in range(size)])]
    ppermute x2 -> x10, waiting for transfers between devices: 15.8 us -> 9.97 us  [the longest x1 9.95 us: on_device(): first = lax.ppermute(first, 'mp', PAIR)]
    unnamed x14 -> x50, local copies, waits for them, and re-layouts: 3.84 us -> 9.34 us
    all_to_all x1 -> x0, starting transfers between devices: 4.63 us -> none  [on_device(): lax.all_to_all(jnp.broadcast_to(own[None], (Y,) + own.shape), 'y', 0, 0,...]
    all_to_all x1, starting transfers between devices: 15.5 us -> 11.3 us  [on_device(): tokens = lax.all_to_all(tokens, FR, 0, 0, tiled=True)]
  transfers between devices with their start and end apart: 25 -> 38, of which waited for: 13 -> 16; matrix products, arithmetic and copies ran while one was open for 7% -> 8% of each run, Pallas kernels for 0% -> 0%
where the time goes in v8:
time: 201 us; the launch traced here: 199 us
  waiting for transfers between devices  87.5 us (44%)
  starting transfers between devices  67 us (33%)
  local copies, waits for them, and re-layouts  21.8 us (11%)
  Pallas kernels  16.2 us (8%)
  other arithmetic  5.95 us (3%)
    ppermute x12, waiting for transfers between devices, across(): return lax.ppermute(x, axis, [(i, i ^ by) for i in range(size)])  35.8 us
    ppermute x12, starting transfers between devices, across(): return lax.ppermute(x, axis, [(i, i ^ by) for i in range(size)])  24.4 us
    all_to_all x1, waiting for transfers between devices, on_device(): tokens = lax.all_to_all(tokens, FR, 0, 0, tiled=True)  22.1 us
    ppermute x12, starting transfers between devices, shift(): return lax.ppermute(x, axis, [(i, (i + by) % size) for i in range(size)])  18.3 us
    pallas_call x1, Pallas kernels, core(): pl.pallas_call(core_kernel, out_shape=(jax.ShapeDtypeStruct((rows, part_c...  15.8 us
    all_to_all x1, starting transfers between devices, on_device(): tokens = lax.all_to_all(tokens, FR, 0, 0, tiled=True)  11.3 us
    ppermute x1, waiting for transfers between devices, on_device(): got = lax.ppermute(give, 'mp', PAIR)  10.3 us
    ppermute x1, waiting for transfers between devices, on_device(): first = lax.ppermute(first, 'mp', PAIR)  9.95 us
  transfers between devices with their start and end apart: 38, of which 16 were waited for; matrix products, arithmetic and copies ran while one was open for 8% of the time, Pallas kernels for 0%

profile of v8, /device:TPU:6, one launch (start us, length us, event | category | flops | bytes accessed | tf_op | source)
XLA Modules:
  0.0 199.5 jit_solution(15459383904229917029)
XLA Ops:
  1.6 6.4 %collective-permute-start.2 = (bf16[12,1152]{1,0:T(8,128)(2,1)S(1)}, bf16[12,1152]{1,0:T(8,128)(2,1)S(1)}, u32[]{:S(2)}, u32[]{:S(2)}) collective-permute-start(bf16[12,1152]{1,0:T(8,128)(2,1)S(1)} %bitcast.49), channel_id=1, source_target_pairs={{0,192},{32,224},{64,128},{96,160},{128,64},{160,96},{192,0},{224,... | collective-permute-start | bytes 82952 | tf_op jit(solution)/shard_map/ppermute | solution.py:179
  8.0 1.0 collective-permute-start.1
  9.0 1.5 collective-permute-start
  10.6 5.8 %collective-permute-done.1 = bf16[12,1152]{1,0:T(8,128)(2,1)S(1)} collective-permute-done((bf16[12,1152]{1,0:T(8,128)(2,1)S(1)}, bf16[12,1152]{1,0:T(8,128)(2,1)S(1)}, u32[]{:S(2)}, u32[]{:S(2)}) %collective-permute-start.1) | collective-permute-done | bytes 27680 | tf_op jit(solution)/shard_map/ppermute | solution.py:179
  17.0 1.9 collective-permute-start.5
  19.0 1.0 collective-permute-start.4
  20.0 1.1 pad_maximum_fusion
  21.1 1.2 reshape.40
  22.3 11.3 %all-to-all-start = ((bf16[128,4,1152]{2,1,0:T(4,128)(2,1)}), bf16[128,4,1152]{2,1,0:T(4,128)(2,1)S(1)}, u32[]{:S(2)}, u32[]{:S(2)}) async-start(bf16[128,4,1152]{2,1,0:T(4,128)(2,1)} %reshape.40), calls=%async_computation | async-start | bytes 2359296 | tf_op jit(solution)/shard_map/all_to_all | solution.py:242
  33.7 1.0 collective-permute-start.3
  34.6 1.0 broadcast_select_fusion.1
  35.7 7.6 %collective-permute-done.3 = bf16[4,12,1152]{2,1,0:T(8,128)(2,1)S(1)} collective-permute-done((bf16[4,12,1152]{2,1,0:T(8,128)(2,1)}, bf16[4,12,1152]{2,1,0:T(8,128)(2,1)S(1)}, u32[]{:S(2)}, u32[]{:S(2)}) %collective-permute-start.3) | collective-permute-done | bytes 110624 | tf_op jit(solution)/shard_map/ppermute | solution.py:179
  43.6 22.1 %all-to-all-done = bf16[128,4,1152]{2,1,0:T(4,128)(2,1)S(1)} async-done(((bf16[128,4,1152]{2,1,0:T(4,128)(2,1)}), bf16[128,4,1152]{2,1,0:T(4,128)(2,1)S(1)}, u32[]{:S(2)}, u32[]{:S(2)}) %all-to-all-start) | async-done | bytes 1179680 | tf_op jit(solution)/shard_map/all_to_all | solution.py:242
  65.6 1.1 fusion.7
  66.9 9.9 %collective-permute-done.6 = bf16[64,4,768]{2,1,0:T(4,128)(2,1)S(1)} collective-permute-done((bf16[64,4,768]{2,1,0:T(4,128)(2,1)S(1)}, bf16[64,4,768]{2,1,0:T(4,128)(2,1)S(1)}, u32[]{:S(2)}, u32[]{:S(2)}) %collective-permute-start.6) | collective-permute-done | bytes 393248 | tf_op jit(solution)/shard_map/ppermute | solution.py:244
  76.8 1.3 collective-permute-start.7
  78.1 1.9 collective-permute-start.8
  80.3 2.4 %reshape.41.t_ref = bf16[512,1152]{1,0:T(8,128)(2,1)S(1)} reshape(bf16[128,4,1152]{2,1,0:T(4,128)(2,1)} %copy-done.13) | data formatting | bytes 2359296 | tf_op jit(solution)/shard_map/reshape | solution.py:251
  82.7 1.4 collective-permute-start.12
  85.6 2.5 %collective-permute-start.9 = (bf16[4,24,1152]{2,1,0:T(8,128)(2,1)}, bf16[4,24,1152]{2,1,0:T(8,128)(2,1)}, u32[]{:S(2)}, u32[]{:S(2)}) collective-permute-start(bf16[4,24,1152]{2,1,0:T(8,128)(2,1)} %collective-permute-done.7.refs_8_), channel_id=1, source_target_pairs={{0,8},{8,16},{16,24},{24,0},{1,9},{9,17},{17,25},{25,1},{2,10},{10... | collective-permute-start | bytes 663560 | tf_op jit(solution)/shard_map/ppermute | solution.py:175
  88.8 2.3 %collective-permute-done.12.refs_4_ = bf16[4,24,1152]{2,1,0:T(8,128)(2,1)S(1)} collective-permute-done((bf16[4,24,1152]{2,1,0:T(8,128)(2,1)S(1)}, bf16[4,24,1152]{2,1,0:T(8,128)(2,1)S(1)}, u32[]{:S(2)}, u32[]{:S(2)}) %collective-permute-start.12) | collective-permute-done | bytes 221216 | tf_op jit(solution)/shard_map/ppermute | solution.py:175
  91.1 1.6 collective-permute-start.13
  95.6 2.8 %collective-permute-done.13.refs_9_ = bf16[4,24,1152]{2,1,0:T(8,128)(2,1)} collective-permute-done((bf16[4,24,1152]{2,1,0:T(8,128)(2,1)S(1)}, bf16[4,24,1152]{2,1,0:T(8,128)(2,1)}, u32[]{:S(2)}, u32[]{:S(2)}) %collective-permute-start.13) | collective-permute-done | bytes 221216 | tf_op jit(solution)/shard_map/ppermute | solution.py:175
  100.4 1.1 reshape.42.refs_0_
  101.5 1.1 reshape.43.refs_1_
  103.6 0.9 copy-done.4
  108.3 15.8 %attention_core.1 = (bf16[512,768]{1,0:T(8,128)(2,1)S(1)}, bf16[512,768]{1,0:T(8,128)(2,1)S(1)}, bf16[4,8,24,1152]{3,2,1,0:T(8,128)(2,1)S(1)}, bf16[4,8,24,1152]{3,2,1,0:T(8,128)(2,1)S(1)}) custom-call(s32[4]{0:T(128)S(1)} %pad_add_fusion.where_ref, bf16[512,1152]{1,0:T(8,128)(2,1)S(1)} %reshape.41.t_ref, bf16[256,768]{1,0:T(8,128)(2,1)S(1)} %reshape.42.refs_0_, ...), custom_call_target="tpu_custom_call" | custom-call | flops 5435817984 | bytes 8388608 | tf_op jit(solution)/shard_map/attention_core/pallas_call | solution.py:110
  124.6 1.3 collective-permute-start.25
  126.0 2.0 collective-permute-done.22.other_ref
  128.4 1.0 collective-permute-start.23
  129.3 2.6 %collective-permute-start.24 = (bf16[4,24,1152]{2,1,0:T(8,128)(2,1)S(1)}, bf16[4,24,1152]{2,1,0:T(8,128)(2,1)S(1)}, u32[]{:S(2)}, u32[]{:S(2)}) collective-permute-start(bf16[4,24,1152]{2,1,0:T(8,128)(2,1)S(1)} %get-tuple-element.46), channel_id=1, source_target_pairs={{0,24},{8,0},{16,8},{24,16},{1,25},{9,1},{17,9},{25,17},{2,26},{10... | collective-permute-start | bytes 663560 | tf_op jit(solution)/shard_map/ppermute | solution.py:175
  132.0 2.0 collective-permute-start.28
  133.9 10.3 %collective-permute-done.25 = bf16[512,768]{1,0:T(8,128)(2,1)S(1)} collective-permute-done((bf16[512,768]{1,0:T(8,128)(2,1)S(1)}, bf16[512,768]{1,0:T(8,128)(2,1)S(1)}, u32[]{:S(2)}, u32[]{:S(2)}) %collective-permute-start.25) | collective-permute-done | bytes 786464 | tf_op jit(solution)/shard_map/ppermute | solution.py:260
  144.2 1.1 add_convert_fusion
  146.1 2.6 %collective-permute-start.29 = (bf16[4,24,1152]{2,1,0:T(8,128)(2,1)S(1)}, bf16[4,24,1152]{2,1,0:T(8,128)(2,1)}, u32[]{:S(2)}, u32[]{:S(2)}) collective-permute-start(bf16[4,24,1152]{2,1,0:T(8,128)(2,1)S(1)} %add_convert_fusion.1), channel_id=1, source_target_pairs={{0,24},{8,0},{16,8},{24,16},{1,25},{9,1},{17,9},{25,17},{2,26},{10... | collective-permute-start | bytes 663560 | tf_op jit(solution)/shard_map/ppermute | solution.py:175
  148.7 2.4 %reshape.44 = bf16[128,4,768]{2,1,0:T(4,128)(2,1)} reshape(bf16[512,768]{1,0:T(8,128)(2,1)} %add_convert_fusion) | data formatting | bytes 1572864 | tf_op jit(solution)/shard_map/reshape | solution.py:266
  151.1 9.6 %all-to-all-start.1 = ((bf16[128,4,768]{2,1,0:T(4,128)(2,1)}), bf16[128,4,768]{2,1,0:T(4,128)(2,1)}, u32[]{:S(2)}, u32[]{:S(2)}) async-start(bf16[128,4,768]{2,1,0:T(4,128)(2,1)} %reshape.44), calls=%async_computation.1 | async-start | bytes 1572864 | tf_op jit(solution)/shard_map/all_to_all | solution.py:266
  160.7 1.4 convert_add_fusion.1
  162.3 1.0 collective-permute-start.31
  163.4 3.5 %collective-permute-start.32 = (bf16[4,12,1152]{2,1,0:T(8,128)(2,1)S(1)}, bf16[4,12,1152]{2,1,0:T(8,128)(2,1)S(1)}, u32[]{:S(2)}, u32[]{:S(2)}) collective-permute-start(bf16[4,12,1152]{2,1,0:T(8,128)(2,1)S(1)} %get-tuple-element.67), channel_id=1, source_target_pairs={{0,36},{4,32},{32,4},{36,0},{64,100},{68,96},{96,68},{100,64},{128... | collective-permute-start | bytes 331784 | tf_op jit(solution)/shard_map/ppermute | solution.py:179
  167.4 5.0 %collective-permute-done.31 = bf16[4,12,1152]{2,1,0:T(8,128)(2,1)S(1)} collective-permute-done((bf16[4,12,1152]{2,1,0:T(8,128)(2,1)S(1)}, bf16[4,12,1152]{2,1,0:T(8,128)(2,1)S(1)}, u32[]{:S(2)}, u32[]{:S(2)}) %collective-permute-start.31) | collective-permute-done | bytes 110624 | tf_op jit(solution)/shard_map/ppermute | solution.py:179
  172.4 10.3 %collective-permute-done.32 = bf16[4,12,1152]{2,1,0:T(8,128)(2,1)S(1)} collective-permute-done((bf16[4,12,1152]{2,1,0:T(8,128)(2,1)S(1)}, bf16[4,12,1152]{2,1,0:T(8,128)(2,1)S(1)}, u32[]{:S(2)}, u32[]{:S(2)}) %collective-permute-start.32) | collective-permute-done | bytes 110624 | tf_op jit(solution)/shard_map/ppermute | solution.py:179
  182.7 2.7 %collective-permute-done.30 = bf16[4,12,1152]{2,1,0:T(8,128)(2,1)S(1)} collective-permute-done((bf16[4,12,1152]{2,1,0:T(8,128)(2,1)S(1)}, bf16[4,12,1152]{2,1,0:T(8,128)(2,1)S(1)}, u32[]{:S(2)}, u32[]{:S(2)}) %collective-permute-start.30) | collective-permute-done | bytes 110624 | tf_op jit(solution)/shard_map/ppermute | solution.py:179
  185.6 2.5 %collective-permute-start.33 = (bf16[12,1152]{1,0:T(8,128)(2,1)S(1)}, bf16[12,1152]{1,0:T(8,128)(2,1)S(1)}, u32[]{:S(2)}, u32[]{:S(2)}) collective-permute-start(bf16[12,1152]{1,0:T(8,128)(2,1)S(1)} %get-tuple-element.72), channel_id=1, source_target_pairs={{0,64},{32,96},{64,0},{96,32},{128,192},{160,224},{192,128},{224,1... | collective-permute-start | bytes 82952 | tf_op jit(solution)/shard_map/ppermute | solution.py:179
  188.1 2.9 %collective-permute-start.35 = (bf16[12,1152]{1,0:T(8,128)(2,1)S(1)}, bf16[12,1152]{1,0:T(8,128)(2,1)S(1)}, u32[]{:S(2)}, u32[]{:S(2)}) collective-permute-start(bf16[12,1152]{1,0:T(8,128)(2,1)S(1)} %get-tuple-element.73), channel_id=1, source_target_pairs={{0,192},{32,224},{64,128},{96,160},{128,64},{160,96},{192,0},{224,... | collective-permute-start | bytes 82952 | tf_op jit(solution)/shard_map/ppermute | solution.py:179
  190.9 1.2 collective-permute-start.34
  192.1 2.3 %reshape.45 = bf16[1,512,768]{2,1,0:T(8,128)(2,1)} reshape(bf16[128,4,768]{2,1,0:T(4,128)(2,1)} %all-to-all-done.1) | data formatting | bytes 1572864 | tf_op jit(solution)/shard_map/reshape | solution.py:269
  194.4 4.4 %collective-permute-done.34 = bf16[12,1152]{1,0:T(8,128)(2,1)S(1)} collective-permute-done((bf16[12,1152]{1,0:T(8,128)(2,1)S(1)}, bf16[12,1152]{1,0:T(8,128)(2,1)S(1)}, u32[]{:S(2)}, u32[]{:S(2)}) %collective-permute-start.34) | collective-permute-done | bytes 27680 | tf_op jit(solution)/shard_map/ppermute | solution.py:179
  (117 shorter events, 17.7 us)
Async XLA Ops:
  0.6 9.8 %copy-start = (bf16[1,512,1536]{2,1,0:T(8,128)(2,1)S(1)}, bf16[1,512,1536]{2,1,0:T(8,128)(2,1)}, u32[]{:S(2)}) copy-start(bf16[1,512,1536]{2,1,0:T(8,128)(2,1)} %param.3) | copy-start | bytes 4718596
  0.6 9.8 %copy-start.17 = (bf16[12,3,384]{2,1,0:T(4,128)(2,1)S(1)}, bf16[12,3,384]{2,1,0:T(4,128)(2,1)}, u32[]{:S(2)}) copy-start(bf16[12,3,384]{2,1,0:T(4,128)(2,1)} %param.5) | copy-start | bytes 82948
  1.6 9.0 %collective-permute-start.2 = (bf16[12,1152]{1,0:T(8,128)(2,1)S(1)}, bf16[12,1152]{1,0:T(8,128)(2,1)S(1)}, u32[]{:S(2)}, u32[]{:S(2)}) collective-permute-start(bf16[12,1152]{1,0:T(8,128)(2,1)S(1)} %bitcast.49), channel_id=1, source_target_pairs={{0,192},{32,224},{64,128},{96,160},{128,64},{160,96},{192,0},{224,... | collective-permute-start | bytes 82952 | tf_op jit(solution)/shard_map/ppermute | solution.py:179
  8.0 8.4 %collective-permute-start.1 = (bf16[12,1152]{1,0:T(8,128)(2,1)S(1)}, bf16[12,1152]{1,0:T(8,128)(2,1)S(1)}, u32[]{:S(2)}, u32[]{:S(2)}) collective-permute-start(bf16[12,1152]{1,0:T(8,128)(2,1)S(1)} %bitcast.50), channel_id=1, source_target_pairs={{0,128},{32,160},{64,192},{96,224},{128,0},{160,32},{192,64},{224,... | collective-permute-start | bytes 82952 | tf_op jit(solution)/shard_map/ppermute | solution.py:179
  9.0 7.4 %collective-permute-start = (bf16[12,1152]{1,0:T(8,128)(2,1)S(1)}, bf16[12,1152]{1,0:T(8,128)(2,1)S(1)}, u32[]{:S(2)}, u32[]{:S(2)}) collective-permute-start(bf16[12,1152]{1,0:T(8,128)(2,1)S(1)} %bitcast.51), channel_id=1, source_target_pairs={{0,64},{32,96},{64,0},{96,32},{128,192},{160,224},{192,128},{224,1... | collective-permute-start | bytes 82952 | tf_op jit(solution)/shard_map/ppermute | solution.py:179
  10.5 8.4 %copy-start.15 = (bf16[1,12,1152]{2,1,0:T(8,128)(2,1)}, bf16[1,12,1152]{2,1,0:T(8,128)(2,1)S(1)}, u32[]{:S(2)}) copy-start(bf16[1,12,1152]{2,1,0:T(8,128)(2,1)S(1)} %stack_reshape.3) | copy-start | bytes 82948
  17.0 17.6 %collective-permute-start.5 = (bf16[4,12,1152]{2,1,0:T(8,128)(2,1)}, bf16[4,12,1152]{2,1,0:T(8,128)(2,1)}, u32[]{:S(2)}, u32[]{:S(2)}) collective-permute-start(bf16[4,12,1152]{2,1,0:T(8,128)(2,1)} %pad_maximum_fusion.4), channel_id=1, source_target_pairs={{0,36},{4,32},{32,4},{36,0},{64,100},{68,96},{96,68},{100,64},{128... | collective-permute-start | bytes 331784 | tf_op jit(solution)/shard_map/ppermute | solution.py:179
  19.0 15.7 %collective-permute-start.4 = (bf16[4,12,1152]{2,1,0:T(8,128)(2,1)}, bf16[4,12,1152]{2,1,0:T(8,128)(2,1)}, u32[]{:S(2)}, u32[]{:S(2)}) collective-permute-start(bf16[4,12,1152]{2,1,0:T(8,128)(2,1)} %pad_maximum_fusion.4), channel_id=1, source_target_pairs={{0,32},{4,36},{32,0},{36,4},{64,96},{68,100},{96,64},{100,68},{128... | collective-permute-start | bytes 331784 | tf_op jit(solution)/shard_map/ppermute | solution.py:179
  22.3 21.0 %copy-start.16 = (bf16[1,12,1152]{2,1,0:T(8,128)(2,1)S(1)}, bf16[1,12,1152]{2,1,0:T(8,128)(2,1)}, u32[]{:S(2)}) copy-start(bf16[1,12,1152]{2,1,0:T(8,128)(2,1)} %copy-done.15) | copy-start | bytes 82948
  22.3 21.0 %copy-start.19 = (bf16[12,1152]{1,0:T(8,128)(2,1)S(1)}, bf16[12,1152]{1,0:T(8,128)(2,1)}, u32[]{:S(2)}) copy-start(bf16[12,1152]{1,0:T(8,128)(2,1)} %copy-done.18) | copy-start | bytes 82948
  22.3 21.0 %copy-start.21 = (bf16[12,1152]{1,0:T(8,128)(2,1)S(1)}, bf16[12,1152]{1,0:T(8,128)(2,1)}, u32[]{:S(2)}) copy-start(bf16[12,1152]{1,0:T(8,128)(2,1)} %copy-done.20) | copy-start | bytes 82948
  22.3 21.0 %copy-start.23 = (bf16[12,1152]{1,0:T(8,128)(2,1)S(1)}, bf16[12,1152]{1,0:T(8,128)(2,1)}, u32[]{:S(2)}) copy-start(bf16[12,1152]{1,0:T(8,128)(2,1)} %copy-done.22) | copy-start | bytes 82948
  22.3 43.3 %all-to-all-start = ((bf16[128,4,1152]{2,1,0:T(4,128)(2,1)}), bf16[128,4,1152]{2,1,0:T(4,128)(2,1)S(1)}, u32[]{:S(2)}, u32[]{:S(2)}) async-start(bf16[128,4,1152]{2,1,0:T(4,128)(2,1)} %reshape.40), calls=%async_computation | async-start | bytes 2359296 | tf_op jit(solution)/shard_map/all_to_all | solution.py:242
  33.7 9.6 %collective-permute-start.3 = (bf16[4,12,1152]{2,1,0:T(8,128)(2,1)}, bf16[4,12,1152]{2,1,0:T(8,128)(2,1)S(1)}, u32[]{:S(2)}, u32[]{:S(2)}) collective-permute-start(bf16[4,12,1152]{2,1,0:T(8,128)(2,1)} %pad_maximum_fusion.4), channel_id=1, source_target_pairs={{0,4},{4,0},{32,36},{36,32},{64,68},{68,64},{96,100},{100,96},{128... | collective-permute-start | bytes 331784 | tf_op jit(solution)/shard_map/ppermute | solution.py:179
  43.5 49.2 %copy-start.1 = (bf16[2,2,24,1152]{3,2,1,0:T(8,128)(2,1)}, bf16[2,2,24,1152]{3,2,1,0:T(8,128)(2,1)S(1)}, u32[]{:S(2)}) copy-start(bf16[2,2,24,1152]{3,2,1,0:T(8,128)(2,1)S(1)} %copy.8) | copy-start | bytes 663556
  65.6 14.4 %copy-start.13 = (bf16[128,4,1152]{2,1,0:T(4,128)(2,1)}, bf16[128,4,1152]{2,1,0:T(4,128)(2,1)S(1)}, u32[]{:S(2)}) copy-start(bf16[128,4,1152]{2,1,0:T(4,128)(2,1)S(1)} %all-to-all-done) | copy-start | bytes 3538948
  66.7 10.1 %collective-permute-start.6 = (bf16[64,4,768]{2,1,0:T(4,128)(2,1)S(1)}, bf16[64,4,768]{2,1,0:T(4,128)(2,1)S(1)}, u32[]{:S(2)}, u32[]{:S(2)}) collective-permute-start(bf16[64,4,768]{2,1,0:T(4,128)(2,1)S(1)} %get-tuple-element.63), channel_id=1, source_target_pairs={{0,1},{1,0},{2,3},{3,2},{4,5},{5,4},{6,7},{7,6},{8,9},{9,8},{10,11... | collective-permute-start | bytes 1179656 | tf_op jit(solution)/shard_map/ppermute | solution.py:244
  66.8 33.5 %copy-start.3 = (bf16[2,2,24,1152]{3,2,1,0:T(8,128)(2,1)}, bf16[2,2,24,1152]{3,2,1,0:T(8,128)(2,1)S(1)}, u32[]{:S(2)}) copy-start(bf16[2,2,24,1152]{3,2,1,0:T(8,128)(2,1)S(1)} %copy.7) | copy-start | bytes 663556
  76.8 8.0 %collective-permute-start.7 = (bf16[4,24,1152]{2,1,0:T(8,128)(2,1)S(1)}, bf16[4,24,1152]{2,1,0:T(8,128)(2,1)}, u32[]{:S(2)}, u32[]{:S(2)}) collective-permute-start(bf16[4,24,1152]{2,1,0:T(8,128)(2,1)S(1)} %bitcast.38), channel_id=1, source_target_pairs={{0,8},{8,16},{16,24},{24,0},{1,9},{9,17},{17,25},{25,1},{2,10},{10... | collective-permute-start | bytes 663560 | tf_op jit(solution)/shard_map/ppermute | solution.py:175
  78.1 7.4 %collective-permute-start.8 = (bf16[4,24,1152]{2,1,0:T(8,128)(2,1)S(1)}, bf16[4,24,1152]{2,1,0:T(8,128)(2,1)}, u32[]{:S(2)}, u32[]{:S(2)}) collective-permute-start(bf16[4,24,1152]{2,1,0:T(8,128)(2,1)S(1)} %bitcast.34), channel_id=1, source_target_pairs={{0,24},{8,0},{16,8},{24,16},{1,25},{9,1},{17,9},{25,17},{2,26},{10... | collective-permute-start | bytes 663560 | tf_op jit(solution)/shard_map/ppermute | solution.py:175
  80.0 12.7 %collective-permute-start.11 = (bf16[64,4,768]{2,1,0:T(4,128)(2,1)}, bf16[64,4,768]{2,1,0:T(4,128)(2,1)}, u32[]{:S(2)}, u32[]{:S(2)}) collective-permute-start(bf16[64,4,768]{2,1,0:T(4,128)(2,1)} %get-tuple-element.37), channel_id=1, source_target_pairs={{0,1},{1,0},{2,3},{3,2},{4,5},{5,4},{6,7},{7,6},{8,9},{9,8},{10,11... | collective-permute-start | bytes 1179656 | tf_op jit(solution)/shard_map/ppermute | solution.py:246
  82.7 8.4 %collective-permute-start.12 = (bf16[4,24,1152]{2,1,0:T(8,128)(2,1)S(1)}, bf16[4,24,1152]{2,1,0:T(8,128)(2,1)S(1)}, u32[]{:S(2)}, u32[]{:S(2)}) collective-permute-start(bf16[4,24,1152]{2,1,0:T(8,128)(2,1)S(1)} %bitcast.39), channel_id=1, source_target_pairs={{0,24},{8,0},{16,8},{24,16},{1,25},{9,1},{17,9},{25,17},{2,26},{10... | collective-permute-start | bytes 663560 | tf_op jit(solution)/shard_map/ppermute | solution.py:175
  85.6 7.5 %collective-permute-start.9 = (bf16[4,24,1152]{2,1,0:T(8,128)(2,1)}, bf16[4,24,1152]{2,1,0:T(8,128)(2,1)}, u32[]{:S(2)}, u32[]{:S(2)}) collective-permute-start(bf16[4,24,1152]{2,1,0:T(8,128)(2,1)} %collective-permute-done.7.refs_8_), channel_id=1, source_target_pairs={{0,8},{8,16},{16,24},{24,0},{1,9},{9,17},{17,25},{25,1},{2,10},{10... | collective-permute-start | bytes 663560 | tf_op jit(solution)/shard_map/ppermute | solution.py:175
  88.1 6.4 %collective-permute-start.10 = (bf16[4,24,1152]{2,1,0:T(8,128)(2,1)}, bf16[4,24,1152]{2,1,0:T(8,128)(2,1)}, u32[]{:S(2)}, u32[]{:S(2)}) collective-permute-start(bf16[4,24,1152]{2,1,0:T(8,128)(2,1)} %collective-permute-done.8.refs_5_), channel_id=1, source_target_pairs={{0,24},{8,0},{16,8},{24,16},{1,25},{9,1},{17,9},{25,17},{2,26},{10... | collective-permute-start | bytes 663560 | tf_op jit(solution)/shard_map/ppermute | solution.py:175
  88.8 5.6 %collective-permute-start.14 = (bf16[4,24,1152]{2,1,0:T(8,128)(2,1)S(1)}, bf16[4,24,1152]{2,1,0:T(8,128)(2,1)S(1)}, u32[]{:S(2)}, u32[]{:S(2)}) collective-permute-start(bf16[4,24,1152]{2,1,0:T(8,128)(2,1)S(1)} %bitcast.40), channel_id=1, source_target_pairs={{0,2},{2,0},{1,3},{3,1},{4,6},{6,4},{5,7},{7,5},{8,10},{10,8},{9,1... | collective-permute-start | bytes 663560 | tf_op jit(solution)/shard_map/ppermute | solution.py:258
  91.1 7.2 %collective-permute-start.13 = (bf16[4,24,1152]{2,1,0:T(8,128)(2,1)S(1)}, bf16[4,24,1152]{2,1,0:T(8,128)(2,1)}, u32[]{:S(2)}, u32[]{:S(2)}) collective-permute-start(bf16[4,24,1152]{2,1,0:T(8,128)(2,1)S(1)} %bitcast.35), channel_id=1, source_target_pairs={{0,8},{8,16},{16,24},{24,0},{1,9},{9,17},{17,25},{25,1},{2,10},{10... | collective-permute-start | bytes 663560 | tf_op jit(solution)/shard_map/ppermute | solution.py:175
  92.7 5.7 %collective-permute-start.15 = (bf16[4,24,1152]{2,1,0:T(8,128)(2,1)S(1)}, bf16[4,24,1152]{2,1,0:T(8,128)(2,1)S(1)}, u32[]{:S(2)}, u32[]{:S(2)}) collective-permute-start(bf16[4,24,1152]{2,1,0:T(8,128)(2,1)S(1)} %bitcast.36), channel_id=1, source_target_pairs={{0,2},{2,0},{1,3},{3,1},{4,6},{6,4},{5,7},{7,5},{8,10},{10,8},{9,1... | collective-permute-start | bytes 663560 | tf_op jit(solution)/shard_map/ppermute | solution.py:258
  93.0 6.6 %collective-permute-start.16 = (bf16[4,24,1152]{2,1,0:T(8,128)(2,1)S(1)}, bf16[4,24,1152]{2,1,0:T(8,128)(2,1)S(1)}, u32[]{:S(2)}, u32[]{:S(2)}) collective-permute-start(bf16[4,24,1152]{2,1,0:T(8,128)(2,1)S(1)} %collective-permute-done.12.refs_4_), channel_id=1, source_target_pairs={{0,2},{2,0},{1,3},{3,1},{4,6},{6,4},{5,7},{7,5},{8,10},{10,8},{9,1... | collective-permute-start | bytes 663560 | tf_op jit(solution)/shard_map/ppermute | solution.py:258
  94.4 8.2 %collective-permute-start.20 = (bf16[4,24,1152]{2,1,0:T(8,128)(2,1)}, bf16[4,24,1152]{2,1,0:T(8,128)(2,1)}, u32[]{:S(2)}, u32[]{:S(2)}) collective-permute-start(bf16[4,24,1152]{2,1,0:T(8,128)(2,1)} %collective-permute-done.7.refs_8_), channel_id=1, source_target_pairs={{0,2},{2,0},{1,3},{3,1},{4,6},{6,4},{5,7},{7,5},{8,10},{10,8},{9,1... | collective-permute-start | bytes 663560 | tf_op jit(solution)/shard_map/ppermute | solution.py:258
  95.1 7.5 %collective-permute-start.17 = (bf16[4,24,1152]{2,1,0:T(8,128)(2,1)}, bf16[4,24,1152]{2,1,0:T(8,128)(2,1)}, u32[]{:S(2)}, u32[]{:S(2)}) collective-permute-start(bf16[4,24,1152]{2,1,0:T(8,128)(2,1)} %collective-permute-done.8.refs_5_), channel_id=1, source_target_pairs={{0,2},{2,0},{1,3},{3,1},{4,6},{6,4},{5,7},{7,5},{8,10},{10,8},{9,1... | collective-permute-start | bytes 663560 | tf_op jit(solution)/shard_map/ppermute | solution.py:258
  98.4 4.2 %collective-permute-start.21 = (bf16[4,24,1152]{2,1,0:T(8,128)(2,1)}, bf16[4,24,1152]{2,1,0:T(8,128)(2,1)}, u32[]{:S(2)}, u32[]{:S(2)}) collective-permute-start(bf16[4,24,1152]{2,1,0:T(8,128)(2,1)} %collective-permute-done.13.refs_9_), channel_id=1, source_target_pairs={{0,2},{2,0},{1,3},{3,1},{4,6},{6,4},{5,7},{7,5},{8,10},{10,8},{9,1... | collective-permute-start | bytes 663560 | tf_op jit(solution)/shard_map/ppermute | solution.py:258
  99.1 3.5 %collective-permute-start.18 = (bf16[4,24,1152]{2,1,0:T(8,128)(2,1)}, bf16[4,24,1152]{2,1,0:T(8,128)(2,1)}, u32[]{:S(2)}, u32[]{:S(2)}) collective-permute-start(bf16[4,24,1152]{2,1,0:T(8,128)(2,1)} %collective-permute-done.9.refs_6_), channel_id=1, source_target_pairs={{0,2},{2,0},{1,3},{3,1},{4,6},{6,4},{5,7},{7,5},{8,10},{10,8},{9,1... | collective-permute-start | bytes 663560 | tf_op jit(solution)/shard_map/ppermute | solution.py:258
  100.3 2.3 %collective-permute-start.19 = (bf16[4,24,1152]{2,1,0:T(8,128)(2,1)}, bf16[4,24,1152]{2,1,0:T(8,128)(2,1)}, u32[]{:S(2)}, u32[]{:S(2)}) collective-permute-start(bf16[4,24,1152]{2,1,0:T(8,128)(2,1)} %collective-permute-done.10.refs_7_), channel_id=1, source_target_pairs={{0,2},{2,0},{1,3},{3,1},{4,6},{6,4},{5,7},{7,5},{8,10},{10,8},{9,1... | collective-permute-start | bytes 663560 | tf_op jit(solution)/shard_map/ppermute | solution.py:258
  124.1 3.9 %collective-permute-start.22 = (bf16[4,8,24,1152]{3,2,1,0:T(8,128)(2,1)S(1)}, bf16[4,8,24,1152]{3,2,1,0:T(8,128)(2,1)S(1)}, u32[]{:S(2)}, u32[]{:S(2)}) collective-permute-start(bf16[4,8,24,1152]{3,2,1,0:T(8,128)(2,1)S(1)} %get-tuple-element.42), channel_id=1, source_target_pairs={{0,2},{2,0},{1,3},{3,1},{4,6},{6,4},{5,7},{7,5},{8,10},{10,8},{9,1... | collective-permute-start | bytes 5308424 | tf_op jit(solution)/shard_map/ppermute | solution.py:200
  124.6 19.5 %collective-permute-start.25 = (bf16[512,768]{1,0:T(8,128)(2,1)S(1)}, bf16[512,768]{1,0:T(8,128)(2,1)S(1)}, u32[]{:S(2)}, u32[]{:S(2)}) collective-permute-start(bf16[512,768]{1,0:T(8,128)(2,1)S(1)} %get-tuple-element.47), channel_id=1, source_target_pairs={{0,1},{1,0},{2,3},{3,2},{4,5},{5,4},{6,7},{7,6},{8,9},{9,8},{10,11... | collective-permute-start | bytes 2359304 | tf_op jit(solution)/shard_map/ppermute | solution.py:260
  128.4 15.8 %collective-permute-start.23 = (bf16[4,24,1152]{2,1,0:T(8,128)(2,1)S(1)}, bf16[4,24,1152]{2,1,0:T(8,128)(2,1)S(1)}, u32[]{:S(2)}, u32[]{:S(2)}) collective-permute-start(bf16[4,24,1152]{2,1,0:T(8,128)(2,1)S(1)} %get-tuple-element.45), channel_id=1, source_target_pairs={{0,8},{8,16},{16,24},{24,0},{1,9},{9,17},{17,25},{25,1},{2,10},{10... | collective-permute-start | bytes 663560 | tf_op jit(solution)/shard_map/ppermute | solution.py:175
  129.3 14.9 %collective-permute-start.24 = (bf16[4,24,1152]{2,1,0:T(8,128)(2,1)S(1)}, bf16[4,24,1152]{2,1,0:T(8,128)(2,1)S(1)}, u32[]{:S(2)}, u32[]{:S(2)}) collective-permute-start(bf16[4,24,1152]{2,1,0:T(8,128)(2,1)S(1)} %get-tuple-element.46), channel_id=1, source_target_pairs={{0,24},{8,0},{16,8},{24,16},{1,25},{9,1},{17,9},{25,17},{2,26},{10... | collective-permute-start | bytes 663560 | tf_op jit(solution)/shard_map/ppermute | solution.py:175
  131.9 28.8 %collective-permute-start.27 = (bf16[4,24,1152]{2,1,0:T(8,128)(2,1)S(1)}, bf16[4,24,1152]{2,1,0:T(8,128)(2,1)}, u32[]{:S(2)}, u32[]{:S(2)}) collective-permute-start(bf16[4,24,1152]{2,1,0:T(8,128)(2,1)S(1)} %get-tuple-element.54), channel_id=1, source_target_pairs={{0,24},{8,0},{16,8},{24,16},{1,25},{9,1},{17,9},{25,17},{2,26},{10... | collective-permute-start | bytes 663560 | tf_op jit(solution)/shard_map/ppermute | solution.py:175
  132.0 28.7 %collective-permute-start.28 = (bf16[4,24,1152]{2,1,0:T(8,128)(2,1)S(1)}, bf16[4,24,1152]{2,1,0:T(8,128)(2,1)}, u32[]{:S(2)}, u32[]{:S(2)}) collective-permute-start(bf16[4,24,1152]{2,1,0:T(8,128)(2,1)S(1)} %get-tuple-element.55), channel_id=1, source_target_pairs={{0,8},{8,16},{16,24},{24,0},{1,9},{9,17},{17,25},{25,1},{2,10},{10... | collective-permute-start | bytes 663560 | tf_op jit(solution)/shard_map/ppermute | solution.py:175
  145.4 15.3 %collective-permute-start.26 = (bf16[4,24,1152]{2,1,0:T(8,128)(2,1)S(1)}, bf16[4,24,1152]{2,1,0:T(8,128)(2,1)}, u32[]{:S(2)}, u32[]{:S(2)}) collective-permute-start(bf16[4,24,1152]{2,1,0:T(8,128)(2,1)S(1)} %add_convert_fusion.2), channel_id=1, source_target_pairs={{0,8},{8,16},{16,24},{24,0},{1,9},{9,17},{17,25},{25,1},{2,10},{10... | collective-permute-start | bytes 663560 | tf_op jit(solution)/shard_map/ppermute | solution.py:175
  146.1 14.6 %collective-permute-start.29 = (bf16[4,24,1152]{2,1,0:T(8,128)(2,1)S(1)}, bf16[4,24,1152]{2,1,0:T(8,128)(2,1)}, u32[]{:S(2)}, u32[]{:S(2)}) collective-permute-start(bf16[4,24,1152]{2,1,0:T(8,128)(2,1)S(1)} %add_convert_fusion.1), channel_id=1, source_target_pairs={{0,24},{8,0},{16,8},{24,16},{1,25},{9,1},{17,9},{25,17},{2,26},{10... | collective-permute-start | bytes 663560 | tf_op jit(solution)/shard_map/ppermute | solution.py:175
  151.1 34.4 %all-to-all-start.1 = ((bf16[128,4,768]{2,1,0:T(4,128)(2,1)}), bf16[128,4,768]{2,1,0:T(4,128)(2,1)}, u32[]{:S(2)}, u32[]{:S(2)}) async-start(bf16[128,4,768]{2,1,0:T(4,128)(2,1)} %reshape.44), calls=%async_computation.1 | async-start | bytes 1572864 | tf_op jit(solution)/shard_map/all_to_all | solution.py:266
  162.3 10.1 %collective-permute-start.31 = (bf16[4,12,1152]{2,1,0:T(8,128)(2,1)S(1)}, bf16[4,12,1152]{2,1,0:T(8,128)(2,1)S(1)}, u32[]{:S(2)}, u32[]{:S(2)}) collective-permute-start(bf16[4,12,1152]{2,1,0:T(8,128)(2,1)S(1)} %get-tuple-element.66), channel_id=1, source_target_pairs={{0,4},{4,0},{32,36},{36,32},{64,68},{68,64},{96,100},{100,96},{128... | collective-permute-start | bytes 331784 | tf_op jit(solution)/shard_map/ppermute | solution.py:179
  163.4 19.3 %collective-permute-start.32 = (bf16[4,12,1152]{2,1,0:T(8,128)(2,1)S(1)}, bf16[4,12,1152]{2,1,0:T(8,128)(2,1)S(1)}, u32[]{:S(2)}, u32[]{:S(2)}) collective-permute-start(bf16[4,12,1152]{2,1,0:T(8,128)(2,1)S(1)} %get-tuple-element.67), channel_id=1, source_target_pairs={{0,36},{4,32},{32,4},{36,0},{64,100},{68,96},{96,68},{100,64},{128... | collective-permute-start | bytes 331784 | tf_op jit(solution)/shard_map/ppermute | solution.py:179
  166.9 18.6 %collective-permute-start.30 = (bf16[4,12,1152]{2,1,0:T(8,128)(2,1)S(1)}, bf16[4,12,1152]{2,1,0:T(8,128)(2,1)S(1)}, u32[]{:S(2)}, u32[]{:S(2)}) collective-permute-start(bf16[4,12,1152]{2,1,0:T(8,128)(2,1)S(1)} %slice.89), channel_id=1, source_target_pairs={{0,32},{4,36},{32,0},{36,4},{64,96},{68,100},{96,64},{100,68},{128... | collective-permute-start | bytes 331784 | tf_op jit(solution)/shard_map/ppermute | solution.py:179
  185.6 8.8 %collective-permute-start.33 = (bf16[12,1152]{1,0:T(8,128)(2,1)S(1)}, bf16[12,1152]{1,0:T(8,128)(2,1)S(1)}, u32[]{:S(2)}, u32[]{:S(2)}) collective-permute-start(bf16[12,1152]{1,0:T(8,128)(2,1)S(1)} %get-tuple-element.72), channel_id=1, source_target_pairs={{0,64},{32,96},{64,0},{96,32},{128,192},{160,224},{192,128},{224,1... | collective-permute-start | bytes 82952 | tf_op jit(solution)/shard_map/ppermute | solution.py:179
  188.1 6.4 %collective-permute-start.35 = (bf16[12,1152]{1,0:T(8,128)(2,1)S(1)}, bf16[12,1152]{1,0:T(8,128)(2,1)S(1)}, u32[]{:S(2)}, u32[]{:S(2)}) collective-permute-start(bf16[12,1152]{1,0:T(8,128)(2,1)S(1)} %get-tuple-element.73), channel_id=1, source_target_pairs={{0,192},{32,224},{64,128},{96,160},{128,64},{160,96},{192,0},{224,... | collective-permute-start | bytes 82952 | tf_op jit(solution)/shard_map/ppermute | solution.py:179
  190.9 7.9 %collective-permute-start.34 = (bf16[12,1152]{1,0:T(8,128)(2,1)S(1)}, bf16[12,1152]{1,0:T(8,128)(2,1)S(1)}, u32[]{:S(2)}, u32[]{:S(2)}) collective-permute-start(bf16[12,1152]{1,0:T(8,128)(2,1)S(1)} %get-tuple-element.74), channel_id=1, source_target_pairs={{0,128},{32,160},{64,192},{96,224},{128,0},{160,32},{192,64},{224,... | collective-permute-start | bytes 82952 | tf_op jit(solution)/shard_map/ppermute | solution.py:179
  (14 other events, 25.3 us)

commit v9 on v8

--- a/solution.py
+++ b/solution.py
@@ -19,11 +19,9 @@
     return lax.dot_general(a, b, dims, preferred_element_type=f32)
 
 
-def core_kernel(where_ref, t_ref, *refs):
-    parts, pieces = refs[:2], refs[2:18]
-    give_ref, keep_ref, mine_ref, rest_ref, w_ref, s_ref, d_ref, g_ref, o_ref = refs[18:]
-    for i, part in enumerate(parts):
-        o_ref[i * part.shape[0] : (i + 1) * part.shape[0]] = part[...]
+def core_kernel(where_ref, t_ref, o_ref, *refs):
+    pieces = refs[:16]
+    give_ref, keep_ref, mine_ref, rest_ref, w_ref, s_ref, d_ref, g_ref = refs[16:]
     z, y, c, m = (where_ref[i] for i in range(4))
     unit = XH * C * ROWS
 
@@ -102,8 +100,8 @@
                 rest_ref[by, t] = jnp.where(c == 0, second, first).astype(bf16)
 
 
-def core(where, tokens, others, own, other):
-    rows, part_cols = tokens.shape[0], others[0].shape[1]
+def core(where, tokens, others, mine, rest):
+    rows, part_cols = others.shape
     half = tokens.shape[1] - part_cols
     width, n = MP * part_cols, 3 * half
     vm = pl.BlockSpec(memory_space=pltpu.VMEM)
@@ -115,21 +113,20 @@
             jax.ShapeDtypeStruct((Y, Z, XH * ROWS, n), bf16),
             jax.ShapeDtypeStruct((Y, Z, XH * ROWS, n), bf16),
         ),
-        in_specs=[pl.BlockSpec(memory_space=pltpu.SMEM)] + [vm] * 19,
+        in_specs=[pl.BlockSpec(memory_space=pltpu.SMEM)] + [vm] * 18,
         out_specs=(vm,) * 4,
         scratch_shapes=[
             pltpu.VMEM((width, n), bf16),
             pltpu.VMEM((4 * half // 128, rows, 128), f32),
             pltpu.VMEM((3 * half // 128, rows, 128), f32),
             pltpu.VMEM((rows, n), bf16),
-            pltpu.VMEM((rows, part_cols), bf16),
         ],
         compiler_params=pltpu.CompilerParams(vmem_limit_bytes=VMEM_LIMIT),
         cost_estimate=pl.CostEstimate(
             flops=6 * rows * width * n, bytes_accessed=8 * 2**20, transcendentals=0
         ),
         name="attention_core",
-    )(where, tokens, *others, *own, *other)
+    )(where, tokens, others, *mine, *rest)
 
 
 def combine_kernel(mine_ref, other_ref, *refs):
@@ -167,6 +164,25 @@
     )(mine, other)
 
 
+def add_kernel(a_ref, b_ref, o_ref):
+    total = a_ref[...].astype(f32) + b_ref[...].astype(f32)
+    o_ref[...] = total.reshape(o_ref.shape).astype(bf16)
+
+
+def add_parts(a, b):
+    rows, cols = a.shape
+    vm = pl.BlockSpec(memory_space=pltpu.VMEM)
+    return pl.pallas_call(
+        add_kernel,
+        out_shape=jax.ShapeDtypeStruct((F, rows // F, cols), bf16),
+        in_specs=[vm, vm],
+        out_specs=vm,
+        compiler_params=pltpu.CompilerParams(vmem_limit_bytes=16 * 2**20),
+        cost_estimate=pl.CostEstimate(flops=0, bytes_accessed=2**20, transcendentals=0),
+        name="add_parts",
+    )(a, b)
+
+
 FR = ("z", "y", "xh", "c")
 PAIR = [(0, 1), (1, 0)]
 
@@ -182,15 +198,18 @@
 ZX = ("z", "xh")
 
 
-def over_z(w):
+def far_z(w):
+    return jnp.stack([w] + [across(w, "z", Z, 2 * i) for i in range(1, Z // 2)], 0)
+
+
+def near_zx(own):
     even = lax.axis_index("xh") == 0
-    own = jnp.stack([w] + [across(w, "z", Z, 2 * i) for i in range(1, Z // 2)], 0)
     a, b, d = (across(own, ZX, Z * XH, by) for by in (1, 2, 3))
 
     def part(at):
         first = jnp.concatenate([jnp.where(even, own, a)[at], jnp.where(even, a, own)[at]], 1)
         second = jnp.concatenate([jnp.where(even, b, d)[at], jnp.where(even, d, b)[at]], 1)
-        return jnp.stack([first, second], 1).reshape(Z // 2, XH * ROWS, w.shape[1])
+        return jnp.stack([first, second], 1).reshape(Z // 2, XH * ROWS, own.shape[2])
 
     return part(slice(0, 2)), part(slice(2, 4))
 
@@ -238,12 +257,13 @@
     part = lax.dynamic_slice_in_dim(normed, m * cols, cols, 2)
     tokens = jnp.concatenate([part, out_grad], axis=2).reshape(F, count, cols + half)
 
-    low, high = over_z(w_qkv.reshape(w_qkv.shape[0], n))
+    rows = far_z(w_qkv.reshape(w_qkv.shape[0], n))
+    tokens, rows = lax.optimization_barrier((tokens, rows))
     tokens = lax.all_to_all(tokens, FR, 0, 0, tiled=True)
-    first, second = tokens[: F // 2, :, :cols], tokens[F // 2 :, :, :cols]
-    first = lax.ppermute(first, "mp", PAIR)
-    low, high, first, second = lax.optimization_barrier((low, high, first, second))
-    second = lax.ppermute(second, "mp", PAIR)
+    low, high = near_zx(rows)
+    part = tokens[:, :, :cols]
+    low, high, part = lax.optimization_barrier((low, high, part))
+    others = lax.ppermute(part, "mp", PAIR)
     before_low = shift(low, "y", Y, 1)
     after_high = shift(high, "y", Y, Y - 1)
     before_high = shift(high, "y", Y, 1)
@@ -252,18 +272,21 @@
     before_low, after_high, tokens = lax.optimization_barrier((before_low, after_high, tokens))
     far_low = shift(before_low, "y", Y, 1)
     far_high = shift(after_high, "y", Y, Y - 1)
-    far_low, far_high, second = lax.optimization_barrier((far_low, far_high, second))
-    others = [x.reshape(F // 2 * count, cols) for x in (first, second)]
-    own = [low, high, after_low, after_high, far_low, far_high, before_low, before_high]
-    other = [lax.ppermute(x, "c", PAIR) for x in own]
-    give, keep, mine, rest = core(where, tokens, others, own, other)
+    mine = [low, high, after_low, after_high, far_low, far_high, before_low, before_high]
+    others = others.reshape(F * count, cols)
+    rest = {i: lax.ppermute(mine[i], "c", PAIR) for i in (0, 1, 2, 3, 6, 7)}
+    mine, others = lax.optimization_barrier((mine, others))
+    rest.update({i: lax.ppermute(mine[i], "c", PAIR) for i in (4, 5)})
+
+    rest = [rest[i] for i in range(8)]
+    give, keep, mine, rest = core(where, tokens, others, mine, rest)
     got = lax.ppermute(give, "mp", PAIR)
 
     def finish(got):
-        return (keep.astype(f32) + got.astype(f32)).astype(bf16)
+        return add_parts(keep, got)
 
     def to_frames(x):
-        return lax.all_to_all(x.reshape(F, count, cols), FR, 0, 0, tiled=True)
+        return lax.all_to_all(x, FR, 0, 0, tiled=True)
 
     weight_grad, back = reduce_weight(mine, rest, got, finish, to_frames)
     input_grad = back.reshape(frames_dev, patches, cols)

time: 201 us -> 181 us (0.900)
  waiting for transfers between devices: 87.5 us -> 77.5 us
  local copies, waits for them, and re-layouts: 21.8 us -> 13.5 us
  other arithmetic: 5.95 us -> 2.2 us
    ppermute x12, waiting for transfers between devices: 35.8 us -> 26.3 us  [across(): return lax.ppermute(x, axis, [(i, i ^ by) for i in range(size)])]
    all_to_all x1, waiting for transfers between devices: 22.1 us -> 30.1 us  [on_device(): tokens = lax.all_to_all(tokens, FR, 0, 0, tiled=True)]
    unnamed x50 -> x14, local copies, waits for them, and re-layouts: 9.34 us -> 2.55 us
    ppermute x10 -> x9, waiting for transfers between devices: 9.97 us -> 5.12 us  [the longest x1 3.46 us: on_device(): others = lax.ppermute(part, 'mp', PAIR)]
    ppermute x12, waiting for transfers between devices: 7.48 us -> 3.11 us  [shift(): return lax.ppermute(x, axis, [(i, (i + by) % size) for i in range(size)])]
    reshape x3 -> x1, local copies, waits for them, and re-layouts: 4.56 us -> 1.56 us  [on_device(): others = others.reshape(F * count, cols)]
  transfers between devices with their start and end apart: 38 -> 37, of which waited for: 16 -> 16; matrix products, arithmetic and copies ran while one was open for 8% -> 6% of each run, Pallas kernels for 0% -> 1%
where the time goes in v9:
time: 181 us; the launch traced here: 180 us
  waiting for transfers between devices  77.5 us (43%)
  starting transfers between devices  68.3 us (38%)
  Pallas kernels  17.7 us (10%)
  local copies, waits for them, and re-layouts  13.5 us (7%)
  other arithmetic  2.2 us (1%)
    all_to_all x1, waiting for transfers between devices, on_device(): tokens = lax.all_to_all(tokens, FR, 0, 0, tiled=True)  30.1 us
    ppermute x12, waiting for transfers between devices, across(): return lax.ppermute(x, axis, [(i, i ^ by) for i in range(size)])  26.3 us
    ppermute x12, starting transfers between devices, across(): return lax.ppermute(x, axis, [(i, i ^ by) for i in range(size)])  25.6 us
    ppermute x12, starting transfers between devices, shift(): return lax.ppermute(x, axis, [(i, (i + by) % size) for i in range(size)])  17.6 us
    pallas_call x1, Pallas kernels, core(): pl.pallas_call(core_kernel, out_shape=(jax.ShapeDtypeStruct((rows, part_c...  16.1 us
    all_to_all x1, starting transfers between devices, on_device(): tokens = lax.all_to_all(tokens, FR, 0, 0, tiled=True)  11.2 us
    ppermute x1, waiting for transfers between devices, on_device(): got = lax.ppermute(give, 'mp', PAIR)  10.5 us
    all_to_all x1, starting transfers between devices, to_frames(): return lax.all_to_all(x, FR, 0, 0, tiled=True)  9.49 us
  transfers between devices with their start and end apart: 37, of which 16 were waited for; matrix products, arithmetic and copies ran while one was open for 6% of the time, Pallas kernels for 1%

profile of v9, /device:TPU:6, one launch (start us, length us, event | category | flops | bytes accessed | tf_op | source)
XLA Modules:
  0.0 180.2 jit_solution(11254929241095225988)
XLA Ops:
  0.7 0.9 pad.26
  1.6 6.4 %collective-permute-start.2 = (bf16[12,1152]{1,0:T(8,128)(2,1)S(1)}, bf16[12,1152]{1,0:T(8,128)(2,1)S(1)}, u32[]{:S(2)}, u32[]{:S(2)}) collective-permute-start(bf16[12,1152]{1,0:T(8,128)(2,1)S(1)} %bitcast.38), channel_id=1, source_target_pairs={{0,192},{32,224},{64,128},{96,160},{128,64},{160,96},{192,0},{224,... | collective-permute-start | bytes 82952 | tf_op jit(solution)/shard_map/ppermute | solution.py:195
  8.0 1.0 collective-permute-start.1
  9.0 1.5 collective-permute-start
  11.3 1.2 reshape.31
  12.6 3.8 %collective-permute-done.1 = bf16[12,1152]{1,0:T(8,128)(2,1)S(1)} collective-permute-done((bf16[12,1152]{1,0:T(8,128)(2,1)S(1)}, bf16[12,1152]{1,0:T(8,128)(2,1)S(1)}, u32[]{:S(2)}, u32[]{:S(2)}) %collective-permute-start.1) | collective-permute-done | bytes 27680 | tf_op jit(solution)/shard_map/ppermute | solution.py:195
  16.4 1.2 collective-permute-start.4
  17.6 1.8 collective-permute-start.5
  19.4 2.1 %collective-permute-start.3 = (bf16[4,12,1152]{2,1,0:T(8,128)(2,1)S(1)}, bf16[4,12,1152]{2,1,0:T(8,128)(2,1)S(1)}, u32[]{:S(2)}, u32[]{:S(2)}) collective-permute-start(bf16[4,12,1152]{2,1,0:T(8,128)(2,1)S(1)} %pad_maximum_fusion.4), channel_id=1, source_target_pairs={{0,4},{4,0},{32,36},{36,32},{64,68},{68,64},{96,100},{100,96},{128... | collective-permute-start | bytes 331784 | tf_op jit(solution)/shard_map/ppermute | solution.py:195
  21.5 11.2 %all-to-all-start = ((bf16[128,4,1152]{2,1,0:T(4,128)(2,1)}), bf16[128,4,1152]{2,1,0:T(4,128)(2,1)S(1)}, u32[]{:S(2)}, u32[]{:S(2)}) async-start(bf16[128,4,1152]{2,1,0:T(4,128)(2,1)} %reshape.31), calls=%async_computation | async-start | bytes 2359296 | tf_op jit(solution)/shard_map/all_to_all | solution.py:262
  33.0 0.7 copy.8
  34.5 30.1 %all-to-all-done = bf16[128,4,1152]{2,1,0:T(4,128)(2,1)S(1)} async-done(((bf16[128,4,1152]{2,1,0:T(4,128)(2,1)}), bf16[128,4,1152]{2,1,0:T(4,128)(2,1)S(1)}, u32[]{:S(2)}, u32[]{:S(2)}) %all-to-all-start) | async-done | bytes 1179680 | tf_op jit(solution)/shard_map/all_to_all | solution.py:262
  64.6 1.3 slice.100
  65.9 0.8 collective-permute-start.12
  67.0 3.0 %collective-permute-start.7 = (bf16[4,24,1152]{2,1,0:T(8,128)(2,1)}, bf16[4,24,1152]{2,1,0:T(8,128)(2,1)}, u32[]{:S(2)}, u32[]{:S(2)}) collective-permute-start(bf16[4,24,1152]{2,1,0:T(8,128)(2,1)} %bitcast.12.refs_1_), channel_id=1, source_target_pairs={{0,24},{8,0},{16,8},{24,16},{1,25},{9,1},{17,9},{25,17},{2,26},{10... | collective-permute-start | bytes 663560 | tf_op jit(solution)/shard_map/ppermute | solution.py:191
  70.0 2.0 %collective-permute-start.11 = (bf16[4,24,1152]{2,1,0:T(8,128)(2,1)}, bf16[4,24,1152]{2,1,0:T(8,128)(2,1)S(1)}, u32[]{:S(2)}, u32[]{:S(2)}) collective-permute-start(bf16[4,24,1152]{2,1,0:T(8,128)(2,1)} %bitcast.12.refs_1_), channel_id=1, source_target_pairs={{0,8},{8,16},{16,24},{24,0},{1,9},{9,17},{17,25},{25,1},{2,10},{10... | collective-permute-start | bytes 663560 | tf_op jit(solution)/shard_map/ppermute | solution.py:191
  72.0 2.4 %reshape.35.t_ref = bf16[512,1152]{1,0:T(8,128)(2,1)S(1)} reshape(bf16[128,4,1152]{2,1,0:T(4,128)(2,1)} %copy-done.3) | data formatting | bytes 2359296 | tf_op jit(solution)/shard_map/reshape | solution.py:271
  74.4 1.0 collective-permute-done.6.refs_6_
  75.3 0.8 collective-permute-done.7.refs_3_
  76.2 3.7 %collective-permute-start.10 = (bf16[4,24,1152]{2,1,0:T(8,128)(2,1)}, bf16[4,24,1152]{2,1,0:T(8,128)(2,1)}, u32[]{:S(2)}, u32[]{:S(2)}) collective-permute-start(bf16[4,24,1152]{2,1,0:T(8,128)(2,1)} %collective-permute-done.7.refs_3_), channel_id=1, source_target_pairs={{0,24},{8,0},{16,8},{24,16},{1,25},{9,1},{17,9},{25,17},{2,26},{10... | collective-permute-start | bytes 663560 | tf_op jit(solution)/shard_map/ppermute | solution.py:191
  79.9 0.9 collective-permute-done.8.refs_2_
  81.2 3.5 %collective-permute-done.12 = bf16[128,4,768]{2,1,0:T(4,128)(2,1)} collective-permute-done((bf16[128,4,768]{2,1,0:T(4,128)(2,1)}, bf16[128,4,768]{2,1,0:T(4,128)(2,1)}, u32[]{:S(2)}, u32[]{:S(2)}) %collective-permute-start.12) | collective-permute-done | bytes 786464 | tf_op jit(solution)/shard_map/ppermute | solution.py:266
  84.7 1.6 reshape.36.o_ref
  88.4 1.0 collective-permute-done.20.refs_15_
  90.1 0.9 copy-done.2
  91.0 16.1 %attention_core.1 = (bf16[512,768]{1,0:T(8,128)(2,1)S(1)}, bf16[512,768]{1,0:T(8,128)(2,1)S(1)}, bf16[4,8,24,1152]{3,2,1,0:T(8,128)(2,1)S(1)}, bf16[4,8,24,1152]{3,2,1,0:T(8,128)(2,1)S(1)}) custom-call(s32[4]{0:T(128)S(1)} %pad_add_fusion.where_ref, bf16[512,1152]{1,0:T(8,128)(2,1)S(1)} %reshape.35.t_ref, bf16[512,768]{1,0:T(8,128)(2,1)S(1)} %reshape.36.o_ref, ...), custom_call_target="tpu_custom_call" | custom-call | flops 5435817984 | bytes 8388608 | tf_op jit(solution)/shard_map/attention_core/pallas_call | solution.py:108
  107.4 1.2 collective-permute-start.24
  108.6 2.3 %collective-permute-done.21.other_ref = bf16[4,8,24,1152]{3,2,1,0:T(8,128)(2,1)S(1)} collective-permute-done((bf16[4,8,24,1152]{3,2,1,0:T(8,128)(2,1)S(1)}, bf16[4,8,24,1152]{3,2,1,0:T(8,128)(2,1)S(1)}, u32[]{:S(2)}, u32[]{:S(2)}) %collective-permute-start.21) | collective-permute-done | bytes 1769504 | tf_op jit(solution)/shard_map/ppermute | solution.py:219
  111.3 1.0 collective-permute-start.22
  112.2 2.3 %collective-permute-start.23 = (bf16[4,24,1152]{2,1,0:T(8,128)(2,1)S(1)}, bf16[4,24,1152]{2,1,0:T(8,128)(2,1)S(1)}, u32[]{:S(2)}, u32[]{:S(2)}) collective-permute-start(bf16[4,24,1152]{2,1,0:T(8,128)(2,1)S(1)} %get-tuple-element.60), channel_id=1, source_target_pairs={{0,24},{8,0},{16,8},{24,16},{1,25},{9,1},{17,9},{25,17},{2,26},{10... | collective-permute-start | bytes 663560 | tf_op jit(solution)/shard_map/ppermute | solution.py:191
  114.6 0.8 collective-permute-start.26
  115.4 1.2 collective-permute-start.27
  116.6 10.5 %collective-permute-done.24.b_ref = bf16[512,768]{1,0:T(8,128)(2,1)S(1)} collective-permute-done((bf16[512,768]{1,0:T(8,128)(2,1)S(1)}, bf16[512,768]{1,0:T(8,128)(2,1)S(1)}, u32[]{:S(2)}, u32[]{:S(2)}) %collective-permute-start.24) | collective-permute-done | bytes 786464 | tf_op jit(solution)/shard_map/ppermute | solution.py:283
  127.1 1.2 add_parts.1
  128.5 1.0 collective-permute-start.25
  129.5 2.3 %collective-permute-start.28 = (bf16[4,24,1152]{2,1,0:T(8,128)(2,1)S(1)}, bf16[4,24,1152]{2,1,0:T(8,128)(2,1)}, u32[]{:S(2)}, u32[]{:S(2)}) collective-permute-start(bf16[4,24,1152]{2,1,0:T(8,128)(2,1)S(1)} %add_convert_fusion), channel_id=1, source_target_pairs={{0,24},{8,0},{16,8},{24,16},{1,25},{9,1},{17,9},{25,17},{2,26},{10... | collective-permute-start | bytes 663560 | tf_op jit(solution)/shard_map/ppermute | solution.py:191
  131.8 9.5 %all-to-all-start.1 = ((bf16[128,4,768]{2,1,0:T(4,128)(2,1)}), bf16[128,4,768]{2,1,0:T(4,128)(2,1)}, u32[]{:S(2)}, u32[]{:S(2)}) async-start(bf16[128,4,768]{2,1,0:T(4,128)(2,1)} %add_parts.1), calls=%async_computation.1 | async-start | bytes 1572864 | tf_op jit(solution)/shard_map/all_to_all | solution.py:289
  141.3 1.4 convert_add_fusion.1
  142.9 1.2 collective-permute-start.30
  144.1 3.5 %collective-permute-start.31 = (bf16[4,12,1152]{2,1,0:T(8,128)(2,1)S(1)}, bf16[4,12,1152]{2,1,0:T(8,128)(2,1)S(1)}, u32[]{:S(2)}, u32[]{:S(2)}) collective-permute-start(bf16[4,12,1152]{2,1,0:T(8,128)(2,1)S(1)} %get-tuple-element.79), channel_id=1, source_target_pairs={{0,36},{4,32},{32,4},{36,0},{64,100},{68,96},{96,68},{100,64},{128... | collective-permute-start | bytes 331784 | tf_op jit(solution)/shard_map/ppermute | solution.py:195
  148.0 4.9 %collective-permute-done.30 = bf16[4,12,1152]{2,1,0:T(8,128)(2,1)S(1)} collective-permute-done((bf16[4,12,1152]{2,1,0:T(8,128)(2,1)S(1)}, bf16[4,12,1152]{2,1,0:T(8,128)(2,1)S(1)}, u32[]{:S(2)}, u32[]{:S(2)}) %collective-permute-start.30) | collective-permute-done | bytes 110624 | tf_op jit(solution)/shard_map/ppermute | solution.py:195
  152.9 10.7 %collective-permute-done.31 = bf16[4,12,1152]{2,1,0:T(8,128)(2,1)S(1)} collective-permute-done((bf16[4,12,1152]{2,1,0:T(8,128)(2,1)S(1)}, bf16[4,12,1152]{2,1,0:T(8,128)(2,1)S(1)}, u32[]{:S(2)}, u32[]{:S(2)}) %collective-permute-start.31) | collective-permute-done | bytes 110624 | tf_op jit(solution)/shard_map/ppermute | solution.py:195
  163.5 2.6 %collective-permute-done.29 = bf16[4,12,1152]{2,1,0:T(8,128)(2,1)S(1)} collective-permute-done((bf16[4,12,1152]{2,1,0:T(8,128)(2,1)S(1)}, bf16[4,12,1152]{2,1,0:T(8,128)(2,1)S(1)}, u32[]{:S(2)}, u32[]{:S(2)}) %collective-permute-start.29) | collective-permute-done | bytes 110624 | tf_op jit(solution)/shard_map/ppermute | solution.py:195
  166.3 2.5 %collective-permute-start.32 = (bf16[12,1152]{1,0:T(8,128)(2,1)S(1)}, bf16[12,1152]{1,0:T(8,128)(2,1)S(1)}, u32[]{:S(2)}, u32[]{:S(2)}) collective-permute-start(bf16[12,1152]{1,0:T(8,128)(2,1)S(1)} %get-tuple-element.84), channel_id=1, source_target_pairs={{0,64},{32,96},{64,0},{96,32},{128,192},{160,224},{192,128},{224,1... | collective-permute-start | bytes 82952 | tf_op jit(solution)/shard_map/ppermute | solution.py:195
  168.8 2.9 %collective-permute-start.34 = (bf16[12,1152]{1,0:T(8,128)(2,1)S(1)}, bf16[12,1152]{1,0:T(8,128)(2,1)S(1)}, u32[]{:S(2)}, u32[]{:S(2)}) collective-permute-start(bf16[12,1152]{1,0:T(8,128)(2,1)S(1)} %get-tuple-element.85), channel_id=1, source_target_pairs={{0,192},{32,224},{64,128},{96,160},{128,64},{160,96},{192,0},{224,... | collective-permute-start | bytes 82952 | tf_op jit(solution)/shard_map/ppermute | solution.py:195
  171.7 1.2 collective-permute-start.33
  172.8 2.3 %reshape.37 = bf16[1,512,768]{2,1,0:T(8,128)(2,1)} reshape(bf16[128,4,768]{2,1,0:T(4,128)(2,1)} %all-to-all-done.1) | data formatting | bytes 1572864 | tf_op jit(solution)/shard_map/reshape | solution.py:292
  175.1 4.4 %collective-permute-done.33 = bf16[12,1152]{1,0:T(8,128)(2,1)S(1)} collective-permute-done((bf16[12,1152]{1,0:T(8,128)(2,1)S(1)}, bf16[12,1152]{1,0:T(8,128)(2,1)S(1)}, u32[]{:S(2)}, u32[]{:S(2)}) %collective-permute-start.33) | collective-permute-done | bytes 27680 | tf_op jit(solution)/shard_map/ppermute | solution.py:195
  (77 shorter events, 7.7 us)
Async XLA Ops:
  0.6 9.8 %copy-start = (bf16[1,512,1536]{2,1,0:T(8,128)(2,1)S(1)}, bf16[1,512,1536]{2,1,0:T(8,128)(2,1)}, u32[]{:S(2)}) copy-start(bf16[1,512,1536]{2,1,0:T(8,128)(2,1)} %param.3) | copy-start | bytes 4718596
  0.6 9.9 %copy-start.4 = (bf16[1,512,384]{2,1,0:T(8,128)(2,1)S(1)}, bf16[1,512,384]{2,1,0:T(8,128)(2,1)}, u32[]{:S(2)}) copy-start(bf16[1,512,384]{2,1,0:T(8,128)(2,1)} %param.4) | copy-start | bytes 1179652
  1.6 11.0 %collective-permute-start.2 = (bf16[12,1152]{1,0:T(8,128)(2,1)S(1)}, bf16[12,1152]{1,0:T(8,128)(2,1)S(1)}, u32[]{:S(2)}, u32[]{:S(2)}) collective-permute-start(bf16[12,1152]{1,0:T(8,128)(2,1)S(1)} %bitcast.38), channel_id=1, source_target_pairs={{0,192},{32,224},{64,128},{96,160},{128,64},{160,96},{192,0},{224,... | collective-permute-start | bytes 82952 | tf_op jit(solution)/shard_map/ppermute | solution.py:195
  8.0 8.4 %collective-permute-start.1 = (bf16[12,1152]{1,0:T(8,128)(2,1)S(1)}, bf16[12,1152]{1,0:T(8,128)(2,1)S(1)}, u32[]{:S(2)}, u32[]{:S(2)}) collective-permute-start(bf16[12,1152]{1,0:T(8,128)(2,1)S(1)} %bitcast.39), channel_id=1, source_target_pairs={{0,128},{32,160},{64,192},{96,224},{128,0},{160,32},{192,64},{224,... | collective-permute-start | bytes 82952 | tf_op jit(solution)/shard_map/ppermute | solution.py:195
  9.0 7.4 %collective-permute-start = (bf16[12,1152]{1,0:T(8,128)(2,1)S(1)}, bf16[12,1152]{1,0:T(8,128)(2,1)S(1)}, u32[]{:S(2)}, u32[]{:S(2)}) collective-permute-start(bf16[12,1152]{1,0:T(8,128)(2,1)S(1)} %bitcast.40), channel_id=1, source_target_pairs={{0,64},{32,96},{64,0},{96,32},{128,192},{160,224},{192,128},{224,1... | collective-permute-start | bytes 82952 | tf_op jit(solution)/shard_map/ppermute | solution.py:195
  10.5 0.8 copy-start.5
  16.4 16.3 %collective-permute-start.4 = (bf16[4,12,1152]{2,1,0:T(8,128)(2,1)S(1)}, bf16[4,12,1152]{2,1,0:T(8,128)(2,1)S(1)}, u32[]{:S(2)}, u32[]{:S(2)}) collective-permute-start(bf16[4,12,1152]{2,1,0:T(8,128)(2,1)S(1)} %pad_maximum_fusion.4), channel_id=1, source_target_pairs={{0,32},{4,36},{32,0},{36,4},{64,96},{68,100},{96,64},{100,68},{128... | collective-permute-start | bytes 331784 | tf_op jit(solution)/shard_map/ppermute | solution.py:195
  17.6 15.1 %collective-permute-start.5 = (bf16[4,12,1152]{2,1,0:T(8,128)(2,1)S(1)}, bf16[4,12,1152]{2,1,0:T(8,128)(2,1)S(1)}, u32[]{:S(2)}, u32[]{:S(2)}) collective-permute-start(bf16[4,12,1152]{2,1,0:T(8,128)(2,1)S(1)} %pad_maximum_fusion.4), channel_id=1, source_target_pairs={{0,36},{4,32},{32,4},{36,0},{64,100},{68,96},{96,68},{100,64},{128... | collective-permute-start | bytes 331784 | tf_op jit(solution)/shard_map/ppermute | solution.py:195
  19.4 13.5 %collective-permute-start.3 = (bf16[4,12,1152]{2,1,0:T(8,128)(2,1)S(1)}, bf16[4,12,1152]{2,1,0:T(8,128)(2,1)S(1)}, u32[]{:S(2)}, u32[]{:S(2)}) collective-permute-start(bf16[4,12,1152]{2,1,0:T(8,128)(2,1)S(1)} %pad_maximum_fusion.4), channel_id=1, source_target_pairs={{0,4},{4,0},{32,36},{36,32},{64,68},{68,64},{96,100},{100,96},{128... | collective-permute-start | bytes 331784 | tf_op jit(solution)/shard_map/ppermute | solution.py:195
  21.5 43.1 %all-to-all-start = ((bf16[128,4,1152]{2,1,0:T(4,128)(2,1)}), bf16[128,4,1152]{2,1,0:T(4,128)(2,1)S(1)}, u32[]{:S(2)}, u32[]{:S(2)}) async-start(bf16[128,4,1152]{2,1,0:T(4,128)(2,1)} %reshape.31), calls=%async_computation | async-start | bytes 2359296 | tf_op jit(solution)/shard_map/all_to_all | solution.py:262
  64.6 5.4 %copy-start.3 = (bf16[128,4,1152]{2,1,0:T(4,128)(2,1)}, bf16[128,4,1152]{2,1,0:T(4,128)(2,1)S(1)}, u32[]{:S(2)}) copy-start(bf16[128,4,1152]{2,1,0:T(4,128)(2,1)S(1)} %all-to-all-done) | copy-start | bytes 3538948
  65.9 18.8 %collective-permute-start.12 = (bf16[128,4,768]{2,1,0:T(4,128)(2,1)}, bf16[128,4,768]{2,1,0:T(4,128)(2,1)}, u32[]{:S(2)}, u32[]{:S(2)}) collective-permute-start(bf16[128,4,768]{2,1,0:T(4,128)(2,1)} %slice.100), channel_id=1, source_target_pairs={{0,1},{1,0},{2,3},{3,2},{4,5},{5,4},{6,7},{7,6},{8,9},{9,8},{10,11... | collective-permute-start | bytes 2359304 | tf_op jit(solution)/shard_map/ppermute | solution.py:266
  66.7 8.6 %collective-permute-start.6 = (bf16[4,24,1152]{2,1,0:T(8,128)(2,1)}, bf16[4,24,1152]{2,1,0:T(8,128)(2,1)}, u32[]{:S(2)}, u32[]{:S(2)}) collective-permute-start(bf16[4,24,1152]{2,1,0:T(8,128)(2,1)} %bitcast.9.refs_0_), channel_id=1, source_target_pairs={{0,8},{8,16},{16,24},{24,0},{1,9},{9,17},{17,25},{25,1},{2,10},{10... | collective-permute-start | bytes 663560 | tf_op jit(solution)/shard_map/ppermute | solution.py:191
  67.0 9.2 %collective-permute-start.7 = (bf16[4,24,1152]{2,1,0:T(8,128)(2,1)}, bf16[4,24,1152]{2,1,0:T(8,128)(2,1)}, u32[]{:S(2)}, u32[]{:S(2)}) collective-permute-start(bf16[4,24,1152]{2,1,0:T(8,128)(2,1)} %bitcast.12.refs_1_), channel_id=1, source_target_pairs={{0,24},{8,0},{16,8},{24,16},{1,25},{9,1},{17,9},{25,17},{2,26},{10... | collective-permute-start | bytes 663560 | tf_op jit(solution)/shard_map/ppermute | solution.py:191
  70.0 10.8 %collective-permute-start.8 = (bf16[4,24,1152]{2,1,0:T(8,128)(2,1)}, bf16[4,24,1152]{2,1,0:T(8,128)(2,1)}, u32[]{:S(2)}, u32[]{:S(2)}) collective-permute-start(bf16[4,24,1152]{2,1,0:T(8,128)(2,1)} %bitcast.9.refs_0_), channel_id=1, source_target_pairs={{0,24},{8,0},{16,8},{24,16},{1,25},{9,1},{17,9},{25,17},{2,26},{10... | collective-permute-start | bytes 663560 | tf_op jit(solution)/shard_map/ppermute | solution.py:191
  70.0 10.7 %collective-permute-start.11 = (bf16[4,24,1152]{2,1,0:T(8,128)(2,1)}, bf16[4,24,1152]{2,1,0:T(8,128)(2,1)S(1)}, u32[]{:S(2)}, u32[]{:S(2)}) collective-permute-start(bf16[4,24,1152]{2,1,0:T(8,128)(2,1)} %bitcast.12.refs_1_), channel_id=1, source_target_pairs={{0,8},{8,16},{16,24},{24,0},{1,9},{9,17},{17,25},{25,1},{2,10},{10... | collective-permute-start | bytes 663560 | tf_op jit(solution)/shard_map/ppermute | solution.py:191
  76.2 10.1 %collective-permute-start.10 = (bf16[4,24,1152]{2,1,0:T(8,128)(2,1)}, bf16[4,24,1152]{2,1,0:T(8,128)(2,1)}, u32[]{:S(2)}, u32[]{:S(2)}) collective-permute-start(bf16[4,24,1152]{2,1,0:T(8,128)(2,1)} %collective-permute-done.7.refs_3_), channel_id=1, source_target_pairs={{0,24},{8,0},{16,8},{24,16},{1,25},{9,1},{17,9},{25,17},{2,26},{10... | collective-permute-start | bytes 663560 | tf_op jit(solution)/shard_map/ppermute | solution.py:191
  79.9 7.5 %collective-permute-start.9 = (bf16[4,24,1152]{2,1,0:T(8,128)(2,1)}, bf16[4,24,1152]{2,1,0:T(8,128)(2,1)}, u32[]{:S(2)}, u32[]{:S(2)}) collective-permute-start(bf16[4,24,1152]{2,1,0:T(8,128)(2,1)} %collective-permute-done.6.refs_6_), channel_id=1, source_target_pairs={{0,8},{8,16},{16,24},{24,0},{1,9},{9,17},{17,25},{25,1},{2,10},{10... | collective-permute-start | bytes 663560 | tf_op jit(solution)/shard_map/ppermute | solution.py:191
  80.7 6.6 %collective-permute-start.13 = (bf16[4,24,1152]{2,1,0:T(8,128)(2,1)}, bf16[4,24,1152]{2,1,0:T(8,128)(2,1)}, u32[]{:S(2)}, u32[]{:S(2)}) collective-permute-start(bf16[4,24,1152]{2,1,0:T(8,128)(2,1)} %bitcast.9.refs_0_), channel_id=1, source_target_pairs={{0,2},{2,0},{1,3},{3,1},{4,6},{6,4},{5,7},{7,5},{8,10},{10,8},{9,1... | collective-permute-start | bytes 663560 | tf_op jit(solution)/shard_map/ppermute | solution.py:277
  80.7 4.0 %copy-start.1 = (bf16[4,24,1152]{2,1,0:T(8,128)(2,1)}, bf16[4,24,1152]{2,1,0:T(8,128)(2,1)S(1)}, u32[]{:S(2)}) copy-start(bf16[4,24,1152]{2,1,0:T(8,128)(2,1)S(1)} %collective-permute-done.11.refs_7_) | copy-start | bytes 663556
  80.7 7.1 %collective-permute-start.14 = (bf16[4,24,1152]{2,1,0:T(8,128)(2,1)}, bf16[4,24,1152]{2,1,0:T(8,128)(2,1)}, u32[]{:S(2)}, u32[]{:S(2)}) collective-permute-start(bf16[4,24,1152]{2,1,0:T(8,128)(2,1)} %bitcast.12.refs_1_), channel_id=1, source_target_pairs={{0,2},{2,0},{1,3},{3,1},{4,6},{6,4},{5,7},{7,5},{8,10},{10,8},{9,1... | collective-permute-start | bytes 663560 | tf_op jit(solution)/shard_map/ppermute | solution.py:277
  84.7 3.2 %collective-permute-start.15 = (bf16[4,24,1152]{2,1,0:T(8,128)(2,1)}, bf16[4,24,1152]{2,1,0:T(8,128)(2,1)}, u32[]{:S(2)}, u32[]{:S(2)}) collective-permute-start(bf16[4,24,1152]{2,1,0:T(8,128)(2,1)} %collective-permute-done.8.refs_2_), channel_id=1, source_target_pairs={{0,2},{2,0},{1,3},{3,1},{4,6},{6,4},{5,7},{7,5},{8,10},{10,8},{9,1... | collective-permute-start | bytes 663560 | tf_op jit(solution)/shard_map/ppermute | solution.py:277
  86.3 3.2 %collective-permute-start.16 = (bf16[4,24,1152]{2,1,0:T(8,128)(2,1)}, bf16[4,24,1152]{2,1,0:T(8,128)(2,1)}, u32[]{:S(2)}, u32[]{:S(2)}) collective-permute-start(bf16[4,24,1152]{2,1,0:T(8,128)(2,1)} %collective-permute-done.7.refs_3_), channel_id=1, source_target_pairs={{0,2},{2,0},{1,3},{3,1},{4,6},{6,4},{5,7},{7,5},{8,10},{10,8},{9,1... | collective-permute-start | bytes 663560 | tf_op jit(solution)/shard_map/ppermute | solution.py:277
  87.3 2.1 %collective-permute-start.19 = (bf16[4,24,1152]{2,1,0:T(8,128)(2,1)}, bf16[4,24,1152]{2,1,0:T(8,128)(2,1)}, u32[]{:S(2)}, u32[]{:S(2)}) collective-permute-start(bf16[4,24,1152]{2,1,0:T(8,128)(2,1)} %collective-permute-done.6.refs_6_), channel_id=1, source_target_pairs={{0,2},{2,0},{1,3},{3,1},{4,6},{6,4},{5,7},{7,5},{8,10},{10,8},{9,1... | collective-permute-start | bytes 663560 | tf_op jit(solution)/shard_map/ppermute | solution.py:277
  87.3 2.1 %collective-permute-start.20 = (bf16[4,24,1152]{2,1,0:T(8,128)(2,1)}, bf16[4,24,1152]{2,1,0:T(8,128)(2,1)}, u32[]{:S(2)}, u32[]{:S(2)}) collective-permute-start(bf16[4,24,1152]{2,1,0:T(8,128)(2,1)} %copy-done.1), channel_id=1, source_target_pairs={{0,2},{2,0},{1,3},{3,1},{4,6},{6,4},{5,7},{7,5},{8,10},{10,8},{9,1... | collective-permute-start | bytes 663560 | tf_op jit(solution)/shard_map/ppermute | solution.py:277
  87.8 1.9 %collective-permute-start.17 = (bf16[4,24,1152]{2,1,0:T(8,128)(2,1)}, bf16[4,24,1152]{2,1,0:T(8,128)(2,1)}, u32[]{:S(2)}, u32[]{:S(2)}) collective-permute-start(bf16[4,24,1152]{2,1,0:T(8,128)(2,1)} %collective-permute-done.9.refs_4_), channel_id=1, source_target_pairs={{0,2},{2,0},{1,3},{3,1},{4,6},{6,4},{5,7},{7,5},{8,10},{10,8},{9,1... | collective-permute-start | bytes 663560 | tf_op jit(solution)/shard_map/ppermute | solution.py:279
  87.9 2.2 %collective-permute-start.18 = (bf16[4,24,1152]{2,1,0:T(8,128)(2,1)}, bf16[4,24,1152]{2,1,0:T(8,128)(2,1)}, u32[]{:S(2)}, u32[]{:S(2)}) collective-permute-start(bf16[4,24,1152]{2,1,0:T(8,128)(2,1)} %collective-permute-done.10.refs_5_), channel_id=1, source_target_pairs={{0,2},{2,0},{1,3},{3,1},{4,6},{6,4},{5,7},{7,5},{8,10},{10,8},{9,1... | collective-permute-start | bytes 663560 | tf_op jit(solution)/shard_map/ppermute | solution.py:279
  90.1 0.9 copy-start.2
  107.1 3.8 %collective-permute-start.21 = (bf16[4,8,24,1152]{3,2,1,0:T(8,128)(2,1)S(1)}, bf16[4,8,24,1152]{3,2,1,0:T(8,128)(2,1)S(1)}, u32[]{:S(2)}, u32[]{:S(2)}) collective-permute-start(bf16[4,8,24,1152]{3,2,1,0:T(8,128)(2,1)S(1)} %get-tuple-element.56), channel_id=1, source_target_pairs={{0,2},{2,0},{1,3},{3,1},{4,6},{6,4},{5,7},{7,5},{8,10},{10,8},{9,1... | collective-permute-start | bytes 5308424 | tf_op jit(solution)/shard_map/ppermute | solution.py:219
  107.4 19.8 %collective-permute-start.24 = (bf16[512,768]{1,0:T(8,128)(2,1)S(1)}, bf16[512,768]{1,0:T(8,128)(2,1)S(1)}, u32[]{:S(2)}, u32[]{:S(2)}) collective-permute-start(bf16[512,768]{1,0:T(8,128)(2,1)S(1)} %get-tuple-element.61), channel_id=1, source_target_pairs={{0,1},{1,0},{2,3},{3,2},{4,5},{5,4},{6,7},{7,6},{8,9},{9,8},{10,11... | collective-permute-start | bytes 2359304 | tf_op jit(solution)/shard_map/ppermute | solution.py:283
  111.3 15.9 %collective-permute-start.22 = (bf16[4,24,1152]{2,1,0:T(8,128)(2,1)S(1)}, bf16[4,24,1152]{2,1,0:T(8,128)(2,1)S(1)}, u32[]{:S(2)}, u32[]{:S(2)}) collective-permute-start(bf16[4,24,1152]{2,1,0:T(8,128)(2,1)S(1)} %get-tuple-element.59), channel_id=1, source_target_pairs={{0,8},{8,16},{16,24},{24,0},{1,9},{9,17},{17,25},{25,1},{2,10},{10... | collective-permute-start | bytes 663560 | tf_op jit(solution)/shard_map/ppermute | solution.py:191
  112.2 14.9 %collective-permute-start.23 = (bf16[4,24,1152]{2,1,0:T(8,128)(2,1)S(1)}, bf16[4,24,1152]{2,1,0:T(8,128)(2,1)S(1)}, u32[]{:S(2)}, u32[]{:S(2)}) collective-permute-start(bf16[4,24,1152]{2,1,0:T(8,128)(2,1)S(1)} %get-tuple-element.60), channel_id=1, source_target_pairs={{0,24},{8,0},{16,8},{24,16},{1,25},{9,1},{17,9},{25,17},{2,26},{10... | collective-permute-start | bytes 663560 | tf_op jit(solution)/shard_map/ppermute | solution.py:191
  114.6 26.7 %collective-permute-start.26 = (bf16[4,24,1152]{2,1,0:T(8,128)(2,1)S(1)}, bf16[4,24,1152]{2,1,0:T(8,128)(2,1)}, u32[]{:S(2)}, u32[]{:S(2)}) collective-permute-start(bf16[4,24,1152]{2,1,0:T(8,128)(2,1)S(1)} %get-tuple-element.68), channel_id=1, source_target_pairs={{0,24},{8,0},{16,8},{24,16},{1,25},{9,1},{17,9},{25,17},{2,26},{10... | collective-permute-start | bytes 663560 | tf_op jit(solution)/shard_map/ppermute | solution.py:191
  115.4 25.9 %collective-permute-start.27 = (bf16[4,24,1152]{2,1,0:T(8,128)(2,1)S(1)}, bf16[4,24,1152]{2,1,0:T(8,128)(2,1)}, u32[]{:S(2)}, u32[]{:S(2)}) collective-permute-start(bf16[4,24,1152]{2,1,0:T(8,128)(2,1)S(1)} %get-tuple-element.69), channel_id=1, source_target_pairs={{0,8},{8,16},{16,24},{24,0},{1,9},{9,17},{17,25},{25,1},{2,10},{10... | collective-permute-start | bytes 663560 | tf_op jit(solution)/shard_map/ppermute | solution.py:191
  128.5 12.8 %collective-permute-start.25 = (bf16[4,24,1152]{2,1,0:T(8,128)(2,1)S(1)}, bf16[4,24,1152]{2,1,0:T(8,128)(2,1)}, u32[]{:S(2)}, u32[]{:S(2)}) collective-permute-start(bf16[4,24,1152]{2,1,0:T(8,128)(2,1)S(1)} %add_convert_fusion.1), channel_id=1, source_target_pairs={{0,8},{8,16},{16,24},{24,0},{1,9},{9,17},{17,25},{25,1},{2,10},{10... | collective-permute-start | bytes 663560 | tf_op jit(solution)/shard_map/ppermute | solution.py:191
  129.5 11.9 %collective-permute-start.28 = (bf16[4,24,1152]{2,1,0:T(8,128)(2,1)S(1)}, bf16[4,24,1152]{2,1,0:T(8,128)(2,1)}, u32[]{:S(2)}, u32[]{:S(2)}) collective-permute-start(bf16[4,24,1152]{2,1,0:T(8,128)(2,1)S(1)} %add_convert_fusion), channel_id=1, source_target_pairs={{0,24},{8,0},{16,8},{24,16},{1,25},{9,1},{17,9},{25,17},{2,26},{10... | collective-permute-start | bytes 663560 | tf_op jit(solution)/shard_map/ppermute | solution.py:191
  131.8 34.4 %all-to-all-start.1 = ((bf16[128,4,768]{2,1,0:T(4,128)(2,1)}), bf16[128,4,768]{2,1,0:T(4,128)(2,1)}, u32[]{:S(2)}, u32[]{:S(2)}) async-start(bf16[128,4,768]{2,1,0:T(4,128)(2,1)} %add_parts.1), calls=%async_computation.1 | async-start | bytes 1572864 | tf_op jit(solution)/shard_map/all_to_all | solution.py:289
  142.9 9.9 %collective-permute-start.30 = (bf16[4,12,1152]{2,1,0:T(8,128)(2,1)S(1)}, bf16[4,12,1152]{2,1,0:T(8,128)(2,1)S(1)}, u32[]{:S(2)}, u32[]{:S(2)}) collective-permute-start(bf16[4,12,1152]{2,1,0:T(8,128)(2,1)S(1)} %get-tuple-element.78), channel_id=1, source_target_pairs={{0,4},{4,0},{32,36},{36,32},{64,68},{68,64},{96,100},{100,96},{128... | collective-permute-start | bytes 331784 | tf_op jit(solution)/shard_map/ppermute | solution.py:195
  144.1 19.5 %collective-permute-start.31 = (bf16[4,12,1152]{2,1,0:T(8,128)(2,1)S(1)}, bf16[4,12,1152]{2,1,0:T(8,128)(2,1)S(1)}, u32[]{:S(2)}, u32[]{:S(2)}) collective-permute-start(bf16[4,12,1152]{2,1,0:T(8,128)(2,1)S(1)} %get-tuple-element.79), channel_id=1, source_target_pairs={{0,36},{4,32},{32,4},{36,0},{64,100},{68,96},{96,68},{100,64},{128... | collective-permute-start | bytes 331784 | tf_op jit(solution)/shard_map/ppermute | solution.py:195
  147.6 18.6 %collective-permute-start.29 = (bf16[4,12,1152]{2,1,0:T(8,128)(2,1)S(1)}, bf16[4,12,1152]{2,1,0:T(8,128)(2,1)S(1)}, u32[]{:S(2)}, u32[]{:S(2)}) collective-permute-start(bf16[4,12,1152]{2,1,0:T(8,128)(2,1)S(1)} %slice.85), channel_id=1, source_target_pairs={{0,32},{4,36},{32,0},{36,4},{64,96},{68,100},{96,64},{100,68},{128... | collective-permute-start | bytes 331784 | tf_op jit(solution)/shard_map/ppermute | solution.py:195
  166.3 8.8 %collective-permute-start.32 = (bf16[12,1152]{1,0:T(8,128)(2,1)S(1)}, bf16[12,1152]{1,0:T(8,128)(2,1)S(1)}, u32[]{:S(2)}, u32[]{:S(2)}) collective-permute-start(bf16[12,1152]{1,0:T(8,128)(2,1)S(1)} %get-tuple-element.84), channel_id=1, source_target_pairs={{0,64},{32,96},{64,0},{96,32},{128,192},{160,224},{192,128},{224,1... | collective-permute-start | bytes 82952 | tf_op jit(solution)/shard_map/ppermute | solution.py:195
  168.8 6.3 %collective-permute-start.34 = (bf16[12,1152]{1,0:T(8,128)(2,1)S(1)}, bf16[12,1152]{1,0:T(8,128)(2,1)S(1)}, u32[]{:S(2)}, u32[]{:S(2)}) collective-permute-start(bf16[12,1152]{1,0:T(8,128)(2,1)S(1)} %get-tuple-element.85), channel_id=1, source_target_pairs={{0,192},{32,224},{64,128},{96,160},{128,64},{160,96},{192,0},{224,... | collective-permute-start | bytes 82952 | tf_op jit(solution)/shard_map/ppermute | solution.py:195
  171.7 7.9 %collective-permute-start.33 = (bf16[12,1152]{1,0:T(8,128)(2,1)S(1)}, bf16[12,1152]{1,0:T(8,128)(2,1)S(1)}, u32[]{:S(2)}, u32[]{:S(2)}) collective-permute-start(bf16[12,1152]{1,0:T(8,128)(2,1)S(1)} %get-tuple-element.86), channel_id=1, source_target_pairs={{0,128},{32,160},{64,192},{96,224},{128,0},{160,32},{192,64},{224,... | collective-permute-start | bytes 82952 | tf_op jit(solution)/shard_map/ppermute | solution.py:195

commit v10 on v9

--- a/solution.py
+++ b/solution.py
@@ -10,6 +10,7 @@
 F = 128
 ROWS = 12
 VMEM_LIMIT = 32 * 2**20
+ROWS_COST = 20 * 10**9
 bf16, f32 = jnp.bfloat16, jnp.float32
 NT = (((1,), (1,)), ((), ()))
 TN = (((0,), (0,)), ((), ()))
@@ -181,6 +182,29 @@
         cost_estimate=pl.CostEstimate(flops=0, bytes_accessed=2**20, transcendentals=0),
         name="add_parts",
     )(a, b)
+
+
+def rows_kernel(x_ref, all_ref, part_ref):
+    rows = x_ref[...].astype(f32).reshape(all_ref.shape).astype(bf16)
+    all_ref[...] = rows
+    part_ref[...] = rows[:, : part_ref.shape[1]]
+
+
+def to_rows(x, part_cols):
+    rows, n = x.shape[0] * x.shape[1], x.shape[2]
+    vm = pl.BlockSpec(memory_space=pltpu.VMEM)
+    return pl.pallas_call(
+        rows_kernel,
+        out_shape=(
+            jax.ShapeDtypeStruct((rows, n), bf16),
+            jax.ShapeDtypeStruct((rows, part_cols), bf16),
+        ),
+        in_specs=[vm],
+        out_specs=(vm, vm),
+        compiler_params=pltpu.CompilerParams(vmem_limit_bytes=24 * 2**20),
+        cost_estimate=pl.CostEstimate(flops=ROWS_COST, bytes_accessed=2**20, transcendentals=0),
+        name="to_rows",
+    )(x)
 
 
 FR = ("z", "y", "xh", "c")
@@ -261,19 +285,16 @@
     tokens, rows = lax.optimization_barrier((tokens, rows))
     tokens = lax.all_to_all(tokens, FR, 0, 0, tiled=True)
     low, high = near_zx(rows)
-    part = tokens[:, :, :cols]
+    tokens, part = to_rows(tokens, cols)
     low, high, part = lax.optimization_barrier((low, high, part))
     others = lax.ppermute(part, "mp", PAIR)
     before_low = shift(low, "y", Y, 1)
     after_high = shift(high, "y", Y, Y - 1)
     before_high = shift(high, "y", Y, 1)
     after_low = shift(low, "y", Y, Y - 1)
-    tokens = tokens.reshape(F * count, cols + half)
-    before_low, after_high, tokens = lax.optimization_barrier((before_low, after_high, tokens))
     far_low = shift(before_low, "y", Y, 1)
     far_high = shift(after_high, "y", Y, Y - 1)
     mine = [low, high, after_low, after_high, far_low, far_high, before_low, before_high]
-    others = others.reshape(F * count, cols)
     rest = {i: lax.ppermute(mine[i], "c", PAIR) for i in (0, 1, 2, 3, 6, 7)}
     mine, others = lax.optimization_barrier((mine, others))
     rest.update({i: lax.ppermute(mine[i], "c", PAIR) for i in (4, 5)})

time: 181 us -> 183 us (1.011)
    unnamed x14 -> x24, local copies, waits for them, and re-layouts: 2.55 us -> 8.78 us
    ppermute x12, waiting for transfers between devices: 3.11 us -> 7.16 us  [shift(): return lax.ppermute(x, axis, [(i, (i + by) % size) for i in range(size)])]
    reshape x2 -> x0, local copies, waits for them, and re-layouts: 3.93 us -> none  [the longest x1 2.37 us: on_device(): tokens = tokens.reshape(F * count, cols + half)]
    ppermute x1, waiting for transfers between devices: 3.46 us -> 0.25 us  [on_device(): others = lax.ppermute(part, 'mp', PAIR)]
  transfers between devices with their start and end apart: 37 -> 37, of which waited for: 16 -> 15; matrix products, arithmetic and copies ran while one was open for 6% -> 4% of each run, Pallas kernels for 1% -> 1%
where the time goes in v10:
time: 183 us; the launch traced here: 182 us
  waiting for transfers between devices  78.5 us (43%)
  starting transfers between devices  69.1 us (38%)
  Pallas kernels  17.5 us (10%)
  local copies, waits for them, and re-layouts  13.1 us (7%)
  other arithmetic  3.11 us (2%)
    all_to_all x1, waiting for transfers between devices, on_device(): tokens = lax.all_to_all(tokens, FR, 0, 0, tiled=True)  30.6 us
    ppermute x12, waiting for transfers between devices, across(): return lax.ppermute(x, axis, [(i, i ^ by) for i in range(size)])  26.3 us
    ppermute x12, starting transfers between devices, across(): return lax.ppermute(x, axis, [(i, i ^ by) for i in range(size)])  25.6 us
    ppermute x12, starting transfers between devices, shift(): return lax.ppermute(x, axis, [(i, (i + by) % size) for i in range(size)])  17.9 us
    pallas_call x1, Pallas kernels, core(): pl.pallas_call(core_kernel, out_shape=(jax.ShapeDtypeStruct((rows, part_c...  15.7 us
    all_to_all x1, starting transfers between devices, on_device(): tokens = lax.all_to_all(tokens, FR, 0, 0, tiled=True)  11.2 us
    ppermute x1, waiting for transfers between devices, on_device(): got = lax.ppermute(give, 'mp', PAIR)  10.5 us
    all_to_all x1, starting transfers between devices, to_frames(): return lax.all_to_all(x, FR, 0, 0, tiled=True)  10.2 us
  transfers between devices with their start and end apart: 37, of which 15 were waited for; matrix products, arithmetic and copies ran while one was open for 4% of the time, Pallas kernels for 1%

profile of v10, /device:TPU:6, one launch (start us, length us, event | category | flops | bytes accessed | tf_op | source)
XLA Modules:
  0.0 182.4 jit_solution(16841681905188428564)
XLA Ops:
  0.7 0.9 pad.26
  1.6 6.4 %collective-permute-start.2 = (bf16[12,1152]{1,0:T(8,128)(2,1)S(1)}, bf16[12,1152]{1,0:T(8,128)(2,1)S(1)}, u32[]{:S(2)}, u32[]{:S(2)}) collective-permute-start(bf16[12,1152]{1,0:T(8,128)(2,1)S(1)} %bitcast.46), channel_id=1, source_target_pairs={{0,192},{32,224},{64,128},{96,160},{128,64},{160,96},{192,0},{224,... | collective-permute-start | bytes 82952 | tf_op jit(solution)/shard_map/ppermute | solution.py:219
  8.0 1.0 collective-permute-start.1
  9.0 1.5 collective-permute-start
  11.3 1.2 reshape.25
  12.5 3.8 %collective-permute-done.1 = bf16[12,1152]{1,0:T(8,128)(2,1)S(1)} collective-permute-done((bf16[12,1152]{1,0:T(8,128)(2,1)S(1)}, bf16[12,1152]{1,0:T(8,128)(2,1)S(1)}, u32[]{:S(2)}, u32[]{:S(2)}) %collective-permute-start.1) | collective-permute-done | bytes 27680 | tf_op jit(solution)/shard_map/ppermute | solution.py:219
  16.4 1.2 collective-permute-start.4
  17.6 1.8 collective-permute-start.5
  19.4 2.1 %collective-permute-start.3 = (bf16[4,12,1152]{2,1,0:T(8,128)(2,1)S(1)}, bf16[4,12,1152]{2,1,0:T(8,128)(2,1)S(1)}, u32[]{:S(2)}, u32[]{:S(2)}) collective-permute-start(bf16[4,12,1152]{2,1,0:T(8,128)(2,1)S(1)} %pad_maximum_fusion.4), channel_id=1, source_target_pairs={{0,4},{4,0},{32,36},{36,32},{64,68},{68,64},{96,100},{100,96},{128... | collective-permute-start | bytes 331784 | tf_op jit(solution)/shard_map/ppermute | solution.py:219
  21.5 11.2 %all-to-all-start = ((bf16[128,4,1152]{2,1,0:T(4,128)(2,1)}), bf16[128,4,1152]{2,1,0:T(4,128)(2,1)S(1)}, u32[]{:S(2)}, u32[]{:S(2)}) async-start(bf16[128,4,1152]{2,1,0:T(4,128)(2,1)} %reshape.25), calls=%async_computation | async-start | bytes 2359296 | tf_op jit(solution)/shard_map/all_to_all | solution.py:286
  32.7 0.9 broadcast_select_fusion.1
  34.0 30.6 %all-to-all-done.x_ref = bf16[128,4,1152]{2,1,0:T(4,128)(2,1)S(1)} async-done(((bf16[128,4,1152]{2,1,0:T(4,128)(2,1)}), bf16[128,4,1152]{2,1,0:T(4,128)(2,1)S(1)}, u32[]{:S(2)}, u32[]{:S(2)}) %all-to-all-start) | async-done | bytes 1179680 | tf_op jit(solution)/shard_map/all_to_all | solution.py:286
  64.9 1.0 copy-done.7
  65.9 0.8 collective-permute-start.12
  67.0 3.0 %collective-permute-start.7 = (bf16[4,24,1152]{2,1,0:T(8,128)(2,1)S(1)}, bf16[4,24,1152]{2,1,0:T(8,128)(2,1)S(1)}, u32[]{:S(2)}, u32[]{:S(2)}) collective-permute-start(bf16[4,24,1152]{2,1,0:T(8,128)(2,1)S(1)} %bitcast.34), channel_id=1, source_target_pairs={{0,24},{8,0},{16,8},{24,16},{1,25},{9,1},{17,9},{25,17},{2,26},{10... | collective-permute-start | bytes 663560 | tf_op jit(solution)/shard_map/ppermute | solution.py:215
  70.0 2.0 %collective-permute-start.11 = (bf16[4,24,1152]{2,1,0:T(8,128)(2,1)S(1)}, bf16[4,24,1152]{2,1,0:T(8,128)(2,1)}, u32[]{:S(2)}, u32[]{:S(2)}) collective-permute-start(bf16[4,24,1152]{2,1,0:T(8,128)(2,1)S(1)} %bitcast.35), channel_id=1, source_target_pairs={{0,8},{8,16},{16,24},{24,0},{1,9},{9,17},{17,25},{25,1},{2,10},{10... | collective-permute-start | bytes 663560 | tf_op jit(solution)/shard_map/ppermute | solution.py:215
  72.0 3.0 %collective-permute-done.8.refs_6_ = bf16[4,24,1152]{2,1,0:T(8,128)(2,1)S(1)} collective-permute-done((bf16[4,24,1152]{2,1,0:T(8,128)(2,1)S(1)}, bf16[4,24,1152]{2,1,0:T(8,128)(2,1)S(1)}, u32[]{:S(2)}, u32[]{:S(2)}) %collective-permute-start.8) | collective-permute-done | bytes 221216 | tf_op jit(solution)/shard_map/ppermute | solution.py:215
  75.9 3.7 %collective-permute-start.10 = (bf16[4,24,1152]{2,1,0:T(8,128)(2,1)S(1)}, bf16[4,24,1152]{2,1,0:T(8,128)(2,1)}, u32[]{:S(2)}, u32[]{:S(2)}) collective-permute-start(bf16[4,24,1152]{2,1,0:T(8,128)(2,1)S(1)} %collective-permute-done.7.refs_3_), channel_id=1, source_target_pairs={{0,24},{8,0},{16,8},{24,16},{1,25},{9,1},{17,9},{25,17},{2,26},{10... | collective-permute-start | bytes 663560 | tf_op jit(solution)/shard_map/ppermute | solution.py:215
  79.5 0.9 collective-permute-done.6.refs_2_
  80.9 2.7 %collective-permute-done.9.refs_4_ = bf16[4,24,1152]{2,1,0:T(8,128)(2,1)} collective-permute-done((bf16[4,24,1152]{2,1,0:T(8,128)(2,1)S(1)}, bf16[4,24,1152]{2,1,0:T(8,128)(2,1)}, u32[]{:S(2)}, u32[]{:S(2)}) %collective-permute-start.9) | collective-permute-done | bytes 221216 | tf_op jit(solution)/shard_map/ppermute | solution.py:215
  86.3 0.7 copy-done.5
  88.1 0.8 collective-permute-done.18.refs_13_
  88.9 0.9 copy-done.2
  89.9 0.9 copy-done.4
  90.8 0.9 copy-done.6
  91.7 1.3 copy-done.8
  93.0 15.7 %attention_core.1 = (bf16[512,768]{1,0:T(8,128)(2,1)S(1)}, bf16[512,768]{1,0:T(8,128)(2,1)S(1)}, bf16[4,8,24,1152]{3,2,1,0:T(8,128)(2,1)S(1)}, bf16[4,8,24,1152]{3,2,1,0:T(8,128)(2,1)S(1)}) custom-call(s32[4]{0:T(128)S(1)} %pad_add_fusion.where_ref, bf16[512,1152]{1,0:T(8,128)(2,1)S(1)} %copy-done.8, bf16[512,768]{1,0:T(8,128)(2,1)S(1)} %collective-permute-done.12.o_ref, ...), custom_call_target="tpu_custom_call" | custom-call | flops 5435817984 | bytes 8388608 | tf_op jit(solution)/shard_map/attention_core/pallas_call | solution.py:109
  109.1 0.9 collective-permute-start.24
  110.1 2.4 %collective-permute-done.21.other_ref = bf16[4,8,24,1152]{3,2,1,0:T(8,128)(2,1)S(1)} collective-permute-done((bf16[4,8,24,1152]{3,2,1,0:T(8,128)(2,1)S(1)}, bf16[4,8,24,1152]{3,2,1,0:T(8,128)(2,1)S(1)}, u32[]{:S(2)}, u32[]{:S(2)}) %collective-permute-start.21) | collective-permute-done | bytes 1769504 | tf_op jit(solution)/shard_map/ppermute | solution.py:243
  112.8 1.4 collective-permute-start.22
  114.3 1.9 %collective-permute-start.23 = (bf16[4,24,1152]{2,1,0:T(8,128)(2,1)S(1)}, bf16[4,24,1152]{2,1,0:T(8,128)(2,1)S(1)}, u32[]{:S(2)}, u32[]{:S(2)}) collective-permute-start(bf16[4,24,1152]{2,1,0:T(8,128)(2,1)S(1)} %get-tuple-element.58), channel_id=1, source_target_pairs={{0,24},{8,0},{16,8},{24,16},{1,25},{9,1},{17,9},{25,17},{2,26},{10... | collective-permute-start | bytes 663560 | tf_op jit(solution)/shard_map/ppermute | solution.py:215
  116.2 1.6 collective-permute-start.26
  118.2 10.5 %collective-permute-done.24.b_ref = bf16[512,768]{1,0:T(8,128)(2,1)S(1)} collective-permute-done((bf16[512,768]{1,0:T(8,128)(2,1)S(1)}, bf16[512,768]{1,0:T(8,128)(2,1)S(1)}, u32[]{:S(2)}, u32[]{:S(2)}) %collective-permute-start.24) | collective-permute-done | bytes 786464 | tf_op jit(solution)/shard_map/ppermute | solution.py:304
  128.7 1.2 add_parts.1
  130.0 1.4 collective-permute-start.25
  131.5 1.9 %collective-permute-start.28 = (bf16[4,24,1152]{2,1,0:T(8,128)(2,1)S(1)}, bf16[4,24,1152]{2,1,0:T(8,128)(2,1)}, u32[]{:S(2)}, u32[]{:S(2)}) collective-permute-start(bf16[4,24,1152]{2,1,0:T(8,128)(2,1)S(1)} %add_convert_fusion), channel_id=1, source_target_pairs={{0,24},{8,0},{16,8},{24,16},{1,25},{9,1},{17,9},{25,17},{2,26},{10... | collective-permute-start | bytes 663560 | tf_op jit(solution)/shard_map/ppermute | solution.py:215
  133.4 10.2 %all-to-all-start.1 = ((bf16[128,4,768]{2,1,0:T(4,128)(2,1)}), bf16[128,4,768]{2,1,0:T(4,128)(2,1)}, u32[]{:S(2)}, u32[]{:S(2)}) async-start(bf16[128,4,768]{2,1,0:T(4,128)(2,1)} %add_parts.1), calls=%async_computation.1 | async-start | bytes 1572864 | tf_op jit(solution)/shard_map/all_to_all | solution.py:310
  143.6 1.4 convert_add_fusion.1
  145.2 1.0 collective-permute-start.30
  146.3 3.5 %collective-permute-start.31 = (bf16[4,12,1152]{2,1,0:T(8,128)(2,1)S(1)}, bf16[4,12,1152]{2,1,0:T(8,128)(2,1)S(1)}, u32[]{:S(2)}, u32[]{:S(2)}) collective-permute-start(bf16[4,12,1152]{2,1,0:T(8,128)(2,1)S(1)} %get-tuple-element.77), channel_id=1, source_target_pairs={{0,36},{4,32},{32,4},{36,0},{64,100},{68,96},{96,68},{100,64},{128... | collective-permute-start | bytes 331784 | tf_op jit(solution)/shard_map/ppermute | solution.py:219
  150.3 5.0 %collective-permute-done.30 = bf16[4,12,1152]{2,1,0:T(8,128)(2,1)S(1)} collective-permute-done((bf16[4,12,1152]{2,1,0:T(8,128)(2,1)S(1)}, bf16[4,12,1152]{2,1,0:T(8,128)(2,1)S(1)}, u32[]{:S(2)}, u32[]{:S(2)}) %collective-permute-start.30) | collective-permute-done | bytes 110624 | tf_op jit(solution)/shard_map/ppermute | solution.py:219
  155.3 10.3 %collective-permute-done.31 = bf16[4,12,1152]{2,1,0:T(8,128)(2,1)S(1)} collective-permute-done((bf16[4,12,1152]{2,1,0:T(8,128)(2,1)S(1)}, bf16[4,12,1152]{2,1,0:T(8,128)(2,1)S(1)}, u32[]{:S(2)}, u32[]{:S(2)}) %collective-permute-start.31) | collective-permute-done | bytes 110624 | tf_op jit(solution)/shard_map/ppermute | solution.py:219
  165.6 2.7 %collective-permute-done.29 = bf16[4,12,1152]{2,1,0:T(8,128)(2,1)S(1)} collective-permute-done((bf16[4,12,1152]{2,1,0:T(8,128)(2,1)S(1)}, bf16[4,12,1152]{2,1,0:T(8,128)(2,1)S(1)}, u32[]{:S(2)}, u32[]{:S(2)}) %collective-permute-start.29) | collective-permute-done | bytes 110624 | tf_op jit(solution)/shard_map/ppermute | solution.py:219
  168.4 2.5 %collective-permute-start.32 = (bf16[12,1152]{1,0:T(8,128)(2,1)S(1)}, bf16[12,1152]{1,0:T(8,128)(2,1)S(1)}, u32[]{:S(2)}, u32[]{:S(2)}) collective-permute-start(bf16[12,1152]{1,0:T(8,128)(2,1)S(1)} %get-tuple-element.82), channel_id=1, source_target_pairs={{0,64},{32,96},{64,0},{96,32},{128,192},{160,224},{192,128},{224,1... | collective-permute-start | bytes 82952 | tf_op jit(solution)/shard_map/ppermute | solution.py:219
  170.9 2.9 %collective-permute-start.34 = (bf16[12,1152]{1,0:T(8,128)(2,1)S(1)}, bf16[12,1152]{1,0:T(8,128)(2,1)S(1)}, u32[]{:S(2)}, u32[]{:S(2)}) collective-permute-start(bf16[12,1152]{1,0:T(8,128)(2,1)S(1)} %get-tuple-element.83), channel_id=1, source_target_pairs={{0,192},{32,224},{64,128},{96,160},{128,64},{160,96},{192,0},{224,... | collective-permute-start | bytes 82952 | tf_op jit(solution)/shard_map/ppermute | solution.py:219
  173.8 1.2 collective-permute-start.33
  175.0 2.3 %reshape.29 = bf16[1,512,768]{2,1,0:T(8,128)(2,1)} reshape(bf16[128,4,768]{2,1,0:T(4,128)(2,1)} %all-to-all-done.1) | data formatting | bytes 1572864 | tf_op jit(solution)/shard_map/reshape | solution.py:313
  177.3 4.4 %collective-permute-done.33 = bf16[12,1152]{1,0:T(8,128)(2,1)S(1)} collective-permute-done((bf16[12,1152]{1,0:T(8,128)(2,1)S(1)}, bf16[12,1152]{1,0:T(8,128)(2,1)S(1)}, u32[]{:S(2)}, u32[]{:S(2)}) %collective-permute-start.33) | collective-permute-done | bytes 27680 | tf_op jit(solution)/shard_map/ppermute | solution.py:219
  (85 shorter events, 9.8 us)
Async XLA Ops:
  0.6 9.8 %copy-start = (bf16[1,512,1536]{2,1,0:T(8,128)(2,1)S(1)}, bf16[1,512,1536]{2,1,0:T(8,128)(2,1)}, u32[]{:S(2)}) copy-start(bf16[1,512,1536]{2,1,0:T(8,128)(2,1)} %param.3) | copy-start | bytes 4718596
  0.6 9.9 %copy-start.9 = (bf16[1,512,384]{2,1,0:T(8,128)(2,1)S(1)}, bf16[1,512,384]{2,1,0:T(8,128)(2,1)}, u32[]{:S(2)}) copy-start(bf16[1,512,384]{2,1,0:T(8,128)(2,1)} %param.4) | copy-start | bytes 1179652
  1.6 10.9 %collective-permute-start.2 = (bf16[12,1152]{1,0:T(8,128)(2,1)S(1)}, bf16[12,1152]{1,0:T(8,128)(2,1)S(1)}, u32[]{:S(2)}, u32[]{:S(2)}) collective-permute-start(bf16[12,1152]{1,0:T(8,128)(2,1)S(1)} %bitcast.46), channel_id=1, source_target_pairs={{0,192},{32,224},{64,128},{96,160},{128,64},{160,96},{192,0},{224,... | collective-permute-start | bytes 82952 | tf_op jit(solution)/shard_map/ppermute | solution.py:219
  8.0 8.4 %collective-permute-start.1 = (bf16[12,1152]{1,0:T(8,128)(2,1)S(1)}, bf16[12,1152]{1,0:T(8,128)(2,1)S(1)}, u32[]{:S(2)}, u32[]{:S(2)}) collective-permute-start(bf16[12,1152]{1,0:T(8,128)(2,1)S(1)} %bitcast.47), channel_id=1, source_target_pairs={{0,128},{32,160},{64,192},{96,224},{128,0},{160,32},{192,64},{224,... | collective-permute-start | bytes 82952 | tf_op jit(solution)/shard_map/ppermute | solution.py:219
  9.0 7.4 %collective-permute-start = (bf16[12,1152]{1,0:T(8,128)(2,1)S(1)}, bf16[12,1152]{1,0:T(8,128)(2,1)S(1)}, u32[]{:S(2)}, u32[]{:S(2)}) collective-permute-start(bf16[12,1152]{1,0:T(8,128)(2,1)S(1)} %bitcast.48), channel_id=1, source_target_pairs={{0,64},{32,96},{64,0},{96,32},{128,192},{160,224},{192,128},{224,1... | collective-permute-start | bytes 82952 | tf_op jit(solution)/shard_map/ppermute | solution.py:219
  10.5 0.8 copy-start.10
  16.4 16.3 %collective-permute-start.4 = (bf16[4,12,1152]{2,1,0:T(8,128)(2,1)S(1)}, bf16[4,12,1152]{2,1,0:T(8,128)(2,1)S(1)}, u32[]{:S(2)}, u32[]{:S(2)}) collective-permute-start(bf16[4,12,1152]{2,1,0:T(8,128)(2,1)S(1)} %pad_maximum_fusion.4), channel_id=1, source_target_pairs={{0,32},{4,36},{32,0},{36,4},{64,96},{68,100},{96,64},{100,68},{128... | collective-permute-start | bytes 331784 | tf_op jit(solution)/shard_map/ppermute | solution.py:219
  17.6 15.1 %collective-permute-start.5 = (bf16[4,12,1152]{2,1,0:T(8,128)(2,1)S(1)}, bf16[4,12,1152]{2,1,0:T(8,128)(2,1)}, u32[]{:S(2)}, u32[]{:S(2)}) collective-permute-start(bf16[4,12,1152]{2,1,0:T(8,128)(2,1)S(1)} %pad_maximum_fusion.4), channel_id=1, source_target_pairs={{0,36},{4,32},{32,4},{36,0},{64,100},{68,96},{96,68},{100,64},{128... | collective-permute-start | bytes 331784 | tf_op jit(solution)/shard_map/ppermute | solution.py:219
  19.4 14.4 %collective-permute-start.3 = (bf16[4,12,1152]{2,1,0:T(8,128)(2,1)S(1)}, bf16[4,12,1152]{2,1,0:T(8,128)(2,1)S(1)}, u32[]{:S(2)}, u32[]{:S(2)}) collective-permute-start(bf16[4,12,1152]{2,1,0:T(8,128)(2,1)S(1)} %pad_maximum_fusion.4), channel_id=1, source_target_pairs={{0,4},{4,0},{32,36},{36,32},{64,68},{68,64},{96,100},{100,96},{128... | collective-permute-start | bytes 331784 | tf_op jit(solution)/shard_map/ppermute | solution.py:219
  21.5 43.1 %all-to-all-start = ((bf16[128,4,1152]{2,1,0:T(4,128)(2,1)}), bf16[128,4,1152]{2,1,0:T(4,128)(2,1)S(1)}, u32[]{:S(2)}, u32[]{:S(2)}) async-start(bf16[128,4,1152]{2,1,0:T(4,128)(2,1)} %reshape.25), calls=%async_computation | async-start | bytes 2359296 | tf_op jit(solution)/shard_map/all_to_all | solution.py:286
  64.9 1.0 copy-start.7
  65.9 18.5 %collective-permute-start.12 = (bf16[512,768]{1,0:T(8,128)(2,1)S(1)}, bf16[512,768]{1,0:T(8,128)(2,1)S(1)}, u32[]{:S(2)}, u32[]{:S(2)}) collective-permute-start(bf16[512,768]{1,0:T(8,128)(2,1)S(1)} %get-tuple-element.43), channel_id=1, source_target_pairs={{0,1},{1,0},{2,3},{3,2},{4,5},{5,4},{6,7},{7,6},{8,9},{9,8},{10,11... | collective-permute-start | bytes 2359304 | tf_op jit(solution)/shard_map/ppermute | solution.py:290
  66.7 8.3 %collective-permute-start.8 = (bf16[4,24,1152]{2,1,0:T(8,128)(2,1)S(1)}, bf16[4,24,1152]{2,1,0:T(8,128)(2,1)S(1)}, u32[]{:S(2)}, u32[]{:S(2)}) collective-permute-start(bf16[4,24,1152]{2,1,0:T(8,128)(2,1)S(1)} %bitcast.38), channel_id=1, source_target_pairs={{0,8},{8,16},{16,24},{24,0},{1,9},{9,17},{17,25},{25,1},{2,10},{10... | collective-permute-start | bytes 663560 | tf_op jit(solution)/shard_map/ppermute | solution.py:215
  67.0 8.9 %collective-permute-start.7 = (bf16[4,24,1152]{2,1,0:T(8,128)(2,1)S(1)}, bf16[4,24,1152]{2,1,0:T(8,128)(2,1)S(1)}, u32[]{:S(2)}, u32[]{:S(2)}) collective-permute-start(bf16[4,24,1152]{2,1,0:T(8,128)(2,1)S(1)} %bitcast.34), channel_id=1, source_target_pairs={{0,24},{8,0},{16,8},{24,16},{1,25},{9,1},{17,9},{25,17},{2,26},{10... | collective-permute-start | bytes 663560 | tf_op jit(solution)/shard_map/ppermute | solution.py:215
  70.0 10.4 %collective-permute-start.6 = (bf16[4,24,1152]{2,1,0:T(8,128)(2,1)S(1)}, bf16[4,24,1152]{2,1,0:T(8,128)(2,1)}, u32[]{:S(2)}, u32[]{:S(2)}) collective-permute-start(bf16[4,24,1152]{2,1,0:T(8,128)(2,1)S(1)} %bitcast.39), channel_id=1, source_target_pairs={{0,24},{8,0},{16,8},{24,16},{1,25},{9,1},{17,9},{25,17},{2,26},{10... | collective-permute-start | bytes 663560 | tf_op jit(solution)/shard_map/ppermute | solution.py:215
  70.0 10.4 %collective-permute-start.11 = (bf16[4,24,1152]{2,1,0:T(8,128)(2,1)S(1)}, bf16[4,24,1152]{2,1,0:T(8,128)(2,1)}, u32[]{:S(2)}, u32[]{:S(2)}) collective-permute-start(bf16[4,24,1152]{2,1,0:T(8,128)(2,1)S(1)} %bitcast.35), channel_id=1, source_target_pairs={{0,8},{8,16},{16,24},{24,0},{1,9},{9,17},{17,25},{25,1},{2,10},{10... | collective-permute-start | bytes 663560 | tf_op jit(solution)/shard_map/ppermute | solution.py:215
  75.0 8.6 %collective-permute-start.9 = (bf16[4,24,1152]{2,1,0:T(8,128)(2,1)S(1)}, bf16[4,24,1152]{2,1,0:T(8,128)(2,1)}, u32[]{:S(2)}, u32[]{:S(2)}) collective-permute-start(bf16[4,24,1152]{2,1,0:T(8,128)(2,1)S(1)} %collective-permute-done.8.refs_6_), channel_id=1, source_target_pairs={{0,8},{8,16},{16,24},{24,0},{1,9},{9,17},{17,25},{25,1},{2,10},{10... | collective-permute-start | bytes 663560 | tf_op jit(solution)/shard_map/ppermute | solution.py:215
  75.9 7.8 %collective-permute-start.10 = (bf16[4,24,1152]{2,1,0:T(8,128)(2,1)S(1)}, bf16[4,24,1152]{2,1,0:T(8,128)(2,1)}, u32[]{:S(2)}, u32[]{:S(2)}) collective-permute-start(bf16[4,24,1152]{2,1,0:T(8,128)(2,1)S(1)} %collective-permute-done.7.refs_3_), channel_id=1, source_target_pairs={{0,24},{8,0},{16,8},{24,16},{1,25},{9,1},{17,9},{25,17},{2,26},{10... | collective-permute-start | bytes 663560 | tf_op jit(solution)/shard_map/ppermute | solution.py:215
  80.4 4.0 %collective-permute-start.13 = (bf16[4,24,1152]{2,1,0:T(8,128)(2,1)S(1)}, bf16[4,24,1152]{2,1,0:T(8,128)(2,1)S(1)}, u32[]{:S(2)}, u32[]{:S(2)}) collective-permute-start(bf16[4,24,1152]{2,1,0:T(8,128)(2,1)S(1)} %bitcast.40), channel_id=1, source_target_pairs={{0,2},{2,0},{1,3},{3,1},{4,6},{6,4},{5,7},{7,5},{8,10},{10,8},{9,1... | collective-permute-start | bytes 663560 | tf_op jit(solution)/shard_map/ppermute | solution.py:298
  80.4 5.2 %collective-permute-start.14 = (bf16[4,24,1152]{2,1,0:T(8,128)(2,1)S(1)}, bf16[4,24,1152]{2,1,0:T(8,128)(2,1)S(1)}, u32[]{:S(2)}, u32[]{:S(2)}) collective-permute-start(bf16[4,24,1152]{2,1,0:T(8,128)(2,1)S(1)} %bitcast.36), channel_id=1, source_target_pairs={{0,2},{2,0},{1,3},{3,1},{4,6},{6,4},{5,7},{7,5},{8,10},{10,8},{9,1... | collective-permute-start | bytes 663560 | tf_op jit(solution)/shard_map/ppermute | solution.py:298
  83.6 2.7 %collective-permute-start.19 = (bf16[4,24,1152]{2,1,0:T(8,128)(2,1)S(1)}, bf16[4,24,1152]{2,1,0:T(8,128)(2,1)S(1)}, u32[]{:S(2)}, u32[]{:S(2)}) collective-permute-start(bf16[4,24,1152]{2,1,0:T(8,128)(2,1)S(1)} %collective-permute-done.8.refs_6_), channel_id=1, source_target_pairs={{0,2},{2,0},{1,3},{3,1},{4,6},{6,4},{5,7},{7,5},{8,10},{10,8},{9,1... | collective-permute-start | bytes 663560 | tf_op jit(solution)/shard_map/ppermute | solution.py:298
  83.6 3.9 %collective-permute-start.15 = (bf16[4,24,1152]{2,1,0:T(8,128)(2,1)}, bf16[4,24,1152]{2,1,0:T(8,128)(2,1)}, u32[]{:S(2)}, u32[]{:S(2)}) collective-permute-start(bf16[4,24,1152]{2,1,0:T(8,128)(2,1)} %collective-permute-done.6.refs_2_), channel_id=1, source_target_pairs={{0,2},{2,0},{1,3},{3,1},{4,6},{6,4},{5,7},{7,5},{8,10},{10,8},{9,1... | collective-permute-start | bytes 663560 | tf_op jit(solution)/shard_map/ppermute | solution.py:298
  84.4 3.2 %collective-permute-start.20 = (bf16[4,24,1152]{2,1,0:T(8,128)(2,1)}, bf16[4,24,1152]{2,1,0:T(8,128)(2,1)}, u32[]{:S(2)}, u32[]{:S(2)}) collective-permute-start(bf16[4,24,1152]{2,1,0:T(8,128)(2,1)} %collective-permute-done.11.refs_7_), channel_id=1, source_target_pairs={{0,2},{2,0},{1,3},{3,1},{4,6},{6,4},{5,7},{7,5},{8,10},{10,8},{9,1... | collective-permute-start | bytes 663560 | tf_op jit(solution)/shard_map/ppermute | solution.py:298
  84.4 0.7 copy-start.1
  85.1 2.5 %collective-permute-start.16 = (bf16[4,24,1152]{2,1,0:T(8,128)(2,1)S(1)}, bf16[4,24,1152]{2,1,0:T(8,128)(2,1)}, u32[]{:S(2)}, u32[]{:S(2)}) collective-permute-start(bf16[4,24,1152]{2,1,0:T(8,128)(2,1)S(1)} %collective-permute-done.7.refs_3_), channel_id=1, source_target_pairs={{0,2},{2,0},{1,3},{3,1},{4,6},{6,4},{5,7},{7,5},{8,10},{10,8},{9,1... | collective-permute-start | bytes 663560 | tf_op jit(solution)/shard_map/ppermute | solution.py:298
  85.6 0.7 copy-start.3
  86.3 1.8 collective-permute-start.17
  86.3 0.7 copy-start.5
  87.0 2.0 %collective-permute-start.18 = (bf16[4,24,1152]{2,1,0:T(8,128)(2,1)}, bf16[4,24,1152]{2,1,0:T(8,128)(2,1)}, u32[]{:S(2)}, u32[]{:S(2)}) collective-permute-start(bf16[4,24,1152]{2,1,0:T(8,128)(2,1)} %collective-permute-done.10.refs_5_), channel_id=1, source_target_pairs={{0,2},{2,0},{1,3},{3,1},{4,6},{6,4},{5,7},{7,5},{8,10},{10,8},{9,1... | collective-permute-start | bytes 663560 | tf_op jit(solution)/shard_map/ppermute | solution.py:300
  88.9 0.9 copy-start.2
  89.9 0.9 copy-start.4
  90.8 0.9 copy-start.6
  91.7 1.3 copy-start.8
  108.7 3.8 %collective-permute-start.21 = (bf16[4,8,24,1152]{3,2,1,0:T(8,128)(2,1)S(1)}, bf16[4,8,24,1152]{3,2,1,0:T(8,128)(2,1)S(1)}, u32[]{:S(2)}, u32[]{:S(2)}) collective-permute-start(bf16[4,8,24,1152]{3,2,1,0:T(8,128)(2,1)S(1)} %get-tuple-element.54), channel_id=1, source_target_pairs={{0,2},{2,0},{1,3},{3,1},{4,6},{6,4},{5,7},{7,5},{8,10},{10,8},{9,1... | collective-permute-start | bytes 5308424 | tf_op jit(solution)/shard_map/ppermute | solution.py:243
  109.1 19.6 %collective-permute-start.24 = (bf16[512,768]{1,0:T(8,128)(2,1)S(1)}, bf16[512,768]{1,0:T(8,128)(2,1)S(1)}, u32[]{:S(2)}, u32[]{:S(2)}) collective-permute-start(bf16[512,768]{1,0:T(8,128)(2,1)S(1)} %get-tuple-element.59), channel_id=1, source_target_pairs={{0,1},{1,0},{2,3},{3,2},{4,5},{5,4},{6,7},{7,6},{8,9},{9,8},{10,11... | collective-permute-start | bytes 2359304 | tf_op jit(solution)/shard_map/ppermute | solution.py:304
  112.8 15.9 %collective-permute-start.22 = (bf16[4,24,1152]{2,1,0:T(8,128)(2,1)S(1)}, bf16[4,24,1152]{2,1,0:T(8,128)(2,1)S(1)}, u32[]{:S(2)}, u32[]{:S(2)}) collective-permute-start(bf16[4,24,1152]{2,1,0:T(8,128)(2,1)S(1)} %get-tuple-element.57), channel_id=1, source_target_pairs={{0,8},{8,16},{16,24},{24,0},{1,9},{9,17},{17,25},{25,1},{2,10},{10... | collective-permute-start | bytes 663560 | tf_op jit(solution)/shard_map/ppermute | solution.py:215
  114.3 14.5 %collective-permute-start.23 = (bf16[4,24,1152]{2,1,0:T(8,128)(2,1)S(1)}, bf16[4,24,1152]{2,1,0:T(8,128)(2,1)S(1)}, u32[]{:S(2)}, u32[]{:S(2)}) collective-permute-start(bf16[4,24,1152]{2,1,0:T(8,128)(2,1)S(1)} %get-tuple-element.58), channel_id=1, source_target_pairs={{0,24},{8,0},{16,8},{24,16},{1,25},{9,1},{17,9},{25,17},{2,26},{10... | collective-permute-start | bytes 663560 | tf_op jit(solution)/shard_map/ppermute | solution.py:215
  116.2 27.4 %collective-permute-start.26 = (bf16[4,24,1152]{2,1,0:T(8,128)(2,1)S(1)}, bf16[4,24,1152]{2,1,0:T(8,128)(2,1)}, u32[]{:S(2)}, u32[]{:S(2)}) collective-permute-start(bf16[4,24,1152]{2,1,0:T(8,128)(2,1)S(1)} %get-tuple-element.66), channel_id=1, source_target_pairs={{0,24},{8,0},{16,8},{24,16},{1,25},{9,1},{17,9},{25,17},{2,26},{10... | collective-permute-start | bytes 663560 | tf_op jit(solution)/shard_map/ppermute | solution.py:215
  117.7 25.9 %collective-permute-start.27 = (bf16[4,24,1152]{2,1,0:T(8,128)(2,1)S(1)}, bf16[4,24,1152]{2,1,0:T(8,128)(2,1)}, u32[]{:S(2)}, u32[]{:S(2)}) collective-permute-start(bf16[4,24,1152]{2,1,0:T(8,128)(2,1)S(1)} %get-tuple-element.67), channel_id=1, source_target_pairs={{0,8},{8,16},{16,24},{24,0},{1,9},{9,17},{17,25},{25,1},{2,10},{10... | collective-permute-start | bytes 663560 | tf_op jit(solution)/shard_map/ppermute | solution.py:215
  130.0 13.5 %collective-permute-start.25 = (bf16[4,24,1152]{2,1,0:T(8,128)(2,1)S(1)}, bf16[4,24,1152]{2,1,0:T(8,128)(2,1)}, u32[]{:S(2)}, u32[]{:S(2)}) collective-permute-start(bf16[4,24,1152]{2,1,0:T(8,128)(2,1)S(1)} %add_convert_fusion.1), channel_id=1, source_target_pairs={{0,8},{8,16},{16,24},{24,0},{1,9},{9,17},{17,25},{25,1},{2,10},{10... | collective-permute-start | bytes 663560 | tf_op jit(solution)/shard_map/ppermute | solution.py:215
  131.5 12.1 %collective-permute-start.28 = (bf16[4,24,1152]{2,1,0:T(8,128)(2,1)S(1)}, bf16[4,24,1152]{2,1,0:T(8,128)(2,1)}, u32[]{:S(2)}, u32[]{:S(2)}) collective-permute-start(bf16[4,24,1152]{2,1,0:T(8,128)(2,1)S(1)} %add_convert_fusion), channel_id=1, source_target_pairs={{0,24},{8,0},{16,8},{24,16},{1,25},{9,1},{17,9},{25,17},{2,26},{10... | collective-permute-start | bytes 663560 | tf_op jit(solution)/shard_map/ppermute | solution.py:215
  133.4 35.0 %all-to-all-start.1 = ((bf16[128,4,768]{2,1,0:T(4,128)(2,1)}), bf16[128,4,768]{2,1,0:T(4,128)(2,1)}, u32[]{:S(2)}, u32[]{:S(2)}) async-start(bf16[128,4,768]{2,1,0:T(4,128)(2,1)} %add_parts.1), calls=%async_computation.1 | async-start | bytes 1572864 | tf_op jit(solution)/shard_map/all_to_all | solution.py:310
  145.2 10.1 %collective-permute-start.30 = (bf16[4,12,1152]{2,1,0:T(8,128)(2,1)S(1)}, bf16[4,12,1152]{2,1,0:T(8,128)(2,1)S(1)}, u32[]{:S(2)}, u32[]{:S(2)}) collective-permute-start(bf16[4,12,1152]{2,1,0:T(8,128)(2,1)S(1)} %get-tuple-element.76), channel_id=1, source_target_pairs={{0,4},{4,0},{32,36},{36,32},{64,68},{68,64},{96,100},{100,96},{128... | collective-permute-start | bytes 331784 | tf_op jit(solution)/shard_map/ppermute | solution.py:219
  146.3 19.3 %collective-permute-start.31 = (bf16[4,12,1152]{2,1,0:T(8,128)(2,1)S(1)}, bf16[4,12,1152]{2,1,0:T(8,128)(2,1)S(1)}, u32[]{:S(2)}, u32[]{:S(2)}) collective-permute-start(bf16[4,12,1152]{2,1,0:T(8,128)(2,1)S(1)} %get-tuple-element.77), channel_id=1, source_target_pairs={{0,36},{4,32},{32,4},{36,0},{64,100},{68,96},{96,68},{100,64},{128... | collective-permute-start | bytes 331784 | tf_op jit(solution)/shard_map/ppermute | solution.py:219
  149.7 18.6 %collective-permute-start.29 = (bf16[4,12,1152]{2,1,0:T(8,128)(2,1)S(1)}, bf16[4,12,1152]{2,1,0:T(8,128)(2,1)S(1)}, u32[]{:S(2)}, u32[]{:S(2)}) collective-permute-start(bf16[4,12,1152]{2,1,0:T(8,128)(2,1)S(1)} %slice.81), channel_id=1, source_target_pairs={{0,32},{4,36},{32,0},{36,4},{64,96},{68,100},{96,64},{100,68},{128... | collective-permute-start | bytes 331784 | tf_op jit(solution)/shard_map/ppermute | solution.py:219
  168.4 8.8 %collective-permute-start.32 = (bf16[12,1152]{1,0:T(8,128)(2,1)S(1)}, bf16[12,1152]{1,0:T(8,128)(2,1)S(1)}, u32[]{:S(2)}, u32[]{:S(2)}) collective-permute-start(bf16[12,1152]{1,0:T(8,128)(2,1)S(1)} %get-tuple-element.82), channel_id=1, source_target_pairs={{0,64},{32,96},{64,0},{96,32},{128,192},{160,224},{192,128},{224,1... | collective-permute-start | bytes 82952 | tf_op jit(solution)/shard_map/ppermute | solution.py:219
  170.9 6.4 %collective-permute-start.34 = (bf16[12,1152]{1,0:T(8,128)(2,1)S(1)}, bf16[12,1152]{1,0:T(8,128)(2,1)S(1)}, u32[]{:S(2)}, u32[]{:S(2)}) collective-permute-start(bf16[12,1152]{1,0:T(8,128)(2,1)S(1)} %get-tuple-element.83), channel_id=1, source_target_pairs={{0,192},{32,224},{64,128},{96,160},{128,64},{160,96},{192,0},{224,... | collective-permute-start | bytes 82952 | tf_op jit(solution)/shard_map/ppermute | solution.py:219
  173.8 7.9 %collective-permute-start.33 = (bf16[12,1152]{1,0:T(8,128)(2,1)S(1)}, bf16[12,1152]{1,0:T(8,128)(2,1)S(1)}, u32[]{:S(2)}, u32[]{:S(2)}) collective-permute-start(bf16[12,1152]{1,0:T(8,128)(2,1)S(1)} %get-tuple-element.84), channel_id=1, source_target_pairs={{0,128},{32,160},{64,192},{96,224},{128,0},{160,32},{192,64},{224,... | collective-permute-start | bytes 82952 | tf_op jit(solution)/shard_map/ppermute | solution.py:219

commit v11 on v10

--- a/solution.py
+++ b/solution.py
@@ -10,7 +10,6 @@
 F = 128
 ROWS = 12
 VMEM_LIMIT = 32 * 2**20
-ROWS_COST = 20 * 10**9
 bf16, f32 = jnp.bfloat16, jnp.float32
 NT = (((1,), (1,)), ((), ()))
 TN = (((0,), (0,)), ((), ()))
@@ -21,17 +20,24 @@
 
 
 def core_kernel(where_ref, t_ref, o_ref, *refs):
-    pieces = refs[:16]
-    give_ref, keep_ref, mine_ref, rest_ref, w_ref, s_ref, d_ref, g_ref = refs[16:]
+    blocks = refs[:16]
+    give_ref, keep_ref, mine_ref, rest_ref, w_ref, s_ref, d_ref, g_ref, pieces, sems = refs[16:]
+    copies = [pltpu.make_async_copy(blocks[i], pieces.at[i], sems.at[i]) for i in range(16)]
+    for i in range(8):
+        copies[i].start()
+        copies[i + 8].start()
     z, y, c, m = (where_ref[i] for i in range(4))
     unit = XH * C * ROWS
 
-    @pl.loop(0, Z // 2)
-    def _(t):
-        for i in range(8):
-            by, high = i // 2, i % 2
-            a = pieces[i][t].astype(f32)
-            b = pieces[i + 8][t].astype(f32)
+    for i in range(8):
+        by, high = i // 2, i % 2
+        copies[i].wait()
+        copies[i + 8].wait()
+
+        @pl.loop(0, Z // 2)
+        def _(t, i=i, by=by, high=high):
+            a = pieces[i, t].astype(f32)
+            b = pieces[i + 8, t].astype(f32)
             first = jnp.where(c == 0, a, b)
             second = jnp.where(c == 0, b, a)
             rows = [first[:ROWS], second[:ROWS], first[ROWS:], second[ROWS:]]
@@ -114,13 +120,16 @@
             jax.ShapeDtypeStruct((Y, Z, XH * ROWS, n), bf16),
             jax.ShapeDtypeStruct((Y, Z, XH * ROWS, n), bf16),
         ),
-        in_specs=[pl.BlockSpec(memory_space=pltpu.SMEM)] + [vm] * 18,
+        in_specs=[pl.BlockSpec(memory_space=pltpu.SMEM), vm, vm]
+        + [pl.BlockSpec(memory_space=pltpu.HBM)] * 16,
         out_specs=(vm,) * 4,
         scratch_shapes=[
             pltpu.VMEM((width, n), bf16),
             pltpu.VMEM((4 * half // 128, rows, 128), f32),
             pltpu.VMEM((3 * half // 128, rows, 128), f32),
             pltpu.VMEM((rows, n), bf16),
+            pltpu.VMEM((16,) + mine[0].shape, bf16),
+            pltpu.SemaphoreType.DMA((16,)),
         ],
         compiler_params=pltpu.CompilerParams(vmem_limit_bytes=VMEM_LIMIT),
         cost_estimate=pl.CostEstimate(
@@ -202,7 +211,7 @@
         in_specs=[vm],
         out_specs=(vm, vm),
         compiler_params=pltpu.CompilerParams(vmem_limit_bytes=24 * 2**20),
-        cost_estimate=pl.CostEstimate(flops=ROWS_COST, bytes_accessed=2**20, transcendentals=0),
+        cost_estimate=pl.CostEstimate(flops=0, bytes_accessed=2**20, transcendentals=0),
         name="to_rows",
     )(x)
 

time: 183 us -> 184 us (level)
  no operation moved by 1% of the time
where the time goes in v11:
time: 184 us
  waiting for transfers between devices  78.5 us (43%)
  starting transfers between devices  69.1 us (38%)
  Pallas kernels  18.7 us (10%)
  local copies, waits for them, and re-layouts  13.1 us (7%)
  other arithmetic  3.11 us (2%)
    all_to_all x1, waiting for transfers between devices, on_device(): tokens = lax.all_to_all(tokens, FR, 0, 0, tiled=True)  30.6 us
    ppermute x12, waiting for transfers between devices, across(): return lax.ppermute(x, axis, [(i, i ^ by) for i in range(size)])  26.3 us
    ppermute x12, starting transfers between devices, across(): return lax.ppermute(x, axis, [(i, i ^ by) for i in range(size)])  25.6 us
    ppermute x12, starting transfers between devices, shift(): return lax.ppermute(x, axis, [(i, (i + by) % size) for i in range(size)])  17.9 us
    pallas_call x1, Pallas kernels, core(): pl.pallas_call(core_kernel, out_shape=(jax.ShapeDtypeStruct((rows, part_c...  16.8 us
    all_to_all x1, starting transfers between devices, on_device(): tokens = lax.all_to_all(tokens, FR, 0, 0, tiled=True)  11.2 us
    ppermute x1, waiting for transfers between devices, on_device(): got = lax.ppermute(give, 'mp', PAIR)  10.5 us
    all_to_all x1, starting transfers between devices, to_frames(): return lax.all_to_all(x, FR, 0, 0, tiled=True)  10.2 us
  transfers between devices with their start and end apart: 37, of which 15 were waited for; matrix products, arithmetic and copies ran while one was open for 4% of the time, Pallas kernels for 1%

profile of v11, /device:TPU:6, one launch (start us, length us, event | category | flops | bytes accessed | tf_op | source)
XLA Modules:
  0.0 183.6 jit_solution(7787336116449530860)
XLA Ops:
  0.7 0.9 pad.26
  1.6 6.4 %collective-permute-start.2 = (bf16[12,1152]{1,0:T(8,128)(2,1)S(1)}, bf16[12,1152]{1,0:T(8,128)(2,1)S(1)}, u32[]{:S(2)}, u32[]{:S(2)}) collective-permute-start(bf16[12,1152]{1,0:T(8,128)(2,1)S(1)} %bitcast.46), channel_id=1, source_target_pairs={{0,192},{32,224},{64,128},{96,160},{128,64},{160,96},{192,0},{224,... | collective-permute-start | bytes 82952 | tf_op jit(solution)/shard_map/ppermute | solution.py:228
  8.0 1.0 collective-permute-start.1
  9.0 1.5 collective-permute-start
  11.3 1.2 reshape.25
  12.5 3.8 %collective-permute-done.1 = bf16[12,1152]{1,0:T(8,128)(2,1)S(1)} collective-permute-done((bf16[12,1152]{1,0:T(8,128)(2,1)S(1)}, bf16[12,1152]{1,0:T(8,128)(2,1)S(1)}, u32[]{:S(2)}, u32[]{:S(2)}) %collective-permute-start.1) | collective-permute-done | bytes 27680 | tf_op jit(solution)/shard_map/ppermute | solution.py:228
  16.4 1.2 collective-permute-start.4
  17.6 1.8 collective-permute-start.5
  19.4 2.1 %collective-permute-start.3 = (bf16[4,12,1152]{2,1,0:T(8,128)(2,1)S(1)}, bf16[4,12,1152]{2,1,0:T(8,128)(2,1)S(1)}, u32[]{:S(2)}, u32[]{:S(2)}) collective-permute-start(bf16[4,12,1152]{2,1,0:T(8,128)(2,1)S(1)} %pad_maximum_fusion.4), channel_id=1, source_target_pairs={{0,4},{4,0},{32,36},{36,32},{64,68},{68,64},{96,100},{100,96},{128... | collective-permute-start | bytes 331784 | tf_op jit(solution)/shard_map/ppermute | solution.py:228
  21.5 11.2 %all-to-all-start = ((bf16[128,4,1152]{2,1,0:T(4,128)(2,1)}), bf16[128,4,1152]{2,1,0:T(4,128)(2,1)S(1)}, u32[]{:S(2)}, u32[]{:S(2)}) async-start(bf16[128,4,1152]{2,1,0:T(4,128)(2,1)} %reshape.25), calls=%async_computation | async-start | bytes 2359296 | tf_op jit(solution)/shard_map/all_to_all | solution.py:295
  32.7 0.9 broadcast_select_fusion.1
  34.0 30.6 %all-to-all-done.x_ref = bf16[128,4,1152]{2,1,0:T(4,128)(2,1)S(1)} async-done(((bf16[128,4,1152]{2,1,0:T(4,128)(2,1)}), bf16[128,4,1152]{2,1,0:T(4,128)(2,1)S(1)}, u32[]{:S(2)}, u32[]{:S(2)}) %all-to-all-start) | async-done | bytes 1179680 | tf_op jit(solution)/shard_map/all_to_all | solution.py:295
  64.9 1.0 copy-done.1
  65.9 0.8 collective-permute-start.12
  67.0 3.0 %collective-permute-start.7 = (bf16[4,24,1152]{2,1,0:T(8,128)(2,1)S(1)}, bf16[4,24,1152]{2,1,0:T(8,128)(2,1)S(1)}, u32[]{:S(2)}, u32[]{:S(2)}) collective-permute-start(bf16[4,24,1152]{2,1,0:T(8,128)(2,1)S(1)} %bitcast.34), channel_id=1, source_target_pairs={{0,24},{8,0},{16,8},{24,16},{1,25},{9,1},{17,9},{25,17},{2,26},{10... | collective-permute-start | bytes 663560 | tf_op jit(solution)/shard_map/ppermute | solution.py:224
  70.0 2.0 %collective-permute-start.11 = (bf16[4,24,1152]{2,1,0:T(8,128)(2,1)S(1)}, bf16[4,24,1152]{2,1,0:T(8,128)(2,1)}, u32[]{:S(2)}, u32[]{:S(2)}) collective-permute-start(bf16[4,24,1152]{2,1,0:T(8,128)(2,1)S(1)} %bitcast.35), channel_id=1, source_target_pairs={{0,8},{8,16},{16,24},{24,0},{1,9},{9,17},{17,25},{25,1},{2,10},{10... | collective-permute-start | bytes 663560 | tf_op jit(solution)/shard_map/ppermute | solution.py:224
  72.0 3.0 %collective-permute-done.8.refs_6_ = bf16[4,24,1152]{2,1,0:T(8,128)(2,1)S(1)} collective-permute-done((bf16[4,24,1152]{2,1,0:T(8,128)(2,1)S(1)}, bf16[4,24,1152]{2,1,0:T(8,128)(2,1)S(1)}, u32[]{:S(2)}, u32[]{:S(2)}) %collective-permute-start.8) | collective-permute-done | bytes 221216 | tf_op jit(solution)/shard_map/ppermute | solution.py:224
  75.9 3.7 %collective-permute-start.10 = (bf16[4,24,1152]{2,1,0:T(8,128)(2,1)S(1)}, bf16[4,24,1152]{2,1,0:T(8,128)(2,1)}, u32[]{:S(2)}, u32[]{:S(2)}) collective-permute-start(bf16[4,24,1152]{2,1,0:T(8,128)(2,1)S(1)} %collective-permute-done.7.refs_3_), channel_id=1, source_target_pairs={{0,24},{8,0},{16,8},{24,16},{1,25},{9,1},{17,9},{25,17},{2,26},{10... | collective-permute-start | bytes 663560 | tf_op jit(solution)/shard_map/ppermute | solution.py:224
  79.5 0.9 collective-permute-done.6.refs_2_
  80.9 2.7 %collective-permute-done.9.refs_4_ = bf16[4,24,1152]{2,1,0:T(8,128)(2,1)} collective-permute-done((bf16[4,24,1152]{2,1,0:T(8,128)(2,1)S(1)}, bf16[4,24,1152]{2,1,0:T(8,128)(2,1)}, u32[]{:S(2)}, u32[]{:S(2)}) %collective-permute-start.9) | collective-permute-done | bytes 221216 | tf_op jit(solution)/shard_map/ppermute | solution.py:224
  86.3 0.7 copy-done.7
  88.1 0.8 collective-permute-done.18.refs_13_
  88.9 1.3 copy-done.2
  90.2 0.9 copy-done.4
  91.1 0.9 copy-done.6
  92.1 0.9 copy-done.8
  93.0 16.8 %attention_core.1 = (bf16[512,768]{1,0:T(8,128)(2,1)S(1)}, bf16[512,768]{1,0:T(8,128)(2,1)S(1)}, bf16[4,8,24,1152]{3,2,1,0:T(8,128)(2,1)S(1)}, bf16[4,8,24,1152]{3,2,1,0:T(8,128)(2,1)S(1)}) custom-call(s32[4]{0:T(128)S(1)} %pad_add_fusion.where_ref, bf16[512,1152]{1,0:T(8,128)(2,1)S(1)} %copy-done.2, bf16[512,768]{1,0:T(8,128)(2,1)S(1)} %collective-permute-done.12.o_ref, ...), custom_call_target="tpu_custom_call" | custom-call | flops 5435817984 | bytes 8388608 | tf_op jit(solution)/shard_map/attention_core/pallas_call | solution.py:115
  110.3 0.9 collective-permute-start.24
  111.3 2.4 %collective-permute-done.21.other_ref = bf16[4,8,24,1152]{3,2,1,0:T(8,128)(2,1)S(1)} collective-permute-done((bf16[4,8,24,1152]{3,2,1,0:T(8,128)(2,1)S(1)}, bf16[4,8,24,1152]{3,2,1,0:T(8,128)(2,1)S(1)}, u32[]{:S(2)}, u32[]{:S(2)}) %collective-permute-start.21) | collective-permute-done | bytes 1769504 | tf_op jit(solution)/shard_map/ppermute | solution.py:252
  114.0 1.4 collective-permute-start.22
  115.5 1.9 %collective-permute-start.23 = (bf16[4,24,1152]{2,1,0:T(8,128)(2,1)S(1)}, bf16[4,24,1152]{2,1,0:T(8,128)(2,1)S(1)}, u32[]{:S(2)}, u32[]{:S(2)}) collective-permute-start(bf16[4,24,1152]{2,1,0:T(8,128)(2,1)S(1)} %get-tuple-element.58), channel_id=1, source_target_pairs={{0,24},{8,0},{16,8},{24,16},{1,25},{9,1},{17,9},{25,17},{2,26},{10... | collective-permute-start | bytes 663560 | tf_op jit(solution)/shard_map/ppermute | solution.py:224
  117.4 1.6 collective-permute-start.26
  119.4 10.5 %collective-permute-done.24.b_ref = bf16[512,768]{1,0:T(8,128)(2,1)S(1)} collective-permute-done((bf16[512,768]{1,0:T(8,128)(2,1)S(1)}, bf16[512,768]{1,0:T(8,128)(2,1)S(1)}, u32[]{:S(2)}, u32[]{:S(2)}) %collective-permute-start.24) | collective-permute-done | bytes 786464 | tf_op jit(solution)/shard_map/ppermute | solution.py:313
  129.9 1.2 add_parts.1
  131.2 1.4 collective-permute-start.25
  132.7 1.9 %collective-permute-start.28 = (bf16[4,24,1152]{2,1,0:T(8,128)(2,1)S(1)}, bf16[4,24,1152]{2,1,0:T(8,128)(2,1)}, u32[]{:S(2)}, u32[]{:S(2)}) collective-permute-start(bf16[4,24,1152]{2,1,0:T(8,128)(2,1)S(1)} %add_convert_fusion), channel_id=1, source_target_pairs={{0,24},{8,0},{16,8},{24,16},{1,25},{9,1},{17,9},{25,17},{2,26},{10... | collective-permute-start | bytes 663560 | tf_op jit(solution)/shard_map/ppermute | solution.py:224
  134.6 10.2 %all-to-all-start.1 = ((bf16[128,4,768]{2,1,0:T(4,128)(2,1)}), bf16[128,4,768]{2,1,0:T(4,128)(2,1)}, u32[]{:S(2)}, u32[]{:S(2)}) async-start(bf16[128,4,768]{2,1,0:T(4,128)(2,1)} %add_parts.1), calls=%async_computation.1 | async-start | bytes 1572864 | tf_op jit(solution)/shard_map/all_to_all | solution.py:319
  144.8 1.4 convert_add_fusion.1
  146.4 1.0 collective-permute-start.30
  147.5 3.5 %collective-permute-start.31 = (bf16[4,12,1152]{2,1,0:T(8,128)(2,1)S(1)}, bf16[4,12,1152]{2,1,0:T(8,128)(2,1)S(1)}, u32[]{:S(2)}, u32[]{:S(2)}) collective-permute-start(bf16[4,12,1152]{2,1,0:T(8,128)(2,1)S(1)} %get-tuple-element.77), channel_id=1, source_target_pairs={{0,36},{4,32},{32,4},{36,0},{64,100},{68,96},{96,68},{100,64},{128... | collective-permute-start | bytes 331784 | tf_op jit(solution)/shard_map/ppermute | solution.py:228
  151.5 5.0 %collective-permute-done.30 = bf16[4,12,1152]{2,1,0:T(8,128)(2,1)S(1)} collective-permute-done((bf16[4,12,1152]{2,1,0:T(8,128)(2,1)S(1)}, bf16[4,12,1152]{2,1,0:T(8,128)(2,1)S(1)}, u32[]{:S(2)}, u32[]{:S(2)}) %collective-permute-start.30) | collective-permute-done | bytes 110624 | tf_op jit(solution)/shard_map/ppermute | solution.py:228
  156.5 10.3 %collective-permute-done.31 = bf16[4,12,1152]{2,1,0:T(8,128)(2,1)S(1)} collective-permute-done((bf16[4,12,1152]{2,1,0:T(8,128)(2,1)S(1)}, bf16[4,12,1152]{2,1,0:T(8,128)(2,1)S(1)}, u32[]{:S(2)}, u32[]{:S(2)}) %collective-permute-start.31) | collective-permute-done | bytes 110624 | tf_op jit(solution)/shard_map/ppermute | solution.py:228
  166.8 2.7 %collective-permute-done.29 = bf16[4,12,1152]{2,1,0:T(8,128)(2,1)S(1)} collective-permute-done((bf16[4,12,1152]{2,1,0:T(8,128)(2,1)S(1)}, bf16[4,12,1152]{2,1,0:T(8,128)(2,1)S(1)}, u32[]{:S(2)}, u32[]{:S(2)}) %collective-permute-start.29) | collective-permute-done | bytes 110624 | tf_op jit(solution)/shard_map/ppermute | solution.py:228
  169.6 2.5 %collective-permute-start.32 = (bf16[12,1152]{1,0:T(8,128)(2,1)S(1)}, bf16[12,1152]{1,0:T(8,128)(2,1)S(1)}, u32[]{:S(2)}, u32[]{:S(2)}) collective-permute-start(bf16[12,1152]{1,0:T(8,128)(2,1)S(1)} %get-tuple-element.82), channel_id=1, source_target_pairs={{0,64},{32,96},{64,0},{96,32},{128,192},{160,224},{192,128},{224,1... | collective-permute-start | bytes 82952 | tf_op jit(solution)/shard_map/ppermute | solution.py:228
  172.1 2.9 %collective-permute-start.34 = (bf16[12,1152]{1,0:T(8,128)(2,1)S(1)}, bf16[12,1152]{1,0:T(8,128)(2,1)S(1)}, u32[]{:S(2)}, u32[]{:S(2)}) collective-permute-start(bf16[12,1152]{1,0:T(8,128)(2,1)S(1)} %get-tuple-element.83), channel_id=1, source_target_pairs={{0,192},{32,224},{64,128},{96,160},{128,64},{160,96},{192,0},{224,... | collective-permute-start | bytes 82952 | tf_op jit(solution)/shard_map/ppermute | solution.py:228
  175.0 1.2 collective-permute-start.33
  176.2 2.3 %reshape.29 = bf16[1,512,768]{2,1,0:T(8,128)(2,1)} reshape(bf16[128,4,768]{2,1,0:T(4,128)(2,1)} %all-to-all-done.1) | data formatting | bytes 1572864 | tf_op jit(solution)/shard_map/reshape | solution.py:322
  178.5 4.4 %collective-permute-done.33 = bf16[12,1152]{1,0:T(8,128)(2,1)S(1)} collective-permute-done((bf16[12,1152]{1,0:T(8,128)(2,1)S(1)}, bf16[12,1152]{1,0:T(8,128)(2,1)S(1)}, u32[]{:S(2)}, u32[]{:S(2)}) %collective-permute-start.33) | collective-permute-done | bytes 27680 | tf_op jit(solution)/shard_map/ppermute | solution.py:228
  (85 shorter events, 9.8 us)
Async XLA Ops:
  0.6 9.8 %copy-start = (bf16[1,512,1536]{2,1,0:T(8,128)(2,1)S(1)}, bf16[1,512,1536]{2,1,0:T(8,128)(2,1)}, u32[]{:S(2)}) copy-start(bf16[1,512,1536]{2,1,0:T(8,128)(2,1)} %param.3) | copy-start | bytes 4718596
  0.6 9.9 %copy-start.9 = (bf16[1,512,384]{2,1,0:T(8,128)(2,1)S(1)}, bf16[1,512,384]{2,1,0:T(8,128)(2,1)}, u32[]{:S(2)}) copy-start(bf16[1,512,384]{2,1,0:T(8,128)(2,1)} %param.4) | copy-start | bytes 1179652
  1.6 10.9 %collective-permute-start.2 = (bf16[12,1152]{1,0:T(8,128)(2,1)S(1)}, bf16[12,1152]{1,0:T(8,128)(2,1)S(1)}, u32[]{:S(2)}, u32[]{:S(2)}) collective-permute-start(bf16[12,1152]{1,0:T(8,128)(2,1)S(1)} %bitcast.46), channel_id=1, source_target_pairs={{0,192},{32,224},{64,128},{96,160},{128,64},{160,96},{192,0},{224,... | collective-permute-start | bytes 82952 | tf_op jit(solution)/shard_map/ppermute | solution.py:228
  8.0 8.4 %collective-permute-start.1 = (bf16[12,1152]{1,0:T(8,128)(2,1)S(1)}, bf16[12,1152]{1,0:T(8,128)(2,1)S(1)}, u32[]{:S(2)}, u32[]{:S(2)}) collective-permute-start(bf16[12,1152]{1,0:T(8,128)(2,1)S(1)} %bitcast.47), channel_id=1, source_target_pairs={{0,128},{32,160},{64,192},{96,224},{128,0},{160,32},{192,64},{224,... | collective-permute-start | bytes 82952 | tf_op jit(solution)/shard_map/ppermute | solution.py:228
  9.0 7.4 %collective-permute-start = (bf16[12,1152]{1,0:T(8,128)(2,1)S(1)}, bf16[12,1152]{1,0:T(8,128)(2,1)S(1)}, u32[]{:S(2)}, u32[]{:S(2)}) collective-permute-start(bf16[12,1152]{1,0:T(8,128)(2,1)S(1)} %bitcast.48), channel_id=1, source_target_pairs={{0,64},{32,96},{64,0},{96,32},{128,192},{160,224},{192,128},{224,1... | collective-permute-start | bytes 82952 | tf_op jit(solution)/shard_map/ppermute | solution.py:228
  10.5 0.8 copy-start.10
  16.4 16.3 %collective-permute-start.4 = (bf16[4,12,1152]{2,1,0:T(8,128)(2,1)S(1)}, bf16[4,12,1152]{2,1,0:T(8,128)(2,1)S(1)}, u32[]{:S(2)}, u32[]{:S(2)}) collective-permute-start(bf16[4,12,1152]{2,1,0:T(8,128)(2,1)S(1)} %pad_maximum_fusion.4), channel_id=1, source_target_pairs={{0,32},{4,36},{32,0},{36,4},{64,96},{68,100},{96,64},{100,68},{128... | collective-permute-start | bytes 331784 | tf_op jit(solution)/shard_map/ppermute | solution.py:228
  17.6 15.1 %collective-permute-start.5 = (bf16[4,12,1152]{2,1,0:T(8,128)(2,1)S(1)}, bf16[4,12,1152]{2,1,0:T(8,128)(2,1)}, u32[]{:S(2)}, u32[]{:S(2)}) collective-permute-start(bf16[4,12,1152]{2,1,0:T(8,128)(2,1)S(1)} %pad_maximum_fusion.4), channel_id=1, source_target_pairs={{0,36},{4,32},{32,4},{36,0},{64,100},{68,96},{96,68},{100,64},{128... | collective-permute-start | bytes 331784 | tf_op jit(solution)/shard_map/ppermute | solution.py:228
  19.4 14.4 %collective-permute-start.3 = (bf16[4,12,1152]{2,1,0:T(8,128)(2,1)S(1)}, bf16[4,12,1152]{2,1,0:T(8,128)(2,1)S(1)}, u32[]{:S(2)}, u32[]{:S(2)}) collective-permute-start(bf16[4,12,1152]{2,1,0:T(8,128)(2,1)S(1)} %pad_maximum_fusion.4), channel_id=1, source_target_pairs={{0,4},{4,0},{32,36},{36,32},{64,68},{68,64},{96,100},{100,96},{128... | collective-permute-start | bytes 331784 | tf_op jit(solution)/shard_map/ppermute | solution.py:228
  21.5 43.1 %all-to-all-start = ((bf16[128,4,1152]{2,1,0:T(4,128)(2,1)}), bf16[128,4,1152]{2,1,0:T(4,128)(2,1)S(1)}, u32[]{:S(2)}, u32[]{:S(2)}) async-start(bf16[128,4,1152]{2,1,0:T(4,128)(2,1)} %reshape.25), calls=%async_computation | async-start | bytes 2359296 | tf_op jit(solution)/shard_map/all_to_all | solution.py:295
  64.9 1.0 copy-start.1
  65.9 18.5 %collective-permute-start.12 = (bf16[512,768]{1,0:T(8,128)(2,1)S(1)}, bf16[512,768]{1,0:T(8,128)(2,1)S(1)}, u32[]{:S(2)}, u32[]{:S(2)}) collective-permute-start(bf16[512,768]{1,0:T(8,128)(2,1)S(1)} %get-tuple-element.43), channel_id=1, source_target_pairs={{0,1},{1,0},{2,3},{3,2},{4,5},{5,4},{6,7},{7,6},{8,9},{9,8},{10,11... | collective-permute-start | bytes 2359304 | tf_op jit(solution)/shard_map/ppermute | solution.py:299
  66.7 8.3 %collective-permute-start.8 = (bf16[4,24,1152]{2,1,0:T(8,128)(2,1)S(1)}, bf16[4,24,1152]{2,1,0:T(8,128)(2,1)S(1)}, u32[]{:S(2)}, u32[]{:S(2)}) collective-permute-start(bf16[4,24,1152]{2,1,0:T(8,128)(2,1)S(1)} %bitcast.38), channel_id=1, source_target_pairs={{0,8},{8,16},{16,24},{24,0},{1,9},{9,17},{17,25},{25,1},{2,10},{10... | collective-permute-start | bytes 663560 | tf_op jit(solution)/shard_map/ppermute | solution.py:224
  67.0 8.9 %collective-permute-start.7 = (bf16[4,24,1152]{2,1,0:T(8,128)(2,1)S(1)}, bf16[4,24,1152]{2,1,0:T(8,128)(2,1)S(1)}, u32[]{:S(2)}, u32[]{:S(2)}) collective-permute-start(bf16[4,24,1152]{2,1,0:T(8,128)(2,1)S(1)} %bitcast.34), channel_id=1, source_target_pairs={{0,24},{8,0},{16,8},{24,16},{1,25},{9,1},{17,9},{25,17},{2,26},{10... | collective-permute-start | bytes 663560 | tf_op jit(solution)/shard_map/ppermute | solution.py:224
  70.0 10.4 %collective-permute-start.6 = (bf16[4,24,1152]{2,1,0:T(8,128)(2,1)S(1)}, bf16[4,24,1152]{2,1,0:T(8,128)(2,1)}, u32[]{:S(2)}, u32[]{:S(2)}) collective-permute-start(bf16[4,24,1152]{2,1,0:T(8,128)(2,1)S(1)} %bitcast.39), channel_id=1, source_target_pairs={{0,24},{8,0},{16,8},{24,16},{1,25},{9,1},{17,9},{25,17},{2,26},{10... | collective-permute-start | bytes 663560 | tf_op jit(solution)/shard_map/ppermute | solution.py:224
  70.0 10.4 %collective-permute-start.11 = (bf16[4,24,1152]{2,1,0:T(8,128)(2,1)S(1)}, bf16[4,24,1152]{2,1,0:T(8,128)(2,1)}, u32[]{:S(2)}, u32[]{:S(2)}) collective-permute-start(bf16[4,24,1152]{2,1,0:T(8,128)(2,1)S(1)} %bitcast.35), channel_id=1, source_target_pairs={{0,8},{8,16},{16,24},{24,0},{1,9},{9,17},{17,25},{25,1},{2,10},{10... | collective-permute-start | bytes 663560 | tf_op jit(solution)/shard_map/ppermute | solution.py:224
  75.0 8.6 %collective-permute-start.9 = (bf16[4,24,1152]{2,1,0:T(8,128)(2,1)S(1)}, bf16[4,24,1152]{2,1,0:T(8,128)(2,1)}, u32[]{:S(2)}, u32[]{:S(2)}) collective-permute-start(bf16[4,24,1152]{2,1,0:T(8,128)(2,1)S(1)} %collective-permute-done.8.refs_6_), channel_id=1, source_target_pairs={{0,8},{8,16},{16,24},{24,0},{1,9},{9,17},{17,25},{25,1},{2,10},{10... | collective-permute-start | bytes 663560 | tf_op jit(solution)/shard_map/ppermute | solution.py:224
  75.9 7.8 %collective-permute-start.10 = (bf16[4,24,1152]{2,1,0:T(8,128)(2,1)S(1)}, bf16[4,24,1152]{2,1,0:T(8,128)(2,1)}, u32[]{:S(2)}, u32[]{:S(2)}) collective-permute-start(bf16[4,24,1152]{2,1,0:T(8,128)(2,1)S(1)} %collective-permute-done.7.refs_3_), channel_id=1, source_target_pairs={{0,24},{8,0},{16,8},{24,16},{1,25},{9,1},{17,9},{25,17},{2,26},{10... | collective-permute-start | bytes 663560 | tf_op jit(solution)/shard_map/ppermute | solution.py:224
  80.4 4.0 %collective-permute-start.13 = (bf16[4,24,1152]{2,1,0:T(8,128)(2,1)S(1)}, bf16[4,24,1152]{2,1,0:T(8,128)(2,1)S(1)}, u32[]{:S(2)}, u32[]{:S(2)}) collective-permute-start(bf16[4,24,1152]{2,1,0:T(8,128)(2,1)S(1)} %bitcast.40), channel_id=1, source_target_pairs={{0,2},{2,0},{1,3},{3,1},{4,6},{6,4},{5,7},{7,5},{8,10},{10,8},{9,1... | collective-permute-start | bytes 663560 | tf_op jit(solution)/shard_map/ppermute | solution.py:307
  80.4 5.2 %collective-permute-start.14 = (bf16[4,24,1152]{2,1,0:T(8,128)(2,1)S(1)}, bf16[4,24,1152]{2,1,0:T(8,128)(2,1)S(1)}, u32[]{:S(2)}, u32[]{:S(2)}) collective-permute-start(bf16[4,24,1152]{2,1,0:T(8,128)(2,1)S(1)} %bitcast.36), channel_id=1, source_target_pairs={{0,2},{2,0},{1,3},{3,1},{4,6},{6,4},{5,7},{7,5},{8,10},{10,8},{9,1... | collective-permute-start | bytes 663560 | tf_op jit(solution)/shard_map/ppermute | solution.py:307
  83.6 2.7 %collective-permute-start.19 = (bf16[4,24,1152]{2,1,0:T(8,128)(2,1)S(1)}, bf16[4,24,1152]{2,1,0:T(8,128)(2,1)S(1)}, u32[]{:S(2)}, u32[]{:S(2)}) collective-permute-start(bf16[4,24,1152]{2,1,0:T(8,128)(2,1)S(1)} %collective-permute-done.8.refs_6_), channel_id=1, source_target_pairs={{0,2},{2,0},{1,3},{3,1},{4,6},{6,4},{5,7},{7,5},{8,10},{10,8},{9,1... | collective-permute-start | bytes 663560 | tf_op jit(solution)/shard_map/ppermute | solution.py:307
  83.6 3.9 %collective-permute-start.15 = (bf16[4,24,1152]{2,1,0:T(8,128)(2,1)}, bf16[4,24,1152]{2,1,0:T(8,128)(2,1)}, u32[]{:S(2)}, u32[]{:S(2)}) collective-permute-start(bf16[4,24,1152]{2,1,0:T(8,128)(2,1)} %collective-permute-done.6.refs_2_), channel_id=1, source_target_pairs={{0,2},{2,0},{1,3},{3,1},{4,6},{6,4},{5,7},{7,5},{8,10},{10,8},{9,1... | collective-permute-start | bytes 663560 | tf_op jit(solution)/shard_map/ppermute | solution.py:307
  84.4 3.2 %collective-permute-start.20 = (bf16[4,24,1152]{2,1,0:T(8,128)(2,1)}, bf16[4,24,1152]{2,1,0:T(8,128)(2,1)}, u32[]{:S(2)}, u32[]{:S(2)}) collective-permute-start(bf16[4,24,1152]{2,1,0:T(8,128)(2,1)} %collective-permute-done.11.refs_7_), channel_id=1, source_target_pairs={{0,2},{2,0},{1,3},{3,1},{4,6},{6,4},{5,7},{7,5},{8,10},{10,8},{9,1... | collective-permute-start | bytes 663560 | tf_op jit(solution)/shard_map/ppermute | solution.py:307
  84.4 0.7 copy-start.3
  85.1 2.5 %collective-permute-start.16 = (bf16[4,24,1152]{2,1,0:T(8,128)(2,1)S(1)}, bf16[4,24,1152]{2,1,0:T(8,128)(2,1)}, u32[]{:S(2)}, u32[]{:S(2)}) collective-permute-start(bf16[4,24,1152]{2,1,0:T(8,128)(2,1)S(1)} %collective-permute-done.7.refs_3_), channel_id=1, source_target_pairs={{0,2},{2,0},{1,3},{3,1},{4,6},{6,4},{5,7},{7,5},{8,10},{10,8},{9,1... | collective-permute-start | bytes 663560 | tf_op jit(solution)/shard_map/ppermute | solution.py:307
  85.6 0.7 copy-start.5
  86.3 1.8 collective-permute-start.17
  86.3 0.7 copy-start.7
  87.0 2.0 %collective-permute-start.18 = (bf16[4,24,1152]{2,1,0:T(8,128)(2,1)}, bf16[4,24,1152]{2,1,0:T(8,128)(2,1)}, u32[]{:S(2)}, u32[]{:S(2)}) collective-permute-start(bf16[4,24,1152]{2,1,0:T(8,128)(2,1)} %collective-permute-done.10.refs_5_), channel_id=1, source_target_pairs={{0,2},{2,0},{1,3},{3,1},{4,6},{6,4},{5,7},{7,5},{8,10},{10,8},{9,1... | collective-permute-start | bytes 663560 | tf_op jit(solution)/shard_map/ppermute | solution.py:309
  88.9 1.3 copy-start.2
  90.2 0.9 copy-start.4
  91.1 0.9 copy-start.6
  92.1 0.9 copy-start.8
  109.9 3.8 %collective-permute-start.21 = (bf16[4,8,24,1152]{3,2,1,0:T(8,128)(2,1)S(1)}, bf16[4,8,24,1152]{3,2,1,0:T(8,128)(2,1)S(1)}, u32[]{:S(2)}, u32[]{:S(2)}) collective-permute-start(bf16[4,8,24,1152]{3,2,1,0:T(8,128)(2,1)S(1)} %get-tuple-element.54), channel_id=1, source_target_pairs={{0,2},{2,0},{1,3},{3,1},{4,6},{6,4},{5,7},{7,5},{8,10},{10,8},{9,1... | collective-permute-start | bytes 5308424 | tf_op jit(solution)/shard_map/ppermute | solution.py:252
  110.3 19.6 %collective-permute-start.24 = (bf16[512,768]{1,0:T(8,128)(2,1)S(1)}, bf16[512,768]{1,0:T(8,128)(2,1)S(1)}, u32[]{:S(2)}, u32[]{:S(2)}) collective-permute-start(bf16[512,768]{1,0:T(8,128)(2,1)S(1)} %get-tuple-element.59), channel_id=1, source_target_pairs={{0,1},{1,0},{2,3},{3,2},{4,5},{5,4},{6,7},{7,6},{8,9},{9,8},{10,11... | collective-permute-start | bytes 2359304 | tf_op jit(solution)/shard_map/ppermute | solution.py:313
  114.0 15.9 %collective-permute-start.22 = (bf16[4,24,1152]{2,1,0:T(8,128)(2,1)S(1)}, bf16[4,24,1152]{2,1,0:T(8,128)(2,1)S(1)}, u32[]{:S(2)}, u32[]{:S(2)}) collective-permute-start(bf16[4,24,1152]{2,1,0:T(8,128)(2,1)S(1)} %get-tuple-element.57), channel_id=1, source_target_pairs={{0,8},{8,16},{16,24},{24,0},{1,9},{9,17},{17,25},{25,1},{2,10},{10... | collective-permute-start | bytes 663560 | tf_op jit(solution)/shard_map/ppermute | solution.py:224
  115.5 14.5 %collective-permute-start.23 = (bf16[4,24,1152]{2,1,0:T(8,128)(2,1)S(1)}, bf16[4,24,1152]{2,1,0:T(8,128)(2,1)S(1)}, u32[]{:S(2)}, u32[]{:S(2)}) collective-permute-start(bf16[4,24,1152]{2,1,0:T(8,128)(2,1)S(1)} %get-tuple-element.58), channel_id=1, source_target_pairs={{0,24},{8,0},{16,8},{24,16},{1,25},{9,1},{17,9},{25,17},{2,26},{10... | collective-permute-start | bytes 663560 | tf_op jit(solution)/shard_map/ppermute | solution.py:224
  117.4 27.4 %collective-permute-start.26 = (bf16[4,24,1152]{2,1,0:T(8,128)(2,1)S(1)}, bf16[4,24,1152]{2,1,0:T(8,128)(2,1)}, u32[]{:S(2)}, u32[]{:S(2)}) collective-permute-start(bf16[4,24,1152]{2,1,0:T(8,128)(2,1)S(1)} %get-tuple-element.66), channel_id=1, source_target_pairs={{0,24},{8,0},{16,8},{24,16},{1,25},{9,1},{17,9},{25,17},{2,26},{10... | collective-permute-start | bytes 663560 | tf_op jit(solution)/shard_map/ppermute | solution.py:224
  118.9 25.9 %collective-permute-start.27 = (bf16[4,24,1152]{2,1,0:T(8,128)(2,1)S(1)}, bf16[4,24,1152]{2,1,0:T(8,128)(2,1)}, u32[]{:S(2)}, u32[]{:S(2)}) collective-permute-start(bf16[4,24,1152]{2,1,0:T(8,128)(2,1)S(1)} %get-tuple-element.67), channel_id=1, source_target_pairs={{0,8},{8,16},{16,24},{24,0},{1,9},{9,17},{17,25},{25,1},{2,10},{10... | collective-permute-start | bytes 663560 | tf_op jit(solution)/shard_map/ppermute | solution.py:224
  131.2 13.5 %collective-permute-start.25 = (bf16[4,24,1152]{2,1,0:T(8,128)(2,1)S(1)}, bf16[4,24,1152]{2,1,0:T(8,128)(2,1)}, u32[]{:S(2)}, u32[]{:S(2)}) collective-permute-start(bf16[4,24,1152]{2,1,0:T(8,128)(2,1)S(1)} %add_convert_fusion.1), channel_id=1, source_target_pairs={{0,8},{8,16},{16,24},{24,0},{1,9},{9,17},{17,25},{25,1},{2,10},{10... | collective-permute-start | bytes 663560 | tf_op jit(solution)/shard_map/ppermute | solution.py:224
  132.7 12.1 %collective-permute-start.28 = (bf16[4,24,1152]{2,1,0:T(8,128)(2,1)S(1)}, bf16[4,24,1152]{2,1,0:T(8,128)(2,1)}, u32[]{:S(2)}, u32[]{:S(2)}) collective-permute-start(bf16[4,24,1152]{2,1,0:T(8,128)(2,1)S(1)} %add_convert_fusion), channel_id=1, source_target_pairs={{0,24},{8,0},{16,8},{24,16},{1,25},{9,1},{17,9},{25,17},{2,26},{10... | collective-permute-start | bytes 663560 | tf_op jit(solution)/shard_map/ppermute | solution.py:224
  134.6 35.0 %all-to-all-start.1 = ((bf16[128,4,768]{2,1,0:T(4,128)(2,1)}), bf16[128,4,768]{2,1,0:T(4,128)(2,1)}, u32[]{:S(2)}, u32[]{:S(2)}) async-start(bf16[128,4,768]{2,1,0:T(4,128)(2,1)} %add_parts.1), calls=%async_computation.1 | async-start | bytes 1572864 | tf_op jit(solution)/shard_map/all_to_all | solution.py:319
  146.4 10.1 %collective-permute-start.30 = (bf16[4,12,1152]{2,1,0:T(8,128)(2,1)S(1)}, bf16[4,12,1152]{2,1,0:T(8,128)(2,1)S(1)}, u32[]{:S(2)}, u32[]{:S(2)}) collective-permute-start(bf16[4,12,1152]{2,1,0:T(8,128)(2,1)S(1)} %get-tuple-element.76), channel_id=1, source_target_pairs={{0,4},{4,0},{32,36},{36,32},{64,68},{68,64},{96,100},{100,96},{128... | collective-permute-start | bytes 331784 | tf_op jit(solution)/shard_map/ppermute | solution.py:228
  147.5 19.3 %collective-permute-start.31 = (bf16[4,12,1152]{2,1,0:T(8,128)(2,1)S(1)}, bf16[4,12,1152]{2,1,0:T(8,128)(2,1)S(1)}, u32[]{:S(2)}, u32[]{:S(2)}) collective-permute-start(bf16[4,12,1152]{2,1,0:T(8,128)(2,1)S(1)} %get-tuple-element.77), channel_id=1, source_target_pairs={{0,36},{4,32},{32,4},{36,0},{64,100},{68,96},{96,68},{100,64},{128... | collective-permute-start | bytes 331784 | tf_op jit(solution)/shard_map/ppermute | solution.py:228
  150.9 18.6 %collective-permute-start.29 = (bf16[4,12,1152]{2,1,0:T(8,128)(2,1)S(1)}, bf16[4,12,1152]{2,1,0:T(8,128)(2,1)S(1)}, u32[]{:S(2)}, u32[]{:S(2)}) collective-permute-start(bf16[4,12,1152]{2,1,0:T(8,128)(2,1)S(1)} %slice.81), channel_id=1, source_target_pairs={{0,32},{4,36},{32,0},{36,4},{64,96},{68,100},{96,64},{100,68},{128... | collective-permute-start | bytes 331784 | tf_op jit(solution)/shard_map/ppermute | solution.py:228
  169.6 8.8 %collective-permute-start.32 = (bf16[12,1152]{1,0:T(8,128)(2,1)S(1)}, bf16[12,1152]{1,0:T(8,128)(2,1)S(1)}, u32[]{:S(2)}, u32[]{:S(2)}) collective-permute-start(bf16[12,1152]{1,0:T(8,128)(2,1)S(1)} %get-tuple-element.82), channel_id=1, source_target_pairs={{0,64},{32,96},{64,0},{96,32},{128,192},{160,224},{192,128},{224,1... | collective-permute-start | bytes 82952 | tf_op jit(solution)/shard_map/ppermute | solution.py:228
  172.1 6.4 %collective-permute-start.34 = (bf16[12,1152]{1,0:T(8,128)(2,1)S(1)}, bf16[12,1152]{1,0:T(8,128)(2,1)S(1)}, u32[]{:S(2)}, u32[]{:S(2)}) collective-permute-start(bf16[12,1152]{1,0:T(8,128)(2,1)S(1)} %get-tuple-element.83), channel_id=1, source_target_pairs={{0,192},{32,224},{64,128},{96,160},{128,64},{160,96},{192,0},{224,... | collective-permute-start | bytes 82952 | tf_op jit(solution)/shard_map/ppermute | solution.py:228
  175.0 7.9 %collective-permute-start.33 = (bf16[12,1152]{1,0:T(8,128)(2,1)S(1)}, bf16[12,1152]{1,0:T(8,128)(2,1)S(1)}, u32[]{:S(2)}, u32[]{:S(2)}) collective-permute-start(bf16[12,1152]{1,0:T(8,128)(2,1)S(1)} %get-tuple-element.84), channel_id=1, source_target_pairs={{0,128},{32,160},{64,192},{96,224},{128,0},{160,32},{192,64},{224,... | collective-permute-start | bytes 82952 | tf_op jit(solution)/shard_map/ppermute | solution.py:228

commit v12 on v9

--- a/solution.py
+++ b/solution.py
@@ -19,9 +19,10 @@
     return lax.dot_general(a, b, dims, preferred_element_type=f32)
 
 
-def core_kernel(where_ref, t_ref, o_ref, *refs):
+def core_kernel(where_ref, x_ref, o_ref, *refs):
     pieces = refs[:16]
-    give_ref, keep_ref, mine_ref, rest_ref, w_ref, s_ref, d_ref, g_ref = refs[16:]
+    give_ref, keep_ref, mine_ref, rest_ref, w_ref, s_ref, d_ref, g_ref, t_ref = refs[16:]
+    t_ref[...] = x_ref[...].astype(f32).reshape(t_ref.shape).astype(bf16)
     z, y, c, m = (where_ref[i] for i in range(4))
     unit = XH * C * ROWS
 
@@ -85,10 +86,8 @@
     keep_ref[...] = dot(g, w_ref[near, :], NT).astype(bf16)
     step = 384
     for ref, of in ((t_ref, m), (o_ref, 1 - m)):
-
-        @pl.loop(0, part_cols // step)
-        def _(i, ref=ref, of=of):
-            total = dot(ref[:, pl.ds(pl.multiple_of(i * step, step), step)], g_ref[...], TN)
+        for i in range(part_cols // step):
+            total = dot(ref[:, i * step : (i + 1) * step], g_ref[...], TN)
             for b in range(step // unit):
                 quarters = [total[b * unit + r * ROWS :][:ROWS] for r in range(4)]
                 first = jnp.concatenate([quarters[0], quarters[2]], 0)
@@ -102,7 +101,7 @@
 
 def core(where, tokens, others, mine, rest):
     rows, part_cols = others.shape
-    half = tokens.shape[1] - part_cols
+    half = tokens.shape[2] - part_cols
     width, n = MP * part_cols, 3 * half
     vm = pl.BlockSpec(memory_space=pltpu.VMEM)
     return pl.pallas_call(
@@ -120,6 +119,7 @@
             pltpu.VMEM((4 * half // 128, rows, 128), f32),
             pltpu.VMEM((3 * half // 128, rows, 128), f32),
             pltpu.VMEM((rows, n), bf16),
+            pltpu.VMEM((rows, part_cols + half), bf16),
         ],
         compiler_params=pltpu.CompilerParams(vmem_limit_bytes=VMEM_LIMIT),
         cost_estimate=pl.CostEstimate(
@@ -181,6 +181,24 @@
         cost_estimate=pl.CostEstimate(flops=0, bytes_accessed=2**20, transcendentals=0),
         name="add_parts",
     )(a, b)
+
+
+def rows_kernel(x_ref, part_ref):
+    cols = part_ref.shape[1]
+    part_ref[...] = x_ref[:, :, :cols].astype(f32).reshape(part_ref.shape).astype(bf16)
+
+
+def part_rows(x, part_cols):
+    vm = pl.BlockSpec(memory_space=pltpu.VMEM)
+    return pl.pallas_call(
+        rows_kernel,
+        out_shape=jax.ShapeDtypeStruct((x.shape[0] * x.shape[1], part_cols), bf16),
+        in_specs=[vm],
+        out_specs=vm,
+        compiler_params=pltpu.CompilerParams(vmem_limit_bytes=16 * 2**20),
+        cost_estimate=pl.CostEstimate(flops=0, bytes_accessed=2**20, transcendentals=0),
+        name="part_rows",
+    )(x)
 
 
 FR = ("z", "y", "xh", "c")
@@ -261,19 +279,16 @@
     tokens, rows = lax.optimization_barrier((tokens, rows))
     tokens = lax.all_to_all(tokens, FR, 0, 0, tiled=True)
     low, high = near_zx(rows)
-    part = tokens[:, :, :cols]
+    part = part_rows(tokens, cols)
     low, high, part = lax.optimization_barrier((low, high, part))
     others = lax.ppermute(part, "mp", PAIR)
     before_low = shift(low, "y", Y, 1)
     after_high = shift(high, "y", Y, Y - 1)
     before_high = shift(high, "y", Y, 1)
     after_low = shift(low, "y", Y, Y - 1)
-    tokens = tokens.reshape(F * count, cols + half)
-    before_low, after_high, tokens = lax.optimization_barrier((before_low, after_high, tokens))
     far_low = shift(before_low, "y", Y, 1)
     far_high = shift(after_high, "y", Y, Y - 1)
     mine = [low, high, after_low, after_high, far_low, far_high, before_low, before_high]
-    others = others.reshape(F * count, cols)
     rest = {i: lax.ppermute(mine[i], "c", PAIR) for i in (0, 1, 2, 3, 6, 7)}
     mine, others = lax.optimization_barrier((mine, others))
     rest.update({i: lax.ppermute(mine[i], "c", PAIR) for i in (4, 5)})

time: 181 us -> 182 us (level)
    unnamed x14 -> x24, local copies, waits for them, and re-layouts: 2.55 us -> 8.47 us
    ppermute x12, waiting for transfers between devices: 3.11 us -> 7.06 us  [shift(): return lax.ppermute(x, axis, [(i, (i + by) % size) for i in range(size)])]
    reshape x2 -> x0, local copies, waits for them, and re-layouts: 3.93 us -> none  [the longest x1 2.37 us: on_device(): tokens = tokens.reshape(F * count, cols + half)]
    ppermute x1, waiting for transfers between devices: 3.46 us -> 0.25 us  [on_device(): others = lax.ppermute(part, 'mp', PAIR)]
  transfers between devices with their start and end apart: 37 -> 37, of which waited for: 16 -> 15; matrix products, arithmetic and copies ran while one was open for 6% -> 3% of each run, Pallas kernels for 1% -> 1%
where the time goes in v12:
time: 182 us
  waiting for transfers between devices  79.1 us (43%)
  starting transfers between devices  69.5 us (38%)
  Pallas kernels  16.9 us (9%)
  local copies, waits for them, and re-layouts  12.8 us (7%)
  other arithmetic  2.2 us (1%)
    all_to_all x1, waiting for transfers between devices, on_device(): tokens = lax.all_to_all(tokens, FR, 0, 0, tiled=True)  31.5 us
    ppermute x12, waiting for transfers between devices, across(): return lax.ppermute(x, axis, [(i, i ^ by) for i in range(size)])  26.2 us
    ppermute x12, starting transfers between devices, across(): return lax.ppermute(x, axis, [(i, i ^ by) for i in range(size)])  25.6 us
    ppermute x12, starting transfers between devices, shift(): return lax.ppermute(x, axis, [(i, (i + by) % size) for i in range(size)])  18.2 us
    pallas_call x1, Pallas kernels, core(): pl.pallas_call(core_kernel, out_shape=(jax.ShapeDtypeStruct((rows, part_c...  15.1 us
    all_to_all x1, starting transfers between devices, on_device(): tokens = lax.all_to_all(tokens, FR, 0, 0, tiled=True)  11.2 us
    ppermute x1, waiting for transfers between devices, on_device(): got = lax.ppermute(give, 'mp', PAIR)  10.4 us
    all_to_all x1, starting transfers between devices, to_frames(): return lax.all_to_all(x, FR, 0, 0, tiled=True)  10.2 us
  transfers between devices with their start and end apart: 37, of which 15 were waited for; matrix products, arithmetic and copies ran while one was open for 3% of the time, Pallas kernels for 1%

profile of v12, /device:TPU:6, one launch (start us, length us, event | category | flops | bytes accessed | tf_op | source)
XLA Modules:
  0.0 181.6 jit_solution(15825934620087709533)
XLA Ops:
  0.7 0.9 pad.26
  1.6 6.4 %collective-permute-start.2 = (bf16[12,1152]{1,0:T(8,128)(2,1)S(1)}, bf16[12,1152]{1,0:T(8,128)(2,1)S(1)}, u32[]{:S(2)}, u32[]{:S(2)}) collective-permute-start(bf16[12,1152]{1,0:T(8,128)(2,1)S(1)} %bitcast.46), channel_id=1, source_target_pairs={{0,192},{32,224},{64,128},{96,160},{128,64},{160,96},{192,0},{224,... | collective-permute-start | bytes 82952 | tf_op jit(solution)/shard_map/ppermute | solution.py:213
  8.0 1.0 collective-permute-start.1
  9.0 1.5 collective-permute-start
  11.3 1.2 reshape.25
  12.5 3.8 %collective-permute-done.1 = bf16[12,1152]{1,0:T(8,128)(2,1)S(1)} collective-permute-done((bf16[12,1152]{1,0:T(8,128)(2,1)S(1)}, bf16[12,1152]{1,0:T(8,128)(2,1)S(1)}, u32[]{:S(2)}, u32[]{:S(2)}) %collective-permute-start.1) | collective-permute-done | bytes 27680 | tf_op jit(solution)/shard_map/ppermute | solution.py:213
  16.4 1.2 collective-permute-start.4
  17.6 1.8 collective-permute-start.5
  19.4 2.1 %collective-permute-start.3 = (bf16[4,12,1152]{2,1,0:T(8,128)(2,1)S(1)}, bf16[4,12,1152]{2,1,0:T(8,128)(2,1)S(1)}, u32[]{:S(2)}, u32[]{:S(2)}) collective-permute-start(bf16[4,12,1152]{2,1,0:T(8,128)(2,1)S(1)} %pad_maximum_fusion.4), channel_id=1, source_target_pairs={{0,4},{4,0},{32,36},{36,32},{64,68},{68,64},{96,100},{100,96},{128... | collective-permute-start | bytes 331784 | tf_op jit(solution)/shard_map/ppermute | solution.py:213
  21.5 11.2 %all-to-all-start = ((bf16[128,4,1152]{2,1,0:T(4,128)(2,1)}), bf16[128,4,1152]{2,1,0:T(4,128)(2,1)S(1)}, u32[]{:S(2)}, u32[]{:S(2)}) async-start(bf16[128,4,1152]{2,1,0:T(4,128)(2,1)} %reshape.25), calls=%async_computation | async-start | bytes 2359296 | tf_op jit(solution)/shard_map/all_to_all | solution.py:280
  33.1 31.5 %all-to-all-done.x_ref = bf16[128,4,1152]{2,1,0:T(4,128)(2,1)S(1)} async-done(((bf16[128,4,1152]{2,1,0:T(4,128)(2,1)}), bf16[128,4,1152]{2,1,0:T(4,128)(2,1)S(1)}, u32[]{:S(2)}, u32[]{:S(2)}) %all-to-all-start) | async-done | bytes 1179680 | tf_op jit(solution)/shard_map/all_to_all | solution.py:280
  64.8 0.9 collective-permute-start.12
  65.9 3.0 %collective-permute-start.7 = (bf16[4,24,1152]{2,1,0:T(8,128)(2,1)S(1)}, bf16[4,24,1152]{2,1,0:T(8,128)(2,1)}, u32[]{:S(2)}, u32[]{:S(2)}) collective-permute-start(bf16[4,24,1152]{2,1,0:T(8,128)(2,1)S(1)} %bitcast.34), channel_id=1, source_target_pairs={{0,24},{8,0},{16,8},{24,16},{1,25},{9,1},{17,9},{25,17},{2,26},{10... | collective-permute-start | bytes 663560 | tf_op jit(solution)/shard_map/ppermute | solution.py:209
  68.9 2.0 %collective-permute-start.11 = (bf16[4,24,1152]{2,1,0:T(8,128)(2,1)S(1)}, bf16[4,24,1152]{2,1,0:T(8,128)(2,1)}, u32[]{:S(2)}, u32[]{:S(2)}) collective-permute-start(bf16[4,24,1152]{2,1,0:T(8,128)(2,1)S(1)} %bitcast.35), channel_id=1, source_target_pairs={{0,8},{8,16},{16,24},{24,0},{1,9},{9,17},{17,25},{25,1},{2,10},{10... | collective-permute-start | bytes 663560 | tf_op jit(solution)/shard_map/ppermute | solution.py:209
  70.9 3.0 %collective-permute-done.8.refs_6_ = bf16[4,24,1152]{2,1,0:T(8,128)(2,1)S(1)} collective-permute-done((bf16[4,24,1152]{2,1,0:T(8,128)(2,1)S(1)}, bf16[4,24,1152]{2,1,0:T(8,128)(2,1)S(1)}, u32[]{:S(2)}, u32[]{:S(2)}) %collective-permute-start.8) | collective-permute-done | bytes 221216 | tf_op jit(solution)/shard_map/ppermute | solution.py:209
  74.8 3.8 %collective-permute-start.10 = (bf16[4,24,1152]{2,1,0:T(8,128)(2,1)}, bf16[4,24,1152]{2,1,0:T(8,128)(2,1)}, u32[]{:S(2)}, u32[]{:S(2)}) collective-permute-start(bf16[4,24,1152]{2,1,0:T(8,128)(2,1)} %collective-permute-done.7.refs_3_), channel_id=1, source_target_pairs={{0,24},{8,0},{16,8},{24,16},{1,25},{9,1},{17,9},{25,17},{2,26},{10... | collective-permute-start | bytes 663560 | tf_op jit(solution)/shard_map/ppermute | solution.py:209
  78.6 0.8 collective-permute-done.6.refs_2_
  79.9 2.7 %collective-permute-done.9.refs_4_ = bf16[4,24,1152]{2,1,0:T(8,128)(2,1)} collective-permute-done((bf16[4,24,1152]{2,1,0:T(8,128)(2,1)S(1)}, bf16[4,24,1152]{2,1,0:T(8,128)(2,1)}, u32[]{:S(2)}, u32[]{:S(2)}) %collective-permute-start.9) | collective-permute-done | bytes 221216 | tf_op jit(solution)/shard_map/ppermute | solution.py:209
  83.3 0.9 copy-done.1
  84.2 0.7 copy-done.3
  85.4 0.7 copy-done.5
  87.9 0.8 collective-permute-done.18.refs_13_
  88.7 1.1 copy-done.2
  89.9 0.9 copy-done.4
  90.8 0.9 copy-done.6
  91.7 0.9 copy-done.8
  92.7 15.1 %attention_core.1 = (bf16[512,768]{1,0:T(8,128)(2,1)S(1)}, bf16[512,768]{1,0:T(8,128)(2,1)S(1)}, bf16[4,8,24,1152]{3,2,1,0:T(8,128)(2,1)S(1)}, bf16[4,8,24,1152]{3,2,1,0:T(8,128)(2,1)S(1)}) custom-call(s32[4]{0:T(128)S(1)} %pad_add_fusion.where_ref, bf16[128,4,1152]{2,1,0:T(4,128)(2,1)S(1)} %all-to-all-done.x_ref, bf16[512,768]{1,0:T(8,128)(2,1)S(1)} %copy-done.2, ...), custom_call_target="tpu_custom_call" | custom-call | flops 5435817984 | bytes 8388608 | tf_op jit(solution)/shard_map/attention_core/pallas_call | solution.py:107
  108.3 0.9 collective-permute-start.24
  109.2 2.4 %collective-permute-done.21.other_ref = bf16[4,8,24,1152]{3,2,1,0:T(8,128)(2,1)S(1)} collective-permute-done((bf16[4,8,24,1152]{3,2,1,0:T(8,128)(2,1)S(1)}, bf16[4,8,24,1152]{3,2,1,0:T(8,128)(2,1)S(1)}, u32[]{:S(2)}, u32[]{:S(2)}) %collective-permute-start.21) | collective-permute-done | bytes 1769504 | tf_op jit(solution)/shard_map/ppermute | solution.py:237
  112.0 1.4 collective-permute-start.22
  113.4 2.1 %collective-permute-start.23 = (bf16[4,24,1152]{2,1,0:T(8,128)(2,1)S(1)}, bf16[4,24,1152]{2,1,0:T(8,128)(2,1)S(1)}, u32[]{:S(2)}, u32[]{:S(2)}) collective-permute-start(bf16[4,24,1152]{2,1,0:T(8,128)(2,1)S(1)} %get-tuple-element.54), channel_id=1, source_target_pairs={{0,24},{8,0},{16,8},{24,16},{1,25},{9,1},{17,9},{25,17},{2,26},{10... | collective-permute-start | bytes 663560 | tf_op jit(solution)/shard_map/ppermute | solution.py:209
  115.5 1.7 collective-permute-start.26
  117.5 10.4 %collective-permute-done.24.b_ref = bf16[512,768]{1,0:T(8,128)(2,1)S(1)} collective-permute-done((bf16[512,768]{1,0:T(8,128)(2,1)S(1)}, bf16[512,768]{1,0:T(8,128)(2,1)S(1)}, u32[]{:S(2)}, u32[]{:S(2)}) %collective-permute-start.24) | collective-permute-done | bytes 786464 | tf_op jit(solution)/shard_map/ppermute | solution.py:298
  127.9 1.2 add_parts.1
  129.2 1.4 collective-permute-start.25
  130.6 1.9 %collective-permute-start.28 = (bf16[4,24,1152]{2,1,0:T(8,128)(2,1)S(1)}, bf16[4,24,1152]{2,1,0:T(8,128)(2,1)}, u32[]{:S(2)}, u32[]{:S(2)}) collective-permute-start(bf16[4,24,1152]{2,1,0:T(8,128)(2,1)S(1)} %add_convert_fusion), channel_id=1, source_target_pairs={{0,24},{8,0},{16,8},{24,16},{1,25},{9,1},{17,9},{25,17},{2,26},{10... | collective-permute-start | bytes 663560 | tf_op jit(solution)/shard_map/ppermute | solution.py:209
  132.5 10.2 %all-to-all-start.1 = ((bf16[128,4,768]{2,1,0:T(4,128)(2,1)}), bf16[128,4,768]{2,1,0:T(4,128)(2,1)}, u32[]{:S(2)}, u32[]{:S(2)}) async-start(bf16[128,4,768]{2,1,0:T(4,128)(2,1)} %add_parts.1), calls=%async_computation.1 | async-start | bytes 1572864 | tf_op jit(solution)/shard_map/all_to_all | solution.py:304
  142.8 1.4 convert_add_fusion.1
  144.4 1.0 collective-permute-start.30
  145.4 3.5 %collective-permute-start.31 = (bf16[4,12,1152]{2,1,0:T(8,128)(2,1)S(1)}, bf16[4,12,1152]{2,1,0:T(8,128)(2,1)S(1)}, u32[]{:S(2)}, u32[]{:S(2)}) collective-permute-start(bf16[4,12,1152]{2,1,0:T(8,128)(2,1)S(1)} %get-tuple-element.73), channel_id=1, source_target_pairs={{0,36},{4,32},{32,4},{36,0},{64,100},{68,96},{96,68},{100,64},{128... | collective-permute-start | bytes 331784 | tf_op jit(solution)/shard_map/ppermute | solution.py:213
  149.5 5.0 %collective-permute-done.30 = bf16[4,12,1152]{2,1,0:T(8,128)(2,1)S(1)} collective-permute-done((bf16[4,12,1152]{2,1,0:T(8,128)(2,1)S(1)}, bf16[4,12,1152]{2,1,0:T(8,128)(2,1)S(1)}, u32[]{:S(2)}, u32[]{:S(2)}) %collective-permute-start.30) | collective-permute-done | bytes 110624 | tf_op jit(solution)/shard_map/ppermute | solution.py:213
  154.5 10.3 %collective-permute-done.31 = bf16[4,12,1152]{2,1,0:T(8,128)(2,1)S(1)} collective-permute-done((bf16[4,12,1152]{2,1,0:T(8,128)(2,1)S(1)}, bf16[4,12,1152]{2,1,0:T(8,128)(2,1)S(1)}, u32[]{:S(2)}, u32[]{:S(2)}) %collective-permute-start.31) | collective-permute-done | bytes 110624 | tf_op jit(solution)/shard_map/ppermute | solution.py:213
  164.8 2.7 %collective-permute-done.29 = bf16[4,12,1152]{2,1,0:T(8,128)(2,1)S(1)} collective-permute-done((bf16[4,12,1152]{2,1,0:T(8,128)(2,1)S(1)}, bf16[4,12,1152]{2,1,0:T(8,128)(2,1)S(1)}, u32[]{:S(2)}, u32[]{:S(2)}) %collective-permute-start.29) | collective-permute-done | bytes 110624 | tf_op jit(solution)/shard_map/ppermute | solution.py:213
  167.6 2.5 %collective-permute-start.32 = (bf16[12,1152]{1,0:T(8,128)(2,1)S(1)}, bf16[12,1152]{1,0:T(8,128)(2,1)S(1)}, u32[]{:S(2)}, u32[]{:S(2)}) collective-permute-start(bf16[12,1152]{1,0:T(8,128)(2,1)S(1)} %get-tuple-element.78), channel_id=1, source_target_pairs={{0,64},{32,96},{64,0},{96,32},{128,192},{160,224},{192,128},{224,1... | collective-permute-start | bytes 82952 | tf_op jit(solution)/shard_map/ppermute | solution.py:213
  170.1 2.9 %collective-permute-start.34 = (bf16[12,1152]{1,0:T(8,128)(2,1)S(1)}, bf16[12,1152]{1,0:T(8,128)(2,1)S(1)}, u32[]{:S(2)}, u32[]{:S(2)}) collective-permute-start(bf16[12,1152]{1,0:T(8,128)(2,1)S(1)} %get-tuple-element.79), channel_id=1, source_target_pairs={{0,192},{32,224},{64,128},{96,160},{128,64},{160,96},{192,0},{224,... | collective-permute-start | bytes 82952 | tf_op jit(solution)/shard_map/ppermute | solution.py:213
  173.0 1.2 collective-permute-start.33
  174.2 2.3 %reshape.29 = bf16[1,512,768]{2,1,0:T(8,128)(2,1)} reshape(bf16[128,4,768]{2,1,0:T(4,128)(2,1)} %all-to-all-done.1) | data formatting | bytes 1572864 | tf_op jit(solution)/shard_map/reshape | solution.py:307
  176.5 4.4 %collective-permute-done.33 = bf16[12,1152]{1,0:T(8,128)(2,1)S(1)} collective-permute-done((bf16[12,1152]{1,0:T(8,128)(2,1)S(1)}, bf16[12,1152]{1,0:T(8,128)(2,1)S(1)}, u32[]{:S(2)}, u32[]{:S(2)}) %collective-permute-start.33) | collective-permute-done | bytes 27680 | tf_op jit(solution)/shard_map/ppermute | solution.py:213
  (85 shorter events, 8.9 us)
Async XLA Ops:
  0.6 9.8 %copy-start = (bf16[1,512,1536]{2,1,0:T(8,128)(2,1)S(1)}, bf16[1,512,1536]{2,1,0:T(8,128)(2,1)}, u32[]{:S(2)}) copy-start(bf16[1,512,1536]{2,1,0:T(8,128)(2,1)} %param.3) | copy-start | bytes 4718596
  0.6 9.9 %copy-start.9 = (bf16[1,512,384]{2,1,0:T(8,128)(2,1)S(1)}, bf16[1,512,384]{2,1,0:T(8,128)(2,1)}, u32[]{:S(2)}) copy-start(bf16[1,512,384]{2,1,0:T(8,128)(2,1)} %param.4) | copy-start | bytes 1179652
  1.6 10.9 %collective-permute-start.2 = (bf16[12,1152]{1,0:T(8,128)(2,1)S(1)}, bf16[12,1152]{1,0:T(8,128)(2,1)S(1)}, u32[]{:S(2)}, u32[]{:S(2)}) collective-permute-start(bf16[12,1152]{1,0:T(8,128)(2,1)S(1)} %bitcast.46), channel_id=1, source_target_pairs={{0,192},{32,224},{64,128},{96,160},{128,64},{160,96},{192,0},{224,... | collective-permute-start | bytes 82952 | tf_op jit(solution)/shard_map/ppermute | solution.py:213
  8.0 8.4 %collective-permute-start.1 = (bf16[12,1152]{1,0:T(8,128)(2,1)S(1)}, bf16[12,1152]{1,0:T(8,128)(2,1)S(1)}, u32[]{:S(2)}, u32[]{:S(2)}) collective-permute-start(bf16[12,1152]{1,0:T(8,128)(2,1)S(1)} %bitcast.47), channel_id=1, source_target_pairs={{0,128},{32,160},{64,192},{96,224},{128,0},{160,32},{192,64},{224,... | collective-permute-start | bytes 82952 | tf_op jit(solution)/shard_map/ppermute | solution.py:213
  9.0 7.4 %collective-permute-start = (bf16[12,1152]{1,0:T(8,128)(2,1)S(1)}, bf16[12,1152]{1,0:T(8,128)(2,1)S(1)}, u32[]{:S(2)}, u32[]{:S(2)}) collective-permute-start(bf16[12,1152]{1,0:T(8,128)(2,1)S(1)} %bitcast.48), channel_id=1, source_target_pairs={{0,64},{32,96},{64,0},{96,32},{128,192},{160,224},{192,128},{224,1... | collective-permute-start | bytes 82952 | tf_op jit(solution)/shard_map/ppermute | solution.py:213
  10.5 0.8 copy-start.10
  16.4 16.3 %collective-permute-start.4 = (bf16[4,12,1152]{2,1,0:T(8,128)(2,1)S(1)}, bf16[4,12,1152]{2,1,0:T(8,128)(2,1)S(1)}, u32[]{:S(2)}, u32[]{:S(2)}) collective-permute-start(bf16[4,12,1152]{2,1,0:T(8,128)(2,1)S(1)} %pad_maximum_fusion.4), channel_id=1, source_target_pairs={{0,32},{4,36},{32,0},{36,4},{64,96},{68,100},{96,64},{100,68},{128... | collective-permute-start | bytes 331784 | tf_op jit(solution)/shard_map/ppermute | solution.py:213
  17.6 15.1 %collective-permute-start.5 = (bf16[4,12,1152]{2,1,0:T(8,128)(2,1)S(1)}, bf16[4,12,1152]{2,1,0:T(8,128)(2,1)S(1)}, u32[]{:S(2)}, u32[]{:S(2)}) collective-permute-start(bf16[4,12,1152]{2,1,0:T(8,128)(2,1)S(1)} %pad_maximum_fusion.4), channel_id=1, source_target_pairs={{0,36},{4,32},{32,4},{36,0},{64,100},{68,96},{96,68},{100,64},{128... | collective-permute-start | bytes 331784 | tf_op jit(solution)/shard_map/ppermute | solution.py:213
  19.4 13.5 %collective-permute-start.3 = (bf16[4,12,1152]{2,1,0:T(8,128)(2,1)S(1)}, bf16[4,12,1152]{2,1,0:T(8,128)(2,1)S(1)}, u32[]{:S(2)}, u32[]{:S(2)}) collective-permute-start(bf16[4,12,1152]{2,1,0:T(8,128)(2,1)S(1)} %pad_maximum_fusion.4), channel_id=1, source_target_pairs={{0,4},{4,0},{32,36},{36,32},{64,68},{68,64},{96,100},{100,96},{128... | collective-permute-start | bytes 331784 | tf_op jit(solution)/shard_map/ppermute | solution.py:213
  21.5 43.1 %all-to-all-start = ((bf16[128,4,1152]{2,1,0:T(4,128)(2,1)}), bf16[128,4,1152]{2,1,0:T(4,128)(2,1)S(1)}, u32[]{:S(2)}, u32[]{:S(2)}) async-start(bf16[128,4,1152]{2,1,0:T(4,128)(2,1)} %reshape.25), calls=%async_computation | async-start | bytes 2359296 | tf_op jit(solution)/shard_map/all_to_all | solution.py:280
  64.8 18.6 %collective-permute-start.12 = (bf16[512,768]{1,0:T(8,128)(2,1)S(1)}, bf16[512,768]{1,0:T(8,128)(2,1)S(1)}, u32[]{:S(2)}, u32[]{:S(2)}) collective-permute-start(bf16[512,768]{1,0:T(8,128)(2,1)S(1)} %part_rows.1), channel_id=1, source_target_pairs={{0,1},{1,0},{2,3},{3,2},{4,5},{5,4},{6,7},{7,6},{8,9},{9,8},{10,11... | collective-permute-start | bytes 2359304 | tf_op jit(solution)/shard_map/ppermute | solution.py:284
  65.7 8.3 %collective-permute-start.8 = (bf16[4,24,1152]{2,1,0:T(8,128)(2,1)S(1)}, bf16[4,24,1152]{2,1,0:T(8,128)(2,1)S(1)}, u32[]{:S(2)}, u32[]{:S(2)}) collective-permute-start(bf16[4,24,1152]{2,1,0:T(8,128)(2,1)S(1)} %bitcast.38), channel_id=1, source_target_pairs={{0,8},{8,16},{16,24},{24,0},{1,9},{9,17},{17,25},{25,1},{2,10},{10... | collective-permute-start | bytes 663560 | tf_op jit(solution)/shard_map/ppermute | solution.py:209
  65.9 8.9 %collective-permute-start.7 = (bf16[4,24,1152]{2,1,0:T(8,128)(2,1)S(1)}, bf16[4,24,1152]{2,1,0:T(8,128)(2,1)}, u32[]{:S(2)}, u32[]{:S(2)}) collective-permute-start(bf16[4,24,1152]{2,1,0:T(8,128)(2,1)S(1)} %bitcast.34), channel_id=1, source_target_pairs={{0,24},{8,0},{16,8},{24,16},{1,25},{9,1},{17,9},{25,17},{2,26},{10... | collective-permute-start | bytes 663560 | tf_op jit(solution)/shard_map/ppermute | solution.py:209
  68.9 10.4 %collective-permute-start.6 = (bf16[4,24,1152]{2,1,0:T(8,128)(2,1)S(1)}, bf16[4,24,1152]{2,1,0:T(8,128)(2,1)}, u32[]{:S(2)}, u32[]{:S(2)}) collective-permute-start(bf16[4,24,1152]{2,1,0:T(8,128)(2,1)S(1)} %bitcast.39), channel_id=1, source_target_pairs={{0,24},{8,0},{16,8},{24,16},{1,25},{9,1},{17,9},{25,17},{2,26},{10... | collective-permute-start | bytes 663560 | tf_op jit(solution)/shard_map/ppermute | solution.py:209
  68.9 10.4 %collective-permute-start.11 = (bf16[4,24,1152]{2,1,0:T(8,128)(2,1)S(1)}, bf16[4,24,1152]{2,1,0:T(8,128)(2,1)}, u32[]{:S(2)}, u32[]{:S(2)}) collective-permute-start(bf16[4,24,1152]{2,1,0:T(8,128)(2,1)S(1)} %bitcast.35), channel_id=1, source_target_pairs={{0,8},{8,16},{16,24},{24,0},{1,9},{9,17},{17,25},{25,1},{2,10},{10... | collective-permute-start | bytes 663560 | tf_op jit(solution)/shard_map/ppermute | solution.py:209
  74.0 8.6 %collective-permute-start.9 = (bf16[4,24,1152]{2,1,0:T(8,128)(2,1)S(1)}, bf16[4,24,1152]{2,1,0:T(8,128)(2,1)}, u32[]{:S(2)}, u32[]{:S(2)}) collective-permute-start(bf16[4,24,1152]{2,1,0:T(8,128)(2,1)S(1)} %collective-permute-done.8.refs_6_), channel_id=1, source_target_pairs={{0,8},{8,16},{16,24},{24,0},{1,9},{9,17},{17,25},{25,1},{2,10},{10... | collective-permute-start | bytes 663560 | tf_op jit(solution)/shard_map/ppermute | solution.py:209
  74.8 7.8 %collective-permute-start.10 = (bf16[4,24,1152]{2,1,0:T(8,128)(2,1)}, bf16[4,24,1152]{2,1,0:T(8,128)(2,1)}, u32[]{:S(2)}, u32[]{:S(2)}) collective-permute-start(bf16[4,24,1152]{2,1,0:T(8,128)(2,1)} %collective-permute-done.7.refs_3_), channel_id=1, source_target_pairs={{0,24},{8,0},{16,8},{24,16},{1,25},{9,1},{17,9},{25,17},{2,26},{10... | collective-permute-start | bytes 663560 | tf_op jit(solution)/shard_map/ppermute | solution.py:209
  79.4 4.9 %collective-permute-start.13 = (bf16[4,24,1152]{2,1,0:T(8,128)(2,1)S(1)}, bf16[4,24,1152]{2,1,0:T(8,128)(2,1)S(1)}, u32[]{:S(2)}, u32[]{:S(2)}) collective-permute-start(bf16[4,24,1152]{2,1,0:T(8,128)(2,1)S(1)} %bitcast.40), channel_id=1, source_target_pairs={{0,2},{2,0},{1,3},{3,1},{4,6},{6,4},{5,7},{7,5},{8,10},{10,8},{9,1... | collective-permute-start | bytes 663560 | tf_op jit(solution)/shard_map/ppermute | solution.py:292
  79.4 6.1 %collective-permute-start.14 = (bf16[4,24,1152]{2,1,0:T(8,128)(2,1)S(1)}, bf16[4,24,1152]{2,1,0:T(8,128)(2,1)S(1)}, u32[]{:S(2)}, u32[]{:S(2)}) collective-permute-start(bf16[4,24,1152]{2,1,0:T(8,128)(2,1)S(1)} %bitcast.36), channel_id=1, source_target_pairs={{0,2},{2,0},{1,3},{3,1},{4,6},{6,4},{5,7},{7,5},{8,10},{10,8},{9,1... | collective-permute-start | bytes 663560 | tf_op jit(solution)/shard_map/ppermute | solution.py:292
  82.6 3.5 %collective-permute-start.19 = (bf16[4,24,1152]{2,1,0:T(8,128)(2,1)S(1)}, bf16[4,24,1152]{2,1,0:T(8,128)(2,1)S(1)}, u32[]{:S(2)}, u32[]{:S(2)}) collective-permute-start(bf16[4,24,1152]{2,1,0:T(8,128)(2,1)S(1)} %collective-permute-done.8.refs_6_), channel_id=1, source_target_pairs={{0,2},{2,0},{1,3},{3,1},{4,6},{6,4},{5,7},{7,5},{8,10},{10,8},{9,1... | collective-permute-start | bytes 663560 | tf_op jit(solution)/shard_map/ppermute | solution.py:292
  82.6 4.8 %collective-permute-start.15 = (bf16[4,24,1152]{2,1,0:T(8,128)(2,1)}, bf16[4,24,1152]{2,1,0:T(8,128)(2,1)}, u32[]{:S(2)}, u32[]{:S(2)}) collective-permute-start(bf16[4,24,1152]{2,1,0:T(8,128)(2,1)} %collective-permute-done.6.refs_2_), channel_id=1, source_target_pairs={{0,2},{2,0},{1,3},{3,1},{4,6},{6,4},{5,7},{7,5},{8,10},{10,8},{9,1... | collective-permute-start | bytes 663560 | tf_op jit(solution)/shard_map/ppermute | solution.py:292
  83.3 0.9 copy-start.1
  84.2 3.2 %collective-permute-start.20 = (bf16[4,24,1152]{2,1,0:T(8,128)(2,1)}, bf16[4,24,1152]{2,1,0:T(8,128)(2,1)}, u32[]{:S(2)}, u32[]{:S(2)}) collective-permute-start(bf16[4,24,1152]{2,1,0:T(8,128)(2,1)} %collective-permute-done.11.refs_7_), channel_id=1, source_target_pairs={{0,2},{2,0},{1,3},{3,1},{4,6},{6,4},{5,7},{7,5},{8,10},{10,8},{9,1... | collective-permute-start | bytes 663560 | tf_op jit(solution)/shard_map/ppermute | solution.py:292
  84.2 0.7 copy-start.3
  84.9 2.5 %collective-permute-start.16 = (bf16[4,24,1152]{2,1,0:T(8,128)(2,1)}, bf16[4,24,1152]{2,1,0:T(8,128)(2,1)}, u32[]{:S(2)}, u32[]{:S(2)}) collective-permute-start(bf16[4,24,1152]{2,1,0:T(8,128)(2,1)} %collective-permute-done.7.refs_3_), channel_id=1, source_target_pairs={{0,2},{2,0},{1,3},{3,1},{4,6},{6,4},{5,7},{7,5},{8,10},{10,8},{9,1... | collective-permute-start | bytes 663560 | tf_op jit(solution)/shard_map/ppermute | solution.py:292
  85.4 0.7 copy-start.5
  86.1 1.8 %collective-permute-start.17 = (bf16[4,24,1152]{2,1,0:T(8,128)(2,1)}, bf16[4,24,1152]{2,1,0:T(8,128)(2,1)}, u32[]{:S(2)}, u32[]{:S(2)}) collective-permute-start(bf16[4,24,1152]{2,1,0:T(8,128)(2,1)} %collective-permute-done.9.refs_4_), channel_id=1, source_target_pairs={{0,2},{2,0},{1,3},{3,1},{4,6},{6,4},{5,7},{7,5},{8,10},{10,8},{9,1... | collective-permute-start | bytes 663560 | tf_op jit(solution)/shard_map/ppermute | solution.py:294
  86.1 0.7 copy-start.7
  86.8 2.0 %collective-permute-start.18 = (bf16[4,24,1152]{2,1,0:T(8,128)(2,1)}, bf16[4,24,1152]{2,1,0:T(8,128)(2,1)}, u32[]{:S(2)}, u32[]{:S(2)}) collective-permute-start(bf16[4,24,1152]{2,1,0:T(8,128)(2,1)} %collective-permute-done.10.refs_5_), channel_id=1, source_target_pairs={{0,2},{2,0},{1,3},{3,1},{4,6},{6,4},{5,7},{7,5},{8,10},{10,8},{9,1... | collective-permute-start | bytes 663560 | tf_op jit(solution)/shard_map/ppermute | solution.py:294
  88.7 1.1 copy-start.2
  89.9 0.9 copy-start.4
  90.8 0.9 copy-start.6
  91.7 0.9 copy-start.8
  107.8 3.8 %collective-permute-start.21 = (bf16[4,8,24,1152]{3,2,1,0:T(8,128)(2,1)S(1)}, bf16[4,8,24,1152]{3,2,1,0:T(8,128)(2,1)S(1)}, u32[]{:S(2)}, u32[]{:S(2)}) collective-permute-start(bf16[4,8,24,1152]{3,2,1,0:T(8,128)(2,1)S(1)} %get-tuple-element.50), channel_id=1, source_target_pairs={{0,2},{2,0},{1,3},{3,1},{4,6},{6,4},{5,7},{7,5},{8,10},{10,8},{9,1... | collective-permute-start | bytes 5308424 | tf_op jit(solution)/shard_map/ppermute | solution.py:237
  108.3 19.6 %collective-permute-start.24 = (bf16[512,768]{1,0:T(8,128)(2,1)S(1)}, bf16[512,768]{1,0:T(8,128)(2,1)S(1)}, u32[]{:S(2)}, u32[]{:S(2)}) collective-permute-start(bf16[512,768]{1,0:T(8,128)(2,1)S(1)} %get-tuple-element.55), channel_id=1, source_target_pairs={{0,1},{1,0},{2,3},{3,2},{4,5},{5,4},{6,7},{7,6},{8,9},{9,8},{10,11... | collective-permute-start | bytes 2359304 | tf_op jit(solution)/shard_map/ppermute | solution.py:298
  112.0 15.9 %collective-permute-start.22 = (bf16[4,24,1152]{2,1,0:T(8,128)(2,1)S(1)}, bf16[4,24,1152]{2,1,0:T(8,128)(2,1)S(1)}, u32[]{:S(2)}, u32[]{:S(2)}) collective-permute-start(bf16[4,24,1152]{2,1,0:T(8,128)(2,1)S(1)} %get-tuple-element.53), channel_id=1, source_target_pairs={{0,8},{8,16},{16,24},{24,0},{1,9},{9,17},{17,25},{25,1},{2,10},{10... | collective-permute-start | bytes 663560 | tf_op jit(solution)/shard_map/ppermute | solution.py:209
  113.4 14.5 %collective-permute-start.23 = (bf16[4,24,1152]{2,1,0:T(8,128)(2,1)S(1)}, bf16[4,24,1152]{2,1,0:T(8,128)(2,1)S(1)}, u32[]{:S(2)}, u32[]{:S(2)}) collective-permute-start(bf16[4,24,1152]{2,1,0:T(8,128)(2,1)S(1)} %get-tuple-element.54), channel_id=1, source_target_pairs={{0,24},{8,0},{16,8},{24,16},{1,25},{9,1},{17,9},{25,17},{2,26},{10... | collective-permute-start | bytes 663560 | tf_op jit(solution)/shard_map/ppermute | solution.py:209
  115.5 27.3 %collective-permute-start.26 = (bf16[4,24,1152]{2,1,0:T(8,128)(2,1)S(1)}, bf16[4,24,1152]{2,1,0:T(8,128)(2,1)}, u32[]{:S(2)}, u32[]{:S(2)}) collective-permute-start(bf16[4,24,1152]{2,1,0:T(8,128)(2,1)S(1)} %get-tuple-element.62), channel_id=1, source_target_pairs={{0,24},{8,0},{16,8},{24,16},{1,25},{9,1},{17,9},{25,17},{2,26},{10... | collective-permute-start | bytes 663560 | tf_op jit(solution)/shard_map/ppermute | solution.py:209
  117.2 25.5 %collective-permute-start.27 = (bf16[4,24,1152]{2,1,0:T(8,128)(2,1)S(1)}, bf16[4,24,1152]{2,1,0:T(8,128)(2,1)}, u32[]{:S(2)}, u32[]{:S(2)}) collective-permute-start(bf16[4,24,1152]{2,1,0:T(8,128)(2,1)S(1)} %get-tuple-element.63), channel_id=1, source_target_pairs={{0,8},{8,16},{16,24},{24,0},{1,9},{9,17},{17,25},{25,1},{2,10},{10... | collective-permute-start | bytes 663560 | tf_op jit(solution)/shard_map/ppermute | solution.py:209
  129.2 13.5 %collective-permute-start.25 = (bf16[4,24,1152]{2,1,0:T(8,128)(2,1)S(1)}, bf16[4,24,1152]{2,1,0:T(8,128)(2,1)}, u32[]{:S(2)}, u32[]{:S(2)}) collective-permute-start(bf16[4,24,1152]{2,1,0:T(8,128)(2,1)S(1)} %add_convert_fusion.1), channel_id=1, source_target_pairs={{0,8},{8,16},{16,24},{24,0},{1,9},{9,17},{17,25},{25,1},{2,10},{10... | collective-permute-start | bytes 663560 | tf_op jit(solution)/shard_map/ppermute | solution.py:209
  130.6 12.1 %collective-permute-start.28 = (bf16[4,24,1152]{2,1,0:T(8,128)(2,1)S(1)}, bf16[4,24,1152]{2,1,0:T(8,128)(2,1)}, u32[]{:S(2)}, u32[]{:S(2)}) collective-permute-start(bf16[4,24,1152]{2,1,0:T(8,128)(2,1)S(1)} %add_convert_fusion), channel_id=1, source_target_pairs={{0,24},{8,0},{16,8},{24,16},{1,25},{9,1},{17,9},{25,17},{2,26},{10... | collective-permute-start | bytes 663560 | tf_op jit(solution)/shard_map/ppermute | solution.py:209
  132.5 35.0 %all-to-all-start.1 = ((bf16[128,4,768]{2,1,0:T(4,128)(2,1)}), bf16[128,4,768]{2,1,0:T(4,128)(2,1)}, u32[]{:S(2)}, u32[]{:S(2)}) async-start(bf16[128,4,768]{2,1,0:T(4,128)(2,1)} %add_parts.1), calls=%async_computation.1 | async-start | bytes 1572864 | tf_op jit(solution)/shard_map/all_to_all | solution.py:304
  144.4 10.1 %collective-permute-start.30 = (bf16[4,12,1152]{2,1,0:T(8,128)(2,1)S(1)}, bf16[4,12,1152]{2,1,0:T(8,128)(2,1)S(1)}, u32[]{:S(2)}, u32[]{:S(2)}) collective-permute-start(bf16[4,12,1152]{2,1,0:T(8,128)(2,1)S(1)} %get-tuple-element.72), channel_id=1, source_target_pairs={{0,4},{4,0},{32,36},{36,32},{64,68},{68,64},{96,100},{100,96},{128... | collective-permute-start | bytes 331784 | tf_op jit(solution)/shard_map/ppermute | solution.py:213
  145.4 19.3 %collective-permute-start.31 = (bf16[4,12,1152]{2,1,0:T(8,128)(2,1)S(1)}, bf16[4,12,1152]{2,1,0:T(8,128)(2,1)S(1)}, u32[]{:S(2)}, u32[]{:S(2)}) collective-permute-start(bf16[4,12,1152]{2,1,0:T(8,128)(2,1)S(1)} %get-tuple-element.73), channel_id=1, source_target_pairs={{0,36},{4,32},{32,4},{36,0},{64,100},{68,96},{96,68},{100,64},{128... | collective-permute-start | bytes 331784 | tf_op jit(solution)/shard_map/ppermute | solution.py:213
  148.9 18.6 %collective-permute-start.29 = (bf16[4,12,1152]{2,1,0:T(8,128)(2,1)S(1)}, bf16[4,12,1152]{2,1,0:T(8,128)(2,1)S(1)}, u32[]{:S(2)}, u32[]{:S(2)}) collective-permute-start(bf16[4,12,1152]{2,1,0:T(8,128)(2,1)S(1)} %slice.81), channel_id=1, source_target_pairs={{0,32},{4,36},{32,0},{36,4},{64,96},{68,100},{96,64},{100,68},{128... | collective-permute-start | bytes 331784 | tf_op jit(solution)/shard_map/ppermute | solution.py:213
  167.6 8.8 %collective-permute-start.32 = (bf16[12,1152]{1,0:T(8,128)(2,1)S(1)}, bf16[12,1152]{1,0:T(8,128)(2,1)S(1)}, u32[]{:S(2)}, u32[]{:S(2)}) collective-permute-start(bf16[12,1152]{1,0:T(8,128)(2,1)S(1)} %get-tuple-element.78), channel_id=1, source_target_pairs={{0,64},{32,96},{64,0},{96,32},{128,192},{160,224},{192,128},{224,1... | collective-permute-start | bytes 82952 | tf_op jit(solution)/shard_map/ppermute | solution.py:213
  170.1 6.4 %collective-permute-start.34 = (bf16[12,1152]{1,0:T(8,128)(2,1)S(1)}, bf16[12,1152]{1,0:T(8,128)(2,1)S(1)}, u32[]{:S(2)}, u32[]{:S(2)}) collective-permute-start(bf16[12,1152]{1,0:T(8,128)(2,1)S(1)} %get-tuple-element.79), channel_id=1, source_target_pairs={{0,192},{32,224},{64,128},{96,160},{128,64},{160,96},{192,0},{224,... | collective-permute-start | bytes 82952 | tf_op jit(solution)/shard_map/ppermute | solution.py:213
  173.0 7.9 %collective-permute-start.33 = (bf16[12,1152]{1,0:T(8,128)(2,1)S(1)}, bf16[12,1152]{1,0:T(8,128)(2,1)S(1)}, u32[]{:S(2)}, u32[]{:S(2)}) collective-permute-start(bf16[12,1152]{1,0:T(8,128)(2,1)S(1)} %get-tuple-element.80), channel_id=1, source_target_pairs={{0,128},{32,160},{64,192},{96,224},{128,0},{160,32},{192,64},{224,... | collective-permute-start | bytes 82952 | tf_op jit(solution)/shard_map/ppermute | solution.py:213

commit v13 on v12

--- a/solution.py
+++ b/solution.py
@@ -9,7 +9,8 @@
 Z, Y, XH, C, MP = 8, 4, 2, 2, 2
 F = 128
 ROWS = 12
-VMEM_LIMIT = 32 * 2**20
+VMEM_LIMIT = 16 * 2**20
+CORE_LIMIT = 56 * 2**20
 bf16, f32 = jnp.bfloat16, jnp.float32
 NT = (((1,), (1,)), ((), ()))
 TN = (((0,), (0,)), ((), ()))
@@ -121,7 +122,7 @@
             pltpu.VMEM((rows, n), bf16),
             pltpu.VMEM((rows, part_cols + half), bf16),
         ],
-        compiler_params=pltpu.CompilerParams(vmem_limit_bytes=VMEM_LIMIT),
+        compiler_params=pltpu.CompilerParams(vmem_limit_bytes=CORE_LIMIT),
         cost_estimate=pl.CostEstimate(
             flops=6 * rows * width * n, bytes_accessed=8 * 2**20, transcendentals=0
         ),

time: 182 us -> 179 us (0.984)
  local copies, waits for them, and re-layouts: 12.8 us -> 9.14 us
  Pallas kernels: 16.9 us -> 19.5 us
    unnamed x24 -> x30, local copies, waits for them, and re-layouts: 8.47 us -> 4.77 us
    pallas_call x1, Pallas kernels: 15.1 us -> 17.7 us  [core(): pl.pallas_call(core_kernel, out_shape=(jax.ShapeDtypeStruct((rows, part_c...]
  transfers between devices with their start and end apart: 37 -> 37, of which waited for: 15 -> 15; matrix products, arithmetic and copies ran while one was open for 3% -> 4% of each run, Pallas kernels for 1% -> 1%
where the time goes in v13:
time: 179 us
  waiting for transfers between devices  78.2 us (44%)
  starting transfers between devices  68.2 us (38%)
  Pallas kernels  19.5 us (11%)
  local copies, waits for them, and re-layouts  9.14 us (5%)
  other arithmetic  2.71 us (2%)
    all_to_all x1, waiting for transfers between devices, on_device(): tokens = lax.all_to_all(tokens, FR, 0, 0, tiled=True)  31.5 us
    ppermute x12, waiting for transfers between devices, across(): return lax.ppermute(x, axis, [(i, i ^ by) for i in range(size)])  26.3 us
    ppermute x12, starting transfers between devices, across(): return lax.ppermute(x, axis, [(i, i ^ by) for i in range(size)])  25.6 us
    ppermute x12, starting transfers between devices, shift(): return lax.ppermute(x, axis, [(i, (i + by) % size) for i in range(size)])  18 us
    pallas_call x1, Pallas kernels, core(): pl.pallas_call(core_kernel, out_shape=(jax.ShapeDtypeStruct((rows, part_c...  17.7 us
    all_to_all x1, starting transfers between devices, on_device(): tokens = lax.all_to_all(tokens, FR, 0, 0, tiled=True)  11.2 us
    all_to_all x1, starting transfers between devices, to_frames(): return lax.all_to_all(x, FR, 0, 0, tiled=True)  9.95 us
    ppermute x1, waiting for transfers between devices, on_device(): got = lax.ppermute(give, 'mp', PAIR)  9.05 us
  transfers between devices with their start and end apart: 37, of which 15 were waited for; matrix products, arithmetic and copies ran while one was open for 4% of the time, Pallas kernels for 1%

profile of v13, /device:TPU:6, one launch (start us, length us, event | category | flops | bytes accessed | tf_op | source)
XLA Modules:
  0.0 178.8 jit_solution(16245721729803763958)
XLA Ops:
  0.7 0.9 pad.26
  1.6 6.4 %collective-permute-start.2 = (bf16[12,1152]{1,0:T(8,128)(2,1)S(1)}, bf16[12,1152]{1,0:T(8,128)(2,1)S(1)}, u32[]{:S(2)}, u32[]{:S(2)}) collective-permute-start(bf16[12,1152]{1,0:T(8,128)(2,1)S(1)} %bitcast.46), channel_id=1, source_target_pairs={{0,192},{32,224},{64,128},{96,160},{128,64},{160,96},{192,0},{224,... | collective-permute-start | bytes 82952 | tf_op jit(solution)/shard_map/ppermute | solution.py:214
  8.0 1.0 collective-permute-start.1
  9.0 1.5 collective-permute-start
  10.6 0.7 copy-done.7
  11.3 1.2 reshape.25
  12.6 3.8 %collective-permute-done.1 = bf16[12,1152]{1,0:T(8,128)(2,1)S(1)} collective-permute-done((bf16[12,1152]{1,0:T(8,128)(2,1)S(1)}, bf16[12,1152]{1,0:T(8,128)(2,1)S(1)}, u32[]{:S(2)}, u32[]{:S(2)}) %collective-permute-start.1) | collective-permute-done | bytes 27680 | tf_op jit(solution)/shard_map/ppermute | solution.py:214
  16.4 1.2 collective-permute-start.4
  17.6 1.8 %collective-permute-start.5 = (bf16[4,12,1152]{2,1,0:T(8,128)(2,1)S(1)}, bf16[4,12,1152]{2,1,0:T(8,128)(2,1)S(1)}, u32[]{:S(2)}, u32[]{:S(2)}) collective-permute-start(bf16[4,12,1152]{2,1,0:T(8,128)(2,1)S(1)} %pad_maximum_fusion.4), channel_id=1, source_target_pairs={{0,36},{4,32},{32,4},{36,0},{64,100},{68,96},{96,68},{100,64},{128... | collective-permute-start | bytes 331784 | tf_op jit(solution)/shard_map/ppermute | solution.py:214
  19.4 2.1 %collective-permute-start.3 = (bf16[4,12,1152]{2,1,0:T(8,128)(2,1)S(1)}, bf16[4,12,1152]{2,1,0:T(8,128)(2,1)S(1)}, u32[]{:S(2)}, u32[]{:S(2)}) collective-permute-start(bf16[4,12,1152]{2,1,0:T(8,128)(2,1)S(1)} %pad_maximum_fusion.4), channel_id=1, source_target_pairs={{0,4},{4,0},{32,36},{36,32},{64,68},{68,64},{96,100},{100,96},{128... | collective-permute-start | bytes 331784 | tf_op jit(solution)/shard_map/ppermute | solution.py:214
  21.5 11.2 %all-to-all-start = ((bf16[128,4,1152]{2,1,0:T(4,128)(2,1)}), bf16[128,4,1152]{2,1,0:T(4,128)(2,1)S(1)}, u32[]{:S(2)}, u32[]{:S(2)}) async-start(bf16[128,4,1152]{2,1,0:T(4,128)(2,1)} %reshape.25), calls=%async_computation | async-start | bytes 2359296 | tf_op jit(solution)/shard_map/all_to_all | solution.py:281
  33.2 31.5 %all-to-all-done.x_ref = bf16[128,4,1152]{2,1,0:T(4,128)(2,1)S(1)} async-done(((bf16[128,4,1152]{2,1,0:T(4,128)(2,1)}), bf16[128,4,1152]{2,1,0:T(4,128)(2,1)S(1)}, u32[]{:S(2)}, u32[]{:S(2)}) %all-to-all-start) | async-done | bytes 1179680 | tf_op jit(solution)/shard_map/all_to_all | solution.py:281
  64.8 0.9 collective-permute-start.12
  65.9 3.0 %collective-permute-start.7 = (bf16[4,24,1152]{2,1,0:T(8,128)(2,1)S(1)}, bf16[4,24,1152]{2,1,0:T(8,128)(2,1)}, u32[]{:S(2)}, u32[]{:S(2)}) collective-permute-start(bf16[4,24,1152]{2,1,0:T(8,128)(2,1)S(1)} %bitcast.34), channel_id=1, source_target_pairs={{0,24},{8,0},{16,8},{24,16},{1,25},{9,1},{17,9},{25,17},{2,26},{10... | collective-permute-start | bytes 663560 | tf_op jit(solution)/shard_map/ppermute | solution.py:210
  68.9 2.0 %collective-permute-start.11 = (bf16[4,24,1152]{2,1,0:T(8,128)(2,1)S(1)}, bf16[4,24,1152]{2,1,0:T(8,128)(2,1)}, u32[]{:S(2)}, u32[]{:S(2)}) collective-permute-start(bf16[4,24,1152]{2,1,0:T(8,128)(2,1)S(1)} %bitcast.35), channel_id=1, source_target_pairs={{0,8},{8,16},{16,24},{24,0},{1,9},{9,17},{17,25},{25,1},{2,10},{10... | collective-permute-start | bytes 663560 | tf_op jit(solution)/shard_map/ppermute | solution.py:210
  70.9 3.0 %collective-permute-done.8.refs_6_ = bf16[4,24,1152]{2,1,0:T(8,128)(2,1)S(1)} collective-permute-done((bf16[4,24,1152]{2,1,0:T(8,128)(2,1)S(1)}, bf16[4,24,1152]{2,1,0:T(8,128)(2,1)S(1)}, u32[]{:S(2)}, u32[]{:S(2)}) %collective-permute-start.8) | collective-permute-done | bytes 221216 | tf_op jit(solution)/shard_map/ppermute | solution.py:210
  74.3 0.5 collective-permute-done.7.refs_3_
  74.8 3.8 %collective-permute-start.10 = (bf16[4,24,1152]{2,1,0:T(8,128)(2,1)}, bf16[4,24,1152]{2,1,0:T(8,128)(2,1)}, u32[]{:S(2)}, u32[]{:S(2)}) collective-permute-start(bf16[4,24,1152]{2,1,0:T(8,128)(2,1)} %collective-permute-done.7.refs_3_), channel_id=1, source_target_pairs={{0,24},{8,0},{16,8},{24,16},{1,25},{9,1},{17,9},{25,17},{2,26},{10... | collective-permute-start | bytes 663560 | tf_op jit(solution)/shard_map/ppermute | solution.py:210
  78.6 0.8 collective-permute-done.6.refs_2_
  79.9 2.7 %collective-permute-done.9.refs_4_ = bf16[4,24,1152]{2,1,0:T(8,128)(2,1)} collective-permute-done((bf16[4,24,1152]{2,1,0:T(8,128)(2,1)S(1)}, bf16[4,24,1152]{2,1,0:T(8,128)(2,1)}, u32[]{:S(2)}, u32[]{:S(2)}) %collective-permute-start.9) | collective-permute-done | bytes 221216 | tf_op jit(solution)/shard_map/ppermute | solution.py:210
  84.3 0.6 copy-done.11
  84.9 0.7 copy-done.12
  85.6 0.6 pad_add_fusion.where_ref
  86.2 1.2 collective-permute-done.18.refs_13_
  87.4 17.7 %attention_core.1 = (bf16[512,768]{1,0:T(8,128)(2,1)}, bf16[512,768]{1,0:T(8,128)(2,1)}, bf16[4,8,24,1152]{3,2,1,0:T(8,128)(2,1)}, bf16[4,8,24,1152]{3,2,1,0:T(8,128)(2,1)}) custom-call(s32[4]{0:T(128)} %pad_add_fusion.where_ref, bf16[128,4,1152]{2,1,0:T(4,128)(2,1)} %copy-done.1, bf16[512,768]{1,0:T(8,128)(2,1)} %copy-done.8, ...), custom_call_target="tpu_custom_call" | custom-call | flops 5435817984 | bytes 8388608 | tf_op jit(solution)/shard_map/attention_core/pallas_call | solution.py:108
  105.3 1.0 collective-permute-start.24
  106.3 2.8 %collective-permute-done.21.other_ref = bf16[4,8,24,1152]{3,2,1,0:T(8,128)(2,1)S(1)} collective-permute-done((bf16[4,8,24,1152]{3,2,1,0:T(8,128)(2,1)}, bf16[4,8,24,1152]{3,2,1,0:T(8,128)(2,1)S(1)}, u32[]{:S(2)}, u32[]{:S(2)}) %collective-permute-start.21) | collective-permute-done | bytes 1769504 | tf_op jit(solution)/shard_map/ppermute | solution.py:238
  109.1 1.5 copy-done.2
  110.9 1.4 collective-permute-start.22
  112.3 1.9 %collective-permute-start.23 = (bf16[4,24,1152]{2,1,0:T(8,128)(2,1)S(1)}, bf16[4,24,1152]{2,1,0:T(8,128)(2,1)S(1)}, u32[]{:S(2)}, u32[]{:S(2)}) collective-permute-start(bf16[4,24,1152]{2,1,0:T(8,128)(2,1)S(1)} %get-tuple-element.54), channel_id=1, source_target_pairs={{0,24},{8,0},{16,8},{24,16},{1,25},{9,1},{17,9},{25,17},{2,26},{10... | collective-permute-start | bytes 663560 | tf_op jit(solution)/shard_map/ppermute | solution.py:210
  114.2 1.7 collective-permute-start.26
  116.3 9.1 %collective-permute-done.24.b_ref = bf16[512,768]{1,0:T(8,128)(2,1)S(1)} collective-permute-done((bf16[512,768]{1,0:T(8,128)(2,1)}, bf16[512,768]{1,0:T(8,128)(2,1)S(1)}, u32[]{:S(2)}, u32[]{:S(2)}) %collective-permute-start.24) | collective-permute-done | bytes 786464 | tf_op jit(solution)/shard_map/ppermute | solution.py:299
  125.3 1.2 add_parts.1
  126.7 1.4 collective-permute-start.25
  128.1 1.9 %collective-permute-start.28 = (bf16[4,24,1152]{2,1,0:T(8,128)(2,1)S(1)}, bf16[4,24,1152]{2,1,0:T(8,128)(2,1)}, u32[]{:S(2)}, u32[]{:S(2)}) collective-permute-start(bf16[4,24,1152]{2,1,0:T(8,128)(2,1)S(1)} %add_convert_fusion), channel_id=1, source_target_pairs={{0,24},{8,0},{16,8},{24,16},{1,25},{9,1},{17,9},{25,17},{2,26},{10... | collective-permute-start | bytes 663560 | tf_op jit(solution)/shard_map/ppermute | solution.py:210
  130.0 10.0 %all-to-all-start.1 = ((bf16[128,4,768]{2,1,0:T(4,128)(2,1)}), bf16[128,4,768]{2,1,0:T(4,128)(2,1)}, u32[]{:S(2)}, u32[]{:S(2)}) async-start(bf16[128,4,768]{2,1,0:T(4,128)(2,1)} %add_parts.1), calls=%async_computation.1 | async-start | bytes 1572864 | tf_op jit(solution)/shard_map/all_to_all | solution.py:305
  140.0 1.4 convert_add_fusion.1
  141.6 1.1 collective-permute-start.30
  142.7 3.5 %collective-permute-start.31 = (bf16[4,12,1152]{2,1,0:T(8,128)(2,1)S(1)}, bf16[4,12,1152]{2,1,0:T(8,128)(2,1)S(1)}, u32[]{:S(2)}, u32[]{:S(2)}) collective-permute-start(bf16[4,12,1152]{2,1,0:T(8,128)(2,1)S(1)} %get-tuple-element.73), channel_id=1, source_target_pairs={{0,36},{4,32},{32,4},{36,0},{64,100},{68,96},{96,68},{100,64},{128... | collective-permute-start | bytes 331784 | tf_op jit(solution)/shard_map/ppermute | solution.py:214
  146.7 5.0 %collective-permute-done.30 = bf16[4,12,1152]{2,1,0:T(8,128)(2,1)S(1)} collective-permute-done((bf16[4,12,1152]{2,1,0:T(8,128)(2,1)S(1)}, bf16[4,12,1152]{2,1,0:T(8,128)(2,1)S(1)}, u32[]{:S(2)}, u32[]{:S(2)}) %collective-permute-start.30) | collective-permute-done | bytes 110624 | tf_op jit(solution)/shard_map/ppermute | solution.py:214
  151.6 10.4 %collective-permute-done.31 = bf16[4,12,1152]{2,1,0:T(8,128)(2,1)S(1)} collective-permute-done((bf16[4,12,1152]{2,1,0:T(8,128)(2,1)S(1)}, bf16[4,12,1152]{2,1,0:T(8,128)(2,1)S(1)}, u32[]{:S(2)}, u32[]{:S(2)}) %collective-permute-start.31) | collective-permute-done | bytes 110624 | tf_op jit(solution)/shard_map/ppermute | solution.py:214
  162.0 2.7 %collective-permute-done.29 = bf16[4,12,1152]{2,1,0:T(8,128)(2,1)S(1)} collective-permute-done((bf16[4,12,1152]{2,1,0:T(8,128)(2,1)S(1)}, bf16[4,12,1152]{2,1,0:T(8,128)(2,1)S(1)}, u32[]{:S(2)}, u32[]{:S(2)}) %collective-permute-start.29) | collective-permute-done | bytes 110624 | tf_op jit(solution)/shard_map/ppermute | solution.py:214
  164.9 2.5 %collective-permute-start.32 = (bf16[12,1152]{1,0:T(8,128)(2,1)S(1)}, bf16[12,1152]{1,0:T(8,128)(2,1)S(1)}, u32[]{:S(2)}, u32[]{:S(2)}) collective-permute-start(bf16[12,1152]{1,0:T(8,128)(2,1)S(1)} %get-tuple-element.78), channel_id=1, source_target_pairs={{0,64},{32,96},{64,0},{96,32},{128,192},{160,224},{192,128},{224,1... | collective-permute-start | bytes 82952 | tf_op jit(solution)/shard_map/ppermute | solution.py:214
  167.4 2.9 %collective-permute-start.34 = (bf16[12,1152]{1,0:T(8,128)(2,1)S(1)}, bf16[12,1152]{1,0:T(8,128)(2,1)S(1)}, u32[]{:S(2)}, u32[]{:S(2)}) collective-permute-start(bf16[12,1152]{1,0:T(8,128)(2,1)S(1)} %get-tuple-element.79), channel_id=1, source_target_pairs={{0,192},{32,224},{64,128},{96,160},{128,64},{160,96},{192,0},{224,... | collective-permute-start | bytes 82952 | tf_op jit(solution)/shard_map/ppermute | solution.py:214
  170.3 1.2 collective-permute-start.33
  171.5 2.3 %reshape.29 = bf16[1,512,768]{2,1,0:T(8,128)(2,1)} reshape(bf16[128,4,768]{2,1,0:T(4,128)(2,1)} %all-to-all-done.1) | data formatting | bytes 1572864 | tf_op jit(solution)/shard_map/reshape | solution.py:308
  173.7 4.4 %collective-permute-done.33 = bf16[12,1152]{1,0:T(8,128)(2,1)S(1)} collective-permute-done((bf16[12,1152]{1,0:T(8,128)(2,1)S(1)}, bf16[12,1152]{1,0:T(8,128)(2,1)S(1)}, u32[]{:S(2)}, u32[]{:S(2)}) %collective-permute-start.33) | collective-permute-done | bytes 27680 | tf_op jit(solution)/shard_map/ppermute | solution.py:214
  178.2 0.7 reshape.30
  (91 shorter events, 5.4 us)
Async XLA Ops:
  0.6 9.8 %copy-start = (bf16[1,512,1536]{2,1,0:T(8,128)(2,1)S(1)}, bf16[1,512,1536]{2,1,0:T(8,128)(2,1)}, u32[]{:S(2)}) copy-start(bf16[1,512,1536]{2,1,0:T(8,128)(2,1)} %param.3) | copy-start | bytes 4718596
  0.6 9.9 %copy-start.4 = (bf16[1,512,384]{2,1,0:T(8,128)(2,1)S(1)}, bf16[1,512,384]{2,1,0:T(8,128)(2,1)}, u32[]{:S(2)}) copy-start(bf16[1,512,384]{2,1,0:T(8,128)(2,1)} %param.4) | copy-start | bytes 1179652
  1.6 11.0 %collective-permute-start.2 = (bf16[12,1152]{1,0:T(8,128)(2,1)S(1)}, bf16[12,1152]{1,0:T(8,128)(2,1)S(1)}, u32[]{:S(2)}, u32[]{:S(2)}) collective-permute-start(bf16[12,1152]{1,0:T(8,128)(2,1)S(1)} %bitcast.46), channel_id=1, source_target_pairs={{0,192},{32,224},{64,128},{96,160},{128,64},{160,96},{192,0},{224,... | collective-permute-start | bytes 82952 | tf_op jit(solution)/shard_map/ppermute | solution.py:214
  8.0 8.4 %collective-permute-start.1 = (bf16[12,1152]{1,0:T(8,128)(2,1)S(1)}, bf16[12,1152]{1,0:T(8,128)(2,1)S(1)}, u32[]{:S(2)}, u32[]{:S(2)}) collective-permute-start(bf16[12,1152]{1,0:T(8,128)(2,1)S(1)} %bitcast.47), channel_id=1, source_target_pairs={{0,128},{32,160},{64,192},{96,224},{128,0},{160,32},{192,64},{224,... | collective-permute-start | bytes 82952 | tf_op jit(solution)/shard_map/ppermute | solution.py:214
  9.0 7.4 %collective-permute-start = (bf16[12,1152]{1,0:T(8,128)(2,1)S(1)}, bf16[12,1152]{1,0:T(8,128)(2,1)S(1)}, u32[]{:S(2)}, u32[]{:S(2)}) collective-permute-start(bf16[12,1152]{1,0:T(8,128)(2,1)S(1)} %bitcast.48), channel_id=1, source_target_pairs={{0,64},{32,96},{64,0},{96,32},{128,192},{160,224},{192,128},{224,1... | collective-permute-start | bytes 82952 | tf_op jit(solution)/shard_map/ppermute | solution.py:214
  16.4 16.3 %collective-permute-start.4 = (bf16[4,12,1152]{2,1,0:T(8,128)(2,1)S(1)}, bf16[4,12,1152]{2,1,0:T(8,128)(2,1)S(1)}, u32[]{:S(2)}, u32[]{:S(2)}) collective-permute-start(bf16[4,12,1152]{2,1,0:T(8,128)(2,1)S(1)} %pad_maximum_fusion.4), channel_id=1, source_target_pairs={{0,32},{4,36},{32,0},{36,4},{64,96},{68,100},{96,64},{100,68},{128... | collective-permute-start | bytes 331784 | tf_op jit(solution)/shard_map/ppermute | solution.py:214
  17.6 15.1 %collective-permute-start.5 = (bf16[4,12,1152]{2,1,0:T(8,128)(2,1)S(1)}, bf16[4,12,1152]{2,1,0:T(8,128)(2,1)S(1)}, u32[]{:S(2)}, u32[]{:S(2)}) collective-permute-start(bf16[4,12,1152]{2,1,0:T(8,128)(2,1)S(1)} %pad_maximum_fusion.4), channel_id=1, source_target_pairs={{0,36},{4,32},{32,4},{36,0},{64,100},{68,96},{96,68},{100,64},{128... | collective-permute-start | bytes 331784 | tf_op jit(solution)/shard_map/ppermute | solution.py:214
  19.4 13.5 %collective-permute-start.3 = (bf16[4,12,1152]{2,1,0:T(8,128)(2,1)S(1)}, bf16[4,12,1152]{2,1,0:T(8,128)(2,1)S(1)}, u32[]{:S(2)}, u32[]{:S(2)}) collective-permute-start(bf16[4,12,1152]{2,1,0:T(8,128)(2,1)S(1)} %pad_maximum_fusion.4), channel_id=1, source_target_pairs={{0,4},{4,0},{32,36},{36,32},{64,68},{68,64},{96,100},{100,96},{128... | collective-permute-start | bytes 331784 | tf_op jit(solution)/shard_map/ppermute | solution.py:214
  21.5 43.1 %all-to-all-start = ((bf16[128,4,1152]{2,1,0:T(4,128)(2,1)}), bf16[128,4,1152]{2,1,0:T(4,128)(2,1)S(1)}, u32[]{:S(2)}, u32[]{:S(2)}) async-start(bf16[128,4,1152]{2,1,0:T(4,128)(2,1)} %reshape.25), calls=%async_computation | async-start | bytes 2359296 | tf_op jit(solution)/shard_map/all_to_all | solution.py:281
  33.0 46.4 %copy-start.5 = (bf16[2,2,24,1152]{3,2,1,0:T(8,128)(2,1)}, bf16[2,2,24,1152]{3,2,1,0:T(8,128)(2,1)S(1)}, u32[]{:S(2)}) copy-start(bf16[2,2,24,1152]{3,2,1,0:T(8,128)(2,1)S(1)} %copy.8) | copy-start | bytes 663556
  33.1 54.3 %copy-start.6 = (bf16[2,2,24,1152]{3,2,1,0:T(8,128)(2,1)}, bf16[2,2,24,1152]{3,2,1,0:T(8,128)(2,1)S(1)}, u32[]{:S(2)}) copy-start(bf16[2,2,24,1152]{3,2,1,0:T(8,128)(2,1)S(1)} %copy.7) | copy-start | bytes 663556
  64.6 22.8 %copy-start.1 = (bf16[128,4,1152]{2,1,0:T(4,128)(2,1)}, bf16[128,4,1152]{2,1,0:T(4,128)(2,1)S(1)}, u32[]{:S(2)}) copy-start(bf16[128,4,1152]{2,1,0:T(4,128)(2,1)S(1)} %all-to-all-done.x_ref) | copy-start | bytes 3538948
  64.8 18.6 %collective-permute-start.12 = (bf16[512,768]{1,0:T(8,128)(2,1)S(1)}, bf16[512,768]{1,0:T(8,128)(2,1)S(1)}, u32[]{:S(2)}, u32[]{:S(2)}) collective-permute-start(bf16[512,768]{1,0:T(8,128)(2,1)S(1)} %part_rows.1), channel_id=1, source_target_pairs={{0,1},{1,0},{2,3},{3,2},{4,5},{5,4},{6,7},{7,6},{8,9},{9,8},{10,11... | collective-permute-start | bytes 2359304 | tf_op jit(solution)/shard_map/ppermute | solution.py:285
  65.7 8.3 %collective-permute-start.8 = (bf16[4,24,1152]{2,1,0:T(8,128)(2,1)S(1)}, bf16[4,24,1152]{2,1,0:T(8,128)(2,1)S(1)}, u32[]{:S(2)}, u32[]{:S(2)}) collective-permute-start(bf16[4,24,1152]{2,1,0:T(8,128)(2,1)S(1)} %bitcast.38), channel_id=1, source_target_pairs={{0,8},{8,16},{16,24},{24,0},{1,9},{9,17},{17,25},{25,1},{2,10},{10... | collective-permute-start | bytes 663560 | tf_op jit(solution)/shard_map/ppermute | solution.py:210
  65.9 8.9 %collective-permute-start.7 = (bf16[4,24,1152]{2,1,0:T(8,128)(2,1)S(1)}, bf16[4,24,1152]{2,1,0:T(8,128)(2,1)}, u32[]{:S(2)}, u32[]{:S(2)}) collective-permute-start(bf16[4,24,1152]{2,1,0:T(8,128)(2,1)S(1)} %bitcast.34), channel_id=1, source_target_pairs={{0,24},{8,0},{16,8},{24,16},{1,25},{9,1},{17,9},{25,17},{2,26},{10... | collective-permute-start | bytes 663560 | tf_op jit(solution)/shard_map/ppermute | solution.py:210
  68.9 10.4 %collective-permute-start.6 = (bf16[4,24,1152]{2,1,0:T(8,128)(2,1)S(1)}, bf16[4,24,1152]{2,1,0:T(8,128)(2,1)}, u32[]{:S(2)}, u32[]{:S(2)}) collective-permute-start(bf16[4,24,1152]{2,1,0:T(8,128)(2,1)S(1)} %bitcast.39), channel_id=1, source_target_pairs={{0,24},{8,0},{16,8},{24,16},{1,25},{9,1},{17,9},{25,17},{2,26},{10... | collective-permute-start | bytes 663560 | tf_op jit(solution)/shard_map/ppermute | solution.py:210
  68.9 10.4 %collective-permute-start.11 = (bf16[4,24,1152]{2,1,0:T(8,128)(2,1)S(1)}, bf16[4,24,1152]{2,1,0:T(8,128)(2,1)}, u32[]{:S(2)}, u32[]{:S(2)}) collective-permute-start(bf16[4,24,1152]{2,1,0:T(8,128)(2,1)S(1)} %bitcast.35), channel_id=1, source_target_pairs={{0,8},{8,16},{16,24},{24,0},{1,9},{9,17},{17,25},{25,1},{2,10},{10... | collective-permute-start | bytes 663560 | tf_op jit(solution)/shard_map/ppermute | solution.py:210
  74.0 13.4 %copy-start.9 = (bf16[4,24,1152]{2,1,0:T(8,128)(2,1)}, bf16[4,24,1152]{2,1,0:T(8,128)(2,1)S(1)}, u32[]{:S(2)}) copy-start(bf16[4,24,1152]{2,1,0:T(8,128)(2,1)S(1)} %collective-permute-done.8.refs_6_) | copy-start | bytes 663556
  74.0 8.6 %collective-permute-start.9 = (bf16[4,24,1152]{2,1,0:T(8,128)(2,1)S(1)}, bf16[4,24,1152]{2,1,0:T(8,128)(2,1)}, u32[]{:S(2)}, u32[]{:S(2)}) collective-permute-start(bf16[4,24,1152]{2,1,0:T(8,128)(2,1)S(1)} %collective-permute-done.8.refs_6_), channel_id=1, source_target_pairs={{0,8},{8,16},{16,24},{24,0},{1,9},{9,17},{17,25},{25,1},{2,10},{10... | collective-permute-start | bytes 663560 | tf_op jit(solution)/shard_map/ppermute | solution.py:210
  74.8 7.8 %collective-permute-start.10 = (bf16[4,24,1152]{2,1,0:T(8,128)(2,1)}, bf16[4,24,1152]{2,1,0:T(8,128)(2,1)}, u32[]{:S(2)}, u32[]{:S(2)}) collective-permute-start(bf16[4,24,1152]{2,1,0:T(8,128)(2,1)} %collective-permute-done.7.refs_3_), channel_id=1, source_target_pairs={{0,24},{8,0},{16,8},{24,16},{1,25},{9,1},{17,9},{25,17},{2,26},{10... | collective-permute-start | bytes 663560 | tf_op jit(solution)/shard_map/ppermute | solution.py:210
  79.4 4.0 %collective-permute-start.13 = (bf16[4,24,1152]{2,1,0:T(8,128)(2,1)S(1)}, bf16[4,24,1152]{2,1,0:T(8,128)(2,1)S(1)}, u32[]{:S(2)}, u32[]{:S(2)}) collective-permute-start(bf16[4,24,1152]{2,1,0:T(8,128)(2,1)S(1)} %bitcast.40), channel_id=1, source_target_pairs={{0,2},{2,0},{1,3},{3,1},{4,6},{6,4},{5,7},{7,5},{8,10},{10,8},{9,1... | collective-permute-start | bytes 663560 | tf_op jit(solution)/shard_map/ppermute | solution.py:293
  79.4 4.5 %collective-permute-start.14 = (bf16[4,24,1152]{2,1,0:T(8,128)(2,1)S(1)}, bf16[4,24,1152]{2,1,0:T(8,128)(2,1)S(1)}, u32[]{:S(2)}, u32[]{:S(2)}) collective-permute-start(bf16[4,24,1152]{2,1,0:T(8,128)(2,1)S(1)} %bitcast.36), channel_id=1, source_target_pairs={{0,2},{2,0},{1,3},{3,1},{4,6},{6,4},{5,7},{7,5},{8,10},{10,8},{9,1... | collective-permute-start | bytes 663560 | tf_op jit(solution)/shard_map/ppermute | solution.py:293
  82.6 1.7 collective-permute-start.19
  82.6 3.6 %collective-permute-start.15 = (bf16[4,24,1152]{2,1,0:T(8,128)(2,1)}, bf16[4,24,1152]{2,1,0:T(8,128)(2,1)}, u32[]{:S(2)}, u32[]{:S(2)}) collective-permute-start(bf16[4,24,1152]{2,1,0:T(8,128)(2,1)} %collective-permute-done.6.refs_2_), channel_id=1, source_target_pairs={{0,2},{2,0},{1,3},{3,1},{4,6},{6,4},{5,7},{7,5},{8,10},{10,8},{9,1... | collective-permute-start | bytes 663560 | tf_op jit(solution)/shard_map/ppermute | solution.py:293
  83.3 0.9 copy-start.8
  83.3 2.8 %collective-permute-start.20 = (bf16[4,24,1152]{2,1,0:T(8,128)(2,1)}, bf16[4,24,1152]{2,1,0:T(8,128)(2,1)}, u32[]{:S(2)}, u32[]{:S(2)}) collective-permute-start(bf16[4,24,1152]{2,1,0:T(8,128)(2,1)} %collective-permute-done.11.refs_7_), channel_id=1, source_target_pairs={{0,2},{2,0},{1,3},{3,1},{4,6},{6,4},{5,7},{7,5},{8,10},{10,8},{9,1... | collective-permute-start | bytes 663560 | tf_op jit(solution)/shard_map/ppermute | solution.py:293
  83.3 0.9 copy-start.10
  83.4 2.8 %collective-permute-start.16 = (bf16[4,24,1152]{2,1,0:T(8,128)(2,1)}, bf16[4,24,1152]{2,1,0:T(8,128)(2,1)}, u32[]{:S(2)}, u32[]{:S(2)}) collective-permute-start(bf16[4,24,1152]{2,1,0:T(8,128)(2,1)} %collective-permute-done.7.refs_3_), channel_id=1, source_target_pairs={{0,2},{2,0},{1,3},{3,1},{4,6},{6,4},{5,7},{7,5},{8,10},{10,8},{9,1... | collective-permute-start | bytes 663560 | tf_op jit(solution)/shard_map/ppermute | solution.py:293
  84.2 2.0 %collective-permute-start.17 = (bf16[4,24,1152]{2,1,0:T(8,128)(2,1)}, bf16[4,24,1152]{2,1,0:T(8,128)(2,1)S(1)}, u32[]{:S(2)}, u32[]{:S(2)}) collective-permute-start(bf16[4,24,1152]{2,1,0:T(8,128)(2,1)} %collective-permute-done.9.refs_4_), channel_id=1, source_target_pairs={{0,2},{2,0},{1,3},{3,1},{4,6},{6,4},{5,7},{7,5},{8,10},{10,8},{9,1... | collective-permute-start | bytes 663560 | tf_op jit(solution)/shard_map/ppermute | solution.py:295
  85.6 1.8 %collective-permute-start.18 = (bf16[4,24,1152]{2,1,0:T(8,128)(2,1)}, bf16[4,24,1152]{2,1,0:T(8,128)(2,1)}, u32[]{:S(2)}, u32[]{:S(2)}) collective-permute-start(bf16[4,24,1152]{2,1,0:T(8,128)(2,1)} %collective-permute-done.10.refs_5_), channel_id=1, source_target_pairs={{0,2},{2,0},{1,3},{3,1},{4,6},{6,4},{5,7},{7,5},{8,10},{10,8},{9,1... | collective-permute-start | bytes 663560 | tf_op jit(solution)/shard_map/ppermute | solution.py:295
  86.2 1.2 copy-start.13
  105.2 3.9 %collective-permute-start.21 = (bf16[4,8,24,1152]{3,2,1,0:T(8,128)(2,1)}, bf16[4,8,24,1152]{3,2,1,0:T(8,128)(2,1)S(1)}, u32[]{:S(2)}, u32[]{:S(2)}) collective-permute-start(bf16[4,8,24,1152]{3,2,1,0:T(8,128)(2,1)} %get-tuple-element.50), channel_id=1, source_target_pairs={{0,2},{2,0},{1,3},{3,1},{4,6},{6,4},{5,7},{7,5},{8,10},{10,8},{9,1... | collective-permute-start | bytes 5308424 | tf_op jit(solution)/shard_map/ppermute | solution.py:238
  105.3 20.0 %collective-permute-start.24 = (bf16[512,768]{1,0:T(8,128)(2,1)}, bf16[512,768]{1,0:T(8,128)(2,1)S(1)}, u32[]{:S(2)}, u32[]{:S(2)}) collective-permute-start(bf16[512,768]{1,0:T(8,128)(2,1)} %get-tuple-element.55), channel_id=1, source_target_pairs={{0,1},{1,0},{2,3},{3,2},{4,5},{5,4},{6,7},{7,6},{8,9},{9,8},{10,11... | collective-permute-start | bytes 2359304 | tf_op jit(solution)/shard_map/ppermute | solution.py:299
  109.1 1.5 copy-start.2
  110.5 14.8 %copy-start.3 = (bf16[512,768]{1,0:T(8,128)(2,1)S(1)}, bf16[512,768]{1,0:T(8,128)(2,1)}, u32[]{:S(2)}) copy-start(bf16[512,768]{1,0:T(8,128)(2,1)} %get-tuple-element.59.a_ref) | copy-start | bytes 2359300
  110.9 14.4 %collective-permute-start.22 = (bf16[4,24,1152]{2,1,0:T(8,128)(2,1)S(1)}, bf16[4,24,1152]{2,1,0:T(8,128)(2,1)S(1)}, u32[]{:S(2)}, u32[]{:S(2)}) collective-permute-start(bf16[4,24,1152]{2,1,0:T(8,128)(2,1)S(1)} %get-tuple-element.53), channel_id=1, source_target_pairs={{0,8},{8,16},{16,24},{24,0},{1,9},{9,17},{17,25},{25,1},{2,10},{10... | collective-permute-start | bytes 663560 | tf_op jit(solution)/shard_map/ppermute | solution.py:210
  112.3 13.0 %collective-permute-start.23 = (bf16[4,24,1152]{2,1,0:T(8,128)(2,1)S(1)}, bf16[4,24,1152]{2,1,0:T(8,128)(2,1)S(1)}, u32[]{:S(2)}, u32[]{:S(2)}) collective-permute-start(bf16[4,24,1152]{2,1,0:T(8,128)(2,1)S(1)} %get-tuple-element.54), channel_id=1, source_target_pairs={{0,24},{8,0},{16,8},{24,16},{1,25},{9,1},{17,9},{25,17},{2,26},{10... | collective-permute-start | bytes 663560 | tf_op jit(solution)/shard_map/ppermute | solution.py:210
  114.2 25.7 %collective-permute-start.26 = (bf16[4,24,1152]{2,1,0:T(8,128)(2,1)S(1)}, bf16[4,24,1152]{2,1,0:T(8,128)(2,1)}, u32[]{:S(2)}, u32[]{:S(2)}) collective-permute-start(bf16[4,24,1152]{2,1,0:T(8,128)(2,1)S(1)} %get-tuple-element.62), channel_id=1, source_target_pairs={{0,24},{8,0},{16,8},{24,16},{1,25},{9,1},{17,9},{25,17},{2,26},{10... | collective-permute-start | bytes 663560 | tf_op jit(solution)/shard_map/ppermute | solution.py:210
  115.9 24.1 %collective-permute-start.27 = (bf16[4,24,1152]{2,1,0:T(8,128)(2,1)S(1)}, bf16[4,24,1152]{2,1,0:T(8,128)(2,1)}, u32[]{:S(2)}, u32[]{:S(2)}) collective-permute-start(bf16[4,24,1152]{2,1,0:T(8,128)(2,1)S(1)} %get-tuple-element.63), channel_id=1, source_target_pairs={{0,8},{8,16},{16,24},{24,0},{1,9},{9,17},{17,25},{25,1},{2,10},{10... | collective-permute-start | bytes 663560 | tf_op jit(solution)/shard_map/ppermute | solution.py:210
  126.7 13.3 %collective-permute-start.25 = (bf16[4,24,1152]{2,1,0:T(8,128)(2,1)S(1)}, bf16[4,24,1152]{2,1,0:T(8,128)(2,1)}, u32[]{:S(2)}, u32[]{:S(2)}) collective-permute-start(bf16[4,24,1152]{2,1,0:T(8,128)(2,1)S(1)} %add_convert_fusion.1), channel_id=1, source_target_pairs={{0,8},{8,16},{16,24},{24,0},{1,9},{9,17},{17,25},{25,1},{2,10},{10... | collective-permute-start | bytes 663560 | tf_op jit(solution)/shard_map/ppermute | solution.py:210
  128.1 11.9 %collective-permute-start.28 = (bf16[4,24,1152]{2,1,0:T(8,128)(2,1)S(1)}, bf16[4,24,1152]{2,1,0:T(8,128)(2,1)}, u32[]{:S(2)}, u32[]{:S(2)}) collective-permute-start(bf16[4,24,1152]{2,1,0:T(8,128)(2,1)S(1)} %add_convert_fusion), channel_id=1, source_target_pairs={{0,24},{8,0},{16,8},{24,16},{1,25},{9,1},{17,9},{25,17},{2,26},{10... | collective-permute-start | bytes 663560 | tf_op jit(solution)/shard_map/ppermute | solution.py:210
  130.0 34.8 %all-to-all-start.1 = ((bf16[128,4,768]{2,1,0:T(4,128)(2,1)}), bf16[128,4,768]{2,1,0:T(4,128)(2,1)}, u32[]{:S(2)}, u32[]{:S(2)}) async-start(bf16[128,4,768]{2,1,0:T(4,128)(2,1)} %add_parts.1), calls=%async_computation.1 | async-start | bytes 1572864 | tf_op jit(solution)/shard_map/all_to_all | solution.py:305
  141.6 10.0 %collective-permute-start.30 = (bf16[4,12,1152]{2,1,0:T(8,128)(2,1)S(1)}, bf16[4,12,1152]{2,1,0:T(8,128)(2,1)S(1)}, u32[]{:S(2)}, u32[]{:S(2)}) collective-permute-start(bf16[4,12,1152]{2,1,0:T(8,128)(2,1)S(1)} %get-tuple-element.72), channel_id=1, source_target_pairs={{0,4},{4,0},{32,36},{36,32},{64,68},{68,64},{96,100},{100,96},{128... | collective-permute-start | bytes 331784 | tf_op jit(solution)/shard_map/ppermute | solution.py:214
  142.7 19.3 %collective-permute-start.31 = (bf16[4,12,1152]{2,1,0:T(8,128)(2,1)S(1)}, bf16[4,12,1152]{2,1,0:T(8,128)(2,1)S(1)}, u32[]{:S(2)}, u32[]{:S(2)}) collective-permute-start(bf16[4,12,1152]{2,1,0:T(8,128)(2,1)S(1)} %get-tuple-element.73), channel_id=1, source_target_pairs={{0,36},{4,32},{32,4},{36,0},{64,100},{68,96},{96,68},{100,64},{128... | collective-permute-start | bytes 331784 | tf_op jit(solution)/shard_map/ppermute | solution.py:214
  146.2 18.6 %collective-permute-start.29 = (bf16[4,12,1152]{2,1,0:T(8,128)(2,1)S(1)}, bf16[4,12,1152]{2,1,0:T(8,128)(2,1)S(1)}, u32[]{:S(2)}, u32[]{:S(2)}) collective-permute-start(bf16[4,12,1152]{2,1,0:T(8,128)(2,1)S(1)} %slice.81), channel_id=1, source_target_pairs={{0,32},{4,36},{32,0},{36,4},{64,96},{68,100},{96,64},{100,68},{128... | collective-permute-start | bytes 331784 | tf_op jit(solution)/shard_map/ppermute | solution.py:214
  164.9 8.8 %collective-permute-start.32 = (bf16[12,1152]{1,0:T(8,128)(2,1)S(1)}, bf16[12,1152]{1,0:T(8,128)(2,1)S(1)}, u32[]{:S(2)}, u32[]{:S(2)}) collective-permute-start(bf16[12,1152]{1,0:T(8,128)(2,1)S(1)} %get-tuple-element.78), channel_id=1, source_target_pairs={{0,64},{32,96},{64,0},{96,32},{128,192},{160,224},{192,128},{224,1... | collective-permute-start | bytes 82952 | tf_op jit(solution)/shard_map/ppermute | solution.py:214
  167.4 6.3 %collective-permute-start.34 = (bf16[12,1152]{1,0:T(8,128)(2,1)S(1)}, bf16[12,1152]{1,0:T(8,128)(2,1)S(1)}, u32[]{:S(2)}, u32[]{:S(2)}) collective-permute-start(bf16[12,1152]{1,0:T(8,128)(2,1)S(1)} %get-tuple-element.79), channel_id=1, source_target_pairs={{0,192},{32,224},{64,128},{96,160},{128,64},{160,96},{192,0},{224,... | collective-permute-start | bytes 82952 | tf_op jit(solution)/shard_map/ppermute | solution.py:214
  170.3 7.9 %collective-permute-start.33 = (bf16[12,1152]{1,0:T(8,128)(2,1)S(1)}, bf16[12,1152]{1,0:T(8,128)(2,1)S(1)}, u32[]{:S(2)}, u32[]{:S(2)}) collective-permute-start(bf16[12,1152]{1,0:T(8,128)(2,1)S(1)} %get-tuple-element.80), channel_id=1, source_target_pairs={{0,128},{32,160},{64,192},{96,224},{128,0},{160,32},{192,64},{224,... | collective-permute-start | bytes 82952 | tf_op jit(solution)/shard_map/ppermute | solution.py:214
  (3 other events, 2.1 us)

commit v14 on v13

--- a/solution.py
+++ b/solution.py
@@ -20,19 +20,30 @@
     return lax.dot_general(a, b, dims, preferred_element_type=f32)
 
 
-def core_kernel(where_ref, x_ref, o_ref, *refs):
-    pieces = refs[:16]
-    give_ref, keep_ref, mine_ref, rest_ref, w_ref, s_ref, d_ref, g_ref, t_ref = refs[16:]
-    t_ref[...] = x_ref[...].astype(f32).reshape(t_ref.shape).astype(bf16)
+def core_kernel(where_ref, x_hbm, o_hbm, *refs):
+    blocks = refs[:16]
+    give_ref, keep_ref, mine_ref, rest_ref, w_ref, s_ref, d_ref, g_ref, t_ref = refs[16:25]
+    x_ref, o_ref, pieces, sems = refs[25:]
+    copies = [pltpu.make_async_copy(blocks[i], pieces.at[i], sems.at[i]) for i in range(16)]
+    copy_x = pltpu.make_async_copy(x_hbm, x_ref, sems.at[16])
+    copy_o = pltpu.make_async_copy(o_hbm, o_ref, sems.at[17])
+    for i in range(8):
+        copies[i].start()
+        copies[i + 8].start()
+    copy_x.start()
+    copy_o.start()
     z, y, c, m = (where_ref[i] for i in range(4))
     unit = XH * C * ROWS
 
-    @pl.loop(0, Z // 2)
-    def _(t):
-        for i in range(8):
-            by, high = i // 2, i % 2
-            a = pieces[i][t].astype(f32)
-            b = pieces[i + 8][t].astype(f32)
+    for i in range(8):
+        by, high = i // 2, i % 2
+        copies[i].wait()
+        copies[i + 8].wait()
+
+        @pl.loop(0, Z // 2)
+        def _(t, i=i, by=by, high=high):
+            a = pieces[i, t].astype(f32)
+            b = pieces[i + 8, t].astype(f32)
             first = jnp.where(c == 0, a, b)
             second = jnp.where(c == 0, b, a)
             rows = [first[:ROWS], second[:ROWS], first[ROWS:], second[ROWS:]]
@@ -40,6 +51,9 @@
             to = pl.ds(pl.multiple_of(to * unit, unit), unit)
             w_ref[to, :] = jnp.concatenate(rows, 0).astype(bf16)
 
+    copy_x.wait()
+    t_ref[...] = x_ref[...].astype(f32).reshape(t_ref.shape).astype(bf16)
+    copy_o.wait()
     part_cols = o_ref.shape[1]
     rows, half = t_ref.shape[0], t_ref.shape[1] - part_cols
     count = rows // F
@@ -113,7 +127,8 @@
             jax.ShapeDtypeStruct((Y, Z, XH * ROWS, n), bf16),
             jax.ShapeDtypeStruct((Y, Z, XH * ROWS, n), bf16),
         ),
-        in_specs=[pl.BlockSpec(memory_space=pltpu.SMEM)] + [vm] * 18,
+        in_specs=[pl.BlockSpec(memory_space=pltpu.SMEM)]
+        + [pl.BlockSpec(memory_space=pl.ANY)] * 18,
         out_specs=(vm,) * 4,
         scratch_shapes=[
             pltpu.VMEM((width, n), bf16),
@@ -121,6 +136,10 @@
             pltpu.VMEM((3 * half // 128, rows, 128), f32),
             pltpu.VMEM((rows, n), bf16),
             pltpu.VMEM((rows, part_cols + half), bf16),
+            pltpu.VMEM(tokens.shape, bf16),
+            pltpu.VMEM(others.shape, bf16),
+            pltpu.VMEM((16,) + mine[0].shape, bf16),
+            pltpu.SemaphoreType.DMA((18,)),
         ],
         compiler_params=pltpu.CompilerParams(vmem_limit_bytes=CORE_LIMIT),
         cost_estimate=pl.CostEstimate(

time: 179 us -> 179 us (level)
  no operation moved by 1% of the time
where the time goes in v14:
time: 179 us; the launch traced here: 178 us
  waiting for transfers between devices  78.2 us (44%)
  starting transfers between devices  68.3 us (38%)
  Pallas kernels  19 us (11%)
  local copies, waits for them, and re-layouts  9.14 us (5%)
  other arithmetic  2.71 us (2%)
    all_to_all x1, waiting for transfers between devices, on_device(): tokens = lax.all_to_all(tokens, FR, 0, 0, tiled=True)  31.5 us
    ppermute x12, waiting for transfers between devices, across(): return lax.ppermute(x, axis, [(i, i ^ by) for i in range(size)])  26.3 us
    ppermute x12, starting transfers between devices, across(): return lax.ppermute(x, axis, [(i, i ^ by) for i in range(size)])  25.6 us
    ppermute x12, starting transfers between devices, shift(): return lax.ppermute(x, axis, [(i, (i + by) % size) for i in range(size)])  18 us
    pallas_call x1, Pallas kernels, core(): pl.pallas_call(core_kernel, out_shape=(jax.ShapeDtypeStruct((rows, part_c...  17.3 us
    all_to_all x1, starting transfers between devices, on_device(): tokens = lax.all_to_all(tokens, FR, 0, 0, tiled=True)  11.2 us
    all_to_all x1, starting transfers between devices, to_frames(): return lax.all_to_all(x, FR, 0, 0, tiled=True)  9.95 us
    ppermute x1, waiting for transfers between devices, on_device(): got = lax.ppermute(give, 'mp', PAIR)  9.05 us
  transfers between devices with their start and end apart: 37, of which 15 were waited for; matrix products, arithmetic and copies ran while one was open for 4% of the time, Pallas kernels for 1%

profile of v14, /device:TPU:6, one launch (start us, length us, event | category | flops | bytes accessed | tf_op | source)
XLA Modules:
  0.0 178.5 jit_solution(14910838612074909931)
XLA Ops:
  0.7 0.9 pad.26
  1.6 6.4 %collective-permute-start.2 = (bf16[12,1152]{1,0:T(8,128)(2,1)S(1)}, bf16[12,1152]{1,0:T(8,128)(2,1)S(1)}, u32[]{:S(2)}, u32[]{:S(2)}) collective-permute-start(bf16[12,1152]{1,0:T(8,128)(2,1)S(1)} %bitcast.46), channel_id=1, source_target_pairs={{0,192},{32,224},{64,128},{96,160},{128,64},{160,96},{192,0},{224,... | collective-permute-start | bytes 82952 | tf_op jit(solution)/shard_map/ppermute | solution.py:233
  8.0 1.0 collective-permute-start.1
  9.0 1.5 collective-permute-start
  10.6 0.7 copy-done.7
  11.3 1.2 reshape.25
  12.6 3.8 %collective-permute-done.1 = bf16[12,1152]{1,0:T(8,128)(2,1)S(1)} collective-permute-done((bf16[12,1152]{1,0:T(8,128)(2,1)S(1)}, bf16[12,1152]{1,0:T(8,128)(2,1)S(1)}, u32[]{:S(2)}, u32[]{:S(2)}) %collective-permute-start.1) | collective-permute-done | bytes 27680 | tf_op jit(solution)/shard_map/ppermute | solution.py:233
  16.4 1.2 collective-permute-start.4
  17.6 1.8 %collective-permute-start.5 = (bf16[4,12,1152]{2,1,0:T(8,128)(2,1)S(1)}, bf16[4,12,1152]{2,1,0:T(8,128)(2,1)S(1)}, u32[]{:S(2)}, u32[]{:S(2)}) collective-permute-start(bf16[4,12,1152]{2,1,0:T(8,128)(2,1)S(1)} %pad_maximum_fusion.4), channel_id=1, source_target_pairs={{0,36},{4,32},{32,4},{36,0},{64,100},{68,96},{96,68},{100,64},{128... | collective-permute-start | bytes 331784 | tf_op jit(solution)/shard_map/ppermute | solution.py:233
  19.4 2.1 %collective-permute-start.3 = (bf16[4,12,1152]{2,1,0:T(8,128)(2,1)S(1)}, bf16[4,12,1152]{2,1,0:T(8,128)(2,1)S(1)}, u32[]{:S(2)}, u32[]{:S(2)}) collective-permute-start(bf16[4,12,1152]{2,1,0:T(8,128)(2,1)S(1)} %pad_maximum_fusion.4), channel_id=1, source_target_pairs={{0,4},{4,0},{32,36},{36,32},{64,68},{68,64},{96,100},{100,96},{128... | collective-permute-start | bytes 331784 | tf_op jit(solution)/shard_map/ppermute | solution.py:233
  21.5 11.2 %all-to-all-start = ((bf16[128,4,1152]{2,1,0:T(4,128)(2,1)}), bf16[128,4,1152]{2,1,0:T(4,128)(2,1)S(1)}, u32[]{:S(2)}, u32[]{:S(2)}) async-start(bf16[128,4,1152]{2,1,0:T(4,128)(2,1)} %reshape.25), calls=%async_computation | async-start | bytes 2359296 | tf_op jit(solution)/shard_map/all_to_all | solution.py:300
  33.2 31.5 %all-to-all-done.x_ref.x_hbm = bf16[128,4,1152]{2,1,0:T(4,128)(2,1)S(1)} async-done(((bf16[128,4,1152]{2,1,0:T(4,128)(2,1)}), bf16[128,4,1152]{2,1,0:T(4,128)(2,1)S(1)}, u32[]{:S(2)}, u32[]{:S(2)}) %all-to-all-start) | async-done | bytes 1179680 | tf_op jit(solution)/shard_map/all_to_all | solution.py:300
  64.8 0.9 collective-permute-start.12
  65.9 3.0 %collective-permute-start.7 = (bf16[4,24,1152]{2,1,0:T(8,128)(2,1)S(1)}, bf16[4,24,1152]{2,1,0:T(8,128)(2,1)}, u32[]{:S(2)}, u32[]{:S(2)}) collective-permute-start(bf16[4,24,1152]{2,1,0:T(8,128)(2,1)S(1)} %bitcast.34), channel_id=1, source_target_pairs={{0,24},{8,0},{16,8},{24,16},{1,25},{9,1},{17,9},{25,17},{2,26},{10... | collective-permute-start | bytes 663560 | tf_op jit(solution)/shard_map/ppermute | solution.py:229
  68.9 2.0 %collective-permute-start.11 = (bf16[4,24,1152]{2,1,0:T(8,128)(2,1)S(1)}, bf16[4,24,1152]{2,1,0:T(8,128)(2,1)}, u32[]{:S(2)}, u32[]{:S(2)}) collective-permute-start(bf16[4,24,1152]{2,1,0:T(8,128)(2,1)S(1)} %bitcast.35), channel_id=1, source_target_pairs={{0,8},{8,16},{16,24},{24,0},{1,9},{9,17},{17,25},{25,1},{2,10},{10... | collective-permute-start | bytes 663560 | tf_op jit(solution)/shard_map/ppermute | solution.py:229
  70.9 3.0 %collective-permute-done.8.refs_6_ = bf16[4,24,1152]{2,1,0:T(8,128)(2,1)S(1)} collective-permute-done((bf16[4,24,1152]{2,1,0:T(8,128)(2,1)S(1)}, bf16[4,24,1152]{2,1,0:T(8,128)(2,1)S(1)}, u32[]{:S(2)}, u32[]{:S(2)}) %collective-permute-start.8) | collective-permute-done | bytes 221216 | tf_op jit(solution)/shard_map/ppermute | solution.py:229
  74.3 0.5 collective-permute-done.7.refs_3_
  74.8 3.8 %collective-permute-start.10 = (bf16[4,24,1152]{2,1,0:T(8,128)(2,1)}, bf16[4,24,1152]{2,1,0:T(8,128)(2,1)}, u32[]{:S(2)}, u32[]{:S(2)}) collective-permute-start(bf16[4,24,1152]{2,1,0:T(8,128)(2,1)} %collective-permute-done.7.refs_3_), channel_id=1, source_target_pairs={{0,24},{8,0},{16,8},{24,16},{1,25},{9,1},{17,9},{25,17},{2,26},{10... | collective-permute-start | bytes 663560 | tf_op jit(solution)/shard_map/ppermute | solution.py:229
  78.6 0.8 collective-permute-done.6.refs_2_
  79.9 2.7 %collective-permute-done.9.refs_4_ = bf16[4,24,1152]{2,1,0:T(8,128)(2,1)} collective-permute-done((bf16[4,24,1152]{2,1,0:T(8,128)(2,1)S(1)}, bf16[4,24,1152]{2,1,0:T(8,128)(2,1)}, u32[]{:S(2)}, u32[]{:S(2)}) %collective-permute-start.9) | collective-permute-done | bytes 221216 | tf_op jit(solution)/shard_map/ppermute | solution.py:229
  84.3 0.6 copy-done.11
  84.9 0.7 copy-done.12
  85.6 0.6 pad_add_fusion.where_ref
  86.2 1.2 collective-permute-done.18.refs_13_
  87.4 17.3 %attention_core.1 = (bf16[512,768]{1,0:T(8,128)(2,1)}, bf16[512,768]{1,0:T(8,128)(2,1)}, bf16[4,8,24,1152]{3,2,1,0:T(8,128)(2,1)}, bf16[4,8,24,1152]{3,2,1,0:T(8,128)(2,1)}) custom-call(s32[4]{0:T(128)} %pad_add_fusion.where_ref, bf16[128,4,1152]{2,1,0:T(4,128)(2,1)} %copy-done.1, bf16[512,768]{1,0:T(8,128)(2,1)} %copy-done.8, ...), custom_call_target="tpu_custom_call" | custom-call | flops 5435817984 | bytes 8388608 | tf_op jit(solution)/shard_map/attention_core/pallas_call | solution.py:122
  104.9 1.0 collective-permute-start.24
  105.9 2.8 %collective-permute-done.21.other_ref = bf16[4,8,24,1152]{3,2,1,0:T(8,128)(2,1)S(1)} collective-permute-done((bf16[4,8,24,1152]{3,2,1,0:T(8,128)(2,1)}, bf16[4,8,24,1152]{3,2,1,0:T(8,128)(2,1)S(1)}, u32[]{:S(2)}, u32[]{:S(2)}) %collective-permute-start.21) | collective-permute-done | bytes 1769504 | tf_op jit(solution)/shard_map/ppermute | solution.py:257
  108.7 1.5 copy-done.2
  110.6 1.4 collective-permute-start.22
  112.0 1.9 %collective-permute-start.23 = (bf16[4,24,1152]{2,1,0:T(8,128)(2,1)S(1)}, bf16[4,24,1152]{2,1,0:T(8,128)(2,1)S(1)}, u32[]{:S(2)}, u32[]{:S(2)}) collective-permute-start(bf16[4,24,1152]{2,1,0:T(8,128)(2,1)S(1)} %get-tuple-element.54), channel_id=1, source_target_pairs={{0,24},{8,0},{16,8},{24,16},{1,25},{9,1},{17,9},{25,17},{2,26},{10... | collective-permute-start | bytes 663560 | tf_op jit(solution)/shard_map/ppermute | solution.py:229
  113.9 1.7 collective-permute-start.26
  115.9 9.1 %collective-permute-done.24.b_ref = bf16[512,768]{1,0:T(8,128)(2,1)S(1)} collective-permute-done((bf16[512,768]{1,0:T(8,128)(2,1)}, bf16[512,768]{1,0:T(8,128)(2,1)S(1)}, u32[]{:S(2)}, u32[]{:S(2)}) %collective-permute-start.24) | collective-permute-done | bytes 786464 | tf_op jit(solution)/shard_map/ppermute | solution.py:318
  125.0 1.2 add_parts.1
  126.3 1.4 collective-permute-start.25
  127.7 1.9 %collective-permute-start.28 = (bf16[4,24,1152]{2,1,0:T(8,128)(2,1)S(1)}, bf16[4,24,1152]{2,1,0:T(8,128)(2,1)}, u32[]{:S(2)}, u32[]{:S(2)}) collective-permute-start(bf16[4,24,1152]{2,1,0:T(8,128)(2,1)S(1)} %add_convert_fusion), channel_id=1, source_target_pairs={{0,24},{8,0},{16,8},{24,16},{1,25},{9,1},{17,9},{25,17},{2,26},{10... | collective-permute-start | bytes 663560 | tf_op jit(solution)/shard_map/ppermute | solution.py:229
  129.6 10.0 %all-to-all-start.1 = ((bf16[128,4,768]{2,1,0:T(4,128)(2,1)}), bf16[128,4,768]{2,1,0:T(4,128)(2,1)}, u32[]{:S(2)}, u32[]{:S(2)}) async-start(bf16[128,4,768]{2,1,0:T(4,128)(2,1)} %add_parts.1), calls=%async_computation.1 | async-start | bytes 1572864 | tf_op jit(solution)/shard_map/all_to_all | solution.py:324
  139.6 1.4 convert_add_fusion.1
  141.2 1.1 collective-permute-start.30
  142.3 3.5 %collective-permute-start.31 = (bf16[4,12,1152]{2,1,0:T(8,128)(2,1)S(1)}, bf16[4,12,1152]{2,1,0:T(8,128)(2,1)S(1)}, u32[]{:S(2)}, u32[]{:S(2)}) collective-permute-start(bf16[4,12,1152]{2,1,0:T(8,128)(2,1)S(1)} %get-tuple-element.73), channel_id=1, source_target_pairs={{0,36},{4,32},{32,4},{36,0},{64,100},{68,96},{96,68},{100,64},{128... | collective-permute-start | bytes 331784 | tf_op jit(solution)/shard_map/ppermute | solution.py:233
  146.3 5.0 %collective-permute-done.30 = bf16[4,12,1152]{2,1,0:T(8,128)(2,1)S(1)} collective-permute-done((bf16[4,12,1152]{2,1,0:T(8,128)(2,1)S(1)}, bf16[4,12,1152]{2,1,0:T(8,128)(2,1)S(1)}, u32[]{:S(2)}, u32[]{:S(2)}) %collective-permute-start.30) | collective-permute-done | bytes 110624 | tf_op jit(solution)/shard_map/ppermute | solution.py:233
  151.3 10.4 %collective-permute-done.31 = bf16[4,12,1152]{2,1,0:T(8,128)(2,1)S(1)} collective-permute-done((bf16[4,12,1152]{2,1,0:T(8,128)(2,1)S(1)}, bf16[4,12,1152]{2,1,0:T(8,128)(2,1)S(1)}, u32[]{:S(2)}, u32[]{:S(2)}) %collective-permute-start.31) | collective-permute-done | bytes 110624 | tf_op jit(solution)/shard_map/ppermute | solution.py:233
  161.7 2.7 %collective-permute-done.29 = bf16[4,12,1152]{2,1,0:T(8,128)(2,1)S(1)} collective-permute-done((bf16[4,12,1152]{2,1,0:T(8,128)(2,1)S(1)}, bf16[4,12,1152]{2,1,0:T(8,128)(2,1)S(1)}, u32[]{:S(2)}, u32[]{:S(2)}) %collective-permute-start.29) | collective-permute-done | bytes 110624 | tf_op jit(solution)/shard_map/ppermute | solution.py:233
  164.5 2.5 %collective-permute-start.32 = (bf16[12,1152]{1,0:T(8,128)(2,1)S(1)}, bf16[12,1152]{1,0:T(8,128)(2,1)S(1)}, u32[]{:S(2)}, u32[]{:S(2)}) collective-permute-start(bf16[12,1152]{1,0:T(8,128)(2,1)S(1)} %get-tuple-element.78), channel_id=1, source_target_pairs={{0,64},{32,96},{64,0},{96,32},{128,192},{160,224},{192,128},{224,1... | collective-permute-start | bytes 82952 | tf_op jit(solution)/shard_map/ppermute | solution.py:233
  167.0 2.9 %collective-permute-start.34 = (bf16[12,1152]{1,0:T(8,128)(2,1)S(1)}, bf16[12,1152]{1,0:T(8,128)(2,1)S(1)}, u32[]{:S(2)}, u32[]{:S(2)}) collective-permute-start(bf16[12,1152]{1,0:T(8,128)(2,1)S(1)} %get-tuple-element.79), channel_id=1, source_target_pairs={{0,192},{32,224},{64,128},{96,160},{128,64},{160,96},{192,0},{224,... | collective-permute-start | bytes 82952 | tf_op jit(solution)/shard_map/ppermute | solution.py:233
  169.9 1.2 collective-permute-start.33
  171.1 2.3 %reshape.29 = bf16[1,512,768]{2,1,0:T(8,128)(2,1)} reshape(bf16[128,4,768]{2,1,0:T(4,128)(2,1)} %all-to-all-done.1) | data formatting | bytes 1572864 | tf_op jit(solution)/shard_map/reshape | solution.py:327
  173.4 4.4 %collective-permute-done.33 = bf16[12,1152]{1,0:T(8,128)(2,1)S(1)} collective-permute-done((bf16[12,1152]{1,0:T(8,128)(2,1)S(1)}, bf16[12,1152]{1,0:T(8,128)(2,1)S(1)}, u32[]{:S(2)}, u32[]{:S(2)}) %collective-permute-start.33) | collective-permute-done | bytes 27680 | tf_op jit(solution)/shard_map/ppermute | solution.py:233
  177.8 0.7 reshape.30
  (91 shorter events, 5.5 us)
Async XLA Ops:
  0.6 9.8 %copy-start = (bf16[1,512,1536]{2,1,0:T(8,128)(2,1)S(1)}, bf16[1,512,1536]{2,1,0:T(8,128)(2,1)}, u32[]{:S(2)}) copy-start(bf16[1,512,1536]{2,1,0:T(8,128)(2,1)} %param.3) | copy-start | bytes 4718596
  0.6 9.9 %copy-start.4 = (bf16[1,512,384]{2,1,0:T(8,128)(2,1)S(1)}, bf16[1,512,384]{2,1,0:T(8,128)(2,1)}, u32[]{:S(2)}) copy-start(bf16[1,512,384]{2,1,0:T(8,128)(2,1)} %param.4) | copy-start | bytes 1179652
  1.6 11.0 %collective-permute-start.2 = (bf16[12,1152]{1,0:T(8,128)(2,1)S(1)}, bf16[12,1152]{1,0:T(8,128)(2,1)S(1)}, u32[]{:S(2)}, u32[]{:S(2)}) collective-permute-start(bf16[12,1152]{1,0:T(8,128)(2,1)S(1)} %bitcast.46), channel_id=1, source_target_pairs={{0,192},{32,224},{64,128},{96,160},{128,64},{160,96},{192,0},{224,... | collective-permute-start | bytes 82952 | tf_op jit(solution)/shard_map/ppermute | solution.py:233
  8.0 8.4 %collective-permute-start.1 = (bf16[12,1152]{1,0:T(8,128)(2,1)S(1)}, bf16[12,1152]{1,0:T(8,128)(2,1)S(1)}, u32[]{:S(2)}, u32[]{:S(2)}) collective-permute-start(bf16[12,1152]{1,0:T(8,128)(2,1)S(1)} %bitcast.47), channel_id=1, source_target_pairs={{0,128},{32,160},{64,192},{96,224},{128,0},{160,32},{192,64},{224,... | collective-permute-start | bytes 82952 | tf_op jit(solution)/shard_map/ppermute | solution.py:233
  9.0 7.4 %collective-permute-start = (bf16[12,1152]{1,0:T(8,128)(2,1)S(1)}, bf16[12,1152]{1,0:T(8,128)(2,1)S(1)}, u32[]{:S(2)}, u32[]{:S(2)}) collective-permute-start(bf16[12,1152]{1,0:T(8,128)(2,1)S(1)} %bitcast.48), channel_id=1, source_target_pairs={{0,64},{32,96},{64,0},{96,32},{128,192},{160,224},{192,128},{224,1... | collective-permute-start | bytes 82952 | tf_op jit(solution)/shard_map/ppermute | solution.py:233
  16.4 16.3 %collective-permute-start.4 = (bf16[4,12,1152]{2,1,0:T(8,128)(2,1)S(1)}, bf16[4,12,1152]{2,1,0:T(8,128)(2,1)S(1)}, u32[]{:S(2)}, u32[]{:S(2)}) collective-permute-start(bf16[4,12,1152]{2,1,0:T(8,128)(2,1)S(1)} %pad_maximum_fusion.4), channel_id=1, source_target_pairs={{0,32},{4,36},{32,0},{36,4},{64,96},{68,100},{96,64},{100,68},{128... | collective-permute-start | bytes 331784 | tf_op jit(solution)/shard_map/ppermute | solution.py:233
  17.6 15.1 %collective-permute-start.5 = (bf16[4,12,1152]{2,1,0:T(8,128)(2,1)S(1)}, bf16[4,12,1152]{2,1,0:T(8,128)(2,1)S(1)}, u32[]{:S(2)}, u32[]{:S(2)}) collective-permute-start(bf16[4,12,1152]{2,1,0:T(8,128)(2,1)S(1)} %pad_maximum_fusion.4), channel_id=1, source_target_pairs={{0,36},{4,32},{32,4},{36,0},{64,100},{68,96},{96,68},{100,64},{128... | collective-permute-start | bytes 331784 | tf_op jit(solution)/shard_map/ppermute | solution.py:233
  19.4 13.5 %collective-permute-start.3 = (bf16[4,12,1152]{2,1,0:T(8,128)(2,1)S(1)}, bf16[4,12,1152]{2,1,0:T(8,128)(2,1)S(1)}, u32[]{:S(2)}, u32[]{:S(2)}) collective-permute-start(bf16[4,12,1152]{2,1,0:T(8,128)(2,1)S(1)} %pad_maximum_fusion.4), channel_id=1, source_target_pairs={{0,4},{4,0},{32,36},{36,32},{64,68},{68,64},{96,100},{100,96},{128... | collective-permute-start | bytes 331784 | tf_op jit(solution)/shard_map/ppermute | solution.py:233
  21.5 43.1 %all-to-all-start = ((bf16[128,4,1152]{2,1,0:T(4,128)(2,1)}), bf16[128,4,1152]{2,1,0:T(4,128)(2,1)S(1)}, u32[]{:S(2)}, u32[]{:S(2)}) async-start(bf16[128,4,1152]{2,1,0:T(4,128)(2,1)} %reshape.25), calls=%async_computation | async-start | bytes 2359296 | tf_op jit(solution)/shard_map/all_to_all | solution.py:300
  33.0 46.4 %copy-start.5 = (bf16[2,2,24,1152]{3,2,1,0:T(8,128)(2,1)}, bf16[2,2,24,1152]{3,2,1,0:T(8,128)(2,1)S(1)}, u32[]{:S(2)}) copy-start(bf16[2,2,24,1152]{3,2,1,0:T(8,128)(2,1)S(1)} %copy.8) | copy-start | bytes 663556
  33.1 54.3 %copy-start.6 = (bf16[2,2,24,1152]{3,2,1,0:T(8,128)(2,1)}, bf16[2,2,24,1152]{3,2,1,0:T(8,128)(2,1)S(1)}, u32[]{:S(2)}) copy-start(bf16[2,2,24,1152]{3,2,1,0:T(8,128)(2,1)S(1)} %copy.7) | copy-start | bytes 663556
  64.6 22.8 %copy-start.1 = (bf16[128,4,1152]{2,1,0:T(4,128)(2,1)}, bf16[128,4,1152]{2,1,0:T(4,128)(2,1)S(1)}, u32[]{:S(2)}) copy-start(bf16[128,4,1152]{2,1,0:T(4,128)(2,1)S(1)} %all-to-all-done.x_ref.x_hbm) | copy-start | bytes 3538948
  64.8 18.6 %collective-permute-start.12 = (bf16[512,768]{1,0:T(8,128)(2,1)S(1)}, bf16[512,768]{1,0:T(8,128)(2,1)S(1)}, u32[]{:S(2)}, u32[]{:S(2)}) collective-permute-start(bf16[512,768]{1,0:T(8,128)(2,1)S(1)} %part_rows.1), channel_id=1, source_target_pairs={{0,1},{1,0},{2,3},{3,2},{4,5},{5,4},{6,7},{7,6},{8,9},{9,8},{10,11... | collective-permute-start | bytes 2359304 | tf_op jit(solution)/shard_map/ppermute | solution.py:304
  65.7 8.3 %collective-permute-start.8 = (bf16[4,24,1152]{2,1,0:T(8,128)(2,1)S(1)}, bf16[4,24,1152]{2,1,0:T(8,128)(2,1)S(1)}, u32[]{:S(2)}, u32[]{:S(2)}) collective-permute-start(bf16[4,24,1152]{2,1,0:T(8,128)(2,1)S(1)} %bitcast.38), channel_id=1, source_target_pairs={{0,8},{8,16},{16,24},{24,0},{1,9},{9,17},{17,25},{25,1},{2,10},{10... | collective-permute-start | bytes 663560 | tf_op jit(solution)/shard_map/ppermute | solution.py:229
  65.9 8.9 %collective-permute-start.7 = (bf16[4,24,1152]{2,1,0:T(8,128)(2,1)S(1)}, bf16[4,24,1152]{2,1,0:T(8,128)(2,1)}, u32[]{:S(2)}, u32[]{:S(2)}) collective-permute-start(bf16[4,24,1152]{2,1,0:T(8,128)(2,1)S(1)} %bitcast.34), channel_id=1, source_target_pairs={{0,24},{8,0},{16,8},{24,16},{1,25},{9,1},{17,9},{25,17},{2,26},{10... | collective-permute-start | bytes 663560 | tf_op jit(solution)/shard_map/ppermute | solution.py:229
  68.9 10.4 %collective-permute-start.6 = (bf16[4,24,1152]{2,1,0:T(8,128)(2,1)S(1)}, bf16[4,24,1152]{2,1,0:T(8,128)(2,1)}, u32[]{:S(2)}, u32[]{:S(2)}) collective-permute-start(bf16[4,24,1152]{2,1,0:T(8,128)(2,1)S(1)} %bitcast.39), channel_id=1, source_target_pairs={{0,24},{8,0},{16,8},{24,16},{1,25},{9,1},{17,9},{25,17},{2,26},{10... | collective-permute-start | bytes 663560 | tf_op jit(solution)/shard_map/ppermute | solution.py:229
  68.9 10.4 %collective-permute-start.11 = (bf16[4,24,1152]{2,1,0:T(8,128)(2,1)S(1)}, bf16[4,24,1152]{2,1,0:T(8,128)(2,1)}, u32[]{:S(2)}, u32[]{:S(2)}) collective-permute-start(bf16[4,24,1152]{2,1,0:T(8,128)(2,1)S(1)} %bitcast.35), channel_id=1, source_target_pairs={{0,8},{8,16},{16,24},{24,0},{1,9},{9,17},{17,25},{25,1},{2,10},{10... | collective-permute-start | bytes 663560 | tf_op jit(solution)/shard_map/ppermute | solution.py:229
  74.0 13.4 %copy-start.9 = (bf16[4,24,1152]{2,1,0:T(8,128)(2,1)}, bf16[4,24,1152]{2,1,0:T(8,128)(2,1)S(1)}, u32[]{:S(2)}) copy-start(bf16[4,24,1152]{2,1,0:T(8,128)(2,1)S(1)} %collective-permute-done.8.refs_6_) | copy-start | bytes 663556
  74.0 8.6 %collective-permute-start.9 = (bf16[4,24,1152]{2,1,0:T(8,128)(2,1)S(1)}, bf16[4,24,1152]{2,1,0:T(8,128)(2,1)}, u32[]{:S(2)}, u32[]{:S(2)}) collective-permute-start(bf16[4,24,1152]{2,1,0:T(8,128)(2,1)S(1)} %collective-permute-done.8.refs_6_), channel_id=1, source_target_pairs={{0,8},{8,16},{16,24},{24,0},{1,9},{9,17},{17,25},{25,1},{2,10},{10... | collective-permute-start | bytes 663560 | tf_op jit(solution)/shard_map/ppermute | solution.py:229
  74.8 7.8 %collective-permute-start.10 = (bf16[4,24,1152]{2,1,0:T(8,128)(2,1)}, bf16[4,24,1152]{2,1,0:T(8,128)(2,1)}, u32[]{:S(2)}, u32[]{:S(2)}) collective-permute-start(bf16[4,24,1152]{2,1,0:T(8,128)(2,1)} %collective-permute-done.7.refs_3_), channel_id=1, source_target_pairs={{0,24},{8,0},{16,8},{24,16},{1,25},{9,1},{17,9},{25,17},{2,26},{10... | collective-permute-start | bytes 663560 | tf_op jit(solution)/shard_map/ppermute | solution.py:229
  79.4 4.0 %collective-permute-start.13 = (bf16[4,24,1152]{2,1,0:T(8,128)(2,1)S(1)}, bf16[4,24,1152]{2,1,0:T(8,128)(2,1)S(1)}, u32[]{:S(2)}, u32[]{:S(2)}) collective-permute-start(bf16[4,24,1152]{2,1,0:T(8,128)(2,1)S(1)} %bitcast.40), channel_id=1, source_target_pairs={{0,2},{2,0},{1,3},{3,1},{4,6},{6,4},{5,7},{7,5},{8,10},{10,8},{9,1... | collective-permute-start | bytes 663560 | tf_op jit(solution)/shard_map/ppermute | solution.py:312
  79.4 4.5 %collective-permute-start.14 = (bf16[4,24,1152]{2,1,0:T(8,128)(2,1)S(1)}, bf16[4,24,1152]{2,1,0:T(8,128)(2,1)S(1)}, u32[]{:S(2)}, u32[]{:S(2)}) collective-permute-start(bf16[4,24,1152]{2,1,0:T(8,128)(2,1)S(1)} %bitcast.36), channel_id=1, source_target_pairs={{0,2},{2,0},{1,3},{3,1},{4,6},{6,4},{5,7},{7,5},{8,10},{10,8},{9,1... | collective-permute-start | bytes 663560 | tf_op jit(solution)/shard_map/ppermute | solution.py:312
  82.6 1.7 collective-permute-start.19
  82.6 3.6 %collective-permute-start.15 = (bf16[4,24,1152]{2,1,0:T(8,128)(2,1)}, bf16[4,24,1152]{2,1,0:T(8,128)(2,1)}, u32[]{:S(2)}, u32[]{:S(2)}) collective-permute-start(bf16[4,24,1152]{2,1,0:T(8,128)(2,1)} %collective-permute-done.6.refs_2_), channel_id=1, source_target_pairs={{0,2},{2,0},{1,3},{3,1},{4,6},{6,4},{5,7},{7,5},{8,10},{10,8},{9,1... | collective-permute-start | bytes 663560 | tf_op jit(solution)/shard_map/ppermute | solution.py:312
  83.3 0.9 copy-start.8
  83.3 2.8 %collective-permute-start.20 = (bf16[4,24,1152]{2,1,0:T(8,128)(2,1)}, bf16[4,24,1152]{2,1,0:T(8,128)(2,1)}, u32[]{:S(2)}, u32[]{:S(2)}) collective-permute-start(bf16[4,24,1152]{2,1,0:T(8,128)(2,1)} %collective-permute-done.11.refs_7_), channel_id=1, source_target_pairs={{0,2},{2,0},{1,3},{3,1},{4,6},{6,4},{5,7},{7,5},{8,10},{10,8},{9,1... | collective-permute-start | bytes 663560 | tf_op jit(solution)/shard_map/ppermute | solution.py:312
  83.3 0.9 copy-start.10
  83.4 2.8 %collective-permute-start.16 = (bf16[4,24,1152]{2,1,0:T(8,128)(2,1)}, bf16[4,24,1152]{2,1,0:T(8,128)(2,1)}, u32[]{:S(2)}, u32[]{:S(2)}) collective-permute-start(bf16[4,24,1152]{2,1,0:T(8,128)(2,1)} %collective-permute-done.7.refs_3_), channel_id=1, source_target_pairs={{0,2},{2,0},{1,3},{3,1},{4,6},{6,4},{5,7},{7,5},{8,10},{10,8},{9,1... | collective-permute-start | bytes 663560 | tf_op jit(solution)/shard_map/ppermute | solution.py:312
  84.2 2.0 %collective-permute-start.17 = (bf16[4,24,1152]{2,1,0:T(8,128)(2,1)}, bf16[4,24,1152]{2,1,0:T(8,128)(2,1)S(1)}, u32[]{:S(2)}, u32[]{:S(2)}) collective-permute-start(bf16[4,24,1152]{2,1,0:T(8,128)(2,1)} %collective-permute-done.9.refs_4_), channel_id=1, source_target_pairs={{0,2},{2,0},{1,3},{3,1},{4,6},{6,4},{5,7},{7,5},{8,10},{10,8},{9,1... | collective-permute-start | bytes 663560 | tf_op jit(solution)/shard_map/ppermute | solution.py:314
  85.6 1.8 %collective-permute-start.18 = (bf16[4,24,1152]{2,1,0:T(8,128)(2,1)}, bf16[4,24,1152]{2,1,0:T(8,128)(2,1)}, u32[]{:S(2)}, u32[]{:S(2)}) collective-permute-start(bf16[4,24,1152]{2,1,0:T(8,128)(2,1)} %collective-permute-done.10.refs_5_), channel_id=1, source_target_pairs={{0,2},{2,0},{1,3},{3,1},{4,6},{6,4},{5,7},{7,5},{8,10},{10,8},{9,1... | collective-permute-start | bytes 663560 | tf_op jit(solution)/shard_map/ppermute | solution.py:314
  86.2 1.2 copy-start.13
  104.7 4.0 %collective-permute-start.21 = (bf16[4,8,24,1152]{3,2,1,0:T(8,128)(2,1)}, bf16[4,8,24,1152]{3,2,1,0:T(8,128)(2,1)S(1)}, u32[]{:S(2)}, u32[]{:S(2)}) collective-permute-start(bf16[4,8,24,1152]{3,2,1,0:T(8,128)(2,1)} %get-tuple-element.50), channel_id=1, source_target_pairs={{0,2},{2,0},{1,3},{3,1},{4,6},{6,4},{5,7},{7,5},{8,10},{10,8},{9,1... | collective-permute-start | bytes 5308424 | tf_op jit(solution)/shard_map/ppermute | solution.py:257
  104.9 20.0 %collective-permute-start.24 = (bf16[512,768]{1,0:T(8,128)(2,1)}, bf16[512,768]{1,0:T(8,128)(2,1)S(1)}, u32[]{:S(2)}, u32[]{:S(2)}) collective-permute-start(bf16[512,768]{1,0:T(8,128)(2,1)} %get-tuple-element.55), channel_id=1, source_target_pairs={{0,1},{1,0},{2,3},{3,2},{4,5},{5,4},{6,7},{7,6},{8,9},{9,8},{10,11... | collective-permute-start | bytes 2359304 | tf_op jit(solution)/shard_map/ppermute | solution.py:318
  108.7 1.5 copy-start.2
  110.2 14.8 %copy-start.3 = (bf16[512,768]{1,0:T(8,128)(2,1)S(1)}, bf16[512,768]{1,0:T(8,128)(2,1)}, u32[]{:S(2)}) copy-start(bf16[512,768]{1,0:T(8,128)(2,1)} %get-tuple-element.59.a_ref) | copy-start | bytes 2359300
  110.6 14.4 %collective-permute-start.22 = (bf16[4,24,1152]{2,1,0:T(8,128)(2,1)S(1)}, bf16[4,24,1152]{2,1,0:T(8,128)(2,1)S(1)}, u32[]{:S(2)}, u32[]{:S(2)}) collective-permute-start(bf16[4,24,1152]{2,1,0:T(8,128)(2,1)S(1)} %get-tuple-element.53), channel_id=1, source_target_pairs={{0,8},{8,16},{16,24},{24,0},{1,9},{9,17},{17,25},{25,1},{2,10},{10... | collective-permute-start | bytes 663560 | tf_op jit(solution)/shard_map/ppermute | solution.py:229
  112.0 13.0 %collective-permute-start.23 = (bf16[4,24,1152]{2,1,0:T(8,128)(2,1)S(1)}, bf16[4,24,1152]{2,1,0:T(8,128)(2,1)S(1)}, u32[]{:S(2)}, u32[]{:S(2)}) collective-permute-start(bf16[4,24,1152]{2,1,0:T(8,128)(2,1)S(1)} %get-tuple-element.54), channel_id=1, source_target_pairs={{0,24},{8,0},{16,8},{24,16},{1,25},{9,1},{17,9},{25,17},{2,26},{10... | collective-permute-start | bytes 663560 | tf_op jit(solution)/shard_map/ppermute | solution.py:229
  113.9 25.7 %collective-permute-start.26 = (bf16[4,24,1152]{2,1,0:T(8,128)(2,1)S(1)}, bf16[4,24,1152]{2,1,0:T(8,128)(2,1)}, u32[]{:S(2)}, u32[]{:S(2)}) collective-permute-start(bf16[4,24,1152]{2,1,0:T(8,128)(2,1)S(1)} %get-tuple-element.62), channel_id=1, source_target_pairs={{0,24},{8,0},{16,8},{24,16},{1,25},{9,1},{17,9},{25,17},{2,26},{10... | collective-permute-start | bytes 663560 | tf_op jit(solution)/shard_map/ppermute | solution.py:229
  115.6 24.1 %collective-permute-start.27 = (bf16[4,24,1152]{2,1,0:T(8,128)(2,1)S(1)}, bf16[4,24,1152]{2,1,0:T(8,128)(2,1)}, u32[]{:S(2)}, u32[]{:S(2)}) collective-permute-start(bf16[4,24,1152]{2,1,0:T(8,128)(2,1)S(1)} %get-tuple-element.63), channel_id=1, source_target_pairs={{0,8},{8,16},{16,24},{24,0},{1,9},{9,17},{17,25},{25,1},{2,10},{10... | collective-permute-start | bytes 663560 | tf_op jit(solution)/shard_map/ppermute | solution.py:229
  126.3 13.3 %collective-permute-start.25 = (bf16[4,24,1152]{2,1,0:T(8,128)(2,1)S(1)}, bf16[4,24,1152]{2,1,0:T(8,128)(2,1)}, u32[]{:S(2)}, u32[]{:S(2)}) collective-permute-start(bf16[4,24,1152]{2,1,0:T(8,128)(2,1)S(1)} %add_convert_fusion.1), channel_id=1, source_target_pairs={{0,8},{8,16},{16,24},{24,0},{1,9},{9,17},{17,25},{25,1},{2,10},{10... | collective-permute-start | bytes 663560 | tf_op jit(solution)/shard_map/ppermute | solution.py:229
  127.7 11.9 %collective-permute-start.28 = (bf16[4,24,1152]{2,1,0:T(8,128)(2,1)S(1)}, bf16[4,24,1152]{2,1,0:T(8,128)(2,1)}, u32[]{:S(2)}, u32[]{:S(2)}) collective-permute-start(bf16[4,24,1152]{2,1,0:T(8,128)(2,1)S(1)} %add_convert_fusion), channel_id=1, source_target_pairs={{0,24},{8,0},{16,8},{24,16},{1,25},{9,1},{17,9},{25,17},{2,26},{10... | collective-permute-start | bytes 663560 | tf_op jit(solution)/shard_map/ppermute | solution.py:229
  129.6 34.8 %all-to-all-start.1 = ((bf16[128,4,768]{2,1,0:T(4,128)(2,1)}), bf16[128,4,768]{2,1,0:T(4,128)(2,1)}, u32[]{:S(2)}, u32[]{:S(2)}) async-start(bf16[128,4,768]{2,1,0:T(4,128)(2,1)} %add_parts.1), calls=%async_computation.1 | async-start | bytes 1572864 | tf_op jit(solution)/shard_map/all_to_all | solution.py:324
  141.2 10.0 %collective-permute-start.30 = (bf16[4,12,1152]{2,1,0:T(8,128)(2,1)S(1)}, bf16[4,12,1152]{2,1,0:T(8,128)(2,1)S(1)}, u32[]{:S(2)}, u32[]{:S(2)}) collective-permute-start(bf16[4,12,1152]{2,1,0:T(8,128)(2,1)S(1)} %get-tuple-element.72), channel_id=1, source_target_pairs={{0,4},{4,0},{32,36},{36,32},{64,68},{68,64},{96,100},{100,96},{128... | collective-permute-start | bytes 331784 | tf_op jit(solution)/shard_map/ppermute | solution.py:233
  142.3 19.3 %collective-permute-start.31 = (bf16[4,12,1152]{2,1,0:T(8,128)(2,1)S(1)}, bf16[4,12,1152]{2,1,0:T(8,128)(2,1)S(1)}, u32[]{:S(2)}, u32[]{:S(2)}) collective-permute-start(bf16[4,12,1152]{2,1,0:T(8,128)(2,1)S(1)} %get-tuple-element.73), channel_id=1, source_target_pairs={{0,36},{4,32},{32,4},{36,0},{64,100},{68,96},{96,68},{100,64},{128... | collective-permute-start | bytes 331784 | tf_op jit(solution)/shard_map/ppermute | solution.py:233
  145.8 18.6 %collective-permute-start.29 = (bf16[4,12,1152]{2,1,0:T(8,128)(2,1)S(1)}, bf16[4,12,1152]{2,1,0:T(8,128)(2,1)S(1)}, u32[]{:S(2)}, u32[]{:S(2)}) collective-permute-start(bf16[4,12,1152]{2,1,0:T(8,128)(2,1)S(1)} %slice.81), channel_id=1, source_target_pairs={{0,32},{4,36},{32,0},{36,4},{64,96},{68,100},{96,64},{100,68},{128... | collective-permute-start | bytes 331784 | tf_op jit(solution)/shard_map/ppermute | solution.py:233
  164.5 8.8 %collective-permute-start.32 = (bf16[12,1152]{1,0:T(8,128)(2,1)S(1)}, bf16[12,1152]{1,0:T(8,128)(2,1)S(1)}, u32[]{:S(2)}, u32[]{:S(2)}) collective-permute-start(bf16[12,1152]{1,0:T(8,128)(2,1)S(1)} %get-tuple-element.78), channel_id=1, source_target_pairs={{0,64},{32,96},{64,0},{96,32},{128,192},{160,224},{192,128},{224,1... | collective-permute-start | bytes 82952 | tf_op jit(solution)/shard_map/ppermute | solution.py:233
  167.0 6.3 %collective-permute-start.34 = (bf16[12,1152]{1,0:T(8,128)(2,1)S(1)}, bf16[12,1152]{1,0:T(8,128)(2,1)S(1)}, u32[]{:S(2)}, u32[]{:S(2)}) collective-permute-start(bf16[12,1152]{1,0:T(8,128)(2,1)S(1)} %get-tuple-element.79), channel_id=1, source_target_pairs={{0,192},{32,224},{64,128},{96,160},{128,64},{160,96},{192,0},{224,... | collective-permute-start | bytes 82952 | tf_op jit(solution)/shard_map/ppermute | solution.py:233
  169.9 7.9 %collective-permute-start.33 = (bf16[12,1152]{1,0:T(8,128)(2,1)S(1)}, bf16[12,1152]{1,0:T(8,128)(2,1)S(1)}, u32[]{:S(2)}, u32[]{:S(2)}) collective-permute-start(bf16[12,1152]{1,0:T(8,128)(2,1)S(1)} %get-tuple-element.80), channel_id=1, source_target_pairs={{0,128},{32,160},{64,192},{96,224},{128,0},{160,32},{192,64},{224,... | collective-permute-start | bytes 82952 | tf_op jit(solution)/shard_map/ppermute | solution.py:233
  (3 other events, 2.1 us)

commit v15 on v14

--- a/solution.py
+++ b/solution.py
@@ -10,7 +10,7 @@
 F = 128
 ROWS = 12
 VMEM_LIMIT = 16 * 2**20
-CORE_LIMIT = 56 * 2**20
+CORE_LIMIT = 48 * 2**20
 bf16, f32 = jnp.bfloat16, jnp.float32
 NT = (((1,), (1,)), ((), ()))
 TN = (((0,), (0,)), ((), ()))

time: 179 us -> 185 us (1.034)
  local copies, waits for them, and re-layouts: 9.14 us -> 14.3 us
    unnamed x30 -> x28, local copies, waits for them, and re-layouts: 4.77 us -> 9.96 us
  transfers between devices with their start and end apart: 37 -> 37, of which waited for: 15 -> 15; matrix products, arithmetic and copies ran while one was open for 4% -> 3% of each run, Pallas kernels for 1% -> 1%
where the time goes in v15:
time: 185 us
  waiting for transfers between devices  77.7 us (42%)
  starting transfers between devices  69.5 us (38%)
  Pallas kernels  19.8 us (11%)
  local copies, waits for them, and re-layouts  14.3 us (8%)
  other arithmetic  2.2 us (1%)
    all_to_all x1, waiting for transfers between devices, on_device(): tokens = lax.all_to_all(tokens, FR, 0, 0, tiled=True)  31.5 us
    ppermute x12, waiting for transfers between devices, across(): return lax.ppermute(x, axis, [(i, i ^ by) for i in range(size)])  26.2 us
    ppermute x12, starting transfers between devices, across(): return lax.ppermute(x, axis, [(i, i ^ by) for i in range(size)])  25.6 us
    ppermute x12, starting transfers between devices, shift(): return lax.ppermute(x, axis, [(i, (i + by) % size) for i in range(size)])  18.2 us
    pallas_call x1, Pallas kernels, core(): pl.pallas_call(core_kernel, out_shape=(jax.ShapeDtypeStruct((rows, part_c...  18.1 us
    all_to_all x1, starting transfers between devices, on_device(): tokens = lax.all_to_all(tokens, FR, 0, 0, tiled=True)  11.2 us
    all_to_all x1, starting transfers between devices, to_frames(): return lax.all_to_all(x, FR, 0, 0, tiled=True)  10.2 us
    unnamed x28, local copies, waits for them, and re-layouts  9.96 us
  transfers between devices with their start and end apart: 37, of which 15 were waited for; matrix products, arithmetic and copies ran while one was open for 3% of the time, Pallas kernels for 1%

profile of v15, /device:TPU:6, one launch (start us, length us, event | category | flops | bytes accessed | tf_op | source)
XLA Modules:
  0.0 184.5 jit_solution(10909379133614782670)
XLA Ops:
  0.7 0.9 pad.26
  1.6 6.4 %collective-permute-start.2 = (bf16[12,1152]{1,0:T(8,128)(2,1)S(1)}, bf16[12,1152]{1,0:T(8,128)(2,1)S(1)}, u32[]{:S(2)}, u32[]{:S(2)}) collective-permute-start(bf16[12,1152]{1,0:T(8,128)(2,1)S(1)} %bitcast.46), channel_id=1, source_target_pairs={{0,192},{32,224},{64,128},{96,160},{128,64},{160,96},{192,0},{224,... | collective-permute-start | bytes 82952 | tf_op jit(solution)/shard_map/ppermute | solution.py:233
  8.0 1.0 collective-permute-start.1
  9.0 1.5 collective-permute-start
  11.3 1.2 reshape.25
  12.6 3.8 %collective-permute-done.1 = bf16[12,1152]{1,0:T(8,128)(2,1)S(1)} collective-permute-done((bf16[12,1152]{1,0:T(8,128)(2,1)S(1)}, bf16[12,1152]{1,0:T(8,128)(2,1)S(1)}, u32[]{:S(2)}, u32[]{:S(2)}) %collective-permute-start.1) | collective-permute-done | bytes 27680 | tf_op jit(solution)/shard_map/ppermute | solution.py:233
  16.4 1.2 collective-permute-start.4
  17.6 1.8 collective-permute-start.5
  19.4 2.1 %collective-permute-start.3 = (bf16[4,12,1152]{2,1,0:T(8,128)(2,1)S(1)}, bf16[4,12,1152]{2,1,0:T(8,128)(2,1)S(1)}, u32[]{:S(2)}, u32[]{:S(2)}) collective-permute-start(bf16[4,12,1152]{2,1,0:T(8,128)(2,1)S(1)} %pad_maximum_fusion.4), channel_id=1, source_target_pairs={{0,4},{4,0},{32,36},{36,32},{64,68},{68,64},{96,100},{100,96},{128... | collective-permute-start | bytes 331784 | tf_op jit(solution)/shard_map/ppermute | solution.py:233
  21.5 11.2 %all-to-all-start = ((bf16[128,4,1152]{2,1,0:T(4,128)(2,1)}), bf16[128,4,1152]{2,1,0:T(4,128)(2,1)S(1)}, u32[]{:S(2)}, u32[]{:S(2)}) async-start(bf16[128,4,1152]{2,1,0:T(4,128)(2,1)} %reshape.25), calls=%async_computation | async-start | bytes 2359296 | tf_op jit(solution)/shard_map/all_to_all | solution.py:300
  33.1 31.5 %all-to-all-done.x_ref.x_hbm = bf16[128,4,1152]{2,1,0:T(4,128)(2,1)S(1)} async-done(((bf16[128,4,1152]{2,1,0:T(4,128)(2,1)}), bf16[128,4,1152]{2,1,0:T(4,128)(2,1)S(1)}, u32[]{:S(2)}, u32[]{:S(2)}) %all-to-all-start) | async-done | bytes 1179680 | tf_op jit(solution)/shard_map/all_to_all | solution.py:300
  64.8 0.9 collective-permute-start.12
  65.9 3.0 %collective-permute-start.7 = (bf16[4,24,1152]{2,1,0:T(8,128)(2,1)S(1)}, bf16[4,24,1152]{2,1,0:T(8,128)(2,1)}, u32[]{:S(2)}, u32[]{:S(2)}) collective-permute-start(bf16[4,24,1152]{2,1,0:T(8,128)(2,1)S(1)} %bitcast.34), channel_id=1, source_target_pairs={{0,24},{8,0},{16,8},{24,16},{1,25},{9,1},{17,9},{25,17},{2,26},{10... | collective-permute-start | bytes 663560 | tf_op jit(solution)/shard_map/ppermute | solution.py:229
  68.9 2.0 %collective-permute-start.11 = (bf16[4,24,1152]{2,1,0:T(8,128)(2,1)S(1)}, bf16[4,24,1152]{2,1,0:T(8,128)(2,1)}, u32[]{:S(2)}, u32[]{:S(2)}) collective-permute-start(bf16[4,24,1152]{2,1,0:T(8,128)(2,1)S(1)} %bitcast.35), channel_id=1, source_target_pairs={{0,8},{8,16},{16,24},{24,0},{1,9},{9,17},{17,25},{25,1},{2,10},{10... | collective-permute-start | bytes 663560 | tf_op jit(solution)/shard_map/ppermute | solution.py:229
  70.9 3.0 %collective-permute-done.8.refs_6_ = bf16[4,24,1152]{2,1,0:T(8,128)(2,1)S(1)} collective-permute-done((bf16[4,24,1152]{2,1,0:T(8,128)(2,1)S(1)}, bf16[4,24,1152]{2,1,0:T(8,128)(2,1)S(1)}, u32[]{:S(2)}, u32[]{:S(2)}) %collective-permute-start.8) | collective-permute-done | bytes 221216 | tf_op jit(solution)/shard_map/ppermute | solution.py:229
  74.8 3.8 %collective-permute-start.10 = (bf16[4,24,1152]{2,1,0:T(8,128)(2,1)}, bf16[4,24,1152]{2,1,0:T(8,128)(2,1)}, u32[]{:S(2)}, u32[]{:S(2)}) collective-permute-start(bf16[4,24,1152]{2,1,0:T(8,128)(2,1)} %collective-permute-done.7.refs_3_), channel_id=1, source_target_pairs={{0,24},{8,0},{16,8},{24,16},{1,25},{9,1},{17,9},{25,17},{2,26},{10... | collective-permute-start | bytes 663560 | tf_op jit(solution)/shard_map/ppermute | solution.py:229
  78.6 0.8 collective-permute-done.6.refs_2_
  79.9 2.7 %collective-permute-done.9.refs_4_ = bf16[4,24,1152]{2,1,0:T(8,128)(2,1)} collective-permute-done((bf16[4,24,1152]{2,1,0:T(8,128)(2,1)S(1)}, bf16[4,24,1152]{2,1,0:T(8,128)(2,1)}, u32[]{:S(2)}, u32[]{:S(2)}) %collective-permute-start.9) | collective-permute-done | bytes 221216 | tf_op jit(solution)/shard_map/ppermute | solution.py:229
  83.3 0.9 copy-done.3
  84.2 0.7 copy-done.5
  87.9 0.8 collective-permute-done.18.refs_13_
  88.8 1.1 copy-done.4
  89.9 0.9 copy-done.6
  90.8 0.9 copy-done.8
  91.8 0.9 copy-done.10
  92.7 18.1 %attention_core.1 = (bf16[512,768]{1,0:T(8,128)(2,1)S(1)}, bf16[512,768]{1,0:T(8,128)(2,1)S(1)}, bf16[4,8,24,1152]{3,2,1,0:T(8,128)(2,1)}, bf16[4,8,24,1152]{3,2,1,0:T(8,128)(2,1)}) custom-call(s32[4]{0:T(128)S(1)} %pad_add_fusion.where_ref, bf16[128,4,1152]{2,1,0:T(4,128)(2,1)} %copy-done.1, bf16[512,768]{1,0:T(8,128)(2,1)S(1)} %copy-done.4, ...), custom_call_target="tpu_custom_call" | custom-call | flops 5435817984 | bytes 8388608 | tf_op jit(solution)/shard_map/attention_core/pallas_call | solution.py:122
  111.2 0.9 collective-permute-start.24
  112.2 2.6 %collective-permute-done.21.other_ref = bf16[4,8,24,1152]{3,2,1,0:T(8,128)(2,1)S(1)} collective-permute-done((bf16[4,8,24,1152]{3,2,1,0:T(8,128)(2,1)}, bf16[4,8,24,1152]{3,2,1,0:T(8,128)(2,1)S(1)}, u32[]{:S(2)}, u32[]{:S(2)}) %collective-permute-start.21) | collective-permute-done | bytes 1769504 | tf_op jit(solution)/shard_map/ppermute | solution.py:257
  114.8 1.5 copy-done.2
  116.6 1.4 collective-permute-start.22
  118.1 2.1 %collective-permute-start.23 = (bf16[4,24,1152]{2,1,0:T(8,128)(2,1)S(1)}, bf16[4,24,1152]{2,1,0:T(8,128)(2,1)S(1)}, u32[]{:S(2)}, u32[]{:S(2)}) collective-permute-start(bf16[4,24,1152]{2,1,0:T(8,128)(2,1)S(1)} %get-tuple-element.54), channel_id=1, source_target_pairs={{0,24},{8,0},{16,8},{24,16},{1,25},{9,1},{17,9},{25,17},{2,26},{10... | collective-permute-start | bytes 663560 | tf_op jit(solution)/shard_map/ppermute | solution.py:229
  120.1 1.7 collective-permute-start.26
  122.2 8.7 %collective-permute-done.24.b_ref = bf16[512,768]{1,0:T(8,128)(2,1)S(1)} collective-permute-done((bf16[512,768]{1,0:T(8,128)(2,1)S(1)}, bf16[512,768]{1,0:T(8,128)(2,1)S(1)}, u32[]{:S(2)}, u32[]{:S(2)}) %collective-permute-start.24) | collective-permute-done | bytes 786464 | tf_op jit(solution)/shard_map/ppermute | solution.py:318
  130.8 1.2 add_parts.1
  132.2 1.4 collective-permute-start.25
  133.6 1.9 %collective-permute-start.28 = (bf16[4,24,1152]{2,1,0:T(8,128)(2,1)S(1)}, bf16[4,24,1152]{2,1,0:T(8,128)(2,1)}, u32[]{:S(2)}, u32[]{:S(2)}) collective-permute-start(bf16[4,24,1152]{2,1,0:T(8,128)(2,1)S(1)} %add_convert_fusion), channel_id=1, source_target_pairs={{0,24},{8,0},{16,8},{24,16},{1,25},{9,1},{17,9},{25,17},{2,26},{10... | collective-permute-start | bytes 663560 | tf_op jit(solution)/shard_map/ppermute | solution.py:229
  135.5 10.2 %all-to-all-start.1 = ((bf16[128,4,768]{2,1,0:T(4,128)(2,1)}), bf16[128,4,768]{2,1,0:T(4,128)(2,1)}, u32[]{:S(2)}, u32[]{:S(2)}) async-start(bf16[128,4,768]{2,1,0:T(4,128)(2,1)} %add_parts.1), calls=%async_computation.1 | async-start | bytes 1572864 | tf_op jit(solution)/shard_map/all_to_all | solution.py:324
  145.7 1.4 convert_add_fusion.1
  147.3 1.0 collective-permute-start.30
  148.4 3.5 %collective-permute-start.31 = (bf16[4,12,1152]{2,1,0:T(8,128)(2,1)S(1)}, bf16[4,12,1152]{2,1,0:T(8,128)(2,1)S(1)}, u32[]{:S(2)}, u32[]{:S(2)}) collective-permute-start(bf16[4,12,1152]{2,1,0:T(8,128)(2,1)S(1)} %get-tuple-element.73), channel_id=1, source_target_pairs={{0,36},{4,32},{32,4},{36,0},{64,100},{68,96},{96,68},{100,64},{128... | collective-permute-start | bytes 331784 | tf_op jit(solution)/shard_map/ppermute | solution.py:233
  152.4 5.0 %collective-permute-done.30 = bf16[4,12,1152]{2,1,0:T(8,128)(2,1)S(1)} collective-permute-done((bf16[4,12,1152]{2,1,0:T(8,128)(2,1)S(1)}, bf16[4,12,1152]{2,1,0:T(8,128)(2,1)S(1)}, u32[]{:S(2)}, u32[]{:S(2)}) %collective-permute-start.30) | collective-permute-done | bytes 110624 | tf_op jit(solution)/shard_map/ppermute | solution.py:233
  157.4 10.3 %collective-permute-done.31 = bf16[4,12,1152]{2,1,0:T(8,128)(2,1)S(1)} collective-permute-done((bf16[4,12,1152]{2,1,0:T(8,128)(2,1)S(1)}, bf16[4,12,1152]{2,1,0:T(8,128)(2,1)S(1)}, u32[]{:S(2)}, u32[]{:S(2)}) %collective-permute-start.31) | collective-permute-done | bytes 110624 | tf_op jit(solution)/shard_map/ppermute | solution.py:233
  167.7 2.7 %collective-permute-done.29 = bf16[4,12,1152]{2,1,0:T(8,128)(2,1)S(1)} collective-permute-done((bf16[4,12,1152]{2,1,0:T(8,128)(2,1)S(1)}, bf16[4,12,1152]{2,1,0:T(8,128)(2,1)S(1)}, u32[]{:S(2)}, u32[]{:S(2)}) %collective-permute-start.29) | collective-permute-done | bytes 110624 | tf_op jit(solution)/shard_map/ppermute | solution.py:233
  170.6 2.5 %collective-permute-start.32 = (bf16[12,1152]{1,0:T(8,128)(2,1)S(1)}, bf16[12,1152]{1,0:T(8,128)(2,1)S(1)}, u32[]{:S(2)}, u32[]{:S(2)}) collective-permute-start(bf16[12,1152]{1,0:T(8,128)(2,1)S(1)} %get-tuple-element.78), channel_id=1, source_target_pairs={{0,64},{32,96},{64,0},{96,32},{128,192},{160,224},{192,128},{224,1... | collective-permute-start | bytes 82952 | tf_op jit(solution)/shard_map/ppermute | solution.py:233
  173.1 2.9 %collective-permute-start.34 = (bf16[12,1152]{1,0:T(8,128)(2,1)S(1)}, bf16[12,1152]{1,0:T(8,128)(2,1)S(1)}, u32[]{:S(2)}, u32[]{:S(2)}) collective-permute-start(bf16[12,1152]{1,0:T(8,128)(2,1)S(1)} %get-tuple-element.79), channel_id=1, source_target_pairs={{0,192},{32,224},{64,128},{96,160},{128,64},{160,96},{192,0},{224,... | collective-permute-start | bytes 82952 | tf_op jit(solution)/shard_map/ppermute | solution.py:233
  176.0 1.2 collective-permute-start.33
  177.2 2.3 %reshape.29 = bf16[1,512,768]{2,1,0:T(8,128)(2,1)} reshape(bf16[128,4,768]{2,1,0:T(4,128)(2,1)} %all-to-all-done.1) | data formatting | bytes 1572864 | tf_op jit(solution)/shard_map/reshape | solution.py:327
  179.4 4.4 %collective-permute-done.33 = bf16[12,1152]{1,0:T(8,128)(2,1)S(1)} collective-permute-done((bf16[12,1152]{1,0:T(8,128)(2,1)S(1)}, bf16[12,1152]{1,0:T(8,128)(2,1)S(1)}, u32[]{:S(2)}, u32[]{:S(2)}) %collective-permute-start.33) | collective-permute-done | bytes 27680 | tf_op jit(solution)/shard_map/ppermute | solution.py:233
  (89 shorter events, 9.6 us)
Async XLA Ops:
  0.6 9.8 %copy-start = (bf16[1,512,1536]{2,1,0:T(8,128)(2,1)S(1)}, bf16[1,512,1536]{2,1,0:T(8,128)(2,1)}, u32[]{:S(2)}) copy-start(bf16[1,512,1536]{2,1,0:T(8,128)(2,1)} %param.3) | copy-start | bytes 4718596
  0.6 9.9 %copy-start.11 = (bf16[1,512,384]{2,1,0:T(8,128)(2,1)S(1)}, bf16[1,512,384]{2,1,0:T(8,128)(2,1)}, u32[]{:S(2)}) copy-start(bf16[1,512,384]{2,1,0:T(8,128)(2,1)} %param.4) | copy-start | bytes 1179652
  1.6 11.0 %collective-permute-start.2 = (bf16[12,1152]{1,0:T(8,128)(2,1)S(1)}, bf16[12,1152]{1,0:T(8,128)(2,1)S(1)}, u32[]{:S(2)}, u32[]{:S(2)}) collective-permute-start(bf16[12,1152]{1,0:T(8,128)(2,1)S(1)} %bitcast.46), channel_id=1, source_target_pairs={{0,192},{32,224},{64,128},{96,160},{128,64},{160,96},{192,0},{224,... | collective-permute-start | bytes 82952 | tf_op jit(solution)/shard_map/ppermute | solution.py:233
  8.0 8.4 %collective-permute-start.1 = (bf16[12,1152]{1,0:T(8,128)(2,1)S(1)}, bf16[12,1152]{1,0:T(8,128)(2,1)S(1)}, u32[]{:S(2)}, u32[]{:S(2)}) collective-permute-start(bf16[12,1152]{1,0:T(8,128)(2,1)S(1)} %bitcast.47), channel_id=1, source_target_pairs={{0,128},{32,160},{64,192},{96,224},{128,0},{160,32},{192,64},{224,... | collective-permute-start | bytes 82952 | tf_op jit(solution)/shard_map/ppermute | solution.py:233
  9.0 7.4 %collective-permute-start = (bf16[12,1152]{1,0:T(8,128)(2,1)S(1)}, bf16[12,1152]{1,0:T(8,128)(2,1)S(1)}, u32[]{:S(2)}, u32[]{:S(2)}) collective-permute-start(bf16[12,1152]{1,0:T(8,128)(2,1)S(1)} %bitcast.48), channel_id=1, source_target_pairs={{0,64},{32,96},{64,0},{96,32},{128,192},{160,224},{192,128},{224,1... | collective-permute-start | bytes 82952 | tf_op jit(solution)/shard_map/ppermute | solution.py:233
  10.5 0.8 copy-start.12
  16.4 16.3 %collective-permute-start.4 = (bf16[4,12,1152]{2,1,0:T(8,128)(2,1)S(1)}, bf16[4,12,1152]{2,1,0:T(8,128)(2,1)S(1)}, u32[]{:S(2)}, u32[]{:S(2)}) collective-permute-start(bf16[4,12,1152]{2,1,0:T(8,128)(2,1)S(1)} %pad_maximum_fusion.4), channel_id=1, source_target_pairs={{0,32},{4,36},{32,0},{36,4},{64,96},{68,100},{96,64},{100,68},{128... | collective-permute-start | bytes 331784 | tf_op jit(solution)/shard_map/ppermute | solution.py:233
  17.6 15.1 %collective-permute-start.5 = (bf16[4,12,1152]{2,1,0:T(8,128)(2,1)S(1)}, bf16[4,12,1152]{2,1,0:T(8,128)(2,1)S(1)}, u32[]{:S(2)}, u32[]{:S(2)}) collective-permute-start(bf16[4,12,1152]{2,1,0:T(8,128)(2,1)S(1)} %pad_maximum_fusion.4), channel_id=1, source_target_pairs={{0,36},{4,32},{32,4},{36,0},{64,100},{68,96},{96,68},{100,64},{128... | collective-permute-start | bytes 331784 | tf_op jit(solution)/shard_map/ppermute | solution.py:233
  19.4 13.5 %collective-permute-start.3 = (bf16[4,12,1152]{2,1,0:T(8,128)(2,1)S(1)}, bf16[4,12,1152]{2,1,0:T(8,128)(2,1)S(1)}, u32[]{:S(2)}, u32[]{:S(2)}) collective-permute-start(bf16[4,12,1152]{2,1,0:T(8,128)(2,1)S(1)} %pad_maximum_fusion.4), channel_id=1, source_target_pairs={{0,4},{4,0},{32,36},{36,32},{64,68},{68,64},{96,100},{100,96},{128... | collective-permute-start | bytes 331784 | tf_op jit(solution)/shard_map/ppermute | solution.py:233
  21.5 43.1 %all-to-all-start = ((bf16[128,4,1152]{2,1,0:T(4,128)(2,1)}), bf16[128,4,1152]{2,1,0:T(4,128)(2,1)S(1)}, u32[]{:S(2)}, u32[]{:S(2)}) async-start(bf16[128,4,1152]{2,1,0:T(4,128)(2,1)} %reshape.25), calls=%async_computation | async-start | bytes 2359296 | tf_op jit(solution)/shard_map/all_to_all | solution.py:300
  64.6 24.1 %copy-start.1 = (bf16[128,4,1152]{2,1,0:T(4,128)(2,1)}, bf16[128,4,1152]{2,1,0:T(4,128)(2,1)S(1)}, u32[]{:S(2)}) copy-start(bf16[128,4,1152]{2,1,0:T(4,128)(2,1)S(1)} %all-to-all-done.x_ref.x_hbm) | copy-start | bytes 3538948
  64.8 18.6 %collective-permute-start.12 = (bf16[512,768]{1,0:T(8,128)(2,1)S(1)}, bf16[512,768]{1,0:T(8,128)(2,1)S(1)}, u32[]{:S(2)}, u32[]{:S(2)}) collective-permute-start(bf16[512,768]{1,0:T(8,128)(2,1)S(1)} %part_rows.1), channel_id=1, source_target_pairs={{0,1},{1,0},{2,3},{3,2},{4,5},{5,4},{6,7},{7,6},{8,9},{9,8},{10,11... | collective-permute-start | bytes 2359304 | tf_op jit(solution)/shard_map/ppermute | solution.py:304
  65.7 8.3 %collective-permute-start.8 = (bf16[4,24,1152]{2,1,0:T(8,128)(2,1)S(1)}, bf16[4,24,1152]{2,1,0:T(8,128)(2,1)S(1)}, u32[]{:S(2)}, u32[]{:S(2)}) collective-permute-start(bf16[4,24,1152]{2,1,0:T(8,128)(2,1)S(1)} %bitcast.38), channel_id=1, source_target_pairs={{0,8},{8,16},{16,24},{24,0},{1,9},{9,17},{17,25},{25,1},{2,10},{10... | collective-permute-start | bytes 663560 | tf_op jit(solution)/shard_map/ppermute | solution.py:229
  65.9 8.9 %collective-permute-start.7 = (bf16[4,24,1152]{2,1,0:T(8,128)(2,1)S(1)}, bf16[4,24,1152]{2,1,0:T(8,128)(2,1)}, u32[]{:S(2)}, u32[]{:S(2)}) collective-permute-start(bf16[4,24,1152]{2,1,0:T(8,128)(2,1)S(1)} %bitcast.34), channel_id=1, source_target_pairs={{0,24},{8,0},{16,8},{24,16},{1,25},{9,1},{17,9},{25,17},{2,26},{10... | collective-permute-start | bytes 663560 | tf_op jit(solution)/shard_map/ppermute | solution.py:229
  68.9 10.4 %collective-permute-start.6 = (bf16[4,24,1152]{2,1,0:T(8,128)(2,1)S(1)}, bf16[4,24,1152]{2,1,0:T(8,128)(2,1)}, u32[]{:S(2)}, u32[]{:S(2)}) collective-permute-start(bf16[4,24,1152]{2,1,0:T(8,128)(2,1)S(1)} %bitcast.39), channel_id=1, source_target_pairs={{0,24},{8,0},{16,8},{24,16},{1,25},{9,1},{17,9},{25,17},{2,26},{10... | collective-permute-start | bytes 663560 | tf_op jit(solution)/shard_map/ppermute | solution.py:229
  68.9 10.4 %collective-permute-start.11 = (bf16[4,24,1152]{2,1,0:T(8,128)(2,1)S(1)}, bf16[4,24,1152]{2,1,0:T(8,128)(2,1)}, u32[]{:S(2)}, u32[]{:S(2)}) collective-permute-start(bf16[4,24,1152]{2,1,0:T(8,128)(2,1)S(1)} %bitcast.35), channel_id=1, source_target_pairs={{0,8},{8,16},{16,24},{24,0},{1,9},{9,17},{17,25},{25,1},{2,10},{10... | collective-permute-start | bytes 663560 | tf_op jit(solution)/shard_map/ppermute | solution.py:229
  74.0 8.6 %collective-permute-start.9 = (bf16[4,24,1152]{2,1,0:T(8,128)(2,1)S(1)}, bf16[4,24,1152]{2,1,0:T(8,128)(2,1)}, u32[]{:S(2)}, u32[]{:S(2)}) collective-permute-start(bf16[4,24,1152]{2,1,0:T(8,128)(2,1)S(1)} %collective-permute-done.8.refs_6_), channel_id=1, source_target_pairs={{0,8},{8,16},{16,24},{24,0},{1,9},{9,17},{17,25},{25,1},{2,10},{10... | collective-permute-start | bytes 663560 | tf_op jit(solution)/shard_map/ppermute | solution.py:229
  74.8 7.8 %collective-permute-start.10 = (bf16[4,24,1152]{2,1,0:T(8,128)(2,1)}, bf16[4,24,1152]{2,1,0:T(8,128)(2,1)}, u32[]{:S(2)}, u32[]{:S(2)}) collective-permute-start(bf16[4,24,1152]{2,1,0:T(8,128)(2,1)} %collective-permute-done.7.refs_3_), channel_id=1, source_target_pairs={{0,24},{8,0},{16,8},{24,16},{1,25},{9,1},{17,9},{25,17},{2,26},{10... | collective-permute-start | bytes 663560 | tf_op jit(solution)/shard_map/ppermute | solution.py:229
  79.4 4.9 %collective-permute-start.13 = (bf16[4,24,1152]{2,1,0:T(8,128)(2,1)S(1)}, bf16[4,24,1152]{2,1,0:T(8,128)(2,1)S(1)}, u32[]{:S(2)}, u32[]{:S(2)}) collective-permute-start(bf16[4,24,1152]{2,1,0:T(8,128)(2,1)S(1)} %bitcast.40), channel_id=1, source_target_pairs={{0,2},{2,0},{1,3},{3,1},{4,6},{6,4},{5,7},{7,5},{8,10},{10,8},{9,1... | collective-permute-start | bytes 663560 | tf_op jit(solution)/shard_map/ppermute | solution.py:312
  79.4 6.1 %collective-permute-start.14 = (bf16[4,24,1152]{2,1,0:T(8,128)(2,1)S(1)}, bf16[4,24,1152]{2,1,0:T(8,128)(2,1)S(1)}, u32[]{:S(2)}, u32[]{:S(2)}) collective-permute-start(bf16[4,24,1152]{2,1,0:T(8,128)(2,1)S(1)} %bitcast.36), channel_id=1, source_target_pairs={{0,2},{2,0},{1,3},{3,1},{4,6},{6,4},{5,7},{7,5},{8,10},{10,8},{9,1... | collective-permute-start | bytes 663560 | tf_op jit(solution)/shard_map/ppermute | solution.py:312
  82.6 3.6 %collective-permute-start.19 = (bf16[4,24,1152]{2,1,0:T(8,128)(2,1)S(1)}, bf16[4,24,1152]{2,1,0:T(8,128)(2,1)S(1)}, u32[]{:S(2)}, u32[]{:S(2)}) collective-permute-start(bf16[4,24,1152]{2,1,0:T(8,128)(2,1)S(1)} %collective-permute-done.8.refs_6_), channel_id=1, source_target_pairs={{0,2},{2,0},{1,3},{3,1},{4,6},{6,4},{5,7},{7,5},{8,10},{10,8},{9,1... | collective-permute-start | bytes 663560 | tf_op jit(solution)/shard_map/ppermute | solution.py:312
  82.6 4.8 %collective-permute-start.15 = (bf16[4,24,1152]{2,1,0:T(8,128)(2,1)}, bf16[4,24,1152]{2,1,0:T(8,128)(2,1)}, u32[]{:S(2)}, u32[]{:S(2)}) collective-permute-start(bf16[4,24,1152]{2,1,0:T(8,128)(2,1)} %collective-permute-done.6.refs_2_), channel_id=1, source_target_pairs={{0,2},{2,0},{1,3},{3,1},{4,6},{6,4},{5,7},{7,5},{8,10},{10,8},{9,1... | collective-permute-start | bytes 663560 | tf_op jit(solution)/shard_map/ppermute | solution.py:312
  83.3 0.9 copy-start.3
  84.2 3.2 %collective-permute-start.20 = (bf16[4,24,1152]{2,1,0:T(8,128)(2,1)}, bf16[4,24,1152]{2,1,0:T(8,128)(2,1)}, u32[]{:S(2)}, u32[]{:S(2)}) collective-permute-start(bf16[4,24,1152]{2,1,0:T(8,128)(2,1)} %collective-permute-done.11.refs_7_), channel_id=1, source_target_pairs={{0,2},{2,0},{1,3},{3,1},{4,6},{6,4},{5,7},{7,5},{8,10},{10,8},{9,1... | collective-permute-start | bytes 663560 | tf_op jit(solution)/shard_map/ppermute | solution.py:312
  84.2 0.7 copy-start.5
  84.9 2.5 %collective-permute-start.16 = (bf16[4,24,1152]{2,1,0:T(8,128)(2,1)}, bf16[4,24,1152]{2,1,0:T(8,128)(2,1)}, u32[]{:S(2)}, u32[]{:S(2)}) collective-permute-start(bf16[4,24,1152]{2,1,0:T(8,128)(2,1)} %collective-permute-done.7.refs_3_), channel_id=1, source_target_pairs={{0,2},{2,0},{1,3},{3,1},{4,6},{6,4},{5,7},{7,5},{8,10},{10,8},{9,1... | collective-permute-start | bytes 663560 | tf_op jit(solution)/shard_map/ppermute | solution.py:312
  86.1 1.8 collective-permute-start.17
  86.8 2.0 %collective-permute-start.18 = (bf16[4,24,1152]{2,1,0:T(8,128)(2,1)}, bf16[4,24,1152]{2,1,0:T(8,128)(2,1)}, u32[]{:S(2)}, u32[]{:S(2)}) collective-permute-start(bf16[4,24,1152]{2,1,0:T(8,128)(2,1)} %collective-permute-done.10.refs_5_), channel_id=1, source_target_pairs={{0,2},{2,0},{1,3},{3,1},{4,6},{6,4},{5,7},{7,5},{8,10},{10,8},{9,1... | collective-permute-start | bytes 663560 | tf_op jit(solution)/shard_map/ppermute | solution.py:314
  88.7 1.1 copy-start.4
  89.9 0.9 copy-start.6
  90.8 0.9 copy-start.8
  91.8 0.9 copy-start.10
  110.8 4.0 %collective-permute-start.21 = (bf16[4,8,24,1152]{3,2,1,0:T(8,128)(2,1)}, bf16[4,8,24,1152]{3,2,1,0:T(8,128)(2,1)S(1)}, u32[]{:S(2)}, u32[]{:S(2)}) collective-permute-start(bf16[4,8,24,1152]{3,2,1,0:T(8,128)(2,1)} %get-tuple-element.50), channel_id=1, source_target_pairs={{0,2},{2,0},{1,3},{3,1},{4,6},{6,4},{5,7},{7,5},{8,10},{10,8},{9,1... | collective-permute-start | bytes 5308424 | tf_op jit(solution)/shard_map/ppermute | solution.py:257
  111.2 19.6 %collective-permute-start.24 = (bf16[512,768]{1,0:T(8,128)(2,1)S(1)}, bf16[512,768]{1,0:T(8,128)(2,1)S(1)}, u32[]{:S(2)}, u32[]{:S(2)}) collective-permute-start(bf16[512,768]{1,0:T(8,128)(2,1)S(1)} %get-tuple-element.55), channel_id=1, source_target_pairs={{0,1},{1,0},{2,3},{3,2},{4,5},{5,4},{6,7},{7,6},{8,9},{9,8},{10,11... | collective-permute-start | bytes 2359304 | tf_op jit(solution)/shard_map/ppermute | solution.py:318
  114.8 1.5 copy-start.2
  116.6 14.2 %collective-permute-start.22 = (bf16[4,24,1152]{2,1,0:T(8,128)(2,1)S(1)}, bf16[4,24,1152]{2,1,0:T(8,128)(2,1)S(1)}, u32[]{:S(2)}, u32[]{:S(2)}) collective-permute-start(bf16[4,24,1152]{2,1,0:T(8,128)(2,1)S(1)} %get-tuple-element.53), channel_id=1, source_target_pairs={{0,8},{8,16},{16,24},{24,0},{1,9},{9,17},{17,25},{25,1},{2,10},{10... | collective-permute-start | bytes 663560 | tf_op jit(solution)/shard_map/ppermute | solution.py:229
  118.1 12.8 %collective-permute-start.23 = (bf16[4,24,1152]{2,1,0:T(8,128)(2,1)S(1)}, bf16[4,24,1152]{2,1,0:T(8,128)(2,1)S(1)}, u32[]{:S(2)}, u32[]{:S(2)}) collective-permute-start(bf16[4,24,1152]{2,1,0:T(8,128)(2,1)S(1)} %get-tuple-element.54), channel_id=1, source_target_pairs={{0,24},{8,0},{16,8},{24,16},{1,25},{9,1},{17,9},{25,17},{2,26},{10... | collective-permute-start | bytes 663560 | tf_op jit(solution)/shard_map/ppermute | solution.py:229
  120.1 25.6 %collective-permute-start.26 = (bf16[4,24,1152]{2,1,0:T(8,128)(2,1)S(1)}, bf16[4,24,1152]{2,1,0:T(8,128)(2,1)}, u32[]{:S(2)}, u32[]{:S(2)}) collective-permute-start(bf16[4,24,1152]{2,1,0:T(8,128)(2,1)S(1)} %get-tuple-element.62), channel_id=1, source_target_pairs={{0,24},{8,0},{16,8},{24,16},{1,25},{9,1},{17,9},{25,17},{2,26},{10... | collective-permute-start | bytes 663560 | tf_op jit(solution)/shard_map/ppermute | solution.py:229
  121.8 23.9 %collective-permute-start.27 = (bf16[4,24,1152]{2,1,0:T(8,128)(2,1)S(1)}, bf16[4,24,1152]{2,1,0:T(8,128)(2,1)}, u32[]{:S(2)}, u32[]{:S(2)}) collective-permute-start(bf16[4,24,1152]{2,1,0:T(8,128)(2,1)S(1)} %get-tuple-element.63), channel_id=1, source_target_pairs={{0,8},{8,16},{16,24},{24,0},{1,9},{9,17},{17,25},{25,1},{2,10},{10... | collective-permute-start | bytes 663560 | tf_op jit(solution)/shard_map/ppermute | solution.py:229
  132.2 13.5 %collective-permute-start.25 = (bf16[4,24,1152]{2,1,0:T(8,128)(2,1)S(1)}, bf16[4,24,1152]{2,1,0:T(8,128)(2,1)}, u32[]{:S(2)}, u32[]{:S(2)}) collective-permute-start(bf16[4,24,1152]{2,1,0:T(8,128)(2,1)S(1)} %add_convert_fusion.1), channel_id=1, source_target_pairs={{0,8},{8,16},{16,24},{24,0},{1,9},{9,17},{17,25},{25,1},{2,10},{10... | collective-permute-start | bytes 663560 | tf_op jit(solution)/shard_map/ppermute | solution.py:229
  133.6 12.1 %collective-permute-start.28 = (bf16[4,24,1152]{2,1,0:T(8,128)(2,1)S(1)}, bf16[4,24,1152]{2,1,0:T(8,128)(2,1)}, u32[]{:S(2)}, u32[]{:S(2)}) collective-permute-start(bf16[4,24,1152]{2,1,0:T(8,128)(2,1)S(1)} %add_convert_fusion), channel_id=1, source_target_pairs={{0,24},{8,0},{16,8},{24,16},{1,25},{9,1},{17,9},{25,17},{2,26},{10... | collective-permute-start | bytes 663560 | tf_op jit(solution)/shard_map/ppermute | solution.py:229
  135.5 35.0 %all-to-all-start.1 = ((bf16[128,4,768]{2,1,0:T(4,128)(2,1)}), bf16[128,4,768]{2,1,0:T(4,128)(2,1)}, u32[]{:S(2)}, u32[]{:S(2)}) async-start(bf16[128,4,768]{2,1,0:T(4,128)(2,1)} %add_parts.1), calls=%async_computation.1 | async-start | bytes 1572864 | tf_op jit(solution)/shard_map/all_to_all | solution.py:324
  147.3 10.1 %collective-permute-start.30 = (bf16[4,12,1152]{2,1,0:T(8,128)(2,1)S(1)}, bf16[4,12,1152]{2,1,0:T(8,128)(2,1)S(1)}, u32[]{:S(2)}, u32[]{:S(2)}) collective-permute-start(bf16[4,12,1152]{2,1,0:T(8,128)(2,1)S(1)} %get-tuple-element.72), channel_id=1, source_target_pairs={{0,4},{4,0},{32,36},{36,32},{64,68},{68,64},{96,100},{100,96},{128... | collective-permute-start | bytes 331784 | tf_op jit(solution)/shard_map/ppermute | solution.py:233
  148.4 19.3 %collective-permute-start.31 = (bf16[4,12,1152]{2,1,0:T(8,128)(2,1)S(1)}, bf16[4,12,1152]{2,1,0:T(8,128)(2,1)S(1)}, u32[]{:S(2)}, u32[]{:S(2)}) collective-permute-start(bf16[4,12,1152]{2,1,0:T(8,128)(2,1)S(1)} %get-tuple-element.73), channel_id=1, source_target_pairs={{0,36},{4,32},{32,4},{36,0},{64,100},{68,96},{96,68},{100,64},{128... | collective-permute-start | bytes 331784 | tf_op jit(solution)/shard_map/ppermute | solution.py:233
  151.9 18.6 %collective-permute-start.29 = (bf16[4,12,1152]{2,1,0:T(8,128)(2,1)S(1)}, bf16[4,12,1152]{2,1,0:T(8,128)(2,1)S(1)}, u32[]{:S(2)}, u32[]{:S(2)}) collective-permute-start(bf16[4,12,1152]{2,1,0:T(8,128)(2,1)S(1)} %slice.81), channel_id=1, source_target_pairs={{0,32},{4,36},{32,0},{36,4},{64,96},{68,100},{96,64},{100,68},{128... | collective-permute-start | bytes 331784 | tf_op jit(solution)/shard_map/ppermute | solution.py:233
  170.6 8.8 %collective-permute-start.32 = (bf16[12,1152]{1,0:T(8,128)(2,1)S(1)}, bf16[12,1152]{1,0:T(8,128)(2,1)S(1)}, u32[]{:S(2)}, u32[]{:S(2)}) collective-permute-start(bf16[12,1152]{1,0:T(8,128)(2,1)S(1)} %get-tuple-element.78), channel_id=1, source_target_pairs={{0,64},{32,96},{64,0},{96,32},{128,192},{160,224},{192,128},{224,1... | collective-permute-start | bytes 82952 | tf_op jit(solution)/shard_map/ppermute | solution.py:233
  173.1 6.4 %collective-permute-start.34 = (bf16[12,1152]{1,0:T(8,128)(2,1)S(1)}, bf16[12,1152]{1,0:T(8,128)(2,1)S(1)}, u32[]{:S(2)}, u32[]{:S(2)}) collective-permute-start(bf16[12,1152]{1,0:T(8,128)(2,1)S(1)} %get-tuple-element.79), channel_id=1, source_target_pairs={{0,192},{32,224},{64,128},{96,160},{128,64},{160,96},{192,0},{224,... | collective-permute-start | bytes 82952 | tf_op jit(solution)/shard_map/ppermute | solution.py:233
  176.0 7.9 %collective-permute-start.33 = (bf16[12,1152]{1,0:T(8,128)(2,1)S(1)}, bf16[12,1152]{1,0:T(8,128)(2,1)S(1)}, u32[]{:S(2)}, u32[]{:S(2)}) collective-permute-start(bf16[12,1152]{1,0:T(8,128)(2,1)S(1)} %get-tuple-element.80), channel_id=1, source_target_pairs={{0,128},{32,160},{64,192},{96,224},{128,0},{160,32},{192,64},{224,... | collective-permute-start | bytes 82952 | tf_op jit(solution)/shard_map/ppermute | solution.py:233
  (2 other events, 1.4 us)
